TPU v7x, 32 devices: a whole 2x2x4 slice. The times are simulated.
32 devices in a mesh: groups: 2 (over y), dp: 4 (over z), tensor: 2 (over x), sub: 2 (over core).
Axes of the slice: x: 2, y: 2, z: 4, core: 2. Of those that a mesh axis runs over, the one named last changes fastest.
Arguments:
- tokens: bfloat16 [5120, 16384], P(('groups', 'dp', 'sub'), 'tensor'), parts along dimension 0, may hold values from -6 to 6
- gate_weight: bfloat16 [1664, 16384], P(('dp', 'sub'), 'tensor'), may hold values from -0.046875 to 0.046875
- up_weight: bfloat16 [1664, 16384], P(('dp', 'sub'), 'tensor'), may hold values from -0.046875 to 0.046875
- down_weight: bfloat16 [1664, 16384], P(('dp', 'sub'), 'tensor'), may hold values from -0.21875 to 0.21875
Outputs:
- ffn_out: bfloat16 [5120, 16384], P(('groups', 'dp', 'sub'), 'tensor'), parts along dimension 0
There are 2 independent parts, one for each index of `groups`. A program takes and returns all parts, laid end to end along the dimension named above; an argument that names none is the same for every part. Nothing has to cross between parts.
All inputs are finite; a program needn't handle non-finite values.
Results may differ from a plain program's by a relative error of at most 0.014.
Values may be sent and summed in bfloat16 or wider, within the bound.
No kernel may reach another device: no remote copies, remote signals or barrier semaphores. Data moves between devices by JAX's collectives and lax.ppermute only.
A program may use at most 192 MiB of HBM per device.

v0:
```python
import jax
import jax.numpy as jnp
from jax import lax
from jax.sharding import PartitionSpec as P

STEPS = 2


def shifted(block, axis, distance):
    devices = range(lax.axis_size(axis))
    route = [((i - distance) % len(devices), i) for i in devices]
    return lax.ppermute(block, axis, route)


def apply_span(tokens, weights):
    span = weights.shape[1]
    both = weights[:2].reshape(2 * span, weights.shape[2])
    partial_value = lax.dot_general(
        tokens, both, (((1,), (1,)), ((), ())), preferred_element_type=jnp.float32
    )
    summed = lax.psum(partial_value.astype(jnp.bfloat16), "tensor").astype(jnp.float32)
    hidden = (jax.nn.silu(summed[:, :span]) * summed[:, span:]).astype(jnp.bfloat16)
    return jnp.dot(hidden, weights[2], preferred_element_type=jnp.float32)


def on_device(tokens, gate_weight, up_weight, down_weight):
    own_share = jnp.stack([gate_weight, up_weight, down_weight])
    total = jnp.zeros((tokens.shape[0], tokens.shape[1]), jnp.float32)
    current = lax.all_gather(own_share, "sub", axis=1, tiled=True)
    for step in range(STEPS):
        if step > 0:
            current = shifted(current, "dp", 1)
        total = total + apply_span(tokens, current)
    result = total.astype(jnp.bfloat16)
    return result


def solution(mesh):
    return jax.shard_map(
        on_device,
        mesh=mesh,
        in_specs=(
            P(("groups", "dp", "sub"), "tensor"),
            P(("dp", "sub"), "tensor"),
            P(("dp", "sub"), "tensor"),
            P(("dp", "sub"), "tensor"),
        ),
        out_specs=P(("groups", "dp", "sub"), "tensor"),
        check_vma=False,
    )
```

profile of v0, /device:TPU:0, one launch (start us, length us, event | category | flops | bytes accessed | tf_op | source)
XLA Modules:
  0.0 581.6 jit_solution(12640557937290656115)
XLA Ops:
  6.5 0.0 all-gather.2.cloned.1.call-start
  6.5 9.8 %pad_maximum_fusion = bf16[3,208,8192]{2,1,0:T(8,128)(2,1)} fusion(bf16[1,208,8192]{2,1,0:T(8,128)(2,1)} %bitcast.21, bf16[1,208,8192]{2,1,0:T(8,128)(2,1)} %bitcast.22, bf16[1,208,8192]{2,1,0:T(8,128)(2,1)} %bitcast.23), kind=kLoop, calls=%fused_computation.2 | loop fusion | flops 10223616 | bytes 20447232 | tf_op jit(solution)/shard_map/stack | solution.py:27
  16.4 0.0 all-gather.2.cloned.1.call-update
  16.4 0.0 all-reduce.3.cloned.1.call-start
  16.4 37.0 %all-gather.2.cloned.1.call-done = bf16[3,416,8192]{2,1,0:T(8,128)(2,1)} async-done(((bf16[3,208,8192]{2,1,0:T(8,128)(2,1)}), bf16[3,416,8192]{2,1,0:T(8,128)(2,1)}) %all-gather.2.cloned.1.call-update) | async-done | bytes 20447248 | tf_op jit(solution)/shard_map/all_gather | solution.py:29
  53.4 1.7 collective-permute-start
  55.1 0.0 slice-start
  55.1 10.4 %slice.32 = bf16[2,416,8192]{2,1,0:T(8,128)(2,1)} slice(bf16[3,416,8192]{2,1,0:T(8,128)(2,1)} %all-gather.2.cloned.1.call-done), slice={[0:2], [0:416], [0:8192]} | slice | bytes 27262976 | tf_op jit(solution)/shard_map/slice | solution.py:17
  65.5 0.0 slice-start.1
  65.5 16.2 %fusion.2 = bf16[320,832]{1,0:T(8,128)(2,1)} fusion(bf16[832,8192]{1,0:T(8,128)(2,1)} %bitcast.19, bf16[320,8192]{1,0:T(8,128)(2,1)} %param.4), kind=kOutput, calls=%fused_computation.8 | convolution fusion | flops 4362342400 | bytes 19406848 | tf_op jit(solution)/shard_map/dot_general | solution.py:18
  81.7 414.9 %collective-permute-done = bf16[3,416,8192]{2,1,0:T(8,128)(2,1)S(1)} collective-permute-done((bf16[3,416,8192]{2,1,0:T(8,128)(2,1)}, bf16[3,416,8192]{2,1,0:T(8,128)(2,1)S(1)}, u32[]{:S(2)}, u32[]{:S(2)}) %collective-permute-start) | collective-permute-done | bytes 20447264 | tf_op jit(solution)/shard_map/ppermute | solution.py:12
  496.5 0.0 copy-start
  496.5 8.0 %slice.36 = bf16[2,416,8192]{2,1,0:T(8,128)(2,1)} slice(bf16[3,416,8192]{2,1,0:T(8,128)(2,1)S(1)} %collective-permute-done), slice={[0:2], [0:416], [0:8192]} | slice | bytes 27262976 | tf_op jit(solution)/shard_map/slice | solution.py:17
  504.5 3.0 copy-done
  507.5 0.0 slice-done
  507.5 0.0 slice-done.1
  507.5 9.7 %fusion.3 = bf16[320,832]{1,0:T(8,128)(2,1)} fusion(bf16[832,8192]{1,0:T(8,128)(2,1)} %bitcast.20, bf16[320,8192]{1,0:T(8,128)(2,1)S(1)} %bitcast.25), kind=kOutput, calls=%fused_computation.9 | convolution fusion | flops 4362342400 | bytes 19406848 | tf_op jit(solution)/shard_map/dot_general | solution.py:18
  517.1 0.0 all-reduce.3.cloned.1.call-update
  517.1 41.8 %all-reduce.3.cloned.1.call-done = (bf16[320,832]{1,0:T(8,128)(2,1)}, bf16[320,832]{1,0:T(8,128)(2,1)}) async-done(((bf16[320,832]{1,0:T(8,128)(2,1)}, bf16[320,832]{1,0:T(8,128)(2,1)}), (bf16[320,832]{1,0:T(8,128)(2,1)}, bf16[320,832]{1,0:T(8,128)(2,1)})) %all-reduce.3.cloned.1.call-update) | async-done | bytes 1064976 | tf_op jit(solution)/shard_map/psum | solution.py:21
  559.0 1.1 convert_element_type.29
  560.1 1.1 convert_element_type.33
  561.3 5.2 fusion.1
  566.5 8.3 %fusion = bf16[320,8192]{1,0:T(8,128)(2,1)} fusion(f32[320,8192]{1,0:T(8,128)S(1)} %fusion.1, bf16[3,416,8192]{2,1,0:T(8,128)(2,1)} %copy-done, f32[320,832]{1,0:T(8,128)S(1)} %convert_element_type.33), kind=kOutput, calls=%fused_computation.1 | convolution fusion | flops 2187079680 | bytes 23855104 | tf_op jit(solution)/shard_map/dot_general | solution.py:23
  (1 shorter events, 0.0 us)
Async XLA Ops:
  6.5 46.9 %all-gather.2.cloned.1.call-start = ((), (), s32[]{:S(2)}) async-start(), calls=%async_computation | async-start | bytes 30670848 | tf_op jit(solution)/shard_map/all_gather | solution.py:29
  16.4 542.6 %all-reduce.3.cloned.1.call-start = ((), (), s32[]{:S(2)}) async-start(), calls=%async_computation.1 | async-start | bytes 2293760 | tf_op jit(solution)/shard_map/psum | solution.py:21
  53.4 443.1 %collective-permute-start = (bf16[3,416,8192]{2,1,0:T(8,128)(2,1)}, bf16[3,416,8192]{2,1,0:T(8,128)(2,1)S(1)}, u32[]{:S(2)}, u32[]{:S(2)}) collective-permute-start(bf16[3,416,8192]{2,1,0:T(8,128)(2,1)} %all-gather.2.cloned.1.call-done), channel_id=1, source_target_pairs={{12,0},{0,4},{4,8},{8,12},{13,1},{1,5},{5,9},{9,13},{14,2},{2,6},{... | collective-permute-start | bytes 61341704 | tf_op jit(solution)/shard_map/ppermute | solution.py:12
  55.1 452.3 %slice-start = ((s8[5242880]{0:T(1024)(128)(4,1)}), s8[4194304]{0:T(1024)(128)(4,1)S(1)}, s32[]{:S(2)}) async-start(s8[5242880]{0:T(1024)(128)(4,1)} %bitcast.24), calls=%async_computation.2 | async-start | bytes 8388608
  65.5 442.0 %slice-start.1 = ((s8[5242880]{0:T(1024)(128)(4,1)}), s8[1048576]{0:T(1024)(128)(4,1)S(1)}, s32[]{:S(2)}) async-start(s8[5242880]{0:T(1024)(128)(4,1)} %bitcast.24), calls=%async_computation.3 | async-start | bytes 2097152
  496.5 10.9 %copy-start = (bf16[3,416,8192]{2,1,0:T(8,128)(2,1)}, bf16[3,416,8192]{2,1,0:T(8,128)(2,1)S(1)}, u32[]{:S(2)}) copy-start(bf16[3,416,8192]{2,1,0:T(8,128)(2,1)S(1)} %collective-permute-done) | copy-start | bytes 61341700
Sparse Core Ops, SparseCore 0:
  16.5 36.8 all-gather.1
  517.3 41.6 all-reduce.2
where the time goes:
time: 582 us
  waiting for transfers between devices  494 us (85%)
  matrix products  39.3 us (7%)
  local copies, waits for them, and re-layouts  21.3 us (4%)
  between operations  13.4 us (2%)
  other arithmetic  12.1 us (2%)
    ppermute x1, waiting for transfers between devices, shifted(): return lax.ppermute(block, axis, route)  415 us
    psum x1, waiting for transfers between devices, apply_span(): lax.psum(partial_value.astype(jnp.bfloat16), 'tensor').astype(jnp.float32)  41.8 us
    all_gather x1, waiting for transfers between devices, on_device(): current = lax.all_gather(own_share, 'sub', axis=1, tiled=True)  37 us
    dot_general x2, matrix products, apply_span(): lax.dot_general(tokens, both, (((1,), (1,)), ((), ())), preferred_element...  25.8 us
    slice x2, local copies, waits for them, and re-layouts, apply_span(): both = weights[:2].reshape(2 * span, weights.shape[2])  18.3 us
    dot_general x2, matrix products, apply_span(): return jnp.dot(hidden, weights[2], preferred_element_type=jnp.float32)  13.5 us
  transfers between devices with their start and end apart: 3, of which 3 were waited for; matrix products, arithmetic and copies ran while one was open for 5% of the time, Pallas kernels for 0%

commit v1 on v0

v1 whole, which is shorter than its diff:
```python
import jax
import jax.numpy as jnp
from jax import lax
from jax.sharding import PartitionSpec as P

ROW_PARTS = 4
LANE_PARTS = 4


def shifted(block, axis, distance):
    devices = range(lax.axis_size(axis))
    route = [((i - distance) % len(devices), i) for i in devices]
    return lax.ppermute(block, axis, route)


def cuts(total, unit, parts):
    units = total // unit
    marks = [units * i // parts * unit for i in range(parts)] + [total]
    return list(zip(marks[:-1], marks[1:]))


def by_features(rows, units):
    return lax.dot_general(
        rows, units, (((1,), (1,)), ((), ())), preferred_element_type=jnp.float32
    )


def partial_values(row_sets, unit_sets):
    return jnp.concatenate(
        [
            jnp.concatenate([by_features(r, u) for u in unit_sets], axis=1)
            for r in row_sets
        ],
        axis=0,
    ).astype(jnp.bfloat16)


def over_slices(partial_value):
    total = partial_value.astype(jnp.float32)
    for distance in range(1, lax.axis_size("tensor")):
        total = total + shifted(partial_value, "tensor", distance).astype(jnp.float32)
    return total


def gated(gate, up):
    return (jax.nn.silu(gate) * up).astype(jnp.bfloat16)


def on_device(tokens, gate_weight, up_weight, down_weight):
    units, width = gate_weight.shape
    rows = tokens.shape[0]
    first = lax.axis_index("groups") == 0

    def mate(block):
        return shifted(block, "sub", 1)

    def across(block):
        return shifted(block, "groups", 1)

    def in_order(own, other, axis):
        return jnp.where(
            first,
            jnp.concatenate([own, other], axis=axis),
            jnp.concatenate([other, own], axis=axis),
        )

    row_cuts = cuts(units, 16, ROW_PARTS)
    lane_cuts = cuts(width, 256, LANE_PARTS)
    pieces = [jnp.where(first, gate_weight[a:b], up_weight[a:b]) for a, b in row_cuts]
    for a, b in lane_cuts:
        mid = (a + b) // 2
        pieces.append(jnp.where(first, down_weight[:, a:mid], down_weight[:, mid:b]))

    landed = []
    for i, piece in enumerate(pieces):
        if i >= 2:
            piece, landed[i - 2] = lax.optimization_barrier((piece, landed[i - 2]))
        landed.append(shifted(piece, "dp", 1))
    crossed = [across(block) for block in landed]

    both_rows = [tokens, mate(tokens)]
    down_mate = mate(down_weight)

    here = over_slices(partial_values(both_rows, [gate_weight, up_weight]))
    here = gated(here[:, :units], here[:, units:])
    here = [here[:rows], mate(here[rows:])]

    there = []
    for i, (a, b) in enumerate(row_cuts):
        pre = over_slices(partial_values(both_rows, [landed[i], crossed[i]]))
        left, right = pre[:, : b - a], pre[:, b - a :]
        there.append(gated(jnp.where(first, left, right), jnp.where(first, right, left)))
    there = jnp.concatenate(there, axis=1)
    there = [there[:rows], mate(there[rows:])]

    results = []
    for i, (a, b) in enumerate(lane_cuts):
        own, other = landed[len(row_cuts) + i], crossed[len(row_cuts) + i]
        arrived = in_order(own, other, 1)
        arrived_mate = in_order(mate(own), mate(other), 1)
        total = jnp.zeros((rows, b - a), jnp.float32)
        for hidden, weight in (
            (here[0], down_weight[:, a:b]),
            (here[1], down_mate[:, a:b]),
            (there[0], arrived),
            (there[1], arrived_mate),
        ):
            total = total + jnp.dot(hidden, weight, preferred_element_type=jnp.float32)
        results.append(total.astype(jnp.bfloat16))
    return jnp.concatenate(results, axis=1)


def solution(mesh):
    return jax.shard_map(
        on_device,
        mesh=mesh,
        in_specs=(
            P(("groups", "dp", "sub"), "tensor"),
            P(("dp", "sub"), "tensor"),
            P(("dp", "sub"), "tensor"),
            P(("dp", "sub"), "tensor"),
        ),
        out_specs=P(("groups", "dp", "sub"), "tensor"),
        check_vma=False,
    )
```

time: 582 us -> 209 us (0.36)
  waiting for transfers between devices: 494 us -> 118 us
  starting transfers between devices: 1.79 us -> 30.1 us
  local copies, waits for them, and re-layouts: 21.3 us -> 2.01 us
  between operations: 13.4 us -> 0.73 us
    ppermute x1 -> x33, waiting for transfers between devices: 415 us -> 118 us  [shifted(): return lax.ppermute(block, axis, route)]
    psum x1 -> x0, waiting for transfers between devices: 41.8 us -> none  [apply_span(): lax.psum(partial_value.astype(jnp.bfloat16), 'tensor').astype(jnp.float32)]
    all_gather x1 -> x0, waiting for transfers between devices: 37 us -> none  [on_device(): current = lax.all_gather(own_share, 'sub', axis=1, tiled=True)]
    ppermute x1 -> x33, starting transfers between devices: 1.74 us -> 30.1 us  [shifted(): return lax.ppermute(block, axis, route)]
    slice x2, local copies, waits for them, and re-layouts: 18.3 us -> 0.22 us  [the longest x1 0.11 us: on_device(): here = [here[:rows], mate(here[rows:])]]
    another operation x1 -> x0, other arithmetic: 9.81 us -> none  [on_device(): own_share = jnp.stack([gate_weight, up_weight, down_weight])]
    dot_general x4 -> x36, matrix products: 39.3 us -> 43.5 us  [the longest x20 34.7 us: by_features(): lax.dot_general(rows, units, (((1,), (1,)), ((), ())), preferred_element_...]
  transfers between devices with their start and end apart: 3 -> 33, of which waited for: 3 -> 12; matrix products, arithmetic and copies ran while one was open for 5% -> 21% of each run, Pallas kernels for 0% -> 0%
where the time goes in v1:
time: 209 us; the launch traced here: 205 us
  waiting for transfers between devices  118 us (56%)
  matrix products  43.5 us (21%)
  starting transfers between devices  30.1 us (14%)
  other arithmetic  10.2 us (5%)
    ppermute x33, waiting for transfers between devices, shifted(): return lax.ppermute(block, axis, route)  118 us
    dot_general x20, matrix products, by_features(): lax.dot_general(rows, units, (((1,), (1,)), ((), ())), preferred_element_...  34.7 us
    ppermute x33, starting transfers between devices, shifted(): return lax.ppermute(block, axis, route)  30.1 us
    dot_general x16, matrix products, on_device(): total = total + jnp.dot(hidden, weight, preferred_element_type=jnp.float32)  8.77 us
    select_n x2, other arithmetic, on_device(): jnp.where(first, gate_weight[a:b], up_weight[a:b])  4.36 us
  transfers between devices with their start and end apart: 33, of which 12 were waited for; matrix products, arithmetic and copies ran while one was open for 21% of the time, Pallas kernels for 0%

profile of v1, /device:TPU:0, one launch (start us, length us, event | category | flops | bytes accessed | tf_op | source)
XLA Modules:
  0.0 204.9 jit_solution(7961655135866450155)
XLA Ops:
  0.0 2.7 %slice_select_fusion.2 = (bf16[48,8192]{1,0:T(8,128)(2,1)S(1)}, bf16[48,8192]{1,0:T(8,128)(2,1)S(1)}, bf16[48,8192]{1,0:T(8,128)(2,1)S(1)}) fusion(bf16[208,8192]{1,0:T(8,128)(2,1)} %param.6, bf16[208,8192]{1,0:T(8,128)(2,1)} %param.5, pred[]{:T(512)S(6)} %eq.3), kind=kLoop, calls=%fused_computation.128 | loop fusion | flops 1179648 | bytes 7077889 | tf_op jit(solution)/shard_map/jit(_where)/select_n | solution.py:69
  2.7 3.1 %collective-permute-start.4 = (bf16[48,8192]{1,0:T(8,128)(2,1)S(1)}, bf16[48,8192]{1,0:T(8,128)(2,1)S(1)}, u32[]{:S(2)}, u32[]{:S(2)}) collective-permute-start(bf16[48,8192]{1,0:T(8,128)(2,1)S(1)} %get-tuple-element.29), channel_id=1, source_target_pairs={{12,0},{0,4},{4,8},{8,12},{13,1},{1,5},{5,9},{9,13},{14,2},{2,6},{... | collective-permute-start | bytes 2359304 | tf_op jit(solution)/shard_map/ppermute | solution.py:13
  7.4 1.7 slice_select_fusion
  9.1 2.2 %convolution_convert_fusion.2 = bf16[320,208]{0,1:T(8,128)(2,1)S(1)} fusion(bf16[320,8192]{1,0:T(8,128)(2,1)S(1)} %copy-done, bf16[208,8192]{1,0:T(8,128)(2,1)S(1)} %copy-done.2), kind=kOutput, calls=%fused_computation.19 | convolution fusion | flops 1090585600 | bytes 8783872 | tf_op jit(solution)/shard_map/dot_general | solution.py:23
  11.4 1.8 copy-done.3
  13.2 2.2 %convolution_convert_fusion.3 = bf16[320,208]{0,1:T(8,128)(2,1)S(1)} fusion(bf16[320,8192]{1,0:T(8,128)(2,1)S(1)} %copy-done, bf16[208,8192]{1,0:T(8,128)(2,1)S(1)} %copy-done.3), kind=kOutput, calls=%fused_computation.20 | convolution fusion | flops 1090585600 | bytes 8783872 | tf_op jit(solution)/shard_map/dot_general | solution.py:23
  15.4 10.8 %collective-permute-done.4 = bf16[48,8192]{1,0:T(8,128)(2,1)S(1)} collective-permute-done((bf16[48,8192]{1,0:T(8,128)(2,1)S(1)}, bf16[48,8192]{1,0:T(8,128)(2,1)S(1)}, u32[]{:S(2)}, u32[]{:S(2)}) %collective-permute-start.4) | collective-permute-done | bytes 786464 | tf_op jit(solution)/shard_map/ppermute | solution.py:13
  26.2 1.8 collective-permute-start.5
  28.0 14.3 %collective-permute-done.7 = bf16[48,8192]{1,0:T(8,128)(2,1)S(1)} collective-permute-done((bf16[48,8192]{1,0:T(8,128)(2,1)S(1)}, bf16[48,8192]{1,0:T(8,128)(2,1)S(1)}, u32[]{:S(2)}, u32[]{:S(2)}) %collective-permute-start.7) | collective-permute-done | bytes 786464 | tf_op jit(solution)/shard_map/ppermute | solution.py:13
  48.3 17.7 %collective-permute-done.10 = bf16[48,8192]{1,0:T(8,128)(2,1)S(1)} collective-permute-done((bf16[48,8192]{1,0:T(8,128)(2,1)S(1)}, bf16[48,8192]{1,0:T(8,128)(2,1)S(1)}, u32[]{:S(2)}, u32[]{:S(2)}) %collective-permute-start.10) | collective-permute-done | bytes 786464 | tf_op jit(solution)/shard_map/ppermute | solution.py:13
  69.8 18.6 %collective-permute-done.13 = bf16[64,8192]{1,0:T(8,128)(2,1)S(1)} collective-permute-done((bf16[64,8192]{1,0:T(8,128)(2,1)S(1)}, bf16[64,8192]{1,0:T(8,128)(2,1)S(1)}, u32[]{:S(2)}, u32[]{:S(2)}) %collective-permute-start.13) | collective-permute-done | bytes 1048608 | tf_op jit(solution)/shard_map/ppermute | solution.py:13
  90.9 1.6 fusion.8
  92.5 5.1 %collective-permute-done.16 = bf16[208,1024]{1,0:T(8,128)(2,1)S(1)} collective-permute-done((bf16[208,1024]{1,0:T(8,128)(2,1)S(1)}, bf16[208,1024]{1,0:T(8,128)(2,1)S(1)}, u32[]{:S(2)}, u32[]{:S(2)}) %collective-permute-start.16) | collective-permute-done | bytes 426016 | tf_op jit(solution)/shard_map/ppermute | solution.py:13
  98.1 6.3 %collective-permute-done.21 = bf16[208,1024]{1,0:T(8,128)(2,1)S(1)} collective-permute-done((bf16[208,1024]{1,0:T(8,128)(2,1)S(1)}, bf16[208,1024]{1,0:T(8,128)(2,1)S(1)}, u32[]{:S(2)}, u32[]{:S(2)}) %collective-permute-start.21) | collective-permute-done | bytes 426016 | tf_op jit(solution)/shard_map/ppermute | solution.py:13
  106.1 8.5 %collective-permute-done.14 = bf16[64,8192]{1,0:T(8,128)(2,1)S(1)} collective-permute-done((bf16[64,8192]{1,0:T(8,128)(2,1)S(1)}, bf16[64,8192]{1,0:T(8,128)(2,1)S(1)}, u32[]{:S(2)}, u32[]{:S(2)}) %collective-permute-start.14) | collective-permute-done | bytes 1048608 | tf_op jit(solution)/shard_map/ppermute | solution.py:13
  131.5 2.2 %convolution_convert_fusion = bf16[320,208]{0,1:T(8,128)(2,1)S(1)} fusion(bf16[320,8192]{1,0:T(8,128)(2,1)S(1)} %collective-permute-done, bf16[208,8192]{1,0:T(8,128)(2,1)S(1)} %copy-done.2), kind=kOutput, calls=%fused_computation.17 | convolution fusion | flops 1090585600 | bytes 8783872 | tf_op jit(solution)/shard_map/dot_general | solution.py:23
  134.6 4.3 %collective-permute-done.9 = bf16[640,96]{0,1:T(8,128)(2,1)S(1)} collective-permute-done((bf16[640,96]{0,1:T(8,128)(2,1)S(1)}, bf16[640,96]{0,1:T(8,128)(2,1)S(1)}, u32[]{:S(2)}, u32[]{:S(2)}) %collective-permute-start.9) | collective-permute-done | bytes 122912 | tf_op jit(solution)/shard_map/ppermute | solution.py:13
  139.6 4.2 %collective-permute-done.12 = bf16[640,96]{0,1:T(8,128)(2,1)S(1)} collective-permute-done((bf16[640,96]{0,1:T(8,128)(2,1)S(1)}, bf16[640,96]{0,1:T(8,128)(2,1)S(1)}, u32[]{:S(2)}, u32[]{:S(2)}) %collective-permute-start.12) | collective-permute-done | bytes 122912 | tf_op jit(solution)/shard_map/ppermute | solution.py:13
  144.6 8.8 %collective-permute-start.29 = (bf16[208,1024]{1,0:T(8,128)(2,1)S(1)}, bf16[208,1024]{1,0:T(8,128)(2,1)S(1)}, u32[]{:S(2)}, u32[]{:S(2)}) collective-permute-start(bf16[208,1024]{1,0:T(8,128)(2,1)S(1)} %get-tuple-element.28), channel_id=1, source_target_pairs={{12,0},{0,4},{4,8},{8,12},{13,1},{1,5},{5,9},{9,13},{14,2},{2,6},{... | collective-permute-start | bytes 1277960 | tf_op jit(solution)/shard_map/ppermute | solution.py:13
  155.9 11.2 %collective-permute-done.29 = bf16[208,1024]{1,0:T(8,128)(2,1)S(1)} collective-permute-done((bf16[208,1024]{1,0:T(8,128)(2,1)S(1)}, bf16[208,1024]{1,0:T(8,128)(2,1)S(1)}, u32[]{:S(2)}, u32[]{:S(2)}) %collective-permute-start.29) | collective-permute-done | bytes 426016 | tf_op jit(solution)/shard_map/ppermute | solution.py:13
  168.6 2.2 %convolution_convert_fusion.1 = bf16[320,208]{0,1:T(8,128)(2,1)S(1)} fusion(bf16[320,8192]{1,0:T(8,128)(2,1)S(1)} %collective-permute-done, bf16[208,8192]{1,0:T(8,128)(2,1)S(1)} %copy-done.3), kind=kOutput, calls=%fused_computation.18 | convolution fusion | flops 1090585600 | bytes 8783872 | tf_op jit(solution)/shard_map/dot_general | solution.py:23
  172.7 5.5 %collective-permute-done.30 = bf16[208,1024]{1,0:T(8,128)(2,1)S(1)} collective-permute-done((bf16[208,1024]{1,0:T(8,128)(2,1)S(1)}, bf16[208,1024]{1,0:T(8,128)(2,1)S(1)}, u32[]{:S(2)}, u32[]{:S(2)}) %collective-permute-start.30) | collective-permute-done | bytes 426016 | tf_op jit(solution)/shard_map/ppermute | solution.py:13
  181.4 11.9 %collective-permute-done.1 = bf16[640,416]{0,1:T(8,128)(2,1)S(1)} collective-permute-done((bf16[640,416]{0,1:T(8,128)(2,1)S(1)}, bf16[640,416]{0,1:T(8,128)(2,1)S(1)}, u32[]{:S(2)}, u32[]{:S(2)}) %collective-permute-start.1) | collective-permute-done | bytes 532512 | tf_op jit(solution)/shard_map/ppermute | solution.py:13
  200.6 4.1 %pad_maximum_fusion = bf16[320,8192]{1,0:T(8,128)(2,1)} fusion(bf16[320,2048]{1,0:T(8,128)(2,1)S(1)} %fusion.7, bf16[320,2048]{1,0:T(8,128)(2,1)S(1)} %fusion.6, bf16[320,2048]{1,0:T(8,128)(2,1)S(1)} %fusion.5, bf16[320,2048]{1,0:T(8,128)(2,1)S(1)} %fusion.4), kind=kLoop, calls=%fused_computation | loop fusion | flops 20971520 | bytes 10485760 | tf_op jit(solution)/shard_map/concatenate | solution.py:110
  (108 shorter events, 51.5 us)
Async XLA Ops:
  2.7 23.5 %collective-permute-start.4 = (bf16[48,8192]{1,0:T(8,128)(2,1)S(1)}, bf16[48,8192]{1,0:T(8,128)(2,1)S(1)}, u32[]{:S(2)}, u32[]{:S(2)}) collective-permute-start(bf16[48,8192]{1,0:T(8,128)(2,1)S(1)} %get-tuple-element.29), channel_id=1, source_target_pairs={{12,0},{0,4},{4,8},{8,12},{13,1},{1,5},{5,9},{9,13},{14,2},{2,6},{... | collective-permute-start | bytes 2359304 | tf_op jit(solution)/shard_map/ppermute | solution.py:13
  5.8 110.9 %collective-permute-start = (bf16[320,8192]{1,0:T(8,128)(2,1)S(1)}, bf16[320,8192]{1,0:T(8,128)(2,1)S(1)}, u32[]{:S(2)}, u32[]{:S(2)}) collective-permute-start(bf16[320,8192]{1,0:T(8,128)(2,1)S(1)} %copy-done), channel_id=1, source_target_pairs={{1,0},{0,1},{3,2},{2,3},{5,4},{4,5},{7,6},{6,7},{9,8},{8,9},{11,10... | collective-permute-start | bytes 15728648 | tf_op jit(solution)/shard_map/ppermute | solution.py:13
  5.8 36.4 %collective-permute-start.7 = (bf16[48,8192]{1,0:T(8,128)(2,1)S(1)}, bf16[48,8192]{1,0:T(8,128)(2,1)S(1)}, u32[]{:S(2)}, u32[]{:S(2)}) collective-permute-start(bf16[48,8192]{1,0:T(8,128)(2,1)S(1)} %get-tuple-element.31), channel_id=1, source_target_pairs={{12,0},{0,4},{4,8},{8,12},{13,1},{1,5},{5,9},{9,13},{14,2},{2,6},{... | collective-permute-start | bytes 2359304 | tf_op jit(solution)/shard_map/ppermute | solution.py:13
  26.2 42.0 %collective-permute-start.5 = (bf16[48,8192]{1,0:T(8,128)(2,1)S(1)}, bf16[48,8192]{1,0:T(8,128)(2,1)S(1)}, u32[]{:S(2)}, u32[]{:S(2)}) collective-permute-start(bf16[48,8192]{1,0:T(8,128)(2,1)S(1)} %collective-permute-done.4), channel_id=1, source_target_pairs={{16,0},{0,16},{17,1},{1,17},{18,2},{2,18},{19,3},{3,19},{20,4},{4,... | collective-permute-start | bytes 2359304 | tf_op jit(solution)/shard_map/ppermute | solution.py:13
  42.2 46.8 %collective-permute-start.8 = (bf16[48,8192]{1,0:T(8,128)(2,1)S(1)}, bf16[48,8192]{1,0:T(8,128)(2,1)S(1)}, u32[]{:S(2)}, u32[]{:S(2)}) collective-permute-start(bf16[48,8192]{1,0:T(8,128)(2,1)S(1)} %collective-permute-done.7), channel_id=1, source_target_pairs={{16,0},{0,16},{17,1},{1,17},{18,2},{2,18},{19,3},{3,19},{20,4},{4,... | collective-permute-start | bytes 2359304 | tf_op jit(solution)/shard_map/ppermute | solution.py:13
  43.7 22.3 %collective-permute-start.10 = (bf16[48,8192]{1,0:T(8,128)(2,1)S(1)}, bf16[48,8192]{1,0:T(8,128)(2,1)S(1)}, u32[]{:S(2)}, u32[]{:S(2)}) collective-permute-start(bf16[48,8192]{1,0:T(8,128)(2,1)S(1)} %get-tuple-element.19), channel_id=1, source_target_pairs={{12,0},{0,4},{4,8},{8,12},{13,1},{1,5},{5,9},{9,13},{14,2},{2,6},{... | collective-permute-start | bytes 2359304 | tf_op jit(solution)/shard_map/ppermute | solution.py:13
  43.7 44.7 %collective-permute-start.13 = (bf16[64,8192]{1,0:T(8,128)(2,1)S(1)}, bf16[64,8192]{1,0:T(8,128)(2,1)S(1)}, u32[]{:S(2)}, u32[]{:S(2)}) collective-permute-start(bf16[64,8192]{1,0:T(8,128)(2,1)S(1)} %slice_select_fusion), channel_id=1, source_target_pairs={{12,0},{0,4},{4,8},{8,12},{13,1},{1,5},{5,9},{9,13},{14,2},{2,6},{... | collective-permute-start | bytes 3145736 | tf_op jit(solution)/shard_map/ppermute | solution.py:13
  66.0 38.5 %collective-permute-start.11 = (bf16[48,8192]{1,0:T(8,128)(2,1)S(1)}, bf16[48,8192]{1,0:T(8,128)(2,1)S(1)}, u32[]{:S(2)}, u32[]{:S(2)}) collective-permute-start(bf16[48,8192]{1,0:T(8,128)(2,1)S(1)} %collective-permute-done.10), channel_id=1, source_target_pairs={{16,0},{0,16},{17,1},{1,17},{18,2},{2,18},{19,3},{3,19},{20,4},{4,... | collective-permute-start | bytes 2359304 | tf_op jit(solution)/shard_map/ppermute | solution.py:13
  68.1 29.5 %collective-permute-start.16 = (bf16[208,1024]{1,0:T(8,128)(2,1)S(1)}, bf16[208,1024]{1,0:T(8,128)(2,1)S(1)}, u32[]{:S(2)}, u32[]{:S(2)}) collective-permute-start(bf16[208,1024]{1,0:T(8,128)(2,1)S(1)} %get-tuple-element.23), channel_id=1, source_target_pairs={{12,0},{0,4},{4,8},{8,12},{13,1},{1,5},{5,9},{9,13},{14,2},{2,6},{... | collective-permute-start | bytes 1277960 | tf_op jit(solution)/shard_map/ppermute | solution.py:13
  88.5 26.1 %collective-permute-start.14 = (bf16[64,8192]{1,0:T(8,128)(2,1)S(1)}, bf16[64,8192]{1,0:T(8,128)(2,1)S(1)}, u32[]{:S(2)}, u32[]{:S(2)}) collective-permute-start(bf16[64,8192]{1,0:T(8,128)(2,1)S(1)} %collective-permute-done.13), channel_id=1, source_target_pairs={{16,0},{0,16},{17,1},{1,17},{18,2},{2,18},{19,3},{3,19},{20,4},{4,... | collective-permute-start | bytes 3145736 | tf_op jit(solution)/shard_map/ppermute | solution.py:13
  89.0 15.5 %collective-permute-start.21 = (bf16[208,1024]{1,0:T(8,128)(2,1)S(1)}, bf16[208,1024]{1,0:T(8,128)(2,1)S(1)}, u32[]{:S(2)}, u32[]{:S(2)}) collective-permute-start(bf16[208,1024]{1,0:T(8,128)(2,1)S(1)} %get-tuple-element.25), channel_id=1, source_target_pairs={{12,0},{0,4},{4,8},{8,12},{13,1},{1,5},{5,9},{9,13},{14,2},{2,6},{... | collective-permute-start | bytes 1277960 | tf_op jit(solution)/shard_map/ppermute | solution.py:13
  97.6 46.9 %collective-permute-start.17 = (bf16[208,1024]{1,0:T(8,128)(2,1)S(1)}, bf16[208,1024]{1,0:T(8,128)(2,1)S(1)}, u32[]{:S(2)}, u32[]{:S(2)}) collective-permute-start(bf16[208,1024]{1,0:T(8,128)(2,1)S(1)} %collective-permute-done.16), channel_id=1, source_target_pairs={{16,0},{0,16},{17,1},{1,17},{18,2},{2,18},{19,3},{3,19},{20,4},{4,... | collective-permute-start | bytes 1277960 | tf_op jit(solution)/shard_map/ppermute | solution.py:13
  104.5 40.2 %collective-permute-start.19 = (bf16[208,1024]{1,0:T(8,128)(2,1)S(1)}, bf16[208,1024]{1,0:T(8,128)(2,1)S(1)}, u32[]{:S(2)}, u32[]{:S(2)}) collective-permute-start(bf16[208,1024]{1,0:T(8,128)(2,1)S(1)} %collective-permute-done.16), channel_id=1, source_target_pairs={{1,0},{0,1},{3,2},{2,3},{5,4},{4,5},{7,6},{6,7},{9,8},{8,9},{11,10... | collective-permute-start | bytes 1277960 | tf_op jit(solution)/shard_map/ppermute | solution.py:13
  104.5 49.6 %collective-permute-start.25 = (bf16[208,1024]{1,0:T(8,128)(2,1)S(1)}, bf16[208,1024]{1,0:T(8,128)(2,1)S(1)}, u32[]{:S(2)}, u32[]{:S(2)}) collective-permute-start(bf16[208,1024]{1,0:T(8,128)(2,1)S(1)} %get-tuple-element.27), channel_id=1, source_target_pairs={{12,0},{0,4},{4,8},{8,12},{13,1},{1,5},{5,9},{9,13},{14,2},{2,6},{... | collective-permute-start | bytes 1277960 | tf_op jit(solution)/shard_map/ppermute | solution.py:13
  114.6 39.9 %collective-permute-start.22 = (bf16[208,1024]{1,0:T(8,128)(2,1)S(1)}, bf16[208,1024]{1,0:T(8,128)(2,1)S(1)}, u32[]{:S(2)}, u32[]{:S(2)}) collective-permute-start(bf16[208,1024]{1,0:T(8,128)(2,1)S(1)} %collective-permute-done.21), channel_id=1, source_target_pairs={{16,0},{0,16},{17,1},{1,17},{18,2},{2,18},{19,3},{3,19},{20,4},{4,... | collective-permute-start | bytes 1277960 | tf_op jit(solution)/shard_map/ppermute | solution.py:13
  120.1 13.8 %collective-permute-start.6 = (bf16[640,96]{0,1:T(8,128)(2,1)S(1)}, bf16[640,96]{0,1:T(8,128)(2,1)S(1)}, u32[]{:S(2)}, u32[]{:S(2)}) collective-permute-start(bf16[640,96]{0,1:T(8,128)(2,1)S(1)} %maximum_maximum_fusion.2), channel_id=1, source_target_pairs={{2,0},{0,2},{3,1},{1,3},{6,4},{4,6},{7,5},{5,7},{10,8},{8,10},{11,... | collective-permute-start | bytes 368648 | tf_op jit(solution)/shard_map/ppermute | solution.py:13
  144.5 11.4 %collective-permute-start.23 = (bf16[208,1024]{1,0:T(8,128)(2,1)S(1)}, bf16[208,1024]{1,0:T(8,128)(2,1)S(1)}, u32[]{:S(2)}, u32[]{:S(2)}) collective-permute-start(bf16[208,1024]{1,0:T(8,128)(2,1)S(1)} %collective-permute-done.21), channel_id=1, source_target_pairs={{1,0},{0,1},{3,2},{2,3},{5,4},{4,5},{7,6},{6,7},{9,8},{8,9},{11,10... | collective-permute-start | bytes 1277960 | tf_op jit(solution)/shard_map/ppermute | solution.py:13
  144.6 22.5 %collective-permute-start.29 = (bf16[208,1024]{1,0:T(8,128)(2,1)S(1)}, bf16[208,1024]{1,0:T(8,128)(2,1)S(1)}, u32[]{:S(2)}, u32[]{:S(2)}) collective-permute-start(bf16[208,1024]{1,0:T(8,128)(2,1)S(1)} %get-tuple-element.28), channel_id=1, source_target_pairs={{12,0},{0,4},{4,8},{8,12},{13,1},{1,5},{5,9},{9,13},{14,2},{2,6},{... | collective-permute-start | bytes 1277960 | tf_op jit(solution)/shard_map/ppermute | solution.py:13
  153.5 15.2 %collective-permute-start.20 = (bf16[208,1024]{1,0:T(8,128)(2,1)S(1)}, bf16[208,1024]{1,0:T(8,128)(2,1)S(1)}, u32[]{:S(2)}, u32[]{:S(2)}) collective-permute-start(bf16[208,1024]{1,0:T(8,128)(2,1)S(1)} %collective-permute-done.17), channel_id=1, source_target_pairs={{1,0},{0,1},{3,2},{2,3},{5,4},{4,5},{7,6},{6,7},{9,8},{8,9},{11,10... | collective-permute-start | bytes 1277960 | tf_op jit(solution)/shard_map/ppermute | solution.py:13
  154.0 42.0 %collective-permute-start.3 = (bf16[208,8192]{1,0:T(8,128)(2,1)S(1)}, bf16[208,8192]{1,0:T(8,128)(2,1)S(1)}, u32[]{:S(2)}, u32[]{:S(2)}) collective-permute-start(bf16[208,8192]{1,0:T(8,128)(2,1)S(1)} %copy-done.1), channel_id=1, source_target_pairs={{1,0},{0,1},{3,2},{2,3},{5,4},{4,5},{7,6},{6,7},{9,8},{8,9},{11,10... | collective-permute-start | bytes 10223624 | tf_op jit(solution)/shard_map/ppermute | solution.py:13
  154.4 16.6 %collective-permute-start.26 = (bf16[208,1024]{1,0:T(8,128)(2,1)S(1)}, bf16[208,1024]{1,0:T(8,128)(2,1)S(1)}, u32[]{:S(2)}, u32[]{:S(2)}) collective-permute-start(bf16[208,1024]{1,0:T(8,128)(2,1)S(1)} %collective-permute-done.25), channel_id=1, source_target_pairs={{16,0},{0,16},{17,1},{1,17},{18,2},{2,18},{19,3},{3,19},{20,4},{4,... | collective-permute-start | bytes 1277960 | tf_op jit(solution)/shard_map/ppermute | solution.py:13
  155.9 16.3 %collective-permute-start.24 = (bf16[208,1024]{1,0:T(8,128)(2,1)S(1)}, bf16[208,1024]{1,0:T(8,128)(2,1)S(1)}, u32[]{:S(2)}, u32[]{:S(2)}) collective-permute-start(bf16[208,1024]{1,0:T(8,128)(2,1)S(1)} %collective-permute-done.22), channel_id=1, source_target_pairs={{1,0},{0,1},{3,2},{2,3},{5,4},{4,5},{7,6},{6,7},{9,8},{8,9},{11,10... | collective-permute-start | bytes 1277960 | tf_op jit(solution)/shard_map/ppermute | solution.py:13
  167.1 11.1 %collective-permute-start.30 = (bf16[208,1024]{1,0:T(8,128)(2,1)S(1)}, bf16[208,1024]{1,0:T(8,128)(2,1)S(1)}, u32[]{:S(2)}, u32[]{:S(2)}) collective-permute-start(bf16[208,1024]{1,0:T(8,128)(2,1)S(1)} %collective-permute-done.29), channel_id=1, source_target_pairs={{16,0},{0,16},{17,1},{1,17},{18,2},{2,18},{19,3},{3,19},{20,4},{4,... | collective-permute-start | bytes 1277960 | tf_op jit(solution)/shard_map/ppermute | solution.py:13
  178.8 14.6 %collective-permute-start.1 = (bf16[640,416]{0,1:T(8,128)(2,1)S(1)}, bf16[640,416]{0,1:T(8,128)(2,1)S(1)}, u32[]{:S(2)}, u32[]{:S(2)}) collective-permute-start(bf16[640,416]{0,1:T(8,128)(2,1)S(1)} %maximum_maximum_fusion), channel_id=1, source_target_pairs={{2,0},{0,2},{3,1},{1,3},{6,4},{4,6},{7,5},{5,7},{10,8},{8,10},{11,... | collective-permute-start | bytes 1597448 | tf_op jit(solution)/shard_map/ppermute | solution.py:13
  (13 other events, 71.4 us)

commit v2 on v0

v2 whole, which is shorter than its diff:
```python
import functools

import jax
import jax.numpy as jnp
from jax import lax
from jax.experimental import pallas as pl
from jax.experimental.pallas import tpu as pltpu
from jax.sharding import PartitionSpec as P

ROW_SHARES = (1, 2, 2, 2, 2, 2, 2)
FIRST_BATCH = 4
LANE_SHARES = (3, 3, 3, 3, 2, 2)
VMEM = 24 * 1024 * 1024


def shifted(block, axis, distance):
    devices = range(lax.axis_size(axis))
    route = [((i - distance) % len(devices), i) for i in devices]
    return lax.ppermute(block, axis, route)


def tied(value, *earlier):
    return lax.optimization_barrier((value, *earlier))[0]


def cuts(total, unit, shares):
    units, whole, done, marks = total // unit, sum(shares), 0, [0]
    for share in shares:
        done += share
        marks.append(units * done // whole * unit)
    marks[-1] = total
    return list(zip(marks[:-1], marks[1:]))


def products_kernel(sets, *refs):
    row_refs, unit_refs, (out_ref, total) = refs[:sets], refs[sets:-2], refs[-2:]
    step = pl.program_id(0)

    @pl.when(step == 0)
    def _():
        total[...] = jnp.zeros_like(total)

    units = jnp.concatenate([ref[...] for ref in unit_refs], axis=0)
    rows = row_refs[0].shape[0]
    for i, ref in enumerate(row_refs):
        total[i * rows : (i + 1) * rows] += lax.dot_general(
            ref[...], units, (((1,), (1,)), ((), ())), preferred_element_type=jnp.float32
        )

    @pl.when(step == pl.num_programs(0) - 1)
    def _():
        out_ref[...] = total[...].astype(out_ref.dtype)


def products(row_sets, unit_sets):
    width = row_sets[0].shape[1]
    block = 1024 if width % 1024 == 0 else width
    count = sum(u.shape[0] for u in unit_sets)
    shape = (sum(r.shape[0] for r in row_sets), count)
    return pl.pallas_call(
        functools.partial(products_kernel, len(row_sets)),
        grid=(width // block,),
        in_specs=[
            pl.BlockSpec((array.shape[0], block), lambda k: (0, k))
            for array in (*row_sets, *unit_sets)
        ],
        out_specs=pl.BlockSpec(shape, lambda k: (0, 0)),
        out_shape=jax.ShapeDtypeStruct(shape, jnp.bfloat16),
        scratch_shapes=[pltpu.VMEM(shape, jnp.float32)],
        compiler_params=pltpu.CompilerParams(vmem_limit_bytes=VMEM),
        cost_estimate=pl.CostEstimate(flops=1, bytes_accessed=1, transcendentals=0),
    )(*row_sets, *unit_sets)


def output_kernel(a, b, side_ref, *refs):
    hidden, arrived, (down, down_mate) = refs[:4], refs[4:8], refs[8:10]
    out, here, here_mate, block, sems = refs[-5:]
    lanes = slice(a, b)
    copies = [
        pltpu.make_async_copy(down.at[:, lanes], here, sems.at[0]),
        pltpu.make_async_copy(down_mate.at[:, lanes], here_mate, sems.at[1]),
    ]
    for copy in copies:
        copy.start()
    half = (b - a) // 2
    side = side_ref[0]
    for copy in copies:
        copy.wait()
    for i in range(2):
        at = pl.ds(pl.multiple_of((side + i - 2 * side * i) * half, 128), half)
        total = None
        for rows, units in (
            (hidden[0], here[:, at]),
            (hidden[1], here_mate[:, at]),
            (hidden[2], arrived[i][...]),
            (hidden[3], arrived[2 + i][...]),
        ):
            term = jnp.dot(rows[...], units, preferred_element_type=jnp.float32)
            total = term if total is None else total + term
        block[:, at] = total.astype(block.dtype)
    copy = pltpu.make_async_copy(block, out.at[:, lanes], sems.at[2])
    copy.start()
    copy.wait()


def output_part(result, a, b, side, hidden, arrived, down, down_mate):
    rows, units, width = hidden[0].shape[0], down.shape[0], down.shape[1]
    any_space = pl.BlockSpec(memory_space=pl.ANY)
    whole = pl.BlockSpec(memory_space=pltpu.VMEM)
    operands = [side, *hidden, *arrived, down, down_mate]
    in_specs = [pl.BlockSpec(memory_space=pltpu.SMEM)] + [whole] * 8 + [any_space] * 2
    aliases = {}
    if result is not None:
        aliases = {len(operands): 0}
        operands.append(result)
        in_specs.append(any_space)
    return pl.pallas_call(
        functools.partial(output_kernel, a, b),
        in_specs=in_specs,
        out_specs=any_space,
        out_shape=jax.ShapeDtypeStruct((rows, width), jnp.bfloat16),
        scratch_shapes=[
            pltpu.VMEM((units, b - a), jnp.bfloat16),
            pltpu.VMEM((units, b - a), jnp.bfloat16),
            pltpu.VMEM((rows, b - a), jnp.bfloat16),
            pltpu.SemaphoreType.DMA((3,)),
        ],
        input_output_aliases=aliases,
        compiler_params=pltpu.CompilerParams(vmem_limit_bytes=VMEM),
        cost_estimate=pl.CostEstimate(flops=1, bytes_accessed=1, transcendentals=0),
    )(*operands)


def over_slices(partial_value):
    return [
        shifted(partial_value, "tensor", distance)
        for distance in range(1, lax.axis_size("tensor"))
    ]


def summed(partial_value, sent):
    total = partial_value.astype(jnp.float32)
    for block in sent:
        total = total + block.astype(jnp.float32)
    return total


def gated(gate, up):
    return (jax.nn.silu(gate) * up).astype(jnp.bfloat16)


def on_device(tokens, gate_weight, up_weight, down_weight):
    units, width = gate_weight.shape
    rows = tokens.shape[0]
    group = lax.axis_index("groups").astype(jnp.int32)
    first = group == 0
    side = group.reshape(1)

    def mate(block):
        return shifted(block, "sub", 1)

    row_cuts = cuts(units, 16, ROW_SHARES)
    lane_cuts = [(2 * a, 2 * b) for a, b in cuts(width // 2, 128, LANE_SHARES)]
    count = len(row_cuts)
    total_count = count + len(lane_cuts)

    def piece(i, *after):
        if i < count:
            a, b = row_cuts[i]
            gate, up = gate_weight, up_weight
            if after:
                gate, up = lax.optimization_barrier((gate, up, *after))[:2]
            return jnp.where(first, gate[a:b], up[a:b])
        a, b = lane_cuts[i - count]
        mid = (a + b) // 2
        down = tied(down_weight, *after) if after else down_weight
        return jnp.where(first, down[:, a:mid], down[:, mid:b])

    pieces = [piece(0)]
    pieces.append(piece(1, pieces[0]))
    pieces += [piece(i, pieces[1]) for i in range(2, total_count)]
    waiting = [shifted(pieces[0], "dp", 1), shifted(pieces[1], "dp", 1)]
    landed, crossed, mates, crossed_mates = [], [], {}, {}

    def advance(*after):
        i = len(landed)
        held = list(after)
        if i >= 1:
            held.append(landed[i - 1])
        if i >= 2:
            held.append(crossed[i - 2])
            if i - 2 >= count:
                held.append(mates[i - 2])
        if i - 3 >= count:
            held.append(crossed_mates[i - 3])
        block = tied(waiting[i], *held) if held else waiting[i]
        landed.append(block)
        crossed.append(shifted(block, "groups", 1))
        if i >= count:
            mates[i] = mate(block)
        if i - 2 >= count:
            crossed_mates[i - 2] = mate(tied(crossed[i - 2], block))
        if i + 2 < total_count:
            waiting.append(shifted(tied(pieces[i + 2], block), "dp", 1))
        return block

    def local(partial_value, sent, now):
        pre = summed(partial_value, [tied(block, now) for block in sent])
        return gated(pre[:, :units], pre[:, units:])

    def batch(lo, hi, now):
        held = lax.optimization_barrier((*landed[lo:hi], *crossed[lo:hi], now))[:-1]
        value = products([tokens, tokens_mate], held)
        return value, over_slices(value)

    def activated(partial_value, sent, now):
        pre = summed(partial_value, [tied(block, now) for block in sent])
        half = pre.shape[1] // 2
        left, right = pre[:, :half], pre[:, half:]
        return gated(jnp.where(first, left, right), jnp.where(first, right, left))

    tokens_mate = mate(tokens)
    down_mate = mate(tied(down_weight, pieces[0]))
    mine = products([tokens], [gate_weight, up_weight])
    mine_sent = over_slices(mine)
    now = advance(mine)
    theirs = products([tied(tokens_mate, now)], [gate_weight, up_weight])
    theirs_sent = over_slices(theirs)
    now = advance(theirs)
    here = local(mine, mine_sent, now)
    now = advance(here)
    here_mate = mate(local(theirs, theirs_sent, now))
    now = advance()
    now = advance(here_mate, down_mate)
    now = advance()
    early, early_sent = batch(0, FIRST_BATCH, now)
    now = advance(early)
    there = [activated(early, early_sent, now)]
    now = advance(there[0])
    now = advance()
    late, late_sent = batch(FIRST_BATCH, count, now)
    now = advance(late)
    there.append(activated(late, late_sent, now))
    there = jnp.concatenate(there, axis=1)
    there_mate = mate(there[rows:])
    there = there[:rows]
    now = advance(there)
    now = advance(there_mate)
    while len(landed) < total_count:
        now = advance()

    result = None
    for i, (a, b) in enumerate(lane_cuts):
        k = count + i
        if k not in crossed_mates:
            crossed_mates[k] = mate(crossed[k])
        result = output_part(
            result,
            a,
            b,
            side,
            [here, here_mate, there, there_mate],
            [landed[k], crossed[k], mates[k], crossed_mates[k]],
            down_weight,
            down_mate,
        )
    return result


def solution(mesh):
    return jax.shard_map(
        on_device,
        mesh=mesh,
        in_specs=(
            P(("groups", "dp", "sub"), "tensor"),
            P(("dp", "sub"), "tensor"),
            P(("dp", "sub"), "tensor"),
            P(("dp", "sub"), "tensor"),
        ),
        out_specs=P(("groups", "dp", "sub"), "tensor"),
        check_vma=False,
    )
```

time: 582 us -> 168 us (0.29)
  waiting for transfers between devices: 494 us -> 85.6 us
  Pallas kernels: 0 us -> 40.4 us
  matrix products: 39.3 us -> 0 us
  starting transfers between devices: 1.79 us -> 30.2 us
  local copies, waits for them, and re-layouts: 21.3 us -> 6.44 us
  between operations: 13.4 us -> 0.53 us
  other arithmetic: 12.1 us -> 3.92 us
    ppermute x1 -> x46, waiting for transfers between devices: 415 us -> 85.6 us  [shifted(): return lax.ppermute(block, axis, route)]
    psum x1 -> x0, waiting for transfers between devices: 41.8 us -> none  [apply_span(): lax.psum(partial_value.astype(jnp.bfloat16), 'tensor').astype(jnp.float32)]
    pallas_call x0 -> x10, Pallas kernels: none -> 40.4 us  [the longest x4 27.6 us: products(): pl.pallas_call(functools.partial(products_kernel, len(row_sets)), grid=(w...]
    dot_general x4 -> x0, matrix products: 39.3 us -> none  [the longest x2 25.8 us: apply_span(): lax.dot_general(tokens, both, (((1,), (1,)), ((), ())), preferred_element...]
    all_gather x1 -> x0, waiting for transfers between devices: 37 us -> none  [on_device(): current = lax.all_gather(own_share, 'sub', axis=1, tiled=True)]
    ppermute x1 -> x46, starting transfers between devices: 1.74 us -> 30.2 us  [shifted(): return lax.ppermute(block, axis, route)]
    slice x2 -> x0, local copies, waits for them, and re-layouts: 18.3 us -> none  [apply_span(): both = weights[:2].reshape(2 * span, weights.shape[2])]
    another operation x1 -> x0, other arithmetic: 9.81 us -> none  [on_device(): own_share = jnp.stack([gate_weight, up_weight, down_weight])]
  transfers between devices with their start and end apart: 3 -> 46, of which waited for: 3 -> 17; matrix products, arithmetic and copies ran while one was open for 5% -> 2% of each run, Pallas kernels for 0% -> 23%
where the time goes in v2:
time: 168 us; the launch traced here: 167 us
  waiting for transfers between devices  85.6 us (51%)
  Pallas kernels  40.4 us (24%)
  starting transfers between devices  30.2 us (18%)
  local copies, waits for them, and re-layouts  6.44 us (4%)
  other arithmetic  3.92 us (2%)
    ppermute x46, waiting for transfers between devices, shifted(): return lax.ppermute(block, axis, route)  85.6 us
    ppermute x46, starting transfers between devices, shifted(): return lax.ppermute(block, axis, route)  30.2 us
    pallas_call x4, Pallas kernels, products(): pl.pallas_call(functools.partial(products_kernel, len(row_sets)), grid=(w...  27.6 us
    pallas_call x6, Pallas kernels, output_part(): pl.pallas_call(functools.partial(output_kernel, a, b), in_specs=in_specs,...  12.7 us
    unnamed x16, local copies, waits for them, and re-layouts  6.44 us
  transfers between devices with their start and end apart: 46, of which 17 were waited for; matrix products, arithmetic and copies ran while one was open for 2% of the time, Pallas kernels for 23%

profile of v2, /device:TPU:0, one launch (start us, length us, event | category | flops | bytes accessed | tf_op | source)
XLA Modules:
  0.0 167.1 jit_solution(1359185231482621154)
XLA Ops:
  1.5 2.6 %collective-permute-start.3 = (bf16[16,8192]{1,0:T(8,128)(2,1)S(1)}, bf16[16,8192]{1,0:T(8,128)(2,1)S(1)}, u32[]{:S(2)}, u32[]{:S(2)}) collective-permute-start(bf16[16,8192]{1,0:T(8,128)(2,1)S(1)} %slice_select_fusion.10), channel_id=1, source_target_pairs={{12,0},{0,4},{4,8},{8,12},{13,1},{1,5},{5,9},{9,13},{14,2},{2,6},{... | collective-permute-start | bytes 786440 | tf_op jit(solution)/shard_map/ppermute | solution.py:19
  7.3 2.5 %copy-done.1 = bf16[320,8192]{1,0:T(8,128)(2,1)S(1)} copy-done((bf16[320,8192]{1,0:T(8,128)(2,1)S(1)}, bf16[320,8192]{1,0:T(8,128)(2,1)}, u32[]{:S(2)}) %copy-start.1) | copy-done | bytes 5242904
  9.7 2.0 %copy-done.2 = bf16[208,8192]{1,0:T(8,128)(2,1)S(1)} copy-done((bf16[208,8192]{1,0:T(8,128)(2,1)S(1)}, bf16[208,8192]{1,0:T(8,128)(2,1)}, u32[]{:S(2)}) %copy-start.2) | copy-done | bytes 3407896
  13.7 5.2 %shard_map.46 = bf16[320,416]{1,0:T(8,128)(2,1)S(1)} custom-call(bf16[320,8192]{1,0:T(8,128)(2,1)S(1)} %copy-done.1, bf16[208,8192]{1,0:T(8,128)(2,1)S(1)} %copy-done.2, bf16[208,8192]{1,0:T(8,128)(2,1)S(1)} %copy-done.4), custom_call_target="tpu_custom_call" | custom-call | flops 1 | bytes 1 | tf_op jit(solution)/shard_map/pallas_call | solution.py:60
  24.0 7.3 %shard_map.47 = bf16[320,416]{1,0:T(8,128)(2,1)S(1)} custom-call(bf16[320,8192]{1,0:T(8,128)(2,1)} %collective-permute-done.2.refs_0_.refs_1_, bf16[208,8192]{1,0:T(8,128)(2,1)S(1)} %copy-done.3, bf16[208,8192]{1,0:T(8,128)(2,1)S(1)} %copy-done.5), custom_call_target="tpu_custom_call" | custom-call | flops 1 | bytes 1 | tf_op jit(solution)/shard_map/pallas_call | solution.py:60
  34.7 3.5 %collective-permute-done.5.refs_4_ = bf16[32,8192]{1,0:T(8,128)(2,1)S(1)} collective-permute-done((bf16[32,8192]{1,0:T(8,128)(2,1)S(1)}, bf16[32,8192]{1,0:T(8,128)(2,1)S(1)}, u32[]{:S(2)}, u32[]{:S(2)}) %collective-permute-start.5) | collective-permute-done | bytes 524320 | tf_op jit(solution)/shard_map/ppermute | solution.py:19
  40.9 8.6 %collective-permute-done.8.refs_5_ = bf16[32,8192]{1,0:T(8,128)(2,1)S(1)} collective-permute-done((bf16[32,8192]{1,0:T(8,128)(2,1)S(1)}, bf16[32,8192]{1,0:T(8,128)(2,1)S(1)}, u32[]{:S(2)}, u32[]{:S(2)}) %collective-permute-start.8) | collective-permute-done | bytes 524320 | tf_op jit(solution)/shard_map/ppermute | solution.py:19
  52.2 8.5 %collective-permute-done.13.refs_2_ = bf16[32,8192]{1,0:T(8,128)(2,1)S(1)} collective-permute-done((bf16[32,8192]{1,0:T(8,128)(2,1)S(1)}, bf16[32,8192]{1,0:T(8,128)(2,1)S(1)}, u32[]{:S(2)}, u32[]{:S(2)}) %collective-permute-start.13) | collective-permute-done | bytes 524320 | tf_op jit(solution)/shard_map/ppermute | solution.py:19
  61.9 10.1 %collective-permute-done.12.refs_3_ = bf16[32,8192]{1,0:T(8,128)(2,1)S(1)} collective-permute-done((bf16[32,8192]{1,0:T(8,128)(2,1)S(1)}, bf16[32,8192]{1,0:T(8,128)(2,1)S(1)}, u32[]{:S(2)}, u32[]{:S(2)}) %collective-permute-start.12) | collective-permute-done | bytes 524320 | tf_op jit(solution)/shard_map/ppermute | solution.py:19
  72.0 7.6 %shard_map.48 = bf16[640,224]{1,0:T(8,128)(2,1)S(1)} custom-call(bf16[320,8192]{1,0:T(8,128)(2,1)S(1)} %bitcast.2, bf16[320,8192]{1,0:T(8,128)(2,1)} %collective-permute-done.2.refs_0_.refs_1_, bf16[16,8192]{1,0:T(8,128)(2,1)S(1)} %collective-permute-done.3.refs_2_, bf16[32,8192]{1,0:T(8,128)(2,1)S(1)} %collective-permute-done.1.refs_3_, ...), custom_call_target="tpu_custom_call" | custom-call | flops 1 | bytes 1 | tf_op jit(solution)/shard_map/pallas_call | solution.py:60
  83.4 4.4 %collective-permute-done.15 = bf16[640,224]{1,0:T(8,128)(2,1)S(1)} collective-permute-done((bf16[640,224]{1,0:T(8,128)(2,1)S(1)}, bf16[640,224]{1,0:T(8,128)(2,1)S(1)}, u32[]{:S(2)}, u32[]{:S(2)}) %collective-permute-start.15) | collective-permute-done | bytes 286752 | tf_op jit(solution)/shard_map/ppermute | solution.py:19
  88.0 6.7 %collective-permute-done.21.refs_4_ = bf16[208,768]{1,0:T(8,128)(2,1)S(1)} collective-permute-done((bf16[208,768]{1,0:T(8,128)(2,1)S(1)}, bf16[208,768]{1,0:T(8,128)(2,1)S(1)}, u32[]{:S(2)}, u32[]{:S(2)}) %collective-permute-start.21) | collective-permute-done | bytes 319520 | tf_op jit(solution)/shard_map/ppermute | solution.py:19
  97.1 4.5 %collective-permute-done.20.refs_4_ = bf16[208,768]{1,0:T(8,128)(2,1)S(1)} collective-permute-done((bf16[208,768]{1,0:T(8,128)(2,1)S(1)}, bf16[208,768]{1,0:T(8,128)(2,1)S(1)}, u32[]{:S(2)}, u32[]{:S(2)}) %collective-permute-start.20) | collective-permute-done | bytes 319520 | tf_op jit(solution)/shard_map/ppermute | solution.py:19
  101.6 5.2 %collective-permute-done.19.refs_7_ = bf16[32,8192]{1,0:T(8,128)(2,1)S(1)} collective-permute-done((bf16[32,8192]{1,0:T(8,128)(2,1)S(1)}, bf16[32,8192]{1,0:T(8,128)(2,1)S(1)}, u32[]{:S(2)}, u32[]{:S(2)}) %collective-permute-start.19) | collective-permute-done | bytes 524320 | tf_op jit(solution)/shard_map/ppermute | solution.py:19
  106.7 7.5 %shard_map.49 = bf16[640,192]{1,0:T(8,128)(2,1)S(1)} custom-call(bf16[320,8192]{1,0:T(8,128)(2,1)S(1)} %bitcast.2, bf16[320,8192]{1,0:T(8,128)(2,1)} %collective-permute-done.2.refs_0_.refs_1_, bf16[32,8192]{1,0:T(8,128)(2,1)S(1)} %collective-permute-done.13.refs_2_, bf16[32,8192]{1,0:T(8,128)(2,1)S(1)} %collective-permute-done.12.refs_3_, ...), custom_call_target="tpu_custom_call" | custom-call | flops 1 | bytes 1 | tf_op jit(solution)/shard_map/pallas_call | solution.py:60
  117.5 3.9 %collective-permute-done.22 = bf16[640,192]{1,0:T(8,128)(2,1)S(1)} collective-permute-done((bf16[640,192]{1,0:T(8,128)(2,1)S(1)}, bf16[640,192]{1,0:T(8,128)(2,1)S(1)}, u32[]{:S(2)}, u32[]{:S(2)}) %collective-permute-start.22) | collective-permute-done | bytes 245792 | tf_op jit(solution)/shard_map/ppermute | solution.py:19
  121.8 6.2 %collective-permute-done.27.refs_4_ = bf16[208,768]{1,0:T(8,128)(2,1)S(1)} collective-permute-done((bf16[208,768]{1,0:T(8,128)(2,1)S(1)}, bf16[208,768]{1,0:T(8,128)(2,1)S(1)}, u32[]{:S(2)}, u32[]{:S(2)}) %collective-permute-start.27) | collective-permute-done | bytes 319520 | tf_op jit(solution)/shard_map/ppermute | solution.py:19
  131.4 6.2 %collective-permute-done.32.refs_4_ = bf16[208,512]{1,0:T(8,128)(2,1)S(1)} collective-permute-done((bf16[208,512]{1,0:T(8,128)(2,1)S(1)}, bf16[208,512]{1,0:T(8,128)(2,1)S(1)}, u32[]{:S(2)}, u32[]{:S(2)}) %collective-permute-start.32) | collective-permute-done | bytes 213024 | tf_op jit(solution)/shard_map/ppermute | solution.py:19
  139.4 8.1 %collective-permute-done.31.refs_4_ = bf16[208,512]{1,0:T(8,128)(2,1)S(1)} collective-permute-done((bf16[208,512]{1,0:T(8,128)(2,1)S(1)}, bf16[208,512]{1,0:T(8,128)(2,1)S(1)}, u32[]{:S(2)}, u32[]{:S(2)}) %collective-permute-start.31) | collective-permute-done | bytes 213024 | tf_op jit(solution)/shard_map/ppermute | solution.py:19
  149.7 4.4 %collective-permute-done.39.refs_5_ = bf16[208,512]{1,0:T(8,128)(2,1)S(1)} collective-permute-done((bf16[208,512]{1,0:T(8,128)(2,1)S(1)}, bf16[208,512]{1,0:T(8,128)(2,1)S(1)}, u32[]{:S(2)}, u32[]{:S(2)}) %collective-permute-start.39) | collective-permute-done | bytes 213024 | tf_op jit(solution)/shard_map/ppermute | solution.py:19
  154.1 2.3 %shard_map.50.refs_10_ = bf16[320,8192]{1,0:T(8,128)(2,1)} custom-call(s32[1]{0:T(128)} %bitcast.side_ref, bf16[320,208]{1,0:T(8,128)(2,1)S(1)} %fusion.1.refs_0_, bf16[320,208]{1,0:T(8,128)(2,1)S(1)} %collective-permute-done.7.refs_1_, bf16[320,208]{1,0:T(8,128)(2,1)S(1)} %get-tuple-element.123.refs_2_, ...), custom_call_target="tpu_custom_call" | custom-call | flops 1 | bytes 1 | tf_op jit(solution)/shard_map/pallas_call | solution.py:117
  156.4 2.3 %shard_map.51.refs_10_ = bf16[320,8192]{1,0:T(8,128)(2,1)} custom-call(s32[1]{0:T(128)} %bitcast.side_ref, bf16[320,208]{1,0:T(8,128)(2,1)S(1)} %fusion.1.refs_0_, bf16[320,208]{1,0:T(8,128)(2,1)S(1)} %collective-permute-done.7.refs_1_, bf16[320,208]{1,0:T(8,128)(2,1)S(1)} %get-tuple-element.123.refs_2_, ...), custom_call_target="tpu_custom_call", output_to_operand_aliasing={{}: (11, {})} | custom-call | flops 1 | bytes 1 | tf_op jit(solution)/shard_map/pallas_call | solution.py:117
  158.7 2.3 %shard_map.52.refs_10_ = bf16[320,8192]{1,0:T(8,128)(2,1)} custom-call(s32[1]{0:T(128)} %bitcast.side_ref, bf16[320,208]{1,0:T(8,128)(2,1)S(1)} %fusion.1.refs_0_, bf16[320,208]{1,0:T(8,128)(2,1)S(1)} %collective-permute-done.7.refs_1_, bf16[320,208]{1,0:T(8,128)(2,1)S(1)} %get-tuple-element.123.refs_2_, ...), custom_call_target="tpu_custom_call", output_to_operand_aliasing={{}: (11, {})} | custom-call | flops 1 | bytes 1 | tf_op jit(solution)/shard_map/pallas_call | solution.py:117
  161.0 2.3 %shard_map.53.refs_10_ = bf16[320,8192]{1,0:T(8,128)(2,1)} custom-call(s32[1]{0:T(128)} %bitcast.side_ref, bf16[320,208]{1,0:T(8,128)(2,1)S(1)} %fusion.1.refs_0_, bf16[320,208]{1,0:T(8,128)(2,1)S(1)} %collective-permute-done.7.refs_1_, bf16[320,208]{1,0:T(8,128)(2,1)S(1)} %get-tuple-element.123.refs_2_, ...), custom_call_target="tpu_custom_call", output_to_operand_aliasing={{}: (11, {})} | custom-call | flops 1 | bytes 1 | tf_op jit(solution)/shard_map/pallas_call | solution.py:117
  (109 shorter events, 42.6 us)
Async XLA Ops:
  0.0 22.3 %collective-permute-start.2 = (bf16[320,8192]{1,0:T(8,128)(2,1)}, bf16[320,8192]{1,0:T(8,128)(2,1)}, u32[]{:S(2)}, u32[]{:S(2)}) collective-permute-start(bf16[320,8192]{1,0:T(8,128)(2,1)} %refs_0_.5), channel_id=1, source_target_pairs={{1,0},{0,1},{3,2},{2,3},{5,4},{4,5},{7,6},{6,7},{9,8},{8,9},{11,10... | collective-permute-start | bytes 15728648 | tf_op jit(solution)/shard_map/ppermute | solution.py:19
  1.5 19.0 %collective-permute-start.3 = (bf16[16,8192]{1,0:T(8,128)(2,1)S(1)}, bf16[16,8192]{1,0:T(8,128)(2,1)S(1)}, u32[]{:S(2)}, u32[]{:S(2)}) collective-permute-start(bf16[16,8192]{1,0:T(8,128)(2,1)S(1)} %slice_select_fusion.10), channel_id=1, source_target_pairs={{12,0},{0,4},{4,8},{8,12},{13,1},{1,5},{5,9},{9,13},{14,2},{2,6},{... | collective-permute-start | bytes 786440 | tf_op jit(solution)/shard_map/ppermute | solution.py:19
  4.1 46.6 %collective-permute-start.14 = (bf16[208,8192]{1,0:T(8,128)(2,1)}, bf16[208,8192]{1,0:T(8,128)(2,1)S(1)}, u32[]{:S(2)}, u32[]{:S(2)}) collective-permute-start(bf16[208,8192]{1,0:T(8,128)(2,1)} %refs_8_.11), channel_id=1, source_target_pairs={{1,0},{0,1},{3,2},{2,3},{5,4},{4,5},{7,6},{6,7},{9,8},{8,9},{11,10... | collective-permute-start | bytes 10223624 | tf_op jit(solution)/shard_map/ppermute | solution.py:19
  5.6 25.7 %collective-permute-start.1 = (bf16[32,8192]{1,0:T(8,128)(2,1)S(1)}, bf16[32,8192]{1,0:T(8,128)(2,1)S(1)}, u32[]{:S(2)}, u32[]{:S(2)}) collective-permute-start(bf16[32,8192]{1,0:T(8,128)(2,1)S(1)} %slice_select_fusion.5), channel_id=1, source_target_pairs={{12,0},{0,4},{4,8},{8,12},{13,1},{1,5},{5,9},{9,13},{14,2},{2,6},{... | collective-permute-start | bytes 1572872 | tf_op jit(solution)/shard_map/ppermute | solution.py:19
  22.3 15.8 %collective-permute-start.5 = (bf16[32,8192]{1,0:T(8,128)(2,1)S(1)}, bf16[32,8192]{1,0:T(8,128)(2,1)S(1)}, u32[]{:S(2)}, u32[]{:S(2)}) collective-permute-start(bf16[32,8192]{1,0:T(8,128)(2,1)S(1)} %get-tuple-element.66), channel_id=1, source_target_pairs={{12,0},{0,4},{4,8},{8,12},{13,1},{1,5},{5,9},{9,13},{14,2},{2,6},{... | collective-permute-start | bytes 1572872 | tf_op jit(solution)/shard_map/ppermute | solution.py:19
  31.9 17.6 %collective-permute-start.9 = (bf16[32,8192]{1,0:T(8,128)(2,1)S(1)}, bf16[32,8192]{1,0:T(8,128)(2,1)S(1)}, u32[]{:S(2)}, u32[]{:S(2)}) collective-permute-start(bf16[32,8192]{1,0:T(8,128)(2,1)S(1)} %collective-permute-done.1.refs_3_), channel_id=1, source_target_pairs={{16,0},{0,16},{17,1},{1,17},{18,2},{2,18},{19,3},{3,19},{20,4},{4,... | collective-permute-start | bytes 1572872 | tf_op jit(solution)/shard_map/ppermute | solution.py:19
  32.8 16.7 %collective-permute-start.8 = (bf16[32,8192]{1,0:T(8,128)(2,1)S(1)}, bf16[32,8192]{1,0:T(8,128)(2,1)S(1)}, u32[]{:S(2)}, u32[]{:S(2)}) collective-permute-start(bf16[32,8192]{1,0:T(8,128)(2,1)S(1)} %get-tuple-element.69), channel_id=1, source_target_pairs={{12,0},{0,4},{4,8},{8,12},{13,1},{1,5},{5,9},{9,13},{14,2},{2,6},{... | collective-permute-start | bytes 1572872 | tf_op jit(solution)/shard_map/ppermute | solution.py:19
  38.2 22.6 %collective-permute-start.10 = (bf16[32,8192]{1,0:T(8,128)(2,1)S(1)}, bf16[32,8192]{1,0:T(8,128)(2,1)S(1)}, u32[]{:S(2)}, u32[]{:S(2)}) collective-permute-start(bf16[32,8192]{1,0:T(8,128)(2,1)S(1)} %collective-permute-done.5.refs_4_), channel_id=1, source_target_pairs={{16,0},{0,16},{17,1},{1,17},{18,2},{2,18},{19,3},{3,19},{20,4},{4,... | collective-permute-start | bytes 1572872 | tf_op jit(solution)/shard_map/ppermute | solution.py:19
  40.3 20.5 %collective-permute-start.13 = (bf16[32,8192]{1,0:T(8,128)(2,1)S(1)}, bf16[32,8192]{1,0:T(8,128)(2,1)S(1)}, u32[]{:S(2)}, u32[]{:S(2)}) collective-permute-start(bf16[32,8192]{1,0:T(8,128)(2,1)S(1)} %get-tuple-element.72), channel_id=1, source_target_pairs={{12,0},{0,4},{4,8},{8,12},{13,1},{1,5},{5,9},{9,13},{14,2},{2,6},{... | collective-permute-start | bytes 1572872 | tf_op jit(solution)/shard_map/ppermute | solution.py:19
  49.5 22.5 %collective-permute-start.11 = (bf16[32,8192]{1,0:T(8,128)(2,1)S(1)}, bf16[32,8192]{1,0:T(8,128)(2,1)S(1)}, u32[]{:S(2)}, u32[]{:S(2)}) collective-permute-start(bf16[32,8192]{1,0:T(8,128)(2,1)S(1)} %collective-permute-done.8.refs_5_), channel_id=1, source_target_pairs={{16,0},{0,16},{17,1},{1,17},{18,2},{2,18},{19,3},{3,19},{20,4},{4,... | collective-permute-start | bytes 1572872 | tf_op jit(solution)/shard_map/ppermute | solution.py:19
  50.6 21.4 %collective-permute-start.12 = (bf16[32,8192]{1,0:T(8,128)(2,1)S(1)}, bf16[32,8192]{1,0:T(8,128)(2,1)S(1)}, u32[]{:S(2)}, u32[]{:S(2)}) collective-permute-start(bf16[32,8192]{1,0:T(8,128)(2,1)S(1)} %get-tuple-element.71), channel_id=1, source_target_pairs={{12,0},{0,4},{4,8},{8,12},{13,1},{1,5},{5,9},{9,13},{14,2},{2,6},{... | collective-permute-start | bytes 1572872 | tf_op jit(solution)/shard_map/ppermute | solution.py:19
  60.7 21.7 %collective-permute-start.16 = (bf16[32,8192]{1,0:T(8,128)(2,1)S(1)}, bf16[32,8192]{1,0:T(8,128)(2,1)S(1)}, u32[]{:S(2)}, u32[]{:S(2)}) collective-permute-start(bf16[32,8192]{1,0:T(8,128)(2,1)S(1)} %get-tuple-element.84), channel_id=1, source_target_pairs={{12,0},{0,4},{4,8},{8,12},{13,1},{1,5},{5,9},{9,13},{14,2},{2,6},{... | collective-permute-start | bytes 1572872 | tf_op jit(solution)/shard_map/ppermute | solution.py:19
  60.7 21.7 %collective-permute-start.17 = (bf16[32,8192]{1,0:T(8,128)(2,1)S(1)}, bf16[32,8192]{1,0:T(8,128)(2,1)S(1)}, u32[]{:S(2)}, u32[]{:S(2)}) collective-permute-start(bf16[32,8192]{1,0:T(8,128)(2,1)S(1)} %collective-permute-done.13.refs_2_), channel_id=1, source_target_pairs={{16,0},{0,16},{17,1},{1,17},{18,2},{2,18},{19,3},{3,19},{20,4},{4,... | collective-permute-start | bytes 1572872 | tf_op jit(solution)/shard_map/ppermute | solution.py:19
  80.7 14.9 %collective-permute-start.18 = (bf16[32,8192]{1,0:T(8,128)(2,1)S(1)}, bf16[32,8192]{1,0:T(8,128)(2,1)S(1)}, u32[]{:S(2)}, u32[]{:S(2)}) collective-permute-start(bf16[32,8192]{1,0:T(8,128)(2,1)S(1)} %collective-permute-done.12.refs_3_), channel_id=1, source_target_pairs={{16,0},{0,16},{17,1},{1,17},{18,2},{2,18},{19,3},{3,19},{20,4},{4,... | collective-permute-start | bytes 1572872 | tf_op jit(solution)/shard_map/ppermute | solution.py:19
  82.4 24.3 %collective-permute-start.19 = (bf16[32,8192]{1,0:T(8,128)(2,1)S(1)}, bf16[32,8192]{1,0:T(8,128)(2,1)S(1)}, u32[]{:S(2)}, u32[]{:S(2)}) collective-permute-start(bf16[32,8192]{1,0:T(8,128)(2,1)S(1)} %collective-permute-done.16.refs_4_), channel_id=1, source_target_pairs={{16,0},{0,16},{17,1},{1,17},{18,2},{2,18},{19,3},{3,19},{20,4},{4,... | collective-permute-start | bytes 1572872 | tf_op jit(solution)/shard_map/ppermute | solution.py:19
  83.0 18.5 %collective-permute-start.20 = (bf16[208,768]{1,0:T(8,128)(2,1)S(1)}, bf16[208,768]{1,0:T(8,128)(2,1)S(1)}, u32[]{:S(2)}, u32[]{:S(2)}) collective-permute-start(bf16[208,768]{1,0:T(8,128)(2,1)S(1)} %get-tuple-element.88), channel_id=1, source_target_pairs={{12,0},{0,4},{4,8},{8,12},{13,1},{1,5},{5,9},{9,13},{14,2},{2,6},{... | collective-permute-start | bytes 958472 | tf_op jit(solution)/shard_map/ppermute | solution.py:19
  95.6 20.6 %collective-permute-start.23 = (bf16[208,768]{1,0:T(8,128)(2,1)S(1)}, bf16[208,768]{1,0:T(8,128)(2,1)S(1)}, u32[]{:S(2)}, u32[]{:S(2)}) collective-permute-start(bf16[208,768]{1,0:T(8,128)(2,1)S(1)} %get-tuple-element.98), channel_id=1, source_target_pairs={{12,0},{0,4},{4,8},{8,12},{13,1},{1,5},{5,9},{9,13},{14,2},{2,6},{... | collective-permute-start | bytes 958472 | tf_op jit(solution)/shard_map/ppermute | solution.py:19
  95.6 20.6 %collective-permute-start.24 = (bf16[208,768]{1,0:T(8,128)(2,1)S(1)}, bf16[208,768]{1,0:T(8,128)(2,1)S(1)}, u32[]{:S(2)}, u32[]{:S(2)}) collective-permute-start(bf16[208,768]{1,0:T(8,128)(2,1)S(1)} %collective-permute-done.21.refs_4_), channel_id=1, source_target_pairs={{16,0},{0,16},{17,1},{1,17},{18,2},{2,18},{19,3},{3,19},{20,4},{4,... | collective-permute-start | bytes 958472 | tf_op jit(solution)/shard_map/ppermute | solution.py:19
  97.1 19.2 %collective-permute-start.25 = (bf16[208,768]{1,0:T(8,128)(2,1)S(1)}, bf16[208,768]{1,0:T(8,128)(2,1)S(1)}, u32[]{:S(2)}, u32[]{:S(2)}) collective-permute-start(bf16[208,768]{1,0:T(8,128)(2,1)S(1)} %collective-permute-done.21.refs_4_), channel_id=1, source_target_pairs={{1,0},{0,1},{3,2},{2,3},{5,4},{4,5},{7,6},{6,7},{9,8},{8,9},{11,10... | collective-permute-start | bytes 958472 | tf_op jit(solution)/shard_map/ppermute | solution.py:19
  116.3 21.3 %collective-permute-start.33 = (bf16[208,768]{1,0:T(8,128)(2,1)S(1)}, bf16[208,768]{1,0:T(8,128)(2,1)S(1)}, u32[]{:S(2)}, u32[]{:S(2)}) collective-permute-start(bf16[208,768]{1,0:T(8,128)(2,1)S(1)} %collective-permute-done.23.refs_4_), channel_id=1, source_target_pairs={{16,0},{0,16},{17,1},{1,17},{18,2},{2,18},{19,3},{3,19},{20,4},{4,... | collective-permute-start | bytes 958472 | tf_op jit(solution)/shard_map/ppermute | solution.py:19
  130.3 17.1 %collective-permute-start.36 = (bf16[208,768]{1,0:T(8,128)(2,1)S(1)}, bf16[208,768]{1,0:T(8,128)(2,1)S(1)}, u32[]{:S(2)}, u32[]{:S(2)}) collective-permute-start(bf16[208,768]{1,0:T(8,128)(2,1)S(1)} %collective-permute-done.27.refs_4_), channel_id=1, source_target_pairs={{16,0},{0,16},{17,1},{1,17},{18,2},{2,18},{19,3},{3,19},{20,4},{4,... | collective-permute-start | bytes 958472 | tf_op jit(solution)/shard_map/ppermute | solution.py:19
  148.6 14.7 %collective-permute-start.43 = (bf16[208,512]{1,0:T(8,128)(2,1)S(1)}, bf16[208,512]{1,0:T(8,128)(2,1)S(1)}, u32[]{:S(2)}, u32[]{:S(2)}) collective-permute-start(bf16[208,512]{1,0:T(8,128)(2,1)S(1)} %collective-permute-done.32.refs_4_), channel_id=1, source_target_pairs={{1,0},{0,1},{3,2},{2,3},{5,4},{4,5},{7,6},{6,7},{9,8},{8,9},{11,10... | collective-permute-start | bytes 638984 | tf_op jit(solution)/shard_map/ppermute | solution.py:19
  149.2 14.2 %collective-permute-start.44 = (bf16[208,512]{1,0:T(8,128)(2,1)S(1)}, bf16[208,512]{1,0:T(8,128)(2,1)S(1)}, u32[]{:S(2)}, u32[]{:S(2)}) collective-permute-start(bf16[208,512]{1,0:T(8,128)(2,1)S(1)} %collective-permute-done.42.refs_5_), channel_id=1, source_target_pairs={{1,0},{0,1},{3,2},{2,3},{5,4},{4,5},{7,6},{6,7},{9,8},{8,9},{11,10... | collective-permute-start | bytes 638984 | tf_op jit(solution)/shard_map/ppermute | solution.py:19
  149.2 16.0 %collective-permute-start.40 = (bf16[208,512]{1,0:T(8,128)(2,1)S(1)}, bf16[208,512]{1,0:T(8,128)(2,1)S(1)}, u32[]{:S(2)}, u32[]{:S(2)}) collective-permute-start(bf16[208,512]{1,0:T(8,128)(2,1)S(1)} %collective-permute-done.31.refs_4_), channel_id=1, source_target_pairs={{1,0},{0,1},{3,2},{2,3},{5,4},{4,5},{7,6},{6,7},{9,8},{8,9},{11,10... | collective-permute-start | bytes 638984 | tf_op jit(solution)/shard_map/ppermute | solution.py:19
  (30 other events, 343.2 us)

commit v3 on v0

v3 whole, which is shorter than its diff:
```python
import functools

import jax
import jax.numpy as jnp
from jax import lax
from jax.experimental import pallas as pl
from jax.experimental.pallas import tpu as pltpu
from jax.sharding import PartitionSpec as P

GATE_SHARES = (6, 7)
UP_SHARES = (6, 7)
LANE_SHARES = (5, 5, 3, 2, 1)
VMEM = 24 * 1024 * 1024
CHEAP = pl.CostEstimate(flops=1, bytes_accessed=1, transcendentals=0)


def shifted(block, axis, distance):
    devices = range(lax.axis_size(axis))
    route = [((i - distance) % len(devices), i) for i in devices]
    return lax.ppermute(block, axis, route)


def mate(block):
    return shifted(block, "sub", 1)


def across(block):
    return shifted(block, "groups", 1)


def tied(value, *earlier):
    earlier = [e for e in earlier if e is not None]
    return lax.optimization_barrier((value, *earlier))[0] if earlier else value


def cuts(total, unit, shares):
    units, whole, done, marks = total // unit, sum(shares), 0, [0]
    for share in shares:
        done += share
        marks.append(units * done // whole * unit)
    marks[-1] = total
    return list(zip(marks[:-1], marks[1:]))


def by_features(rows, units):
    return lax.dot_general(
        rows, units, (((1,), (1,)), ((), ())), preferred_element_type=jnp.float32
    )


def products_kernel(sets, outs, block, steps, side_ref, *refs):
    count = len(refs) - len(outs) - 1
    operands, out_refs, total = refs[:count], refs[count:-1], refs[-1]
    side = side_ref[0]
    total[...] = jnp.zeros_like(total)

    def body(*blocks):
        units = jnp.concatenate([ref[...] for ref in blocks[len(sets) :]], axis=0)
        at = 0
        for ref in blocks[: len(sets)]:
            rows = ref.shape[0]
            total[at : at + rows] += by_features(ref[...], units)
            at += rows

    pltpu.emit_pipeline(
        body,
        grid=(steps,),
        in_specs=[
            pl.BlockSpec(
                (ref.shape[0], block),
                (lambda k: (0, side * steps + k))
                if i < len(sets) and sets[i]
                else (lambda k: (0, k)),
            )
            for i, ref in enumerate(operands)
        ],
    )(*operands)
    at = 0
    for out_ref in out_refs:
        rows = out_ref.shape[0]
        out_ref[...] = total[at : at + rows].astype(out_ref.dtype)
        at += rows


def products(side, row_sets, halved, unit_sets, out_types):
    width = unit_sets[0].shape[1]
    block = 1024 if width % 1024 == 0 else width
    count = sum(u.shape[0] for u in unit_sets)
    rows = sum(r.shape[0] for r in row_sets)
    part = rows // len(out_types)
    operands = (*row_sets, *unit_sets)
    return pl.pallas_call(
        functools.partial(
            products_kernel, halved, out_types, block, width // block
        ),
        in_specs=[pl.BlockSpec(memory_space=pltpu.SMEM)]
        + [pl.BlockSpec(memory_space=pltpu.HBM)] * len(operands),
        out_specs=[pl.BlockSpec(memory_space=pltpu.VMEM)] * len(out_types),
        out_shape=[jax.ShapeDtypeStruct((part, count), t) for t in out_types],
        scratch_shapes=[pltpu.VMEM((rows, count), jnp.float32)],
        compiler_params=pltpu.CompilerParams(vmem_limit_bytes=VMEM),
        cost_estimate=CHEAP,
    )(side, *operands)


def output_kernel(parts, side_ref, *refs):
    hidden, (down, down_mate) = refs[:4], refs[4:6]
    arrived = refs[6 : 6 + 4 * len(parts)]
    out, here, here_mate, block, sems = refs[-5:]
    side = side_ref[0]
    loads, stores, at = [], [], 0
    for i, (a, b, _) in enumerate(parts):
        spot = pl.ds(at, b - a)
        loads.append(
            [
                pltpu.make_async_copy(down.at[:, a:b], here.at[:, spot], sems.at[i, 0]),
                pltpu.make_async_copy(
                    down_mate.at[:, a:b], here_mate.at[:, spot], sems.at[i, 1]
                ),
            ]
        )
        stores.append(
            pltpu.make_async_copy(block.at[:, spot], out.at[:, a:b], sems.at[i, 2])
        )
        at += b - a
    for pair in loads:
        for copy in pair:
            copy.start()
    at = 0
    for i, (a, b, whole) in enumerate(parts):
        for copy in loads[i]:
            copy.wait()
        half = (b - a) // 2
        for j in range(2):
            where = (j if whole else side + j - 2 * side * j) * half
            lanes = pl.ds(pl.multiple_of(at + where, 128), half)
            sources = arrived[4 * i : 4 * i + 4]
            if whole:
                own = sources[0][:, j * half : (j + 1) * half]
                own_mate = sources[2][:, j * half : (j + 1) * half]
            else:
                own, own_mate = sources[j][...], sources[2 + j][...]
            total = None
            for rows, units in (
                (hidden[0], here[:, lanes]),
                (hidden[1], here_mate[:, lanes]),
                (hidden[2], own),
                (hidden[3], own_mate),
            ):
                term = jnp.dot(rows[...], units, preferred_element_type=jnp.float32)
                total = term if total is None else total + term
            block[:, lanes] = total.astype(block.dtype)
        stores[i].start()
        at += b - a
    for copy in stores:
        copy.wait()


def output_part(result, parts, side, hidden, arrived, down, down_mate):
    rows, units, width = hidden[0].shape[0], down.shape[0], down.shape[1]
    lanes = sum(b - a for a, b, _ in parts)
    any_space = pl.BlockSpec(memory_space=pl.ANY)
    whole = pl.BlockSpec(memory_space=pltpu.VMEM)
    operands = [side, *hidden, down, down_mate, *arrived]
    in_specs = (
        [pl.BlockSpec(memory_space=pltpu.SMEM)]
        + [whole] * 4
        + [any_space] * 2
        + [whole] * len(arrived)
    )
    aliases = {}
    if result is not None:
        aliases = {len(operands): 0}
        operands.append(result)
        in_specs.append(any_space)
    return pl.pallas_call(
        functools.partial(output_kernel, parts),
        in_specs=in_specs,
        out_specs=any_space,
        out_shape=jax.ShapeDtypeStruct((rows, width), jnp.bfloat16),
        scratch_shapes=[
            pltpu.VMEM((units, lanes), jnp.bfloat16),
            pltpu.VMEM((units, lanes), jnp.bfloat16),
            pltpu.VMEM((rows, lanes), jnp.bfloat16),
            pltpu.SemaphoreType.DMA((len(parts), 3)),
        ],
        input_output_aliases=aliases,
        compiler_params=pltpu.CompilerParams(vmem_limit_bytes=VMEM),
        cost_estimate=CHEAP,
    )(*operands)


def over_slices(partial_value):
    return [
        shifted(partial_value, "tensor", distance)
        for distance in range(1, lax.axis_size("tensor"))
    ]


def summed(partial_value, sent):
    total = partial_value.astype(jnp.float32)
    for block in sent:
        total = total + block.astype(jnp.float32)
    return total


def gated(gate, up):
    return (jax.nn.silu(gate) * up).astype(jnp.bfloat16)


def on_device(tokens, gate_weight, up_weight, down_weight):
    units, width = gate_weight.shape
    rows = tokens.shape[0]
    half = width // 2
    group = lax.axis_index("groups").astype(jnp.int32)
    side = group.reshape(1)

    def own_half(array, a, b):
        return lax.dynamic_slice(array, (a, group * half), (b - a, half))

    lane_cuts = [(2 * a, 2 * b) for a, b in cuts(half, 128, LANE_SHARES)]
    last = len(lane_cuts) - 1

    def down_piece(i):
        a, b = lane_cuts[i]
        if i == last:
            return down_later[:, a:b]
        return lax.dynamic_slice(
            down_later, (0, a + group * ((b - a) // 2)), (units, (b - a) // 2)
        )

    gate_cuts, up_cuts = cuts(units, 16, GATE_SHARES), cuts(units, 16, UP_SHARES)
    first = own_half(gate_weight, *gate_cuts[0])
    second = own_half(tied(gate_weight, first), *gate_cuts[1])
    swapped = lax.dynamic_slice(
        tied(tokens, second), (0, (1 - group) * half), (rows, half)
    )
    tokens_later, up_later, down_later = (
        tied(array, swapped) for array in (tokens, up_weight, down_weight)
    )
    pieces = [first, second]
    pieces += [own_half(up_later, a, b) for a, b in up_cuts]
    pieces += [down_piece(i) for i in range(len(lane_cuts))]
    base = len(pieces) - len(lane_cuts)

    waiting = [shifted(piece, "dp", 1) for piece in pieces[:2]]
    landed = []

    def take(*after):
        i = len(landed)
        landed.append(tied(waiting[i], *landed[-1:], *after))
        if i + 2 < len(pieces):
            waiting.append(shifted(tied(pieces[i + 2], landed[i]), "dp", 1))
        return landed[i]

    tokens_other = across(swapped)
    weights = [gate_weight, up_later]
    weights += [mate(weight) for weight in weights]
    down_mate = mate(down_later)

    def joint(unit_sets, *after):
        return products(
            side,
            [tokens_later, tokens_other],
            [True, False],
            [tied(u, *after) for u in unit_sets],
            [jnp.float32, jnp.bfloat16],
        )

    def one_slice(kept, given, *after):
        return (kept + tied(given, *after).astype(jnp.float32)).astype(jnp.bfloat16)

    own, other, own_mate, other_mate = {}, {}, {}, {}

    def spread(i, block):
        own[i] = block
        own_mate[i] = mate(block)
        if i < last:
            other[i] = across(block)

    def pass_on(i, *after):
        other[i] = tied(other[i], *after)
        other_mate[i] = mate(other[i])
        return other[i]

    def activated(pre):
        parts = [pre[:, i * units : (i + 1) * units] for i in range(4)]
        return gated(parts[0], parts[1]), gated(parts[2], parts[3])

    now = take()
    gate_a, gate_a_mate = now, mate(now)
    (mine,) = products(
        side, [tied(tokens_later, now)], [False], weights, [jnp.bfloat16]
    )
    mine_sent = over_slices(mine)

    now = take(mine)
    gate_b, gate_b_mate = now, mate(now)
    here, here_mate = activated(summed(mine, [tied(block, now) for block in mine_sent]))

    now = take(here, here_mate)
    up_a, up_a_mate = now, mate(now)
    tokens_other = tied(tokens_other, now)
    kept_a, sent_a = joint([gate_a, gate_b, gate_a_mate, gate_b_mate], tokens_other)
    given_a = across(sent_a)

    now = take(sent_a)
    kept_b, sent_b = joint([up_a, now, up_a_mate, mate(now)], now)
    given_b = across(sent_b)
    part_a = one_slice(kept_a, given_a, sent_b)
    slices_a = over_slices(part_a)

    now = take(part_a)
    spread(0, now)
    part_b = one_slice(kept_b, given_b, now)
    slices_b = over_slices(part_b)

    now = take(part_b)
    spread(1, now)
    gate_pre = summed(part_a, [tied(block, now) for block in slices_a])
    up_pre = summed(part_b, [tied(block, now) for block in slices_b])
    there = gated(gate_pre[:, :units], up_pre[:, :units])
    there_mate = gated(gate_pre[:, units:], up_pre[:, units:])
    now = pass_on(0, there, there_mate)

    now = take(now)
    spread(2, now)
    now = pass_on(1, now, down_mate)

    hidden = [here, here_mate, there, there_mate]

    def write(result, *which):
        parts, arrived = [], []
        for i in which:
            a, b = lane_cuts[i]
            whole = i == last
            parts.append((a, b, whole))
            arrived += (
                [own[i], own[i], own_mate[i], own_mate[i]]
                if whole
                else [own[i], other[i], own_mate[i], other_mate[i]]
            )
        return output_part(
            result, tuple(parts), side, hidden, arrived, down_weight, down_mate
        )

    result = write(None, 0, 1)
    now = take(now, result)
    spread(3, now)
    now = pass_on(2, now)
    now = take(now)
    spread(4, now)
    pass_on(3, now)
    result = write(result, 2)
    return write(result, 3, 4)


def solution(mesh):
    return jax.shard_map(
        on_device,
        mesh=mesh,
        in_specs=(
            P(("groups", "dp", "sub"), "tensor"),
            P(("dp", "sub"), "tensor"),
            P(("dp", "sub"), "tensor"),
            P(("dp", "sub"), "tensor"),
        ),
        out_specs=P(("groups", "dp", "sub"), "tensor"),
        check_vma=False,
    )
```

time: 582 us -> 173 us (0.30)
  waiting for transfers between devices: 494 us -> 88.7 us
  matrix products: 39.3 us -> 0 us
  Pallas kernels: 0 us -> 36.7 us
  starting transfers between devices: 1.79 us -> 16.7 us
  between operations: 13.4 us -> 0.42 us
  other arithmetic: 12.1 us -> 5.35 us
    ppermute x1 -> x35, waiting for transfers between devices: 415 us -> 88.7 us  [shifted(): return lax.ppermute(block, axis, route)]
    psum x1 -> x0, waiting for transfers between devices: 41.8 us -> none  [apply_span(): lax.psum(partial_value.astype(jnp.bfloat16), 'tensor').astype(jnp.float32)]
    dot_general x4 -> x0, matrix products: 39.3 us -> none  [the longest x2 25.8 us: apply_span(): lax.dot_general(tokens, both, (((1,), (1,)), ((), ())), preferred_element...]
    all_gather x1 -> x0, waiting for transfers between devices: 37 us -> none  [on_device(): current = lax.all_gather(own_share, 'sub', axis=1, tiled=True)]
    pallas_call x0 -> x6, Pallas kernels: none -> 36.7 us  [the longest x3 21.8 us: products(): pl.pallas_call(functools.partial(products_kernel, halved, out_types, bloc...]
    slice x2 -> x1, local copies, waits for them, and re-layouts: 18.3 us -> 0.05 us  [down_piece(): return down_later[:, a:b]]
    ppermute x1 -> x35, starting transfers between devices: 1.74 us -> 16.7 us  [shifted(): return lax.ppermute(block, axis, route)]
    unnamed x6 -> x36, local copies, waits for them, and re-layouts: 2.97 us -> 15.3 us
  transfers between devices with their start and end apart: 3 -> 35, of which waited for: 3 -> 15; matrix products, arithmetic and copies ran while one was open for 5% -> 4% of each run, Pallas kernels for 0% -> 20%
where the time goes in v3:
time: 173 us; the launch traced here: 172 us
  waiting for transfers between devices  88.7 us (51%)
  Pallas kernels  36.7 us (21%)
  local copies, waits for them, and re-layouts  24 us (14%)
  starting transfers between devices  16.7 us (10%)
  other arithmetic  5.35 us (3%)
    ppermute x35, waiting for transfers between devices, shifted(): return lax.ppermute(block, axis, route)  88.7 us
    pallas_call x3, Pallas kernels, products(): pl.pallas_call(functools.partial(products_kernel, halved, out_types, bloc...  21.8 us
    ppermute x35, starting transfers between devices, shifted(): return lax.ppermute(block, axis, route)  16.7 us
    unnamed x36, local copies, waits for them, and re-layouts  15.3 us
    pallas_call x3, Pallas kernels, output_part(): pl.pallas_call(functools.partial(output_kernel, parts), in_specs=in_specs...  14.9 us
    dynamic_slice x4, local copies, waits for them, and re-layouts, own_half(): return lax.dynamic_slice(array, (a, group * half), (b - a, half))  5.66 us
  transfers between devices with their start and end apart: 35, of which 15 were waited for; matrix products, arithmetic and copies ran while one was open for 4% of the time, Pallas kernels for 20%

profile of v3, /device:TPU:0, one launch (start us, length us, event | category | flops | bytes accessed | tf_op | source)
XLA Modules:
  0.0 171.9 jit_solution(633373949117922406)
XLA Ops:
  0.0 2.1 %constant_dynamic-slice_fusion.6 = bf16[96,4096]{1,0:T(8,128)(2,1)} fusion(bf16[208,8192]{1,0:T(8,128)(2,1)} %refs_1_.1, s32[]{:T(128)S(6)} %select_n.21), kind=kLoop, calls=%fused_computation.19 | loop fusion | bytes 1572868 | tf_op jit(solution)/shard_map/dynamic_slice | solution.py:219
  2.1 2.3 %constant_dynamic-slice_fusion.8 = bf16[112,4096]{1,0:T(8,128)(2,1)} fusion(bf16[208,8192]{1,0:T(8,128)(2,1)} %refs_1_.1, s32[]{:T(128)S(6)} %select_n.21), kind=kLoop, calls=%fused_computation.21 | loop fusion | bytes 1835012 | tf_op jit(solution)/shard_map/dynamic_slice | solution.py:219
  4.4 2.1 %constant_dynamic-slice_fusion.5 = bf16[320,4096]{1,0:T(8,128)(2,1)S(1)} fusion(bf16[320,8192]{1,0:T(8,128)(2,1)} %refs_0_.2, s32[]{:T(128)S(6)} %select_n.22), kind=kLoop, calls=%fused_computation.18 | loop fusion | bytes 5242884 | tf_op jit(solution)/shard_map/dynamic_slice | solution.py:235
  7.1 2.9 %collective-permute-start.5 = (bf16[320,4096]{1,0:T(8,128)(2,1)S(1)}, bf16[320,4096]{1,0:T(8,128)(2,1)S(1)}, u32[]{:S(2)}, u32[]{:S(2)}) collective-permute-start(bf16[320,4096]{1,0:T(8,128)(2,1)S(1)} %constant_dynamic-slice_fusion.5), channel_id=1, source_target_pairs={{16,0},{0,16},{17,1},{1,17},{18,2},{2,18},{19,3},{3,19},{20,4},{4,... | collective-permute-start | bytes 7864328 | tf_op jit(solution)/shard_map/ppermute | solution.py:20
  14.4 18.1 %collective-permute-done.refs_2_ = bf16[96,4096]{1,0:T(8,128)(2,1)S(1)} collective-permute-done((bf16[96,4096]{1,0:T(8,128)(2,1)}, bf16[96,4096]{1,0:T(8,128)(2,1)S(1)}, u32[]{:S(2)}, u32[]{:S(2)}) %collective-permute-start) | collective-permute-done | bytes 786464 | tf_op jit(solution)/shard_map/ppermute | solution.py:20
  32.6 2.0 %copy-done.5 = bf16[208,8192]{1,0:T(8,128)(2,1)S(1)} copy-done((bf16[208,8192]{1,0:T(8,128)(2,1)S(1)}, bf16[208,8192]{1,0:T(8,128)(2,1)}, u32[]{:S(2)}) %copy-start.5) | copy-done | bytes 3407896
  34.5 2.0 %copy-done.6 = bf16[208,8192]{1,0:T(8,128)(2,1)S(1)} copy-done((bf16[208,8192]{1,0:T(8,128)(2,1)S(1)}, bf16[208,8192]{1,0:T(8,128)(2,1)}, u32[]{:S(2)}) %copy-start.6) | copy-done | bytes 3407896
  36.5 10.6 %shard_map.46 = bf16[320,832]{1,0:T(8,128)(2,1)S(1)} custom-call(s32[1]{0:T(128)} %bitcast.side_ref, bf16[320,8192]{1,0:T(8,128)(2,1)S(1)} %copy-done, bf16[208,8192]{1,0:T(8,128)(2,1)S(1)} %copy-done.5, bf16[208,8192]{1,0:T(8,128)(2,1)S(1)} %copy-done.6, bf16[208,8192]{1,0:T(8,128)(2,1)S(1)} %collective-permute-done.1.refs_3_, ...), custom_call_target="tpu_custom_call" | custom-call | flops 1 | bytes 1 | tf_op jit(solution)/shard_map/pallas_call | solution.py:92
  48.7 3.5 %collective-permute-done.4.refs_3_ = bf16[112,4096]{1,0:T(8,128)(2,1)S(1)} collective-permute-done((bf16[112,4096]{1,0:T(8,128)(2,1)}, bf16[112,4096]{1,0:T(8,128)(2,1)S(1)}, u32[]{:S(2)}, u32[]{:S(2)}) %collective-permute-start.4) | collective-permute-done | bytes 917536 | tf_op jit(solution)/shard_map/ppermute | solution.py:20
  52.2 15.8 %collective-permute-done.6.refs_2_ = bf16[96,4096]{1,0:T(8,128)(2,1)} collective-permute-done((bf16[96,4096]{1,0:T(8,128)(2,1)S(1)}, bf16[96,4096]{1,0:T(8,128)(2,1)}, u32[]{:S(2)}, u32[]{:S(2)}) %collective-permute-start.6) | collective-permute-done | bytes 786464 | tf_op jit(solution)/shard_map/ppermute | solution.py:20
  70.3 5.2 %shard_map.47 = (f32[320,416]{1,0:T(8,128)S(1)}, bf16[320,416]{1,0:T(8,128)(2,1)S(1)}) custom-call(s32[1]{0:T(128)} %bitcast.side_ref, bf16[320,8192]{1,0:T(8,128)(2,1)S(1)} %copy-done, bf16[320,4096]{1,0:T(8,128)(2,1)S(1)} %collective-permute-done.5.refs_1_, bf16[96,4096]{1,0:T(8,128)(2,1)S(1)} %collective-permute-done.refs_2_, ...), custom_call_target="tpu_custom_call" | custom-call | flops 1 | bytes 1 | tf_op jit(solution)/shard_map/pallas_call | solution.py:92
  77.1 14.0 %collective-permute-done.10.refs_3_ = bf16[112,4096]{1,0:T(8,128)(2,1)} collective-permute-done((bf16[112,4096]{1,0:T(8,128)(2,1)S(1)}, bf16[112,4096]{1,0:T(8,128)(2,1)}, u32[]{:S(2)}, u32[]{:S(2)}) %collective-permute-start.10) | collective-permute-done | bytes 917536 | tf_op jit(solution)/shard_map/ppermute | solution.py:20
  95.1 2.5 %copy-done.1 = bf16[320,8192]{1,0:T(8,128)(2,1)S(1)} copy-done((bf16[320,8192]{1,0:T(8,128)(2,1)S(1)}, bf16[320,8192]{1,0:T(8,128)(2,1)}, u32[]{:S(2)}) %copy-start.1) | copy-done | bytes 5242904
  97.5 1.7 %copy-done.4 = bf16[320,4096]{1,0:T(8,128)(2,1)S(1)} copy-done((bf16[320,4096]{1,0:T(8,128)(2,1)S(1)}, bf16[320,4096]{1,0:T(8,128)(2,1)}, u32[]{:S(2)}) %copy-start.4) | copy-done | bytes 2621464
  99.3 6.0 %shard_map.48 = (f32[320,416]{1,0:T(8,128)S(1)}, bf16[320,416]{1,0:T(8,128)(2,1)S(1)}) custom-call(s32[1]{0:T(128)} %bitcast.side_ref, bf16[320,8192]{1,0:T(8,128)(2,1)S(1)} %copy-done.1, bf16[320,4096]{1,0:T(8,128)(2,1)S(1)} %copy-done.4, bf16[96,4096]{1,0:T(8,128)(2,1)} %collective-permute-done.6.refs_2_, ...), custom_call_target="tpu_custom_call" | custom-call | flops 1 | bytes 1 | tf_op jit(solution)/shard_map/pallas_call | solution.py:92
  108.4 6.7 %collective-permute-done.16 = bf16[320,416]{1,0:T(8,128)(2,1)S(1)} collective-permute-done((bf16[320,416]{1,0:T(8,128)(2,1)S(1)}, bf16[320,416]{1,0:T(8,128)(2,1)S(1)}, u32[]{:S(2)}, u32[]{:S(2)}) %collective-permute-start.16) | collective-permute-done | bytes 266272 | tf_op jit(solution)/shard_map/ppermute | solution.py:20
  118.0 4.0 %collective-permute-done.14.refs_10_ = bf16[208,1280]{1,0:T(8,128)(2,1)} collective-permute-done((bf16[208,1280]{1,0:T(8,128)(2,1)}, bf16[208,1280]{1,0:T(8,128)(2,1)}, u32[]{:S(2)}, u32[]{:S(2)}) %collective-permute-start.14) | collective-permute-done | bytes 532512 | tf_op jit(solution)/shard_map/ppermute | solution.py:20
  122.1 3.2 %collective-permute-done.17 = bf16[320,416]{1,0:T(8,128)(2,1)} collective-permute-done((bf16[320,416]{1,0:T(8,128)(2,1)}, bf16[320,416]{1,0:T(8,128)(2,1)}, u32[]{:S(2)}, u32[]{:S(2)}) %collective-permute-start.17) | collective-permute-done | bytes 266272 | tf_op jit(solution)/shard_map/ppermute | solution.py:20
  128.5 4.4 %collective-permute-done.21.refs_7_ = bf16[208,1280]{1,0:T(8,128)(2,1)} collective-permute-done((bf16[208,1280]{1,0:T(8,128)(2,1)}, bf16[208,1280]{1,0:T(8,128)(2,1)}, u32[]{:S(2)}, u32[]{:S(2)}) %collective-permute-start.21) | collective-permute-done | bytes 532512 | tf_op jit(solution)/shard_map/ppermute | solution.py:20
  134.6 7.8 %collective-permute-done.22.refs_11_ = bf16[208,1280]{1,0:T(8,128)(2,1)} collective-permute-done((bf16[208,1280]{1,0:T(8,128)(2,1)}, bf16[208,1280]{1,0:T(8,128)(2,1)}, u32[]{:S(2)}, u32[]{:S(2)}) %collective-permute-start.22) | collective-permute-done | bytes 532512 | tf_op jit(solution)/shard_map/ppermute | solution.py:20
  149.4 8.4 %shard_map.49.refs_10_ = bf16[320,8192]{1,0:T(8,128)(2,1)} custom-call(s32[1]{0:T(128)} %bitcast.side_ref, bf16[320,208]{1,0:T(8,128)(2,1)S(1)} %copy-done.8, bf16[320,208]{1,0:T(8,128)(2,1)S(1)} %copy-done.7, bf16[320,208]{1,0:T(8,128)(2,1)S(1)} %copy-done.10, bf16[320,208]{1,0:T(8,128)(2,1)S(1)} %copy-done.9, bf16[208,8192]{1,0:T(8,128)(2,1)S(1)} %copy-done.2, ...), custom_call_target="tpu_custom_call" | custom-call | flops 1 | bytes 1 | tf_op jit(solution)/shard_map/pallas_call | solution.py:176
  159.4 5.8 %collective-permute-done.27.refs_7_ = bf16[208,512]{1,0:T(8,128)(2,1)S(1)} collective-permute-done((bf16[208,512]{1,0:T(8,128)(2,1)S(1)}, bf16[208,512]{1,0:T(8,128)(2,1)S(1)}, u32[]{:S(2)}, u32[]{:S(2)}) %collective-permute-start.27) | collective-permute-done | bytes 213024 | tf_op jit(solution)/shard_map/ppermute | solution.py:20
  165.2 3.3 %shard_map.50.refs_14_ = bf16[320,8192]{1,0:T(8,128)(2,1)} custom-call(s32[1]{0:T(128)} %bitcast.side_ref, bf16[320,208]{1,0:T(8,128)(2,1)S(1)} %copy-done.8, bf16[320,208]{1,0:T(8,128)(2,1)S(1)} %copy-done.7, bf16[320,208]{1,0:T(8,128)(2,1)S(1)} %copy-done.10, bf16[320,208]{1,0:T(8,128)(2,1)S(1)} %copy-done.9, ...), custom_call_target="tpu_custom_call", output_to_operand_aliasing={{}: (11, {})} | custom-call | flops 1 | bytes 1 | tf_op jit(solution)/shard_map/pallas_call | solution.py:176
  168.6 3.2 %shard_map.51 = bf16[320,8192]{1,0:T(8,128)(2,1)} custom-call(s32[1]{0:T(128)} %bitcast.side_ref, bf16[320,208]{1,0:T(8,128)(2,1)S(1)} %copy-done.8, bf16[320,208]{1,0:T(8,128)(2,1)S(1)} %copy-done.7, bf16[320,208]{1,0:T(8,128)(2,1)S(1)} %copy-done.10, bf16[320,208]{1,0:T(8,128)(2,1)S(1)} %copy-done.9, ...), custom_call_target="tpu_custom_call", output_to_operand_aliasing={{}: (15, {})} | custom-call | flops 1 | bytes 1 | tf_op jit(solution)/shard_map/pallas_call | solution.py:176
  (102 shorter events, 34.0 us)
Async XLA Ops:
  6.5 26.0 %collective-permute-start.2 = (bf16[208,8192]{1,0:T(8,128)(2,1)}, bf16[208,8192]{1,0:T(8,128)(2,1)S(1)}, u32[]{:S(2)}, u32[]{:S(2)}) collective-permute-start(bf16[208,8192]{1,0:T(8,128)(2,1)} %refs_2_), channel_id=1, source_target_pairs={{1,0},{0,1},{3,2},{2,3},{5,4},{4,5},{7,6},{6,7},{9,8},{8,9},{11,10... | collective-permute-start | bytes 10223624 | tf_op jit(solution)/shard_map/ppermute | solution.py:20
  7.0 25.6 %collective-permute-start.1 = (bf16[208,8192]{1,0:T(8,128)(2,1)}, bf16[208,8192]{1,0:T(8,128)(2,1)S(1)}, u32[]{:S(2)}, u32[]{:S(2)}) collective-permute-start(bf16[208,8192]{1,0:T(8,128)(2,1)} %refs_1_.1), channel_id=1, source_target_pairs={{1,0},{0,1},{3,2},{2,3},{5,4},{4,5},{7,6},{6,7},{9,8},{8,9},{11,10... | collective-permute-start | bytes 10223624 | tf_op jit(solution)/shard_map/ppermute | solution.py:20
  7.1 62.1 %collective-permute-start.5 = (bf16[320,4096]{1,0:T(8,128)(2,1)S(1)}, bf16[320,4096]{1,0:T(8,128)(2,1)S(1)}, u32[]{:S(2)}, u32[]{:S(2)}) collective-permute-start(bf16[320,4096]{1,0:T(8,128)(2,1)S(1)} %constant_dynamic-slice_fusion.5), channel_id=1, source_target_pairs={{16,0},{0,16},{17,1},{1,17},{18,2},{2,18},{19,3},{3,19},{20,4},{4,... | collective-permute-start | bytes 7864328 | tf_op jit(solution)/shard_map/ppermute | solution.py:20
  10.0 22.4 %collective-permute-start = (bf16[96,4096]{1,0:T(8,128)(2,1)}, bf16[96,4096]{1,0:T(8,128)(2,1)S(1)}, u32[]{:S(2)}, u32[]{:S(2)}) collective-permute-start(bf16[96,4096]{1,0:T(8,128)(2,1)} %constant_dynamic-slice_fusion.6), channel_id=1, source_target_pairs={{12,0},{0,4},{4,8},{8,12},{13,1},{1,5},{5,9},{9,13},{14,2},{2,6},{... | collective-permute-start | bytes 2359304 | tf_op jit(solution)/shard_map/ppermute | solution.py:20
  11.6 40.5 %collective-permute-start.4 = (bf16[112,4096]{1,0:T(8,128)(2,1)}, bf16[112,4096]{1,0:T(8,128)(2,1)S(1)}, u32[]{:S(2)}, u32[]{:S(2)}) collective-permute-start(bf16[112,4096]{1,0:T(8,128)(2,1)} %constant_dynamic-slice_fusion.8), channel_id=1, source_target_pairs={{12,0},{0,4},{4,8},{8,12},{13,1},{1,5},{5,9},{9,13},{14,2},{2,6},{... | collective-permute-start | bytes 2752520 | tf_op jit(solution)/shard_map/ppermute | solution.py:20
  32.5 35.5 %collective-permute-start.6 = (bf16[96,4096]{1,0:T(8,128)(2,1)S(1)}, bf16[96,4096]{1,0:T(8,128)(2,1)}, u32[]{:S(2)}, u32[]{:S(2)}) collective-permute-start(bf16[96,4096]{1,0:T(8,128)(2,1)S(1)} %constant_dynamic-slice_fusion.4), channel_id=1, source_target_pairs={{12,0},{0,4},{4,8},{8,12},{13,1},{1,5},{5,9},{9,13},{14,2},{2,6},{... | collective-permute-start | bytes 2359304 | tf_op jit(solution)/shard_map/ppermute | solution.py:20
  32.5 101.3 %collective-permute-start.18 = (bf16[208,8192]{1,0:T(8,128)(2,1)S(1)}, bf16[208,8192]{1,0:T(8,128)(2,1)}, u32[]{:S(2)}, u32[]{:S(2)}) collective-permute-start(bf16[208,8192]{1,0:T(8,128)(2,1)S(1)} %copy-done.2), channel_id=1, source_target_pairs={{1,0},{0,1},{3,2},{2,3},{5,4},{4,5},{7,6},{6,7},{9,8},{8,9},{11,10... | collective-permute-start | bytes 10223624 | tf_op jit(solution)/shard_map/ppermute | solution.py:20
  47.1 20.9 %collective-permute-start.3 = (bf16[320,832]{1,0:T(8,128)(2,1)S(1)}, bf16[320,832]{1,0:T(8,128)(2,1)S(1)}, u32[]{:S(2)}, u32[]{:S(2)}) collective-permute-start(bf16[320,832]{1,0:T(8,128)(2,1)S(1)} %shard_map.46), channel_id=1, source_target_pairs={{2,0},{0,2},{3,1},{1,3},{6,4},{4,6},{7,5},{5,7},{10,8},{8,10},{11,... | collective-permute-start | bytes 1597448 | tf_op jit(solution)/shard_map/ppermute | solution.py:20
  52.1 18.1 %collective-permute-start.8 = (bf16[112,4096]{1,0:T(8,128)(2,1)S(1)}, bf16[112,4096]{1,0:T(8,128)(2,1)S(1)}, u32[]{:S(2)}, u32[]{:S(2)}) collective-permute-start(bf16[112,4096]{1,0:T(8,128)(2,1)S(1)} %collective-permute-done.4.refs_3_), channel_id=1, source_target_pairs={{1,0},{0,1},{3,2},{2,3},{5,4},{4,5},{7,6},{6,7},{9,8},{8,9},{11,10... | collective-permute-start | bytes 2752520 | tf_op jit(solution)/shard_map/ppermute | solution.py:20
  68.0 23.1 %collective-permute-start.10 = (bf16[112,4096]{1,0:T(8,128)(2,1)S(1)}, bf16[112,4096]{1,0:T(8,128)(2,1)}, u32[]{:S(2)}, u32[]{:S(2)}) collective-permute-start(bf16[112,4096]{1,0:T(8,128)(2,1)S(1)} %constant_dynamic-slice_fusion.7), channel_id=1, source_target_pairs={{12,0},{0,4},{4,8},{8,12},{13,1},{1,5},{5,9},{9,13},{14,2},{2,6},{... | collective-permute-start | bytes 2752520 | tf_op jit(solution)/shard_map/ppermute | solution.py:20
  92.6 15.8 %collective-permute-start.15 = (bf16[208,1280]{1,0:T(8,128)(2,1)S(1)}, bf16[208,1280]{1,0:T(8,128)(2,1)S(1)}, u32[]{:S(2)}, u32[]{:S(2)}) collective-permute-start(bf16[208,1280]{1,0:T(8,128)(2,1)S(1)} %get-tuple-element.74), channel_id=1, source_target_pairs={{12,0},{0,4},{4,8},{8,12},{13,1},{1,5},{5,9},{9,13},{14,2},{2,6},{... | collective-permute-start | bytes 1597448 | tf_op jit(solution)/shard_map/ppermute | solution.py:20
  92.6 13.5 %collective-permute-start.9 = (bf16[320,416]{1,0:T(8,128)(2,1)}, bf16[320,416]{1,0:T(8,128)(2,1)S(1)}, u32[]{:S(2)}, u32[]{:S(2)}) collective-permute-start(bf16[320,416]{1,0:T(8,128)(2,1)} %copy-done.17), channel_id=1, source_target_pairs={{16,0},{0,16},{17,1},{1,17},{18,2},{2,18},{19,3},{3,19},{20,4},{4,... | collective-permute-start | bytes 798728 | tf_op jit(solution)/shard_map/ppermute | solution.py:20
  105.3 9.8 %collective-permute-start.16 = (bf16[320,416]{1,0:T(8,128)(2,1)S(1)}, bf16[320,416]{1,0:T(8,128)(2,1)S(1)}, u32[]{:S(2)}, u32[]{:S(2)}) collective-permute-start(bf16[320,416]{1,0:T(8,128)(2,1)S(1)} %get-tuple-element.70), channel_id=1, source_target_pairs={{16,0},{0,16},{17,1},{1,17},{18,2},{2,18},{19,3},{3,19},{20,4},{4,... | collective-permute-start | bytes 798728 | tf_op jit(solution)/shard_map/ppermute | solution.py:20
  106.1 16.0 %collective-permute-start.14 = (bf16[208,1280]{1,0:T(8,128)(2,1)}, bf16[208,1280]{1,0:T(8,128)(2,1)}, u32[]{:S(2)}, u32[]{:S(2)}) collective-permute-start(bf16[208,1280]{1,0:T(8,128)(2,1)} %get-tuple-element.73), channel_id=1, source_target_pairs={{12,0},{0,4},{4,8},{8,12},{13,1},{1,5},{5,9},{9,13},{14,2},{2,6},{... | collective-permute-start | bytes 1597448 | tf_op jit(solution)/shard_map/ppermute | solution.py:20
  106.9 15.1 %collective-permute-start.13 = (bf16[320,416]{1,0:T(8,128)(2,1)}, bf16[320,416]{1,0:T(8,128)(2,1)}, u32[]{:S(2)}, u32[]{:S(2)}) collective-permute-start(bf16[320,416]{1,0:T(8,128)(2,1)} %add_convert_fusion.1), channel_id=1, source_target_pairs={{2,0},{0,2},{3,1},{1,3},{6,4},{4,6},{7,5},{5,7},{10,8},{8,10},{11,... | collective-permute-start | bytes 798728 | tf_op jit(solution)/shard_map/ppermute | solution.py:20
  117.5 15.4 %collective-permute-start.21 = (bf16[208,1280]{1,0:T(8,128)(2,1)}, bf16[208,1280]{1,0:T(8,128)(2,1)}, u32[]{:S(2)}, u32[]{:S(2)}) collective-permute-start(bf16[208,1280]{1,0:T(8,128)(2,1)} %copy-done.13), channel_id=1, source_target_pairs={{16,0},{0,16},{17,1},{1,17},{18,2},{2,18},{19,3},{3,19},{20,4},{4,... | collective-permute-start | bytes 1597448 | tf_op jit(solution)/shard_map/ppermute | solution.py:20
  122.1 20.4 %collective-permute-start.23 = (bf16[208,1280]{1,0:T(8,128)(2,1)}, bf16[208,1280]{1,0:T(8,128)(2,1)}, u32[]{:S(2)}, u32[]{:S(2)}) collective-permute-start(bf16[208,1280]{1,0:T(8,128)(2,1)} %copy-done.13), channel_id=1, source_target_pairs={{1,0},{0,1},{3,2},{2,3},{5,4},{4,5},{7,6},{6,7},{9,8},{8,9},{11,10... | collective-permute-start | bytes 1597448 | tf_op jit(solution)/shard_map/ppermute | solution.py:20
  122.1 11.7 %collective-permute-start.20 = (bf16[208,768]{1,0:T(8,128)(2,1)S(1)}, bf16[208,768]{1,0:T(8,128)(2,1)S(1)}, u32[]{:S(2)}, u32[]{:S(2)}) collective-permute-start(bf16[208,768]{1,0:T(8,128)(2,1)S(1)} %constant_dynamic-slice_fusion), channel_id=1, source_target_pairs={{12,0},{0,4},{4,8},{8,12},{13,1},{1,5},{5,9},{9,13},{14,2},{2,6},{... | collective-permute-start | bytes 958472 | tf_op jit(solution)/shard_map/ppermute | solution.py:20
  125.3 17.1 %collective-permute-start.22 = (bf16[208,1280]{1,0:T(8,128)(2,1)}, bf16[208,1280]{1,0:T(8,128)(2,1)}, u32[]{:S(2)}, u32[]{:S(2)}) collective-permute-start(bf16[208,1280]{1,0:T(8,128)(2,1)} %collective-permute-done.14.refs_10_), channel_id=1, source_target_pairs={{16,0},{0,16},{17,1},{1,17},{18,2},{2,18},{19,3},{3,19},{20,4},{4,... | collective-permute-start | bytes 1597448 | tf_op jit(solution)/shard_map/ppermute | solution.py:20
  132.9 10.2 %collective-permute-start.25 = (bf16[208,1280]{1,0:T(8,128)(2,1)}, bf16[208,1280]{1,0:T(8,128)(2,1)}, u32[]{:S(2)}, u32[]{:S(2)}) collective-permute-start(bf16[208,1280]{1,0:T(8,128)(2,1)} %collective-permute-done.14.refs_10_), channel_id=1, source_target_pairs={{1,0},{0,1},{3,2},{2,3},{5,4},{4,5},{7,6},{6,7},{9,8},{8,9},{11,10... | collective-permute-start | bytes 1597448 | tf_op jit(solution)/shard_map/ppermute | solution.py:20
  142.4 15.4 %collective-permute-start.19 = (bf16[208,512]{1,0:T(8,128)(2,1)S(1)}, bf16[208,512]{1,0:T(8,128)(2,1)S(1)}, u32[]{:S(2)}, u32[]{:S(2)}) collective-permute-start(bf16[208,512]{1,0:T(8,128)(2,1)S(1)} %get-tuple-element.81), channel_id=1, source_target_pairs={{12,0},{0,4},{4,8},{8,12},{13,1},{1,5},{5,9},{9,13},{14,2},{2,6},{... | collective-permute-start | bytes 638984 | tf_op jit(solution)/shard_map/ppermute | solution.py:20
  142.5 15.9 %collective-permute-start.29 = (bf16[208,768]{1,0:T(8,128)(2,1)}, bf16[208,768]{1,0:T(8,128)(2,1)S(1)}, u32[]{:S(2)}, u32[]{:S(2)}) collective-permute-start(bf16[208,768]{1,0:T(8,128)(2,1)} %copy-done.15), channel_id=1, source_target_pairs={{16,0},{0,16},{17,1},{1,17},{18,2},{2,18},{19,3},{3,19},{20,4},{4,... | collective-permute-start | bytes 958472 | tf_op jit(solution)/shard_map/ppermute | solution.py:20
  143.1 15.9 %collective-permute-start.28 = (bf16[208,512]{1,0:T(8,128)(2,1)S(1)}, bf16[208,512]{1,0:T(8,128)(2,1)S(1)}, u32[]{:S(2)}, u32[]{:S(2)}) collective-permute-start(bf16[208,512]{1,0:T(8,128)(2,1)S(1)} %get-tuple-element.87), channel_id=1, source_target_pairs={{12,0},{0,4},{4,8},{8,12},{13,1},{1,5},{5,9},{9,13},{14,2},{2,6},{... | collective-permute-start | bytes 638984 | tf_op jit(solution)/shard_map/ppermute | solution.py:20
  158.9 9.6 %collective-permute-start.30 = (bf16[208,512]{1,0:T(8,128)(2,1)S(1)}, bf16[208,512]{1,0:T(8,128)(2,1)S(1)}, u32[]{:S(2)}, u32[]{:S(2)}) collective-permute-start(bf16[208,512]{1,0:T(8,128)(2,1)S(1)} %collective-permute-done.19.refs_6_), channel_id=1, source_target_pairs={{1,0},{0,1},{3,2},{2,3},{5,4},{4,5},{7,6},{6,7},{9,8},{8,9},{11,10... | collective-permute-start | bytes 638984 | tf_op jit(solution)/shard_map/ppermute | solution.py:20
  (29 other events, 176.1 us)

commit v4 on v0

v4 whole, which is shorter than its diff:
```python
import functools

import jax
import jax.numpy as jnp
from jax import lax
from jax.experimental import pallas as pl
from jax.experimental.pallas import tpu as pltpu
from jax.sharding import PartitionSpec as P

LANE_SHARES = (7, 5, 3, 1)
VMEM = 52 * 1024 * 1024
SMALL = 1_750_000
UP_SHARES = (7, 6)
CHEAP = pl.CostEstimate(flops=1, bytes_accessed=1, transcendentals=0)
ANY = pl.BlockSpec(memory_space=pl.ANY)
HBM = pl.BlockSpec(memory_space=pltpu.HBM)


def shifted(block, axis, distance):
    devices = range(lax.axis_size(axis))
    route = [((i - distance) % len(devices), i) for i in devices]
    return lax.ppermute(block, axis, route)


def across(block):
    return shifted(block, "groups", 1)


def tied(value, *earlier):
    return lax.optimization_barrier((value, *earlier))[0] if earlier else value


def cuts(total, unit, shares):
    units, whole, done, marks = total // unit, sum(shares), 0, [0]
    for share in shares:
        done += share
        marks.append(units * done // whole * unit)
    marks[-1] = total
    return list(zip(marks[:-1], marks[1:]))


def call(kernel, operands, outs, out_specs, scratch, aliases=None):
    aliases = aliases or {}
    return pl.pallas_call(
        kernel,
        in_specs=[pl.BlockSpec(memory_space=pltpu.SMEM)]
        + [
            ANY if i in aliases or array.size * array.dtype.itemsize < SMALL else HBM
            for i, array in enumerate(operands)
        ][1:],
        out_specs=out_specs,
        out_shape=outs,
        scratch_shapes=scratch,
        input_output_aliases=aliases,
        compiler_params=pltpu.CompilerParams(vmem_limit_bytes=VMEM),
        cost_estimate=CHEAP,
    )(*operands)


def pieces_kernel(cuts_of, side_ref, *refs):
    count = len(cuts_of)
    sources, outs, sems = refs[:-1 - count], refs[-1 - count : -1], refs[-1]
    side = side_ref[0]
    copies = []
    for i, (source, base, offset, lanes) in enumerate(cuts_of):
        start = pl.multiple_of(base + (side if offset > 0 else 1 - side) * abs(offset), 128)
        copies.append(
            pltpu.make_async_copy(
                sources[source].at[:, pl.ds(start, lanes)], outs[i], sems.at[i]
            )
        )
    for copy in copies:
        copy.start()
    for copy in copies:
        copy.wait()


def cut_pieces(side, arrays, cuts_of):
    return call(
        functools.partial(pieces_kernel, cuts_of),
        (side, *arrays),
        [
            jax.ShapeDtypeStruct((arrays[i].shape[0], lanes), arrays[i].dtype)
            for i, _, _, lanes in cuts_of
        ],
        [ANY] * len(cuts_of),
        [pltpu.SemaphoreType.DMA((len(cuts_of),))],
    )


def products_kernel(halved, outs, block, steps, side_ref, *refs):
    operands, out_refs, total = refs[: -1 - outs], refs[-1 - outs : -1], refs[-1]
    side = side_ref[0]
    total[...] = jnp.zeros_like(total)

    def body(*blocks):
        units = [ref[...] for ref in blocks[len(halved) :]]
        units = units[0] if len(units) == 1 else jnp.concatenate(units, axis=0)
        at = 0
        for ref in blocks[: len(halved)]:
            rows = ref.shape[0]
            total[at : at + rows] += lax.dot_general(
                ref[...], units, (((1,), (1,)), ((), ())), preferred_element_type=jnp.float32
            )
            at += rows

    pltpu.emit_pipeline(
        body,
        grid=(steps,),
        in_specs=[
            pl.BlockSpec(
                (ref.shape[0], block),
                (lambda k: (0, side * steps + k))
                if i < len(halved) and halved[i]
                else (lambda k: (0, k)),
            )
            for i, ref in enumerate(operands)
        ],
    )(*operands)
    at = 0
    for out_ref in out_refs:
        rows = out_ref.shape[0]
        out_ref[...] = total[at : at + rows].astype(out_ref.dtype)
        at += rows


def products(side, row_sets, halved, unit_sets, out_types):
    width = unit_sets[0].shape[1]
    block = 1024 if width % 1024 == 0 else width
    count = sum(u.shape[0] for u in unit_sets)
    rows = sum(r.shape[0] for r in row_sets)
    part = rows // len(out_types)
    return call(
        functools.partial(
            products_kernel, halved, len(out_types), block, width // block
        ),
        (side, *row_sets, *unit_sets),
        [jax.ShapeDtypeStruct((part, count), t) for t in out_types],
        [pl.BlockSpec(memory_space=pltpu.VMEM)] * len(out_types),
        [pltpu.VMEM((rows, count), jnp.float32)],
    )


def blocks_of(parts):
    found = []
    for i, (a, b) in enumerate(parts):
        half = (b - a) // 2
        size = 512 if half % 512 == 0 else 256 if half % 256 == 0 else 128
        for j in range(2):
            for at in range(0, half, size):
                found.append((i, j, at, size, a + j * half + at))
    return found


def output_kernel(parts, side_ref, *refs):
    hidden, down, arrived = refs[:2], refs[2], refs[3 : 3 + len(parts)]
    out, rows, near, far, result, sems, row_sems = refs[-7:]
    units = down.shape[0]
    share = units // 2
    core = side_ref[1]
    blocks = blocks_of(parts)
    row_copies = [
        pltpu.make_async_copy(hidden[i], rows.at[i], row_sems.at[i]) for i in range(2)
    ]
    loads, stores, spots, at = [], [], [], 0
    for n, (i, j, lane, size, column) in enumerate(blocks):
        spot = pl.ds(at, size)
        spots.append(slice(at, at + size))
        at += size
        loads.append(
            [
                pltpu.make_async_copy(
                    down.at[:, pl.ds(column, size)], near.at[:, spot], sems.at[0, n]
                )
            ]
            + [
                pltpu.make_async_copy(
                    arrived[i].at[
                        pl.ds(pl.multiple_of(j * units + from_core * share, 16), share),
                        pl.ds(lane, size),
                    ],
                    far.at[pl.ds(k * share, share), spot],
                    sems.at[1 + k, n],
                )
                for k, from_core in enumerate((core, 1 - core))
            ]
        )
        stores.append(
            pltpu.make_async_copy(
                result.at[:, spot], out.at[:, pl.ds(column, size)], sems.at[3, n]
            )
        )
    for copy in row_copies:
        copy.start()
    for group in loads:
        for copy in group:
            copy.start()
    for copy in row_copies:
        copy.wait()
    for n, spot in enumerate(spots):
        for copy in loads[n]:
            copy.wait()
        total = jnp.dot(rows[0], near[:, spot], preferred_element_type=jnp.float32)
        total += jnp.dot(rows[1], far[:, spot], preferred_element_type=jnp.float32)
        result[:, spot] = total.astype(result.dtype)
        stores[n].start()
    for copy in stores:
        copy.wait()


def output_part(result, parts, side, hidden, down, arrived):
    rows, units, width = hidden[0].shape[0], down.shape[0], down.shape[1]
    lanes = sum(b - a for a, b in parts)
    count = len(blocks_of(parts))
    operands = (side, *hidden, down, *arrived)
    aliases = None
    if result is not None:
        aliases = {len(operands): 0}
        operands += (result,)
    return call(
        functools.partial(output_kernel, parts),
        operands,
        jax.ShapeDtypeStruct((rows, width), jnp.bfloat16),
        ANY,
        [
            pltpu.VMEM((2, rows, units), jnp.bfloat16),
            pltpu.VMEM((units, lanes), jnp.bfloat16),
            pltpu.VMEM((units, lanes), jnp.bfloat16),
            pltpu.VMEM((rows, lanes), jnp.bfloat16),
            pltpu.SemaphoreType.DMA((4, count)),
            pltpu.SemaphoreType.DMA((2,)),
        ],
        aliases,
    )


def over_slices(partial_value):
    return [
        shifted(partial_value, "tensor", distance)
        for distance in range(1, lax.axis_size("tensor"))
    ]


def summed(partial_value, sent):
    total = partial_value.astype(jnp.float32)
    for block in sent:
        total = total + block.astype(jnp.float32)
    return total


def gated(gate, up):
    return (jax.nn.silu(gate) * up).astype(jnp.bfloat16)


def on_device(tokens, gate_weight, up_weight, down_weight):
    width, rows = gate_weight.shape[1], tokens.shape[0]
    half = width // 2
    units = gate_weight.shape[0]
    side = jnp.stack([lax.axis_index("groups"), lax.axis_index("sub")]).astype(jnp.int32)
    lane_cuts = tuple((2 * a, 2 * b) for a, b in cuts(half, 128, LANE_SHARES))

    (gate_piece,) = cut_pieces(side, (gate_weight,), ((0, 0, half, half),))
    up_piece, swapped = cut_pieces(
        side,
        (tied(up_weight, gate_piece), tokens),
        ((0, 0, half, half), (1, 0, -half, half)),
    )
    down_pieces = cut_pieces(
        side,
        (tied(down_weight, swapped),),
        tuple((0, a, (b - a) // 2, (b - a) // 2) for a, b in lane_cuts),
    )
    gate_next = shifted(gate_piece, "dp", 1)
    up_next = [shifted(up_piece[a:b], "dp", 1) for a, b in cuts(units, 16, UP_SHARES)]
    down_next = [shifted(piece, "dp", 1) for piece in down_pieces]

    def both_cores(block):
        return lax.all_gather(block, "sub", axis=0, tiled=True)

    def all_four(block):
        return lax.all_gather(block, ("groups", "sub"), axis=0, tiled=True)

    def mate(block, parts):
        return [
            shifted(block[a:b], "sub", 1)
            for a, b in cuts(block.shape[0], 16, (1,) * parts)
        ]

    gate_here, up_here, down_here = (
        both_cores(tied(w, gate_piece)) for w in (gate_weight, up_weight, down_weight)
    )
    tokens_other = [across(swapped[a:b]) for a, b in cuts(rows, 16, (1, 1))]

    def joint(unit_sets):
        return products(
            side,
            [tokens, *tokens_other],
            [True] + [False] * len(tokens_other),
            unit_sets,
            [jnp.float32, jnp.bfloat16],
        )

    def one_slice(kept, given):
        return (kept + given.astype(jnp.float32)).astype(jnp.bfloat16)

    gate_own = gate_next
    gate_mate = mate(gate_own, 4)
    (mine,) = products(
        side, [tied(tokens, gate_own)], [False], [gate_here, up_here], [jnp.bfloat16]
    )
    mine_sent = over_slices(mine)

    up_own = [tied(up_next[0], mine)]
    up_mate = mate(up_own[0], 2)
    tokens_other = [tied(block, up_own[0]) for block in tokens_other]
    gate_kept, gate_sent = joint([gate_own, *gate_mate])
    gate_given = across(gate_sent)
    pre = summed(mine, [tied(block, gate_sent) for block in mine_sent])
    count = pre.shape[1] // 2
    here = gated(pre[:, :count], pre[:, count:])

    up_own.append(tied(up_next[1], here))
    up_mate += mate(up_own[1], 2)
    gate_slice = one_slice(gate_kept, tied(gate_given, up_own[1]))
    gate_slices = over_slices(gate_slice)
    up_mate = [tied(block, gate_slice) for block in up_mate]
    up_kept, up_sent = joint([*up_own, *up_mate])
    up_given = across(up_sent)

    gathered = []
    gate_slices = [tied(block, up_sent) for block in gate_slices]
    up_slice = one_slice(up_kept, tied(up_given, *gate_slices))
    now = tied(down_next[0], up_slice)
    gathered.append(all_four(now))
    up_slices = over_slices(up_slice)
    there = gated(summed(gate_slice, gate_slices), summed(up_slice, up_slices))
    now = tied(down_next[1], there)
    gathered.append(all_four(now))
    now = tied(down_next[2], now)
    gathered.append(all_four(now))

    hidden = (here, there)
    result = output_part(
        None, lane_cuts[:1], side, hidden, down_here, [tied(gathered[0], now)]
    )
    now = tied(down_next[3], result)
    gathered.append(all_four(now))
    result = output_part(
        result, lane_cuts[1:2], side, hidden, down_here, [tied(gathered[1], now)]
    )
    return output_part(result, lane_cuts[2:], side, hidden, down_here, gathered[2:])


def solution(mesh):
    return jax.shard_map(
        on_device,
        mesh=mesh,
        in_specs=(
            P(("groups", "dp", "sub"), "tensor"),
            P(("dp", "sub"), "tensor"),
            P(("dp", "sub"), "tensor"),
            P(("dp", "sub"), "tensor"),
        ),
        out_specs=P(("groups", "dp", "sub"), "tensor"),
        check_vma=False,
    )
```

time: 582 us -> 310 us (0.53)
  waiting for transfers between devices: 494 us -> 117 us
  Pallas kernels: 0 us -> 137 us
  matrix products: 39.3 us -> 0 us
  starting transfers between devices: 1.79 us -> 17.8 us
  other arithmetic: 12.1 us -> 1.99 us
  blocking collectives: 0 us -> 9.01 us
  local copies, waits for them, and re-layouts: 21.3 us -> 12.5 us
    ppermute x1 -> x22, waiting for transfers between devices: 415 us -> 75.9 us  [shifted(): return lax.ppermute(block, axis, route)]
    pallas_call x0 -> x9, Pallas kernels: none -> 137 us  [call(): pl.pallas_call(kernel, in_specs=[pl.BlockSpec(memory_space=pltpu.SMEM)] +...]
    psum x1 -> x0, waiting for transfers between devices: 41.8 us -> none  [apply_span(): lax.psum(partial_value.astype(jnp.bfloat16), 'tensor').astype(jnp.float32)]
    dot_general x4 -> x0, matrix products: 39.3 us -> none  [the longest x2 25.8 us: apply_span(): lax.dot_general(tokens, both, (((1,), (1,)), ((), ())), preferred_element...]
    ppermute x1 -> x22, starting transfers between devices: 1.74 us -> 17.6 us  [shifted(): return lax.ppermute(block, axis, route)]
    another operation x1, other arithmetic: 9.81 us -> 0.07 us  [on_device(): jnp.stack([lax.axis_index('groups'), lax.axis_index('sub')])]
    slice x2 -> x8, local copies, waits for them, and re-layouts: 18.3 us -> 8.97 us  [the longest x5 4.38 us: mate(): block[a:b]]
    all_gather x0 -> x1, blocking collectives: none -> 9.01 us  [all_four(): return lax.all_gather(block, ('groups', 'sub'), axis=0, tiled=True)]
  transfers between devices with their start and end apart: 3 -> 28, of which waited for: 3 -> 14; matrix products, arithmetic and copies ran while one was open for 5% -> 4% of each run, Pallas kernels for 0% -> 41%
where the time goes in v4:
time: 310 us; the launch traced here: 309 us
  Pallas kernels  137 us (44%)
  waiting for transfers between devices  117 us (38%)
  starting transfers between devices  17.8 us (6%)
  between operations  13.7 us (4%)
  local copies, waits for them, and re-layouts  12.5 us (4%)
  blocking collectives  9.01 us (3%)
    pallas_call x9, Pallas kernels, call(): pl.pallas_call(kernel, in_specs=[pl.BlockSpec(memory_space=pltpu.SMEM)] +...  137 us
    ppermute x22, waiting for transfers between devices, shifted(): return lax.ppermute(block, axis, route)  75.9 us
    all_gather x3, waiting for transfers between devices, all_four(): return lax.all_gather(block, ('groups', 'sub'), axis=0, tiled=True)  21.2 us
    all_gather x3, waiting for transfers between devices, both_cores(): return lax.all_gather(block, 'sub', axis=0, tiled=True)  19 us
    ppermute x22, starting transfers between devices, shifted(): return lax.ppermute(block, axis, route)  17.6 us
    all_gather x1, blocking collectives, all_four(): return lax.all_gather(block, ('groups', 'sub'), axis=0, tiled=True)  9.01 us
  transfers between devices with their start and end apart: 28, of which 14 were waited for; matrix products, arithmetic and copies ran while one was open for 4% of the time, Pallas kernels for 41%

profile of v4, /device:TPU:0, one launch (start us, length us, event | category | flops | bytes accessed | tf_op | source)
XLA Modules:
  0.0 309.3 jit_solution(2696832914568311253)
XLA Ops:
  6.6 2.0 shard_map.46
  9.4 3.1 collective-permute-start
  12.5 81.1 %shard_map.48 = (bf16[208,4096]{1,0:T(8,128)(2,1)S(1)}, bf16[320,4096]{1,0:T(8,128)(2,1)}) custom-call(s32[2]{0:T(128)S(1)} %pad_add_fusion.side_ref, bf16[208,8192]{1,0:T(8,128)(2,1)} %refs_0_.5, bf16[320,8192]{1,0:T(8,128)(2,1)} %refs_0_.7), custom_call_target="tpu_custom_call" | custom-call | flops 1 | bytes 1 | tf_op jit(solution)/shard_map/pallas_call | solution.py:44
  93.6 3.5 %fusion.1 = (bf16[160,4096]{1,0:T(8,128)(2,1)}, bf16[160,4096]{1,0:T(8,128)(2,1)}) fusion(bf16[320,4096]{1,0:T(8,128)(2,1)} %get-tuple-element.41), kind=kLoop, calls=%fused_computation.7 | loop fusion | bytes 5242880 | tf_op jit(solution)/shard_map/slice | solution.py:292
  103.2 12.3 %shard_map.47 = bf16[320,832]{1,0:T(8,128)(2,1)S(1)} custom-call(s32[2]{0:T(128)S(1)} %pad_add_fusion.side_ref, bf16[320,8192]{1,0:T(8,128)(2,1)} %refs_0_.7, bf16[416,8192]{1,0:T(8,128)(2,1)} %all-gather.7.cloned.1.call-done.refs_1_, bf16[416,8192]{1,0:T(8,128)(2,1)} %all-gather.9.cloned.1.call-done.refs_2_), custom_call_target="tpu_custom_call" | custom-call | flops 1 | bytes 1 | tf_op jit(solution)/shard_map/pallas_call | solution.py:44
  118.1 5.4 %collective-permute-done.3.refs_3_ = bf16[112,4096]{1,0:T(8,128)(2,1)} collective-permute-done((bf16[112,4096]{1,0:T(8,128)(2,1)}, bf16[112,4096]{1,0:T(8,128)(2,1)}, u32[]{:S(2)}, u32[]{:S(2)}) %collective-permute-start.3) | collective-permute-done | bytes 917536 | tf_op jit(solution)/shard_map/ppermute | solution.py:22
  123.5 5.6 %collective-permute-done.4.refs_2_ = bf16[160,4096]{1,0:T(8,128)(2,1)} collective-permute-done((bf16[160,4096]{1,0:T(8,128)(2,1)}, bf16[160,4096]{1,0:T(8,128)(2,1)}, u32[]{:S(2)}, u32[]{:S(2)}) %collective-permute-start.4) | collective-permute-done | bytes 1310752 | tf_op jit(solution)/shard_map/ppermute | solution.py:22
  129.2 26.6 %collective-permute-done.2.refs_1_ = bf16[160,4096]{1,0:T(8,128)(2,1)} collective-permute-done((bf16[160,4096]{1,0:T(8,128)(2,1)}, bf16[160,4096]{1,0:T(8,128)(2,1)}, u32[]{:S(2)}, u32[]{:S(2)}) %collective-permute-start.2) | collective-permute-done | bytes 1310752 | tf_op jit(solution)/shard_map/ppermute | solution.py:22
  155.8 1.6 collective-permute-start.10
  158.5 7.6 %shard_map.49 = (f32[320,416]{1,0:T(8,128)}, bf16[320,416]{1,0:T(8,128)(2,1)S(1)}) custom-call(s32[2]{0:T(128)S(1)} %pad_add_fusion.side_ref, bf16[320,8192]{1,0:T(8,128)(2,1)} %refs_0_.7, bf16[160,4096]{1,0:T(8,128)(2,1)} %collective-permute-done.2.refs_1_, bf16[160,4096]{1,0:T(8,128)(2,1)} %collective-permute-done.4.refs_2_, bf16[208,4096]{1,0:T(8,128)(2,1)} %copy-done, ...), custom_call_target="tpu_custom_call" | custom-call | flops 1 | bytes 1 | tf_op jit(solution)/shard_map/pallas_call | solution.py:44
  170.7 6.9 %collective-permute-done.10.refs_4_ = bf16[96,4096]{1,0:T(8,128)(2,1)S(1)} collective-permute-done((bf16[96,4096]{1,0:T(8,128)(2,1)S(1)}, bf16[96,4096]{1,0:T(8,128)(2,1)S(1)}, u32[]{:S(2)}, u32[]{:S(2)}) %collective-permute-start.10) | collective-permute-done | bytes 786464 | tf_op jit(solution)/shard_map/ppermute | solution.py:22
  178.3 2.0 shard_map.51
  182.1 7.6 %shard_map.50 = (f32[320,416]{1,0:T(8,128)}, bf16[320,416]{1,0:T(8,128)(2,1)S(1)}) custom-call(s32[2]{0:T(128)S(1)} %pad_add_fusion.side_ref, bf16[320,8192]{1,0:T(8,128)(2,1)} %refs_0_.7, bf16[160,4096]{1,0:T(8,128)(2,1)} %collective-permute-done.2.refs_1_, bf16[160,4096]{1,0:T(8,128)(2,1)} %collective-permute-done.4.refs_2_, ...), custom_call_target="tpu_custom_call" | custom-call | flops 1 | bytes 1 | tf_op jit(solution)/shard_map/pallas_call | solution.py:44
  191.2 7.9 %collective-permute-done.16 = bf16[320,416]{1,0:T(8,128)(2,1)S(1)} collective-permute-done((bf16[320,416]{1,0:T(8,128)(2,1)S(1)}, bf16[320,416]{1,0:T(8,128)(2,1)S(1)}, u32[]{:S(2)}, u32[]{:S(2)}) %collective-permute-start.16) | collective-permute-done | bytes 266272 | tf_op jit(solution)/shard_map/ppermute | solution.py:22
  203.9 7.3 %collective-permute-done.17 = bf16[320,416]{1,0:T(8,128)(2,1)S(1)} collective-permute-done((bf16[320,416]{1,0:T(8,128)(2,1)S(1)}, bf16[320,416]{1,0:T(8,128)(2,1)S(1)}, u32[]{:S(2)}, u32[]{:S(2)}) %collective-permute-start.17) | collective-permute-done | bytes 266272 | tf_op jit(solution)/shard_map/ppermute | solution.py:22
  211.6 5.8 %collective-permute-done.19 = bf16[208,1280]{1,0:T(8,128)(2,1)S(1)} collective-permute-done((bf16[208,1280]{1,0:T(8,128)(2,1)S(1)}, bf16[208,1280]{1,0:T(8,128)(2,1)S(1)}, u32[]{:S(2)}, u32[]{:S(2)}) %collective-permute-start.19) | collective-permute-done | bytes 532512 | tf_op jit(solution)/shard_map/ppermute | solution.py:22
  218.3 9.5 %collective-permute-done.18 = bf16[208,768]{1,0:T(8,128)(2,1)S(1)} collective-permute-done((bf16[208,768]{1,0:T(8,128)(2,1)S(1)}, bf16[208,768]{1,0:T(8,128)(2,1)S(1)}, u32[]{:S(2)}, u32[]{:S(2)}) %collective-permute-start.18) | collective-permute-done | bytes 319520 | tf_op jit(solution)/shard_map/ppermute | solution.py:22
  229.7 19.0 %all-gather.11.cloned.1.call-done.refs_2_ = bf16[416,8192]{1,0:T(8,128)(2,1)} async-done(((bf16[208,8192]{1,0:T(8,128)(2,1)}), bf16[416,8192]{1,0:T(8,128)(2,1)}) %all-gather.11.cloned.1.call-update) | async-done | bytes 6815760 | tf_op jit(solution)/shard_map/all_gather | solution.py:278
  248.6 9.9 %shard_map.52.refs_4_ = bf16[320,8192]{1,0:T(8,128)(2,1)} custom-call(s32[2]{0:T(128)S(1)} %pad_add_fusion.side_ref, bf16[320,416]{1,0:T(8,128)(2,1)S(1)} %fusion.refs_0_, bf16[320,416]{1,0:T(8,128)(2,1)S(1)} %multiply_convert_fusion.refs_1_, bf16[416,8192]{1,0:T(8,128)(2,1)} %all-gather.11.cloned.1.call-done.refs_2_, ...), custom_call_target="tpu_custom_call" | custom-call | flops 1 | bytes 1 | tf_op jit(solution)/shard_map/pallas_call | solution.py:44
  258.5 15.5 %all-gather.17.cloned.1.call-done.refs_3_ = bf16[832,1280]{1,0:T(8,128)(2,1)} async-done(((bf16[208,1280]{1,0:T(8,128)(2,1)}), bf16[832,1280]{1,0:T(8,128)(2,1)}) %all-gather.17.cloned.1.call-update) | async-done | bytes 2129936 | tf_op jit(solution)/shard_map/all_gather | solution.py:281
  274.0 7.8 %shard_map.53.refs_5_ = bf16[320,8192]{1,0:T(8,128)(2,1)} custom-call(s32[2]{0:T(128)S(1)} %pad_add_fusion.side_ref, bf16[320,416]{1,0:T(8,128)(2,1)S(1)} %fusion.refs_0_, bf16[320,416]{1,0:T(8,128)(2,1)S(1)} %multiply_convert_fusion.refs_1_, bf16[416,8192]{1,0:T(8,128)(2,1)} %all-gather.11.cloned.1.call-done.refs_2_, ...), custom_call_target="tpu_custom_call", output_to_operand_aliasing={{}: (5, {})} | custom-call | flops 1 | bytes 1 | tf_op jit(solution)/shard_map/pallas_call | solution.py:44
  281.8 9.0 %all_gather.26.refs_4_ = bf16[832,256]{1,0:T(8,128)(2,1)S(1)} all-gather(bf16[208,256]{1,0:T(8,128)(2,1)S(1)} %collective-permute-done.20), channel_id=1, replica_groups=mesh['groups'=2,'dp'=4,'tensor'=2,'sub'=2] {'groups','sub'}, dimensions={0}, use_global_device_ids=true | all-gather | bytes 532480 | tf_op jit(solution)/shard_map/all_gather | solution.py:281
  290.8 5.0 %all-gather.13.cloned.1.call-done.refs_3_ = bf16[832,768]{1,0:T(8,128)(2,1)} async-done(((bf16[208,768]{1,0:T(8,128)(2,1)}), bf16[832,768]{1,0:T(8,128)(2,1)}) %all-gather.13.cloned.1.call-update) | async-done | bytes 1277968 | tf_op jit(solution)/shard_map/all_gather | solution.py:281
  295.8 6.7 %shard_map.54 = bf16[320,8192]{1,0:T(8,128)(2,1)} custom-call(s32[2]{0:T(128)S(1)} %pad_add_fusion.side_ref, bf16[320,416]{1,0:T(8,128)(2,1)S(1)} %fusion.refs_0_, bf16[320,416]{1,0:T(8,128)(2,1)S(1)} %multiply_convert_fusion.refs_1_, bf16[416,8192]{1,0:T(8,128)(2,1)} %all-gather.11.cloned.1.call-done.refs_2_, ...), custom_call_target="tpu_custom_call", output_to_operand_aliasing={{}: (6, {})} | custom-call | flops 1 | bytes 1 | tf_op jit(solution)/shard_map/pallas_call | solution.py:44
  (82 shorter events, 26.8 us)
Async XLA Ops:
  6.5 96.7 %all-gather.9.cloned.1.call-start = ((), (), s32[]{:S(2)}) async-start(), calls=%async_computation.1 | async-start | bytes 10223616 | tf_op jit(solution)/shard_map/all_gather | solution.py:278
  8.7 94.6 %all-gather.7.cloned.1.call-start = ((), (), s32[]{:S(2)}) async-start(), calls=%async_computation | async-start | bytes 10223616 | tf_op jit(solution)/shard_map/all_gather | solution.py:278
  9.4 220.2 %all-gather.15.cloned.1.call-start = ((), (), s32[]{:S(2)}) async-start(), calls=%async_computation.4 | async-start | bytes 3727360 | tf_op jit(solution)/shard_map/all_gather | solution.py:281
  9.4 92.3 %collective-permute-start = (bf16[208,4096]{1,0:T(8,128)(2,1)S(1)}, bf16[208,4096]{1,0:T(8,128)(2,1)S(1)}, u32[]{:S(2)}, u32[]{:S(2)}) collective-permute-start(bf16[208,4096]{1,0:T(8,128)(2,1)S(1)} %shard_map.46), channel_id=1, source_target_pairs={{12,0},{0,4},{4,8},{8,12},{13,1},{1,5},{5,9},{9,13},{14,2},{2,6},{... | collective-permute-start | bytes 5111816 | tf_op jit(solution)/shard_map/ppermute | solution.py:22
  97.1 32.0 %collective-permute-start.4 = (bf16[160,4096]{1,0:T(8,128)(2,1)}, bf16[160,4096]{1,0:T(8,128)(2,1)}, u32[]{:S(2)}, u32[]{:S(2)}) collective-permute-start(bf16[160,4096]{1,0:T(8,128)(2,1)} %get-tuple-element.71), channel_id=1, source_target_pairs={{16,0},{0,16},{17,1},{1,17},{18,2},{2,18},{19,3},{3,19},{20,4},{4,... | collective-permute-start | bytes 3932168 | tf_op jit(solution)/shard_map/ppermute | solution.py:22
  98.6 57.1 %collective-permute-start.2 = (bf16[160,4096]{1,0:T(8,128)(2,1)}, bf16[160,4096]{1,0:T(8,128)(2,1)}, u32[]{:S(2)}, u32[]{:S(2)}) collective-permute-start(bf16[160,4096]{1,0:T(8,128)(2,1)} %get-tuple-element.72), channel_id=1, source_target_pairs={{16,0},{0,16},{17,1},{1,17},{18,2},{2,18},{19,3},{3,19},{20,4},{4,... | collective-permute-start | bytes 3932168 | tf_op jit(solution)/shard_map/ppermute | solution.py:22
  100.2 23.3 %collective-permute-start.3 = (bf16[112,4096]{1,0:T(8,128)(2,1)}, bf16[112,4096]{1,0:T(8,128)(2,1)}, u32[]{:S(2)}, u32[]{:S(2)}) collective-permute-start(bf16[112,4096]{1,0:T(8,128)(2,1)} %slice.43), channel_id=1, source_target_pairs={{12,0},{0,4},{4,8},{8,12},{13,1},{1,5},{5,9},{9,13},{14,2},{2,6},{... | collective-permute-start | bytes 2752520 | tf_op jit(solution)/shard_map/ppermute | solution.py:22
  103.2 52.6 %collective-permute-start.5 = (bf16[48,4096]{1,0:T(8,128)(2,1)S(1)}, bf16[48,4096]{1,0:T(8,128)(2,1)S(1)}, u32[]{:S(2)}, u32[]{:S(2)}) collective-permute-start(bf16[48,4096]{1,0:T(8,128)(2,1)S(1)} %get-tuple-element.75), channel_id=1, source_target_pairs={{1,0},{0,1},{3,2},{2,3},{5,4},{4,5},{7,6},{6,7},{9,8},{8,9},{11,10... | collective-permute-start | bytes 1179656 | tf_op jit(solution)/shard_map/ppermute | solution.py:22
  115.5 54.9 %collective-permute-start.1 = (bf16[320,832]{1,0:T(8,128)(2,1)S(1)}, bf16[320,832]{1,0:T(8,128)(2,1)S(1)}, u32[]{:S(2)}, u32[]{:S(2)}) collective-permute-start(bf16[320,832]{1,0:T(8,128)(2,1)S(1)} %shard_map.47), channel_id=1, source_target_pairs={{2,0},{0,2},{3,1},{1,3},{6,4},{4,6},{7,5},{5,7},{10,8},{8,10},{11,... | collective-permute-start | bytes 1597448 | tf_op jit(solution)/shard_map/ppermute | solution.py:22
  123.5 34.2 %collective-permute-start.8 = (bf16[64,4096]{1,0:T(8,128)(2,1)S(1)}, bf16[64,4096]{1,0:T(8,128)(2,1)S(1)}, u32[]{:S(2)}, u32[]{:S(2)}) collective-permute-start(bf16[64,4096]{1,0:T(8,128)(2,1)S(1)} %slice.59), channel_id=1, source_target_pairs={{1,0},{0,1},{3,2},{2,3},{5,4},{4,5},{7,6},{6,7},{9,8},{8,9},{11,10... | collective-permute-start | bytes 1572872 | tf_op jit(solution)/shard_map/ppermute | solution.py:22
  129.2 28.3 %collective-permute-start.6 = (bf16[48,4096]{1,0:T(8,128)(2,1)}, bf16[48,4096]{1,0:T(8,128)(2,1)S(1)}, u32[]{:S(2)}, u32[]{:S(2)}) collective-permute-start(bf16[48,4096]{1,0:T(8,128)(2,1)} %get-tuple-element.74), channel_id=1, source_target_pairs={{1,0},{0,1},{3,2},{2,3},{5,4},{4,5},{7,6},{6,7},{9,8},{8,9},{11,10... | collective-permute-start | bytes 1179656 | tf_op jit(solution)/shard_map/ppermute | solution.py:22
  155.8 21.8 %collective-permute-start.10 = (bf16[96,4096]{1,0:T(8,128)(2,1)S(1)}, bf16[96,4096]{1,0:T(8,128)(2,1)S(1)}, u32[]{:S(2)}, u32[]{:S(2)}) collective-permute-start(bf16[96,4096]{1,0:T(8,128)(2,1)S(1)} %slice.51), channel_id=1, source_target_pairs={{12,0},{0,4},{4,8},{8,12},{13,1},{1,5},{5,9},{9,13},{14,2},{2,6},{... | collective-permute-start | bytes 2359304 | tf_op jit(solution)/shard_map/ppermute | solution.py:22
  168.2 12.0 %collective-permute-start.9 = (bf16[320,416]{1,0:T(8,128)(2,1)S(1)}, bf16[320,416]{1,0:T(8,128)(2,1)S(1)}, u32[]{:S(2)}, u32[]{:S(2)}) collective-permute-start(bf16[320,416]{1,0:T(8,128)(2,1)S(1)} %get-tuple-element.46), channel_id=1, source_target_pairs={{16,0},{0,16},{17,1},{1,17},{18,2},{2,18},{19,3},{3,19},{20,4},{4,... | collective-permute-start | bytes 798728 | tf_op jit(solution)/shard_map/ppermute | solution.py:22
  169.8 10.6 %collective-permute-start.13 = (bf16[64,4096]{1,0:T(8,128)(2,1)S(1)}, bf16[64,4096]{1,0:T(8,128)(2,1)S(1)}, u32[]{:S(2)}, u32[]{:S(2)}) collective-permute-start(bf16[64,4096]{1,0:T(8,128)(2,1)S(1)} %slice.53), channel_id=1, source_target_pairs={{1,0},{0,1},{3,2},{2,3},{5,4},{4,5},{7,6},{6,7},{9,8},{8,9},{11,10... | collective-permute-start | bytes 1572872 | tf_op jit(solution)/shard_map/ppermute | solution.py:22
  169.8 12.2 %collective-permute-start.12 = (bf16[48,4096]{1,0:T(8,128)(2,1)S(1)}, bf16[48,4096]{1,0:T(8,128)(2,1)S(1)}, u32[]{:S(2)}, u32[]{:S(2)}) collective-permute-start(bf16[48,4096]{1,0:T(8,128)(2,1)S(1)} %slice.52), channel_id=1, source_target_pairs={{1,0},{0,1},{3,2},{2,3},{5,4},{4,5},{7,6},{6,7},{9,8},{8,9},{11,10... | collective-permute-start | bytes 1179656 | tf_op jit(solution)/shard_map/ppermute | solution.py:22
  180.3 20.5 %collective-permute-start.21 = (bf16[208,1792]{1,0:T(8,128)(2,1)S(1)}, bf16[208,1792]{1,0:T(8,128)(2,1)S(1)}, u32[]{:S(2)}, u32[]{:S(2)}) collective-permute-start(bf16[208,1792]{1,0:T(8,128)(2,1)S(1)} %get-tuple-element.66), channel_id=1, source_target_pairs={{12,0},{0,4},{4,8},{8,12},{13,1},{1,5},{5,9},{9,13},{14,2},{2,6},{... | collective-permute-start | bytes 2236424 | tf_op jit(solution)/shard_map/ppermute | solution.py:22
  180.5 10.7 %collective-permute-start.11 = (bf16[320,416]{1,0:T(8,128)(2,1)S(1)}, bf16[320,416]{1,0:T(8,128)(2,1)S(1)}, u32[]{:S(2)}, u32[]{:S(2)}) collective-permute-start(bf16[320,416]{1,0:T(8,128)(2,1)S(1)} %add_convert_fusion.1), channel_id=1, source_target_pairs={{2,0},{0,2},{3,1},{1,3},{6,4},{4,6},{7,5},{5,7},{10,8},{8,10},{11,... | collective-permute-start | bytes 798728 | tf_op jit(solution)/shard_map/ppermute | solution.py:22
  189.7 9.4 %collective-permute-start.16 = (bf16[320,416]{1,0:T(8,128)(2,1)S(1)}, bf16[320,416]{1,0:T(8,128)(2,1)S(1)}, u32[]{:S(2)}, u32[]{:S(2)}) collective-permute-start(bf16[320,416]{1,0:T(8,128)(2,1)S(1)} %get-tuple-element.55), channel_id=1, source_target_pairs={{16,0},{0,16},{17,1},{1,17},{18,2},{2,18},{19,3},{3,19},{20,4},{4,... | collective-permute-start | bytes 798728 | tf_op jit(solution)/shard_map/ppermute | solution.py:22
  201.7 46.9 %all-gather.11.cloned.1.call-start = ((), (), s32[]{:S(2)}) async-start(), calls=%async_computation.2 | async-start | bytes 10223616 | tf_op jit(solution)/shard_map/all_gather | solution.py:278
  202.3 71.7 %all-gather.17.cloned.1.call-start = ((), (), s32[]{:S(2)}) async-start(), calls=%async_computation.5 | async-start | bytes 2662400 | tf_op jit(solution)/shard_map/all_gather | solution.py:281
  202.3 15.1 %collective-permute-start.19 = (bf16[208,1280]{1,0:T(8,128)(2,1)S(1)}, bf16[208,1280]{1,0:T(8,128)(2,1)S(1)}, u32[]{:S(2)}, u32[]{:S(2)}) collective-permute-start(bf16[208,1280]{1,0:T(8,128)(2,1)S(1)} %get-tuple-element.62), channel_id=1, source_target_pairs={{12,0},{0,4},{4,8},{8,12},{13,1},{1,5},{5,9},{9,13},{14,2},{2,6},{... | collective-permute-start | bytes 1597448 | tf_op jit(solution)/shard_map/ppermute | solution.py:22
  218.2 77.5 %all-gather.13.cloned.1.call-start = ((), (), s32[]{:S(2)}) async-start(), calls=%async_computation.3 | async-start | bytes 1597440 | tf_op jit(solution)/shard_map/all_gather | solution.py:281
  218.3 9.6 %collective-permute-start.18 = (bf16[208,768]{1,0:T(8,128)(2,1)S(1)}, bf16[208,768]{1,0:T(8,128)(2,1)S(1)}, u32[]{:S(2)}, u32[]{:S(2)}) collective-permute-start(bf16[208,768]{1,0:T(8,128)(2,1)S(1)} %get-tuple-element.61), channel_id=1, source_target_pairs={{12,0},{0,4},{4,8},{8,12},{13,1},{1,5},{5,9},{9,13},{14,2},{2,6},{... | collective-permute-start | bytes 958472 | tf_op jit(solution)/shard_map/ppermute | solution.py:22
  228.6 29.8 %collective-permute-start.20 = (bf16[208,256]{1,0:T(8,128)(2,1)S(1)}, bf16[208,256]{1,0:T(8,128)(2,1)S(1)}, u32[]{:S(2)}, u32[]{:S(2)}) collective-permute-start(bf16[208,256]{1,0:T(8,128)(2,1)S(1)} %get-tuple-element.65), channel_id=1, source_target_pairs={{12,0},{0,4},{4,8},{8,12},{13,1},{1,5},{5,9},{9,13},{14,2},{2,6},{... | collective-permute-start | bytes 319496 | tf_op jit(solution)/shard_map/ppermute | solution.py:22
  (14 other events, 47.8 us)
Sparse Core Ops, SparseCore 0:
  8.9 20.2 all-gather.8
  30.7 18.6 all-gather.6
  201.8 27.8 all-gather.14
  231.0 17.5 all-gather.10
  250.0 23.9 all-gather.16
  275.4 20.2 all-gather.12

commit v5 on v0

v5 whole, which is shorter than its diff:
```python
import functools

import jax
import jax.numpy as jnp
from jax import lax
from jax.experimental import pallas as pl
from jax.experimental.pallas import tpu as pltpu
from jax.sharding import PartitionSpec as P

ROW_SHARES = (1, 2, 2, 2, 2, 2, 2)
LANE_SHARES = (4, 4, 3, 3, 2)
QUEUE = 2
SLOTS = 3
VMEM = 52 * 1024 * 1024
ANY = pl.BlockSpec(memory_space=pl.ANY)


def shifted(block, axis, distance):
    devices = range(lax.axis_size(axis))
    route = [((i - distance) % len(devices), i) for i in devices]
    return lax.ppermute(block, axis, route)


def mate(block):
    return shifted(block, "sub", 1)


def across(block):
    return shifted(block, "groups", 1)


def tied(value, *earlier):
    return lax.optimization_barrier((value, *earlier))[0] if earlier else value


def cuts(total, unit, shares):
    units, whole, done, marks = total // unit, sum(shares), 0, [0]
    for share in shares:
        done += share
        marks.append(units * done // whole * unit)
    marks[-1] = total
    return list(zip(marks[:-1], marks[1:]))


def call(kernel, operands, in_specs, out, out_spec, scratch, aliases):
    return pl.pallas_call(
        kernel,
        in_specs=in_specs,
        out_specs=out_spec,
        out_shape=out,
        scratch_shapes=scratch,
        input_output_aliases=aliases,
        compiler_params=pltpu.CompilerParams(vmem_limit_bytes=VMEM),
        cost_estimate=pl.CostEstimate(flops=1, bytes_accessed=1, transcendentals=0),
    )(*operands)


def products_kernel(sets, block, *refs):
    operands, (out, rows, units, total, sems) = refs[:-5], refs[-5:]
    steps = operands[0].shape[1] // block

    def loads(step):
        slot, found, at = step % SLOTS, [], [0, 0]
        for i, ref in enumerate(operands):
            kind = 0 if i < sets else 1
            spot = pl.ds(at[kind], ref.shape[0])
            found.append(
                pltpu.make_async_copy(
                    ref.at[:, pl.ds(step * block, block)],
                    (rows, units)[kind].at[slot, spot],
                    sems.at[slot, i],
                )
            )
            at[kind] += ref.shape[0]
        return found

    for step in range(min(SLOTS - 1, steps)):
        for copy in loads(step):
            copy.start()
    for step in range(steps):
        if step + SLOTS - 1 < steps:
            for copy in loads(step + SLOTS - 1):
                copy.start()
        for copy in loads(step):
            copy.wait()
        value = lax.dot_general(
            rows[step % SLOTS],
            units[step % SLOTS],
            (((1,), (1,)), ((), ())),
            preferred_element_type=jnp.float32,
        )
        if step > 0:
            value += total[...]
        if step < steps - 1:
            total[...] = value
        else:
            out[...] = value.astype(out.dtype)


def products(row_sets, unit_sets):
    width = row_sets[0].shape[1]
    block = 1024 if width % 1024 == 0 else width
    shape = (sum(r.shape[0] for r in row_sets), sum(u.shape[0] for u in unit_sets))
    operands = (*row_sets, *unit_sets)
    return call(
        functools.partial(products_kernel, len(row_sets), block),
        operands,
        [ANY] * len(operands),
        jax.ShapeDtypeStruct(shape, jnp.bfloat16),
        pl.BlockSpec(memory_space=pltpu.VMEM),
        [
            pltpu.VMEM((SLOTS, shape[0], block), jnp.bfloat16),
            pltpu.VMEM((SLOTS, shape[1], block), jnp.bfloat16),
            pltpu.VMEM(shape, jnp.float32),
            pltpu.SemaphoreType.DMA((SLOTS, len(operands))),
        ],
        {},
    )


def blocks_of(parts):
    found = []
    for i, (a, b, whole) in enumerate(parts):
        half = (b - a) // 2
        size = 512 if half % 512 == 0 else 256 if half % 256 == 0 else 128
        for k in range(2):
            for lane in range(0, half, size):
                if whole:
                    found.append((i, 0, k * half + lane, size, (a + k * half + lane, 0)))
                else:
                    found.append((i, k, lane, size, (a + k * half + lane, half - 2 * k * half)))
    return found


def output_kernel(parts, side_ref, *refs):
    hidden, down = refs[:4], refs[4:6]
    arrived = refs[6 : 6 + 4 * len(parts)]
    out, weights, result, sems = refs[-4:]
    share = down[0].shape[0]
    side = side_ref[0]
    loads, stores, spots, at = [], [], [], 0
    for n, (i, k, lane, size, (fixed, turn)) in enumerate(blocks_of(parts)):
        column = pl.ds(pl.multiple_of(fixed + side * turn, 128), size)
        spot = pl.ds(at, size)
        spots.append(slice(at, at + size))
        at += size
        sources = [ref.at[:, column] for ref in down]
        sources += [arrived[4 * i + 2 * m + k].at[:, pl.ds(lane, size)] for m in range(2)]
        loads.append(
            [
                pltpu.make_async_copy(source, weights.at[m, :, spot], sems.at[m, n])
                for m, source in enumerate(sources)
            ]
        )
        stores.append(
            pltpu.make_async_copy(result.at[:, spot], out.at[:, column], sems.at[4, n])
        )
    for group in loads:
        for copy in group:
            copy.start()
    for n, spot in enumerate(spots):
        for copy in loads[n]:
            copy.wait()
        total = None
        for m in range(4):
            term = jnp.dot(
                hidden[m][...], weights[m, :, spot], preferred_element_type=jnp.float32
            )
            total = term if total is None else total + term
        result[:, spot] = total.astype(result.dtype)
        stores[n].start()
    for copy in stores:
        copy.wait()


def output_part(result, parts, side, hidden, down, arrived):
    rows, units, width = hidden[0].shape[0], down[0].shape[0], down[0].shape[1]
    lanes = sum(b - a for a, b, _ in parts)
    operands = [side, *hidden, *down, *arrived]
    in_specs = (
        [pl.BlockSpec(memory_space=pltpu.SMEM)]
        + [pl.BlockSpec(memory_space=pltpu.VMEM)] * 4
        + [ANY] * (2 + len(arrived))
    )
    aliases = {}
    if result is not None:
        aliases = {len(operands): 0}
        operands.append(result)
        in_specs.append(ANY)
    return call(
        functools.partial(output_kernel, parts),
        operands,
        in_specs,
        jax.ShapeDtypeStruct((rows, width), jnp.bfloat16),
        ANY,
        [
            pltpu.VMEM((4, units, lanes), jnp.bfloat16),
            pltpu.VMEM((rows, lanes), jnp.bfloat16),
            pltpu.SemaphoreType.DMA((5, len(blocks_of(parts)))),
        ],
        aliases,
    )


def over_slices(partial_value):
    return [
        shifted(partial_value, "tensor", distance)
        for distance in range(1, lax.axis_size("tensor"))
    ]


def summed(partial_value, sent):
    total = partial_value.astype(jnp.float32)
    for block in sent:
        total = total + block.astype(jnp.float32)
    return total


def gated(gate, up):
    return (jax.nn.silu(gate) * up).astype(jnp.bfloat16)


def on_device(tokens, gate_weight, up_weight, down_weight):
    units, width = gate_weight.shape
    rows = tokens.shape[0]
    group = lax.axis_index("groups").astype(jnp.int32)
    first = group == 0
    side = group.reshape(1)

    row_cuts = cuts(units, 16, ROW_SHARES)
    lane_cuts = [(2 * a, 2 * b) for a, b in cuts(width // 2, 128, LANE_SHARES)]
    count = len(row_cuts)
    total_count = count + len(lane_cuts)
    last = total_count - 1

    def piece(i, *after):
        if i < count:
            a, b = row_cuts[i]
            gate, up = gate_weight, up_weight
            if after:
                gate, up = lax.optimization_barrier((gate, up, *after))[:2]
            return jnp.where(first, gate[a:b], up[a:b])
        a, b = lane_cuts[i - count]
        mid = (a + b) // 2
        down = tied(down_weight, *after)
        if i == last:
            return down[:, a:b]
        return jnp.where(first, down[:, a:mid], down[:, mid:b])

    pieces = [piece(0)]
    pieces.append(piece(1, pieces[0]))
    pieces += [piece(i, pieces[1]) for i in range(2, total_count)]
    waiting = [shifted(pieces[i], "dp", 1) for i in range(QUEUE)]
    landed, crossed, mates, crossed_mates = [], {}, {}, {}

    def advance(*after):
        i = len(landed)
        held = [*after, *landed[-1:]]
        for swapped, j in ((crossed, i - 2), (mates, i - 2), (crossed_mates, i - 4)):
            if j in swapped:
                held.append(swapped[j])
        block = tied(waiting[i], *held)
        landed.append(block)
        if i < last:
            crossed[i] = across(block)
        if i >= count:
            mates[i] = mate(block)
        if i - 2 in range(count, last):
            crossed_mates[i - 2] = mate(tied(crossed[i - 2], block))
        if i + QUEUE < total_count:
            waiting.append(shifted(tied(pieces[i + QUEUE], block), "dp", 1))
        return block

    def local(partial_value, sent):
        pre = summed(partial_value, sent)
        return gated(pre[:, :units], pre[:, units:])

    def batch(lo, hi, now):
        held = [landed[i] for i in range(lo, hi)] + [crossed[i] for i in range(lo, hi)]
        held = lax.optimization_barrier((*held, now))[:-1]
        value = products([tokens, tokens_mate], held)
        return value, over_slices(value)

    def activated(partial_value, sent):
        pre = summed(partial_value, sent)
        half = pre.shape[1] // 2
        left, right = pre[:, :half], pre[:, half:]
        return gated(jnp.where(first, left, right), jnp.where(first, right, left))

    tokens_mate = mate(tied(tokens, pieces[0]))
    down_mate = mate(tied(down_weight, pieces[1]))
    now = advance()
    mine = products([tied(tokens, now)], [gate_weight, up_weight])
    mine_sent = over_slices(mine)
    now = advance(mine)
    theirs = products([tied(tokens_mate, now)], [gate_weight, up_weight])
    theirs_sent = over_slices(theirs)
    now = advance(theirs)
    here = local(mine, [tied(block, now) for block in mine_sent])
    now = advance(here)
    here_mate = mate(local(theirs, [tied(block, now) for block in theirs_sent]))
    now = advance()
    now = advance(here_mate)
    early, early_sent = batch(0, 4, now)
    now = advance(early)
    there = [activated(early, [tied(block, now) for block in early_sent])]
    now = advance(there[0], down_mate)
    late, late_sent = batch(4, count, now)
    now = advance(late)
    now = advance()
    there.append(activated(late, [tied(block, now) for block in late_sent]))
    there = jnp.concatenate(there, axis=1)
    there_mate = mate(there[rows:])
    there = there[:rows]
    now = advance(there)
    there_mate = tied(there_mate, now)

    def write(result, *which):
        parts, arrived = [], []
        for n in which:
            i = count + n
            parts.append((*lane_cuts[n], i == last))
            if i == last:
                arrived += [landed[i], landed[i], mates[i], mates[i]]
            else:
                if i not in crossed_mates:
                    crossed_mates[i] = mate(crossed[i])
                arrived += [landed[i], crossed[i], mates[i], crossed_mates[i]]
        return output_part(
            result,
            tuple(parts),
            side,
            [here, here_mate, there, there_mate],
            [down_weight, down_mate],
            arrived,
        )

    result = write(None, 0)
    now = advance(result)
    result = write(result, 1)
    crossed[last - 1] = tied(crossed[last - 1], crossed_mates[last - 2])
    result = write(result, 2, 4)
    return write(result, 3)


def solution(mesh):
    return jax.shard_map(
        on_device,
        mesh=mesh,
        in_specs=(
            P(("groups", "dp", "sub"), "tensor"),
            P(("dp", "sub"), "tensor"),
            P(("dp", "sub"), "tensor"),
            P(("dp", "sub"), "tensor"),
        ),
        out_specs=P(("groups", "dp", "sub"), "tensor"),
        check_vma=False,
    )
```

time: 582 us -> 174 us (0.30)
  waiting for transfers between devices: 494 us -> 85.3 us
  Pallas kernels: 0 us -> 48.4 us
  matrix products: 39.3 us -> 0 us
  starting transfers between devices: 1.79 us -> 26.5 us
  local copies, waits for them, and re-layouts: 21.3 us -> 3.86 us
  between operations: 13.4 us -> 0.5 us
    ppermute x1 -> x40, waiting for transfers between devices: 415 us -> 85.3 us  [shifted(): return lax.ppermute(block, axis, route)]
    pallas_call x0 -> x8, Pallas kernels: none -> 48.4 us  [call(): pl.pallas_call(kernel, in_specs=in_specs, out_specs=out_spec, out_shape=o...]
    psum x1 -> x0, waiting for transfers between devices: 41.8 us -> none  [apply_span(): lax.psum(partial_value.astype(jnp.bfloat16), 'tensor').astype(jnp.float32)]
    dot_general x4 -> x0, matrix products: 39.3 us -> none  [the longest x2 25.8 us: apply_span(): lax.dot_general(tokens, both, (((1,), (1,)), ((), ())), preferred_element...]
    all_gather x1 -> x0, waiting for transfers between devices: 37 us -> none  [on_device(): current = lax.all_gather(own_share, 'sub', axis=1, tiled=True)]
    ppermute x1 -> x40, starting transfers between devices: 1.74 us -> 26.5 us  [shifted(): return lax.ppermute(block, axis, route)]
    slice x2 -> x0, local copies, waits for them, and re-layouts: 18.3 us -> none  [apply_span(): both = weights[:2].reshape(2 * span, weights.shape[2])]
    another operation x1 -> x0, other arithmetic: 9.81 us -> none  [on_device(): own_share = jnp.stack([gate_weight, up_weight, down_weight])]
  transfers between devices with their start and end apart: 3 -> 40, of which waited for: 3 -> 19; matrix products, arithmetic and copies ran while one was open for 5% -> 5% of each run, Pallas kernels for 0% -> 25%
where the time goes in v5:
time: 174 us
  waiting for transfers between devices  85.3 us (49%)
  Pallas kernels  48.4 us (28%)
  starting transfers between devices  26.5 us (15%)
  other arithmetic  9.18 us (5%)
  local copies, waits for them, and re-layouts  3.86 us (2%)
    ppermute x40, waiting for transfers between devices, shifted(): return lax.ppermute(block, axis, route)  85.3 us
    pallas_call x8, Pallas kernels, call(): pl.pallas_call(kernel, in_specs=in_specs, out_specs=out_spec, out_shape=o...  48.4 us
    ppermute x40, starting transfers between devices, shifted(): return lax.ppermute(block, axis, route)  26.5 us
    select_n x3, other arithmetic, piece(): return jnp.where(first, gate[a:b], up[a:b])  6.21 us
    unnamed x22, local copies, waits for them, and re-layouts  3.86 us
  transfers between devices with their start and end apart: 40, of which 19 were waited for; matrix products, arithmetic and copies ran while one was open for 5% of the time, Pallas kernels for 25%

profile of v5, /device:TPU:0, one launch (start us, length us, event | category | flops | bytes accessed | tf_op | source)
XLA Modules:
  0.0 173.7 jit_solution(13569993082774952137)
XLA Ops:
  1.6 2.6 %collective-permute-start = (bf16[16,8192]{1,0:T(8,128)(2,1)S(1)}, bf16[16,8192]{1,0:T(8,128)(2,1)S(1)}, u32[]{:S(2)}, u32[]{:S(2)}) collective-permute-start(bf16[16,8192]{1,0:T(8,128)(2,1)S(1)} %slice_select_fusion.10), channel_id=1, source_target_pairs={{12,0},{0,4},{4,8},{8,12},{13,1},{1,5},{5,9},{9,13},{14,2},{2,6},{... | collective-permute-start | bytes 786440 | tf_op jit(solution)/shard_map/ppermute | solution.py:21
  7.1 3.9 %slice_select_fusion = (bf16[32,8192]{1,0:T(8,128)(2,1)}, bf16[32,8192]{1,0:T(8,128)(2,1)}, bf16[32,8192]{1,0:T(8,128)(2,1)}, bf16[32,8192]{1,0:T(8,128)(2,1)}, bf16[32,8192]{1,0:T(8,128)(2,1)S(1)}) fusion(bf16[208,8192]{1,0:T(8,128)(2,1)} %refs_2_.3, bf16[208,8192]{1,0:T(8,128)(2,1)} %refs_1_.3, pred[]{:T(512)S(6)} %eq.3), kind=kLoop, calls=%fused_computation.4 | loop fusion | flops 1310720 | bytes 7864321 | tf_op jit(solution)/shard_map/jit(_where)/select_n | solution.py:242
  11.0 2.4 %collective-permute-done.refs_2_ = bf16[16,8192]{1,0:T(8,128)(2,1)S(1)} collective-permute-done((bf16[16,8192]{1,0:T(8,128)(2,1)S(1)}, bf16[16,8192]{1,0:T(8,128)(2,1)S(1)}, u32[]{:S(2)}, u32[]{:S(2)}) %collective-permute-start) | collective-permute-done | bytes 262176 | tf_op jit(solution)/shard_map/ppermute | solution.py:21
  15.1 6.1 %shard_map.46 = bf16[320,416]{1,0:T(8,128)(2,1)S(1)} custom-call(bf16[320,8192]{1,0:T(8,128)(2,1)} %refs_0_.4, bf16[208,8192]{1,0:T(8,128)(2,1)} %refs_1_.3, bf16[208,8192]{1,0:T(8,128)(2,1)} %refs_2_.3), custom_call_target="tpu_custom_call" | custom-call | flops 1 | bytes 1 | tf_op jit(solution)/shard_map/pallas_call | solution.py:46
  21.2 3.4 %collective-permute-done.4.refs_3_ = bf16[32,8192]{1,0:T(8,128)(2,1)S(1)} collective-permute-done((bf16[32,8192]{1,0:T(8,128)(2,1)S(1)}, bf16[32,8192]{1,0:T(8,128)(2,1)S(1)}, u32[]{:S(2)}, u32[]{:S(2)}) %collective-permute-start.4) | collective-permute-done | bytes 524320 | tf_op jit(solution)/shard_map/ppermute | solution.py:21
  28.6 6.1 %shard_map.47 = bf16[320,416]{1,0:T(8,128)(2,1)S(1)} custom-call(bf16[320,8192]{1,0:T(8,128)(2,1)} %copy-done.2, bf16[208,8192]{1,0:T(8,128)(2,1)} %refs_1_.3, bf16[208,8192]{1,0:T(8,128)(2,1)} %refs_2_.3), custom_call_target="tpu_custom_call" | custom-call | flops 1 | bytes 1 | tf_op jit(solution)/shard_map/pallas_call | solution.py:46
  37.8 9.4 %collective-permute-done.7.refs_5_ = bf16[32,8192]{1,0:T(8,128)(2,1)} collective-permute-done((bf16[32,8192]{1,0:T(8,128)(2,1)}, bf16[32,8192]{1,0:T(8,128)(2,1)}, u32[]{:S(2)}, u32[]{:S(2)}) %collective-permute-start.7) | collective-permute-done | bytes 524320 | tf_op jit(solution)/shard_map/ppermute | solution.py:21
  49.5 8.8 %collective-permute-done.13.refs_2_ = bf16[32,8192]{1,0:T(8,128)(2,1)S(1)} collective-permute-done((bf16[32,8192]{1,0:T(8,128)(2,1)}, bf16[32,8192]{1,0:T(8,128)(2,1)S(1)}, u32[]{:S(2)}, u32[]{:S(2)}) %collective-permute-start.13) | collective-permute-done | bytes 524320 | tf_op jit(solution)/shard_map/ppermute | solution.py:21
  58.3 3.7 %collective-permute-done.10.refs_8_ = bf16[32,8192]{1,0:T(8,128)(2,1)S(1)} collective-permute-done((bf16[32,8192]{1,0:T(8,128)(2,1)S(1)}, bf16[32,8192]{1,0:T(8,128)(2,1)S(1)}, u32[]{:S(2)}, u32[]{:S(2)}) %collective-permute-start.10) | collective-permute-done | bytes 524320 | tf_op jit(solution)/shard_map/ppermute | solution.py:21
  63.8 5.8 %collective-permute-done.12.refs_3_ = bf16[32,8192]{1,0:T(8,128)(2,1)S(1)} collective-permute-done((bf16[32,8192]{1,0:T(8,128)(2,1)}, bf16[32,8192]{1,0:T(8,128)(2,1)S(1)}, u32[]{:S(2)}, u32[]{:S(2)}) %collective-permute-start.12) | collective-permute-done | bytes 524320 | tf_op jit(solution)/shard_map/ppermute | solution.py:21
  69.6 3.7 %collective-permute-done.11.refs_9_ = bf16[32,8192]{1,0:T(8,128)(2,1)S(1)} collective-permute-done((bf16[32,8192]{1,0:T(8,128)(2,1)}, bf16[32,8192]{1,0:T(8,128)(2,1)S(1)}, u32[]{:S(2)}, u32[]{:S(2)}) %collective-permute-start.11) | collective-permute-done | bytes 524320 | tf_op jit(solution)/shard_map/ppermute | solution.py:21
  74.1 8.9 %shard_map.48 = bf16[640,224]{1,0:T(8,128)(2,1)S(1)} custom-call(bf16[320,8192]{1,0:T(8,128)(2,1)} %refs_0_.4, bf16[320,8192]{1,0:T(8,128)(2,1)} %copy-done.2, bf16[16,8192]{1,0:T(8,128)(2,1)S(1)} %collective-permute-done.refs_2_, bf16[32,8192]{1,0:T(8,128)(2,1)S(1)} %collective-permute-done.4.refs_3_, bf16[32,8192]{1,0:T(8,128)(2,1)S(1)} %collective-permute-done.2.refs_4_, ...), custom_call_target="tpu_custom_call" | custom-call | flops 1 | bytes 1 | tf_op jit(solution)/shard_map/pallas_call | solution.py:46
  90.4 6.8 %collective-permute-done.19.refs_6_ = bf16[208,1024]{1,0:T(8,128)(2,1)S(1)} collective-permute-done((bf16[208,1024]{1,0:T(8,128)(2,1)S(1)}, bf16[208,1024]{1,0:T(8,128)(2,1)S(1)}, u32[]{:S(2)}, u32[]{:S(2)}) %collective-permute-start.19) | collective-permute-done | bytes 426016 | tf_op jit(solution)/shard_map/ppermute | solution.py:21
  97.2 2.5 %collective-permute-done.17.refs_6_ = bf16[32,8192]{1,0:T(8,128)(2,1)} collective-permute-done((bf16[32,8192]{1,0:T(8,128)(2,1)S(1)}, bf16[32,8192]{1,0:T(8,128)(2,1)}, u32[]{:S(2)}, u32[]{:S(2)}) %collective-permute-start.17) | collective-permute-done | bytes 524320 | tf_op jit(solution)/shard_map/ppermute | solution.py:21
  103.4 7.5 %collective-permute-done.18.refs_7_ = bf16[32,8192]{1,0:T(8,128)(2,1)} collective-permute-done((bf16[32,8192]{1,0:T(8,128)(2,1)S(1)}, bf16[32,8192]{1,0:T(8,128)(2,1)}, u32[]{:S(2)}, u32[]{:S(2)}) %collective-permute-start.18) | collective-permute-done | bytes 524320 | tf_op jit(solution)/shard_map/ppermute | solution.py:21
  110.9 8.6 %shard_map.49 = bf16[640,192]{1,0:T(8,128)(2,1)S(1)} custom-call(bf16[320,8192]{1,0:T(8,128)(2,1)} %refs_0_.4, bf16[320,8192]{1,0:T(8,128)(2,1)} %copy-done.2, bf16[32,8192]{1,0:T(8,128)(2,1)S(1)} %collective-permute-done.13.refs_2_, bf16[32,8192]{1,0:T(8,128)(2,1)S(1)} %collective-permute-done.12.refs_3_, ...), custom_call_target="tpu_custom_call" | custom-call | flops 1 | bytes 1 | tf_op jit(solution)/shard_map/pallas_call | solution.py:46
  123.0 3.7 %collective-permute-done.21 = bf16[640,192]{1,0:T(8,128)(2,1)S(1)} collective-permute-done((bf16[640,192]{1,0:T(8,128)(2,1)S(1)}, bf16[640,192]{1,0:T(8,128)(2,1)S(1)}, u32[]{:S(2)}, u32[]{:S(2)}) %collective-permute-start.21) | collective-permute-done | bytes 245792 | tf_op jit(solution)/shard_map/ppermute | solution.py:21
  126.8 6.5 %collective-permute-done.27.refs_6_ = bf16[208,768]{1,0:T(8,128)(2,1)S(1)} collective-permute-done((bf16[208,768]{1,0:T(8,128)(2,1)S(1)}, bf16[208,768]{1,0:T(8,128)(2,1)S(1)}, u32[]{:S(2)}, u32[]{:S(2)}) %collective-permute-start.27) | collective-permute-done | bytes 319520 | tf_op jit(solution)/shard_map/ppermute | solution.py:21
  136.1 4.0 %shard_map.50.refs_10_ = bf16[320,8192]{1,0:T(8,128)(2,1)} custom-call(s32[1]{0:T(128)} %bitcast.side_ref, bf16[320,208]{1,0:T(8,128)(2,1)S(1)} %fusion.1.refs_0_, bf16[320,208]{1,0:T(8,128)(2,1)S(1)} %collective-permute-done.9.refs_1_, bf16[320,208]{1,0:T(8,128)(2,1)S(1)} %get-tuple-element.120.refs_2_, ...), custom_call_target="tpu_custom_call" | custom-call | flops 1 | bytes 1 | tf_op jit(solution)/shard_map/pallas_call | solution.py:46
  140.1 7.2 %collective-permute-done.32.refs_10_.refs_11_ = bf16[208,1024]{1,0:T(8,128)(2,1)S(1)} collective-permute-done((bf16[208,1024]{1,0:T(8,128)(2,1)S(1)}, bf16[208,1024]{1,0:T(8,128)(2,1)S(1)}, u32[]{:S(2)}, u32[]{:S(2)}) %collective-permute-start.32) | collective-permute-done | bytes 426016 | tf_op jit(solution)/shard_map/ppermute | solution.py:21
  148.9 8.3 %collective-permute-done.30.refs_7_ = bf16[208,768]{1,0:T(8,128)(2,1)S(1)} collective-permute-done((bf16[208,768]{1,0:T(8,128)(2,1)S(1)}, bf16[208,768]{1,0:T(8,128)(2,1)S(1)}, u32[]{:S(2)}, u32[]{:S(2)}) %collective-permute-start.30) | collective-permute-done | bytes 319520 | tf_op jit(solution)/shard_map/ppermute | solution.py:21
  158.0 4.0 %shard_map.51.refs_14_ = bf16[320,8192]{1,0:T(8,128)(2,1)} custom-call(s32[1]{0:T(128)} %bitcast.side_ref, bf16[320,208]{1,0:T(8,128)(2,1)S(1)} %fusion.1.refs_0_, bf16[320,208]{1,0:T(8,128)(2,1)S(1)} %collective-permute-done.9.refs_1_, bf16[320,208]{1,0:T(8,128)(2,1)S(1)} %get-tuple-element.120.refs_2_, ...), custom_call_target="tpu_custom_call", output_to_operand_aliasing={{}: (11, {})} | custom-call | flops 1 | bytes 1 | tf_op jit(solution)/shard_map/pallas_call | solution.py:46
  162.8 5.9 %shard_map.52.refs_10_ = bf16[320,8192]{1,0:T(8,128)(2,1)} custom-call(s32[1]{0:T(128)} %bitcast.side_ref, bf16[320,208]{1,0:T(8,128)(2,1)S(1)} %fusion.1.refs_0_, bf16[320,208]{1,0:T(8,128)(2,1)S(1)} %collective-permute-done.9.refs_1_, bf16[320,208]{1,0:T(8,128)(2,1)S(1)} %get-tuple-element.120.refs_2_, ...), custom_call_target="tpu_custom_call", output_to_operand_aliasing={{}: (15, {})} | custom-call | flops 1 | bytes 1 | tf_op jit(solution)/shard_map/pallas_call | solution.py:46
  168.7 4.8 %shard_map.53 = bf16[320,8192]{1,0:T(8,128)(2,1)} custom-call(s32[1]{0:T(128)} %bitcast.side_ref, bf16[320,208]{1,0:T(8,128)(2,1)S(1)} %fusion.1.refs_0_, bf16[320,208]{1,0:T(8,128)(2,1)S(1)} %collective-permute-done.9.refs_1_, bf16[320,208]{1,0:T(8,128)(2,1)S(1)} %get-tuple-element.120.refs_2_, ...), custom_call_target="tpu_custom_call", output_to_operand_aliasing={{}: (11, {})} | custom-call | flops 1 | bytes 1 | tf_op jit(solution)/shard_map/pallas_call | solution.py:46
  (100 shorter events, 38.5 us)
Async XLA Ops:
  1.1 25.2 %collective-permute-start.3 = (bf16[320,8192]{1,0:T(8,128)(2,1)}, bf16[320,8192]{1,0:T(8,128)(2,1)S(1)}, u32[]{:S(2)}, u32[]{:S(2)}) collective-permute-start(bf16[320,8192]{1,0:T(8,128)(2,1)} %refs_0_.4), channel_id=1, source_target_pairs={{1,0},{0,1},{3,2},{2,3},{5,4},{4,5},{7,6},{6,7},{9,8},{8,9},{11,10... | collective-permute-start | bytes 15728648 | tf_op jit(solution)/shard_map/ppermute | solution.py:21
  5.5 19.2 %collective-permute-start.4 = (bf16[32,8192]{1,0:T(8,128)(2,1)S(1)}, bf16[32,8192]{1,0:T(8,128)(2,1)S(1)}, u32[]{:S(2)}, u32[]{:S(2)}) collective-permute-start(bf16[32,8192]{1,0:T(8,128)(2,1)S(1)} %slice_select_fusion.5), channel_id=1, source_target_pairs={{12,0},{0,4},{4,8},{8,12},{13,1},{1,5},{5,9},{9,13},{14,2},{2,6},{... | collective-permute-start | bytes 1572872 | tf_op jit(solution)/shard_map/ppermute | solution.py:21
  7.1 83.3 %collective-permute-start.20 = (bf16[208,8192]{1,0:T(8,128)(2,1)}, bf16[208,8192]{1,0:T(8,128)(2,1)S(1)}, u32[]{:S(2)}, u32[]{:S(2)}) collective-permute-start(bf16[208,8192]{1,0:T(8,128)(2,1)} %refs_4_.7), channel_id=1, source_target_pairs={{1,0},{0,1},{3,2},{2,3},{5,4},{4,5},{7,6},{6,7},{9,8},{8,9},{11,10... | collective-permute-start | bytes 10223624 | tf_op jit(solution)/shard_map/ppermute | solution.py:21
  13.4 22.5 %collective-permute-start.2 = (bf16[32,8192]{1,0:T(8,128)(2,1)S(1)}, bf16[32,8192]{1,0:T(8,128)(2,1)S(1)}, u32[]{:S(2)}, u32[]{:S(2)}) collective-permute-start(bf16[32,8192]{1,0:T(8,128)(2,1)S(1)} %get-tuple-element.62), channel_id=1, source_target_pairs={{12,0},{0,4},{4,8},{8,12},{13,1},{1,5},{5,9},{9,13},{14,2},{2,6},{... | collective-permute-start | bytes 1572872 | tf_op jit(solution)/shard_map/ppermute | solution.py:21
  26.3 20.9 %collective-permute-start.7 = (bf16[32,8192]{1,0:T(8,128)(2,1)}, bf16[32,8192]{1,0:T(8,128)(2,1)}, u32[]{:S(2)}, u32[]{:S(2)}) collective-permute-start(bf16[32,8192]{1,0:T(8,128)(2,1)} %get-tuple-element.68), channel_id=1, source_target_pairs={{12,0},{0,4},{4,8},{8,12},{13,1},{1,5},{5,9},{9,13},{14,2},{2,6},{... | collective-permute-start | bytes 1572872 | tf_op jit(solution)/shard_map/ppermute | solution.py:21
  26.3 22.6 %collective-permute-start.8 = (bf16[32,8192]{1,0:T(8,128)(2,1)S(1)}, bf16[32,8192]{1,0:T(8,128)(2,1)}, u32[]{:S(2)}, u32[]{:S(2)}) collective-permute-start(bf16[32,8192]{1,0:T(8,128)(2,1)S(1)} %collective-permute-done.4.refs_3_), channel_id=1, source_target_pairs={{16,0},{0,16},{17,1},{1,17},{18,2},{2,18},{19,3},{3,19},{20,4},{4,... | collective-permute-start | bytes 1572872 | tf_op jit(solution)/shard_map/ppermute | solution.py:21
  35.9 13.4 %collective-permute-start.6 = (bf16[320,416]{1,0:T(8,128)(2,1)S(1)}, bf16[320,416]{1,0:T(8,128)(2,1)S(1)}, u32[]{:S(2)}, u32[]{:S(2)}) collective-permute-start(bf16[320,416]{1,0:T(8,128)(2,1)S(1)} %shard_map.47), channel_id=1, source_target_pairs={{2,0},{0,2},{3,1},{1,3},{6,4},{4,6},{7,5},{5,7},{10,8},{8,10},{11,... | collective-permute-start | bytes 798728 | tf_op jit(solution)/shard_map/ppermute | solution.py:21
  37.6 20.7 %collective-permute-start.13 = (bf16[32,8192]{1,0:T(8,128)(2,1)}, bf16[32,8192]{1,0:T(8,128)(2,1)S(1)}, u32[]{:S(2)}, u32[]{:S(2)}) collective-permute-start(bf16[32,8192]{1,0:T(8,128)(2,1)} %get-tuple-element.72), channel_id=1, source_target_pairs={{12,0},{0,4},{4,8},{8,12},{13,1},{1,5},{5,9},{9,13},{14,2},{2,6},{... | collective-permute-start | bytes 1572872 | tf_op jit(solution)/shard_map/ppermute | solution.py:21
  47.2 14.8 %collective-permute-start.10 = (bf16[32,8192]{1,0:T(8,128)(2,1)S(1)}, bf16[32,8192]{1,0:T(8,128)(2,1)S(1)}, u32[]{:S(2)}, u32[]{:S(2)}) collective-permute-start(bf16[32,8192]{1,0:T(8,128)(2,1)S(1)} %collective-permute-done.2.refs_4_), channel_id=1, source_target_pairs={{16,0},{0,16},{17,1},{1,17},{18,2},{2,18},{19,3},{3,19},{20,4},{4,... | collective-permute-start | bytes 1572872 | tf_op jit(solution)/shard_map/ppermute | solution.py:21
  48.9 24.4 %collective-permute-start.11 = (bf16[32,8192]{1,0:T(8,128)(2,1)}, bf16[32,8192]{1,0:T(8,128)(2,1)S(1)}, u32[]{:S(2)}, u32[]{:S(2)}) collective-permute-start(bf16[32,8192]{1,0:T(8,128)(2,1)} %collective-permute-done.7.refs_5_), channel_id=1, source_target_pairs={{16,0},{0,16},{17,1},{1,17},{18,2},{2,18},{19,3},{3,19},{20,4},{4,... | collective-permute-start | bytes 1572872 | tf_op jit(solution)/shard_map/ppermute | solution.py:21
  49.2 20.3 %collective-permute-start.12 = (bf16[32,8192]{1,0:T(8,128)(2,1)}, bf16[32,8192]{1,0:T(8,128)(2,1)S(1)}, u32[]{:S(2)}, u32[]{:S(2)}) collective-permute-start(bf16[32,8192]{1,0:T(8,128)(2,1)} %get-tuple-element.71), channel_id=1, source_target_pairs={{12,0},{0,4},{4,8},{8,12},{13,1},{1,5},{5,9},{9,13},{14,2},{2,6},{... | collective-permute-start | bytes 1572872 | tf_op jit(solution)/shard_map/ppermute | solution.py:21
  62.1 25.2 %collective-permute-start.15 = (bf16[32,8192]{1,0:T(8,128)(2,1)}, bf16[32,8192]{1,0:T(8,128)(2,1)S(1)}, u32[]{:S(2)}, u32[]{:S(2)}) collective-permute-start(bf16[32,8192]{1,0:T(8,128)(2,1)} %get-tuple-element.83), channel_id=1, source_target_pairs={{12,0},{0,4},{4,8},{8,12},{13,1},{1,5},{5,9},{9,13},{14,2},{2,6},{... | collective-permute-start | bytes 1572872 | tf_op jit(solution)/shard_map/ppermute | solution.py:21
  62.1 25.2 %collective-permute-start.16 = (bf16[32,8192]{1,0:T(8,128)(2,1)S(1)}, bf16[32,8192]{1,0:T(8,128)(2,1)}, u32[]{:S(2)}, u32[]{:S(2)}) collective-permute-start(bf16[32,8192]{1,0:T(8,128)(2,1)S(1)} %collective-permute-done.13.refs_2_), channel_id=1, source_target_pairs={{16,0},{0,16},{17,1},{1,17},{18,2},{2,18},{19,3},{3,19},{20,4},{4,... | collective-permute-start | bytes 1572872 | tf_op jit(solution)/shard_map/ppermute | solution.py:21
  84.7 15.0 %collective-permute-start.17 = (bf16[32,8192]{1,0:T(8,128)(2,1)S(1)}, bf16[32,8192]{1,0:T(8,128)(2,1)}, u32[]{:S(2)}, u32[]{:S(2)}) collective-permute-start(bf16[32,8192]{1,0:T(8,128)(2,1)S(1)} %collective-permute-done.12.refs_3_), channel_id=1, source_target_pairs={{16,0},{0,16},{17,1},{1,17},{18,2},{2,18},{19,3},{3,19},{20,4},{4,... | collective-permute-start | bytes 1572872 | tf_op jit(solution)/shard_map/ppermute | solution.py:21
  87.3 23.6 %collective-permute-start.18 = (bf16[32,8192]{1,0:T(8,128)(2,1)S(1)}, bf16[32,8192]{1,0:T(8,128)(2,1)}, u32[]{:S(2)}, u32[]{:S(2)}) collective-permute-start(bf16[32,8192]{1,0:T(8,128)(2,1)S(1)} %collective-permute-done.15.refs_4_), channel_id=1, source_target_pairs={{16,0},{0,16},{17,1},{1,17},{18,2},{2,18},{19,3},{3,19},{20,4},{4,... | collective-permute-start | bytes 1572872 | tf_op jit(solution)/shard_map/ppermute | solution.py:21
  99.7 22.6 %collective-permute-start.24 = (bf16[208,1024]{1,0:T(8,128)(2,1)S(1)}, bf16[208,1024]{1,0:T(8,128)(2,1)S(1)}, u32[]{:S(2)}, u32[]{:S(2)}) collective-permute-start(bf16[208,1024]{1,0:T(8,128)(2,1)S(1)} %collective-permute-done.19.refs_6_), channel_id=1, source_target_pairs={{16,0},{0,16},{17,1},{1,17},{18,2},{2,18},{19,3},{3,19},{20,4},{4,... | collective-permute-start | bytes 1277960 | tf_op jit(solution)/shard_map/ppermute | solution.py:21
  101.2 21.2 %collective-permute-start.25 = (bf16[208,1024]{1,0:T(8,128)(2,1)S(1)}, bf16[208,1024]{1,0:T(8,128)(2,1)S(1)}, u32[]{:S(2)}, u32[]{:S(2)}) collective-permute-start(bf16[208,1024]{1,0:T(8,128)(2,1)S(1)} %collective-permute-done.19.refs_6_), channel_id=1, source_target_pairs={{1,0},{0,1},{3,2},{2,3},{5,4},{4,5},{7,6},{6,7},{9,8},{8,9},{11,10... | collective-permute-start | bytes 1277960 | tf_op jit(solution)/shard_map/ppermute | solution.py:21
  101.2 18.8 %collective-permute-start.23 = (bf16[208,1024]{1,0:T(8,128)(2,1)}, bf16[208,1024]{1,0:T(8,128)(2,1)S(1)}, u32[]{:S(2)}, u32[]{:S(2)}) collective-permute-start(bf16[208,1024]{1,0:T(8,128)(2,1)} %get-tuple-element.96), channel_id=1, source_target_pairs={{12,0},{0,4},{4,8},{8,12},{13,1},{1,5},{5,9},{9,13},{14,2},{2,6},{... | collective-permute-start | bytes 1277960 | tf_op jit(solution)/shard_map/ppermute | solution.py:21
  102.0 20.3 %collective-permute-start.22 = (bf16[208,768]{1,0:T(8,128)(2,1)S(1)}, bf16[208,768]{1,0:T(8,128)(2,1)S(1)}, u32[]{:S(2)}, u32[]{:S(2)}) collective-permute-start(bf16[208,768]{1,0:T(8,128)(2,1)S(1)} %get-tuple-element.95), channel_id=1, source_target_pairs={{12,0},{0,4},{4,8},{8,12},{13,1},{1,5},{5,9},{9,13},{14,2},{2,6},{... | collective-permute-start | bytes 958472 | tf_op jit(solution)/shard_map/ppermute | solution.py:21
  122.4 17.7 %collective-permute-start.31 = (bf16[208,768]{1,0:T(8,128)(2,1)S(1)}, bf16[208,768]{1,0:T(8,128)(2,1)S(1)}, u32[]{:S(2)}, u32[]{:S(2)}) collective-permute-start(bf16[208,768]{1,0:T(8,128)(2,1)S(1)} %collective-permute-done.22.refs_6_), channel_id=1, source_target_pairs={{16,0},{0,16},{17,1},{1,17},{18,2},{2,18},{19,3},{3,19},{20,4},{4,... | collective-permute-start | bytes 958472 | tf_op jit(solution)/shard_map/ppermute | solution.py:21
  126.7 13.4 %collective-permute-start.34 = (bf16[208,768]{1,0:T(8,128)(2,1)S(1)}, bf16[208,768]{1,0:T(8,128)(2,1)S(1)}, u32[]{:S(2)}, u32[]{:S(2)}) collective-permute-start(bf16[208,768]{1,0:T(8,128)(2,1)S(1)} %collective-permute-done.22.refs_6_), channel_id=1, source_target_pairs={{1,0},{0,1},{3,2},{2,3},{5,4},{4,5},{7,6},{6,7},{9,8},{8,9},{11,10... | collective-permute-start | bytes 958472 | tf_op jit(solution)/shard_map/ppermute | solution.py:21
  133.3 14.0 %collective-permute-start.32 = (bf16[208,1024]{1,0:T(8,128)(2,1)S(1)}, bf16[208,1024]{1,0:T(8,128)(2,1)S(1)}, u32[]{:S(2)}, u32[]{:S(2)}) collective-permute-start(bf16[208,1024]{1,0:T(8,128)(2,1)S(1)} %copy-done.7), channel_id=1, source_target_pairs={{12,0},{0,4},{4,8},{8,12},{13,1},{1,5},{5,9},{9,13},{14,2},{2,6},{... | collective-permute-start | bytes 1277960 | tf_op jit(solution)/shard_map/ppermute | solution.py:21
  148.0 14.0 %collective-permute-start.38 = (bf16[208,1024]{1,0:T(8,128)(2,1)S(1)}, bf16[208,1024]{1,0:T(8,128)(2,1)S(1)}, u32[]{:S(2)}, u32[]{:S(2)}) collective-permute-start(bf16[208,1024]{1,0:T(8,128)(2,1)S(1)} %collective-permute-done.32.refs_10_.refs_11_), channel_id=1, source_target_pairs={{1,0},{0,1},{3,2},{2,3},{5,4},{4,5},{7,6},{6,7},{9,8},{8,9},{11,10... | collective-permute-start | bytes 1277960 | tf_op jit(solution)/shard_map/ppermute | solution.py:21
  148.3 20.4 %collective-permute-start.36 = (bf16[208,768]{1,0:T(8,128)(2,1)S(1)}, bf16[208,768]{1,0:T(8,128)(2,1)S(1)}, u32[]{:S(2)}, u32[]{:S(2)}) collective-permute-start(bf16[208,768]{1,0:T(8,128)(2,1)S(1)} %collective-permute-done.27.refs_6_), channel_id=1, source_target_pairs={{1,0},{0,1},{3,2},{2,3},{5,4},{4,5},{7,6},{6,7},{9,8},{8,9},{11,10... | collective-permute-start | bytes 958472 | tf_op jit(solution)/shard_map/ppermute | solution.py:21
  (27 other events, 273.6 us)

commit v6 on v5

--- a/solution.py
+++ b/solution.py
@@ -7,9 +7,9 @@
 from jax.experimental.pallas import tpu as pltpu
 from jax.sharding import PartitionSpec as P
 
-ROW_SHARES = (1, 2, 2, 2, 2, 2, 2)
-LANE_SHARES = (4, 4, 3, 3, 2)
-QUEUE = 2
+ROW_SHARES = (2, 2, 2, 2, 2, 2, 1)
+LANE_SHARES = (5, 5, 3, 3)
+QUEUE = 3
 SLOTS = 3
 VMEM = 52 * 1024 * 1024
 ANY = pl.BlockSpec(memory_space=pl.ANY)
@@ -120,32 +120,36 @@
 
 def blocks_of(parts):
     found = []
-    for i, (a, b, whole) in enumerate(parts):
-        half = (b - a) // 2
-        size = 512 if half % 512 == 0 else 256 if half % 256 == 0 else 128
-        for k in range(2):
-            for lane in range(0, half, size):
-                if whole:
-                    found.append((i, 0, k * half + lane, size, (a + k * half + lane, 0)))
-                else:
-                    found.append((i, k, lane, size, (a + k * half + lane, half - 2 * k * half)))
+    for i, (a, half, own, other) in enumerate(parts):
+        arrays = [(0, lanes) for lanes in own] + [(1, lanes) for lanes in other]
+        filled = [0, 0]
+        for n, (k, lanes) in enumerate(arrays):
+            for lane in range(0, lanes, 512):
+                size = min(512, lanes - lane)
+                turn = half - 2 * k * half if other else 0
+                found.append((i, n, lane, size, (a + k * half + filled[k] + lane, turn)))
+            filled[k] += lanes
     return found
 
 
 def output_kernel(parts, side_ref, *refs):
     hidden, down = refs[:4], refs[4:6]
-    arrived = refs[6 : 6 + 4 * len(parts)]
+    arrived, at = [], 6
+    for _, _, own, other in parts:
+        count = len(own) + len(other)
+        arrived.append((refs[at : at + count], refs[at + count : at + 2 * count]))
+        at += 2 * count
     out, weights, result, sems = refs[-4:]
     share = down[0].shape[0]
     side = side_ref[0]
     loads, stores, spots, at = [], [], [], 0
-    for n, (i, k, lane, size, (fixed, turn)) in enumerate(blocks_of(parts)):
+    for n, (i, array, lane, size, (fixed, turn)) in enumerate(blocks_of(parts)):
         column = pl.ds(pl.multiple_of(fixed + side * turn, 128), size)
         spot = pl.ds(at, size)
         spots.append(slice(at, at + size))
         at += size
         sources = [ref.at[:, column] for ref in down]
-        sources += [arrived[4 * i + 2 * m + k].at[:, pl.ds(lane, size)] for m in range(2)]
+        sources += [arrays[array].at[:, pl.ds(lane, size)] for arrays in arrived[i]]
         loads.append(
             [
                 pltpu.make_async_copy(source, weights.at[m, :, spot], sems.at[m, n])
@@ -175,7 +179,7 @@
 
 def output_part(result, parts, side, hidden, down, arrived):
     rows, units, width = hidden[0].shape[0], down[0].shape[0], down[0].shape[1]
-    lanes = sum(b - a for a, b, _ in parts)
+    lanes = sum(sum(own) + sum(other) for _, _, own, other in parts)
     operands = [side, *hidden, *down, *arrived]
     in_specs = (
         [pl.BlockSpec(memory_space=pltpu.SMEM)]
@@ -253,30 +257,40 @@
     waiting = [shifted(pieces[i], "dp", 1) for i in range(QUEUE)]
     landed, crossed, mates, crossed_mates = [], {}, {}, {}
 
+    def in_two(block):
+        mid = max(128, block.shape[1] // 256 * 128)
+        if mid >= block.shape[1]:
+            return [block]
+        return [block[:, :mid], block[:, mid:]]
+
     def advance(*after):
         i = len(landed)
         held = [*after, *landed[-1:]]
-        for swapped, j in ((crossed, i - 2), (mates, i - 2), (crossed_mates, i - 4)):
-            if j in swapped:
-                held.append(swapped[j])
+        if 0 <= i - QUEUE < count:
+            held.append(crossed[i - QUEUE])
         block = tied(waiting[i], *held)
         landed.append(block)
         if i < last:
             crossed[i] = across(block)
         if i >= count:
             mates[i] = mate(block)
-        if i - 2 in range(count, last):
-            crossed_mates[i - 2] = mate(tied(crossed[i - 2], block))
         if i + QUEUE < total_count:
             waiting.append(shifted(tied(pieces[i + QUEUE], block), "dp", 1))
         return block
 
+    def pass_on(n, *after):
+        i = count + n
+        crossed[i] = tied(crossed[i], *after)
+        crossed_mates[i] = [mate(part) for part in in_two(crossed[i])]
+        return crossed[i]
+
     def local(partial_value, sent):
         pre = summed(partial_value, sent)
         return gated(pre[:, :units], pre[:, units:])
 
     def batch(lo, hi, now):
-        held = [landed[i] for i in range(lo, hi)] + [crossed[i] for i in range(lo, hi)]
+        held = [landed[i] for i in range(lo, hi)]
+        held += [crossed[i] for i in range(lo, hi)]
         held = lax.optimization_barrier((*held, now))[:-1]
         value = products([tokens, tokens_mate], held)
         return value, over_slices(value)
@@ -289,43 +303,44 @@
 
     tokens_mate = mate(tied(tokens, pieces[0]))
     down_mate = mate(tied(down_weight, pieces[1]))
+    mine = products([tokens], [gate_weight, up_weight])
+    mine_sent = over_slices(mine)
+    advance(mine)
     now = advance()
-    mine = products([tied(tokens, now)], [gate_weight, up_weight])
-    mine_sent = over_slices(mine)
-    now = advance(mine)
     theirs = products([tied(tokens_mate, now)], [gate_weight, up_weight])
     theirs_sent = over_slices(theirs)
-    now = advance(theirs)
+    advance(theirs)
+    now = advance()
     here = local(mine, [tied(block, now) for block in mine_sent])
     now = advance(here)
+    early, early_sent = batch(0, 3, now)
+    now = advance(early)
     here_mate = mate(local(theirs, [tied(block, now) for block in theirs_sent]))
     now = advance()
-    now = advance(here_mate)
-    early, early_sent = batch(0, 4, now)
-    now = advance(early)
     there = [activated(early, [tied(block, now) for block in early_sent])]
-    now = advance(there[0], down_mate)
-    late, late_sent = batch(4, count, now)
-    now = advance(late)
-    now = advance()
+    now = advance(there[0], here_mate)
+    late, late_sent = batch(3, count, now)
+    now = advance(late, down_mate)
+    now = pass_on(0, now)
+    now = advance(now)
     there.append(activated(late, [tied(block, now) for block in late_sent]))
     there = jnp.concatenate(there, axis=1)
     there_mate = mate(there[rows:])
     there = there[:rows]
-    now = advance(there)
-    there_mate = tied(there_mate, now)
 
     def write(result, *which):
         parts, arrived = [], []
         for n in which:
             i = count + n
-            parts.append((*lane_cuts[n], i == last))
+            a, b = lane_cuts[n]
             if i == last:
-                arrived += [landed[i], landed[i], mates[i], mates[i]]
+                parts.append((a, (b - a) // 2, (b - a,), ()))
+                arrived += [landed[i], mates[i]]
             else:
-                if i not in crossed_mates:
-                    crossed_mates[i] = mate(crossed[i])
-                arrived += [landed[i], crossed[i], mates[i], crossed_mates[i]]
+                half = (b - a) // 2
+                lanes = tuple(part.shape[1] for part in crossed_mates[i])
+                parts.append((a, half, (half,), lanes))
+                arrived += [landed[i], *in_two(crossed[i]), mates[i], *crossed_mates[i]]
         return output_part(
             result,
             tuple(parts),
@@ -336,11 +351,11 @@
         )
 
     result = write(None, 0)
+    pass_on(1, result)
+    result = write(result, 1)
     now = advance(result)
-    result = write(result, 1)
-    crossed[last - 1] = tied(crossed[last - 1], crossed_mates[last - 2])
-    result = write(result, 2, 4)
-    return write(result, 3)
+    pass_on(2, now)
+    return write(result, 2, 3)
 
 
 def solution(mesh):

time: 174 us -> 169 us (0.971)
  waiting for transfers between devices: 85.3 us -> 66.4 us
  starting transfers between devices: 26.5 us -> 38.1 us
    ppermute x40 -> x39, waiting for transfers between devices: 85.3 us -> 66.4 us  [shifted(): return lax.ppermute(block, axis, route)]
    ppermute x40 -> x39, starting transfers between devices: 26.5 us -> 38.1 us  [shifted(): return lax.ppermute(block, axis, route)]
    unnamed x22, local copies, waits for them, and re-layouts: 3.86 us -> 1.67 us
    select_n x3 -> x4, other arithmetic: 6.21 us -> 7.48 us  [piece(): return jnp.where(first, gate[a:b], up[a:b])]
    pallas_call x8 -> x7, Pallas kernels: 48.4 us -> 49.5 us  [call(): pl.pallas_call(kernel, in_specs=in_specs, out_specs=out_spec, out_shape=o...]
  transfers between devices with their start and end apart: 40 -> 39, of which waited for: 19 -> 16; matrix products, arithmetic and copies ran while one was open for 5% -> 6% of each run, Pallas kernels for 25% -> 25%
where the time goes in v6:
time: 169 us; the launch traced here: 168 us
  waiting for transfers between devices  66.4 us (39%)
  Pallas kernels  49.5 us (29%)
  starting transfers between devices  38.1 us (23%)
  other arithmetic  10.7 us (6%)
  local copies, waits for them, and re-layouts  2.87 us (2%)
    ppermute x39, waiting for transfers between devices, shifted(): return lax.ppermute(block, axis, route)  66.4 us
    pallas_call x7, Pallas kernels, call(): pl.pallas_call(kernel, in_specs=in_specs, out_specs=out_spec, out_shape=o...  49.5 us
    ppermute x39, starting transfers between devices, shifted(): return lax.ppermute(block, axis, route)  38.1 us
    select_n x4, other arithmetic, piece(): return jnp.where(first, gate[a:b], up[a:b])  7.48 us
  transfers between devices with their start and end apart: 39, of which 16 were waited for; matrix products, arithmetic and copies ran while one was open for 6% of the time, Pallas kernels for 25%

profile of v6, /device:TPU:0, one launch (start us, length us, event | category | flops | bytes accessed | tf_op | source)
XLA Modules:
  0.0 168.1 jit_solution(15597982853685562469)
XLA Ops:
  1.8 2.6 %collective-permute-start.1 = (bf16[32,8192]{1,0:T(8,128)(2,1)S(1)}, bf16[32,8192]{1,0:T(8,128)(2,1)S(1)}, u32[]{:S(2)}, u32[]{:S(2)}) collective-permute-start(bf16[32,8192]{1,0:T(8,128)(2,1)S(1)} %slice_select_fusion.7), channel_id=1, source_target_pairs={{12,0},{0,4},{4,8},{8,12},{13,1},{1,5},{5,9},{9,13},{14,2},{2,6},{... | collective-permute-start | bytes 1572872 | tf_op jit(solution)/shard_map/ppermute | solution.py:21
  5.7 1.6 collective-permute-start.5
  7.3 3.2 %slice_select_fusion.2 = (bf16[32,8192]{1,0:T(8,128)(2,1)S(1)}, bf16[32,8192]{1,0:T(8,128)(2,1)}, bf16[32,8192]{1,0:T(8,128)(2,1)S(1)}, bf16[32,8192]{1,0:T(8,128)(2,1)S(1)}) fusion(bf16[208,8192]{1,0:T(8,128)(2,1)} %refs_2_.3, bf16[208,8192]{1,0:T(8,128)(2,1)} %refs_1_.3, pred[]{:T(512)S(6)} %eq.3), kind=kLoop, calls=%fused_computation.6 | loop fusion | flops 1048576 | bytes 6291457 | tf_op jit(solution)/shard_map/jit(_where)/select_n | solution.py:246
  12.1 6.1 %shard_map.46 = bf16[320,416]{1,0:T(8,128)(2,1)S(1)} custom-call(bf16[320,8192]{1,0:T(8,128)(2,1)} %refs_0_.5, bf16[208,8192]{1,0:T(8,128)(2,1)} %refs_1_.3, bf16[208,8192]{1,0:T(8,128)(2,1)} %refs_2_.3), custom_call_target="tpu_custom_call" | custom-call | flops 1 | bytes 1 | tf_op jit(solution)/shard_map/pallas_call | solution.py:46
  19.8 10.7 %collective-permute-done.5.refs_3_ = bf16[32,8192]{1,0:T(8,128)(2,1)S(1)} collective-permute-done((bf16[32,8192]{1,0:T(8,128)(2,1)S(1)}, bf16[32,8192]{1,0:T(8,128)(2,1)S(1)}, u32[]{:S(2)}, u32[]{:S(2)}) %collective-permute-start.5) | collective-permute-done | bytes 524320 | tf_op jit(solution)/shard_map/ppermute | solution.py:21
  30.5 1.7 collective-permute-start.6
  32.1 9.3 %collective-permute-done.3.refs_4_ = bf16[32,8192]{1,0:T(8,128)(2,1)S(1)} collective-permute-done((bf16[32,8192]{1,0:T(8,128)(2,1)S(1)}, bf16[32,8192]{1,0:T(8,128)(2,1)S(1)}, u32[]{:S(2)}, u32[]{:S(2)}) %collective-permute-start.3) | collective-permute-done | bytes 524320 | tf_op jit(solution)/shard_map/ppermute | solution.py:21
  42.7 1.8 %slice_select_fusion.9 = bf16[16,8192]{1,0:T(8,128)(2,1)} fusion(bf16[208,8192]{1,0:T(8,128)(2,1)} %refs_2_.3, bf16[208,8192]{1,0:T(8,128)(2,1)} %refs_1_.3, pred[]{:T(512)S(6)} %eq.3), kind=kLoop, calls=%fused_computation.21 | loop fusion | flops 131072 | bytes 786433 | tf_op jit(solution)/shard_map/jit(_where)/select_n | solution.py:246
  44.5 6.1 %shard_map.47 = bf16[320,416]{1,0:T(8,128)(2,1)S(1)} custom-call(bf16[320,8192]{1,0:T(8,128)(2,1)} %collective-permute-done.4.refs_0_.refs_1_, bf16[208,8192]{1,0:T(8,128)(2,1)} %refs_1_.3, bf16[208,8192]{1,0:T(8,128)(2,1)} %refs_2_.3), custom_call_target="tpu_custom_call" | custom-call | flops 1 | bytes 1 | tf_op jit(solution)/shard_map/pallas_call | solution.py:46
  52.2 5.8 %collective-permute-done.2.refs_2_ = bf16[32,8192]{1,0:T(8,128)(2,1)S(1)} collective-permute-done((bf16[32,8192]{1,0:T(8,128)(2,1)S(1)}, bf16[32,8192]{1,0:T(8,128)(2,1)S(1)}, u32[]{:S(2)}, u32[]{:S(2)}) %collective-permute-start.2) | collective-permute-done | bytes 524320 | tf_op jit(solution)/shard_map/ppermute | solution.py:21
  60.7 8.6 %collective-permute-done.11.refs_3_ = bf16[32,8192]{1,0:T(8,128)(2,1)S(1)} collective-permute-done((bf16[32,8192]{1,0:T(8,128)(2,1)S(1)}, bf16[32,8192]{1,0:T(8,128)(2,1)S(1)}, u32[]{:S(2)}, u32[]{:S(2)}) %collective-permute-start.11) | collective-permute-done | bytes 524320 | tf_op jit(solution)/shard_map/ppermute | solution.py:21
  70.9 1.6 collective-permute-start.15
  72.5 4.3 %collective-permute-done.10.refs_7_ = bf16[32,8192]{1,0:T(8,128)(2,1)S(1)} collective-permute-done((bf16[32,8192]{1,0:T(8,128)(2,1)S(1)}, bf16[32,8192]{1,0:T(8,128)(2,1)S(1)}, u32[]{:S(2)}, u32[]{:S(2)}) %collective-permute-start.10) | collective-permute-done | bytes 524320 | tf_op jit(solution)/shard_map/ppermute | solution.py:21
  78.6 8.6 %shard_map.48 = bf16[640,192]{1,0:T(8,128)(2,1)S(1)} custom-call(bf16[320,8192]{1,0:T(8,128)(2,1)} %refs_0_.5, bf16[320,8192]{1,0:T(8,128)(2,1)} %collective-permute-done.4.refs_0_.refs_1_, bf16[32,8192]{1,0:T(8,128)(2,1)S(1)} %collective-permute-done.1.refs_2_, bf16[32,8192]{1,0:T(8,128)(2,1)S(1)} %collective-permute-done.5.refs_3_, ...), custom_call_target="tpu_custom_call" | custom-call | flops 1 | bytes 1 | tf_op jit(solution)/shard_map/pallas_call | solution.py:46
  91.4 2.1 %collective-permute-start.19 = (bf16[208,1280]{1,0:T(8,128)(2,1)}, bf16[208,1280]{1,0:T(8,128)(2,1)S(1)}, u32[]{:S(2)}, u32[]{:S(2)}) collective-permute-start(bf16[208,1280]{1,0:T(8,128)(2,1)} %get-tuple-element.79), channel_id=1, source_target_pairs={{12,0},{0,4},{4,8},{8,12},{13,1},{1,5},{5,9},{9,13},{14,2},{2,6},{... | collective-permute-start | bytes 1597448 | tf_op jit(solution)/shard_map/ppermute | solution.py:21
  94.3 1.6 collective-permute-done.13
  96.5 5.7 %collective-permute-done.16.refs_7_ = bf16[32,8192]{1,0:T(8,128)(2,1)S(1)} collective-permute-done((bf16[32,8192]{1,0:T(8,128)(2,1)S(1)}, bf16[32,8192]{1,0:T(8,128)(2,1)S(1)}, u32[]{:S(2)}, u32[]{:S(2)}) %collective-permute-start.16) | collective-permute-done | bytes 524320 | tf_op jit(solution)/shard_map/ppermute | solution.py:21
  106.1 12.9 %collective-permute-done.18.refs_9_ = bf16[16,8192]{1,0:T(8,128)(2,1)S(1)} collective-permute-done((bf16[16,8192]{1,0:T(8,128)(2,1)S(1)}, bf16[16,8192]{1,0:T(8,128)(2,1)S(1)}, u32[]{:S(2)}, u32[]{:S(2)}) %collective-permute-start.18) | collective-permute-done | bytes 262176 | tf_op jit(solution)/shard_map/ppermute | solution.py:21
  119.0 2.1 %collective-permute-start.21 = (bf16[208,768]{1,0:T(8,128)(2,1)S(1)}, bf16[208,768]{1,0:T(8,128)(2,1)S(1)}, u32[]{:S(2)}, u32[]{:S(2)}) collective-permute-start(bf16[208,768]{1,0:T(8,128)(2,1)S(1)} %slice_select_fusion.8), channel_id=1, source_target_pairs={{12,0},{0,4},{4,8},{8,12},{13,1},{1,5},{5,9},{9,13},{14,2},{2,6},{... | collective-permute-start | bytes 958472 | tf_op jit(solution)/shard_map/ppermute | solution.py:21
  121.1 8.9 %shard_map.49 = bf16[640,224]{1,0:T(8,128)(2,1)S(1)} custom-call(bf16[320,8192]{1,0:T(8,128)(2,1)} %refs_0_.5, bf16[320,8192]{1,0:T(8,128)(2,1)} %collective-permute-done.4.refs_0_.refs_1_, bf16[32,8192]{1,0:T(8,128)(2,1)S(1)} %collective-permute-done.2.refs_2_, bf16[32,8192]{1,0:T(8,128)(2,1)S(1)} %collective-permute-done.11.refs_3_, ...), custom_call_target="tpu_custom_call" | custom-call | flops 1 | bytes 1 | tf_op jit(solution)/shard_map/pallas_call | solution.py:46
  133.9 3.3 %collective-permute-done.20 = bf16[640,224]{1,0:T(8,128)(2,1)S(1)} collective-permute-done((bf16[640,224]{1,0:T(8,128)(2,1)S(1)}, bf16[640,224]{1,0:T(8,128)(2,1)S(1)}, u32[]{:S(2)}, u32[]{:S(2)}) %collective-permute-start.20) | collective-permute-done | bytes 286752 | tf_op jit(solution)/shard_map/ppermute | solution.py:21
  139.2 6.2 %shard_map.50.refs_12_ = bf16[320,8192]{1,0:T(8,128)(2,1)} custom-call(s32[1]{0:T(128)} %bitcast.side_ref, bf16[320,208]{1,0:T(8,128)(2,1)S(1)} %fusion.1.refs_0_, bf16[320,208]{1,0:T(8,128)(2,1)S(1)} %collective-permute-done.12.refs_1_, bf16[320,208]{1,0:T(8,128)(2,1)S(1)} %get-tuple-element.110.refs_2_, ...), custom_call_target="tpu_custom_call" | custom-call | flops 1 | bytes 1 | tf_op jit(solution)/shard_map/pallas_call | solution.py:46
  150.5 6.1 %shard_map.51.refs_14_ = bf16[320,8192]{1,0:T(8,128)(2,1)} custom-call(s32[1]{0:T(128)} %bitcast.side_ref, bf16[320,208]{1,0:T(8,128)(2,1)S(1)} %fusion.1.refs_0_, bf16[320,208]{1,0:T(8,128)(2,1)S(1)} %collective-permute-done.12.refs_1_, bf16[320,208]{1,0:T(8,128)(2,1)S(1)} %get-tuple-element.110.refs_2_, ...), custom_call_target="tpu_custom_call", output_to_operand_aliasing={{}: (13, {})} | custom-call | flops 1 | bytes 1 | tf_op jit(solution)/shard_map/pallas_call | solution.py:46
  160.6 7.4 %shard_map.52 = bf16[320,8192]{1,0:T(8,128)(2,1)} custom-call(s32[1]{0:T(128)} %bitcast.side_ref, bf16[320,208]{1,0:T(8,128)(2,1)S(1)} %fusion.1.refs_0_, bf16[320,208]{1,0:T(8,128)(2,1)S(1)} %collective-permute-done.12.refs_1_, bf16[320,208]{1,0:T(8,128)(2,1)S(1)} %get-tuple-element.110.refs_2_, ...), custom_call_target="tpu_custom_call", output_to_operand_aliasing={{}: (15, {})} | custom-call | flops 1 | bytes 1 | tf_op jit(solution)/shard_map/pallas_call | solution.py:46
  (102 shorter events, 39.2 us)
Async XLA Ops:
  1.3 40.2 %collective-permute-start.4 = (bf16[320,8192]{1,0:T(8,128)(2,1)}, bf16[320,8192]{1,0:T(8,128)(2,1)}, u32[]{:S(2)}, u32[]{:S(2)}) collective-permute-start(bf16[320,8192]{1,0:T(8,128)(2,1)} %refs_0_.5), channel_id=1, source_target_pairs={{1,0},{0,1},{3,2},{2,3},{5,4},{4,5},{7,6},{6,7},{9,8},{8,9},{11,10... | collective-permute-start | bytes 15728648 | tf_op jit(solution)/shard_map/ppermute | solution.py:21
  1.8 18.0 %collective-permute-start.1 = (bf16[32,8192]{1,0:T(8,128)(2,1)S(1)}, bf16[32,8192]{1,0:T(8,128)(2,1)S(1)}, u32[]{:S(2)}, u32[]{:S(2)}) collective-permute-start(bf16[32,8192]{1,0:T(8,128)(2,1)S(1)} %slice_select_fusion.7), channel_id=1, source_target_pairs={{12,0},{0,4},{4,8},{8,12},{13,1},{1,5},{5,9},{9,13},{14,2},{2,6},{... | collective-permute-start | bytes 1572872 | tf_op jit(solution)/shard_map/ppermute | solution.py:21
  5.7 24.8 %collective-permute-start.5 = (bf16[32,8192]{1,0:T(8,128)(2,1)S(1)}, bf16[32,8192]{1,0:T(8,128)(2,1)S(1)}, u32[]{:S(2)}, u32[]{:S(2)}) collective-permute-start(bf16[32,8192]{1,0:T(8,128)(2,1)S(1)} %slice_select_fusion.6), channel_id=1, source_target_pairs={{12,0},{0,4},{4,8},{8,12},{13,1},{1,5},{5,9},{9,13},{14,2},{2,6},{... | collective-permute-start | bytes 1572872 | tf_op jit(solution)/shard_map/ppermute | solution.py:21
  10.5 30.9 %collective-permute-start.3 = (bf16[32,8192]{1,0:T(8,128)(2,1)S(1)}, bf16[32,8192]{1,0:T(8,128)(2,1)S(1)}, u32[]{:S(2)}, u32[]{:S(2)}) collective-permute-start(bf16[32,8192]{1,0:T(8,128)(2,1)S(1)} %get-tuple-element.101), channel_id=1, source_target_pairs={{12,0},{0,4},{4,8},{8,12},{13,1},{1,5},{5,9},{9,13},{14,2},{2,6},{... | collective-permute-start | bytes 1572872 | tf_op jit(solution)/shard_map/ppermute | solution.py:21
  18.2 32.4 %collective-permute-start = (bf16[320,416]{1,0:T(8,128)(2,1)S(1)}, bf16[320,416]{1,0:T(8,128)(2,1)S(1)}, u32[]{:S(2)}, u32[]{:S(2)}) collective-permute-start(bf16[320,416]{1,0:T(8,128)(2,1)S(1)} %shard_map.46), channel_id=1, source_target_pairs={{2,0},{0,2},{3,1},{1,3},{6,4},{4,6},{7,5},{5,7},{10,8},{8,10},{11,... | collective-permute-start | bytes 798728 | tf_op jit(solution)/shard_map/ppermute | solution.py:21
  19.8 111.8 %collective-permute-start.24 = (bf16[208,8192]{1,0:T(8,128)(2,1)S(1)}, bf16[208,8192]{1,0:T(8,128)(2,1)S(1)}, u32[]{:S(2)}, u32[]{:S(2)}) collective-permute-start(bf16[208,8192]{1,0:T(8,128)(2,1)S(1)} %copy-done), channel_id=1, source_target_pairs={{1,0},{0,1},{3,2},{2,3},{5,4},{4,5},{7,6},{6,7},{9,8},{8,9},{11,10... | collective-permute-start | bytes 10223624 | tf_op jit(solution)/shard_map/ppermute | solution.py:21
  30.5 29.1 %collective-permute-start.6 = (bf16[32,8192]{1,0:T(8,128)(2,1)S(1)}, bf16[32,8192]{1,0:T(8,128)(2,1)}, u32[]{:S(2)}, u32[]{:S(2)}) collective-permute-start(bf16[32,8192]{1,0:T(8,128)(2,1)S(1)} %collective-permute-done.1.refs_2_), channel_id=1, source_target_pairs={{16,0},{0,16},{17,1},{1,17},{18,2},{2,18},{19,3},{3,19},{20,4},{4,... | collective-permute-start | bytes 1572872 | tf_op jit(solution)/shard_map/ppermute | solution.py:21
  41.4 16.6 %collective-permute-start.2 = (bf16[32,8192]{1,0:T(8,128)(2,1)S(1)}, bf16[32,8192]{1,0:T(8,128)(2,1)S(1)}, u32[]{:S(2)}, u32[]{:S(2)}) collective-permute-start(bf16[32,8192]{1,0:T(8,128)(2,1)S(1)} %get-tuple-element.57), channel_id=1, source_target_pairs={{12,0},{0,4},{4,8},{8,12},{13,1},{1,5},{5,9},{9,13},{14,2},{2,6},{... | collective-permute-start | bytes 1572872 | tf_op jit(solution)/shard_map/ppermute | solution.py:21
  41.4 27.8 %collective-permute-start.11 = (bf16[32,8192]{1,0:T(8,128)(2,1)S(1)}, bf16[32,8192]{1,0:T(8,128)(2,1)S(1)}, u32[]{:S(2)}, u32[]{:S(2)}) collective-permute-start(bf16[32,8192]{1,0:T(8,128)(2,1)S(1)} %get-tuple-element.65), channel_id=1, source_target_pairs={{12,0},{0,4},{4,8},{8,12},{13,1},{1,5},{5,9},{9,13},{14,2},{2,6},{... | collective-permute-start | bytes 1572872 | tf_op jit(solution)/shard_map/ppermute | solution.py:21
  50.7 20.2 %collective-permute-start.9 = (bf16[32,8192]{1,0:T(8,128)(2,1)S(1)}, bf16[32,8192]{1,0:T(8,128)(2,1)S(1)}, u32[]{:S(2)}, u32[]{:S(2)}) collective-permute-start(bf16[32,8192]{1,0:T(8,128)(2,1)S(1)} %collective-permute-done.5.refs_3_), channel_id=1, source_target_pairs={{16,0},{0,16},{17,1},{1,17},{18,2},{2,18},{19,3},{3,19},{20,4},{4,... | collective-permute-start | bytes 1572872 | tf_op jit(solution)/shard_map/ppermute | solution.py:21
  58.0 18.8 %collective-permute-start.10 = (bf16[32,8192]{1,0:T(8,128)(2,1)S(1)}, bf16[32,8192]{1,0:T(8,128)(2,1)S(1)}, u32[]{:S(2)}, u32[]{:S(2)}) collective-permute-start(bf16[32,8192]{1,0:T(8,128)(2,1)S(1)} %collective-permute-done.3.refs_4_), channel_id=1, source_target_pairs={{16,0},{0,16},{17,1},{1,17},{18,2},{2,18},{19,3},{3,19},{20,4},{4,... | collective-permute-start | bytes 1572872 | tf_op jit(solution)/shard_map/ppermute | solution.py:21
  59.6 27.7 %collective-permute-start.8 = (bf16[32,8192]{1,0:T(8,128)(2,1)}, bf16[32,8192]{1,0:T(8,128)(2,1)S(1)}, u32[]{:S(2)}, u32[]{:S(2)}) collective-permute-start(bf16[32,8192]{1,0:T(8,128)(2,1)} %get-tuple-element.64), channel_id=1, source_target_pairs={{12,0},{0,4},{4,8},{8,12},{13,1},{1,5},{5,9},{9,13},{14,2},{2,6},{... | collective-permute-start | bytes 1572872 | tf_op jit(solution)/shard_map/ppermute | solution.py:21
  69.3 19.6 %collective-permute-start.7 = (bf16[320,416]{1,0:T(8,128)(2,1)S(1)}, bf16[320,416]{1,0:T(8,128)(2,1)}, u32[]{:S(2)}, u32[]{:S(2)}) collective-permute-start(bf16[320,416]{1,0:T(8,128)(2,1)S(1)} %shard_map.47), channel_id=1, source_target_pairs={{2,0},{0,2},{3,1},{1,3},{6,4},{4,6},{7,5},{5,7},{10,8},{8,10},{11,... | collective-permute-start | bytes 798728 | tf_op jit(solution)/shard_map/ppermute | solution.py:21
  70.9 22.8 %collective-permute-start.15 = (bf16[32,8192]{1,0:T(8,128)(2,1)S(1)}, bf16[32,8192]{1,0:T(8,128)(2,1)}, u32[]{:S(2)}, u32[]{:S(2)}) collective-permute-start(bf16[32,8192]{1,0:T(8,128)(2,1)S(1)} %collective-permute-done.2.refs_2_), channel_id=1, source_target_pairs={{16,0},{0,16},{17,1},{1,17},{18,2},{2,18},{19,3},{3,19},{20,4},{4,... | collective-permute-start | bytes 1572872 | tf_op jit(solution)/shard_map/ppermute | solution.py:21
  76.8 14.6 %collective-permute-start.14 = (bf16[16,8192]{1,0:T(8,128)(2,1)}, bf16[16,8192]{1,0:T(8,128)(2,1)S(1)}, u32[]{:S(2)}, u32[]{:S(2)}) collective-permute-start(bf16[16,8192]{1,0:T(8,128)(2,1)} %slice_select_fusion.9), channel_id=1, source_target_pairs={{12,0},{0,4},{4,8},{8,12},{13,1},{1,5},{5,9},{9,13},{14,2},{2,6},{... | collective-permute-start | bytes 786440 | tf_op jit(solution)/shard_map/ppermute | solution.py:21
  87.3 14.9 %collective-permute-start.16 = (bf16[32,8192]{1,0:T(8,128)(2,1)S(1)}, bf16[32,8192]{1,0:T(8,128)(2,1)S(1)}, u32[]{:S(2)}, u32[]{:S(2)}) collective-permute-start(bf16[32,8192]{1,0:T(8,128)(2,1)S(1)} %collective-permute-done.11.refs_3_), channel_id=1, source_target_pairs={{16,0},{0,16},{17,1},{1,17},{18,2},{2,18},{19,3},{3,19},{20,4},{4,... | collective-permute-start | bytes 1572872 | tf_op jit(solution)/shard_map/ppermute | solution.py:21
  91.4 11.8 %collective-permute-start.19 = (bf16[208,1280]{1,0:T(8,128)(2,1)}, bf16[208,1280]{1,0:T(8,128)(2,1)S(1)}, u32[]{:S(2)}, u32[]{:S(2)}) collective-permute-start(bf16[208,1280]{1,0:T(8,128)(2,1)} %get-tuple-element.79), channel_id=1, source_target_pairs={{12,0},{0,4},{4,8},{8,12},{13,1},{1,5},{5,9},{9,13},{14,2},{2,6},{... | collective-permute-start | bytes 1597448 | tf_op jit(solution)/shard_map/ppermute | solution.py:21
  93.7 27.4 %collective-permute-start.17 = (bf16[32,8192]{1,0:T(8,128)(2,1)}, bf16[32,8192]{1,0:T(8,128)(2,1)}, u32[]{:S(2)}, u32[]{:S(2)}) collective-permute-start(bf16[32,8192]{1,0:T(8,128)(2,1)} %copy-done.7), channel_id=1, source_target_pairs={{16,0},{0,16},{17,1},{1,17},{18,2},{2,18},{19,3},{3,19},{20,4},{4,... | collective-permute-start | bytes 1572872 | tf_op jit(solution)/shard_map/ppermute | solution.py:21
  95.9 23.1 %collective-permute-start.18 = (bf16[16,8192]{1,0:T(8,128)(2,1)S(1)}, bf16[16,8192]{1,0:T(8,128)(2,1)S(1)}, u32[]{:S(2)}, u32[]{:S(2)}) collective-permute-start(bf16[16,8192]{1,0:T(8,128)(2,1)S(1)} %collective-permute-done.14.refs_5_), channel_id=1, source_target_pairs={{16,0},{0,16},{17,1},{1,17},{18,2},{2,18},{19,3},{3,19},{20,4},{4,... | collective-permute-start | bytes 786440 | tf_op jit(solution)/shard_map/ppermute | solution.py:21
  103.2 28.5 %collective-permute-start.23 = (bf16[208,1280]{1,0:T(8,128)(2,1)}, bf16[208,1280]{1,0:T(8,128)(2,1)}, u32[]{:S(2)}, u32[]{:S(2)}) collective-permute-start(bf16[208,1280]{1,0:T(8,128)(2,1)} %get-tuple-element.90), channel_id=1, source_target_pairs={{12,0},{0,4},{4,8},{8,12},{13,1},{1,5},{5,9},{9,13},{14,2},{2,6},{... | collective-permute-start | bytes 1597448 | tf_op jit(solution)/shard_map/ppermute | solution.py:21
  104.5 28.7 %collective-permute-start.22 = (bf16[208,1280]{1,0:T(8,128)(2,1)S(1)}, bf16[208,1280]{1,0:T(8,128)(2,1)S(1)}, u32[]{:S(2)}, u32[]{:S(2)}) collective-permute-start(bf16[208,1280]{1,0:T(8,128)(2,1)S(1)} %collective-permute-done.19.refs_6_), channel_id=1, source_target_pairs={{16,0},{0,16},{17,1},{1,17},{18,2},{2,18},{19,3},{3,19},{20,4},{4,... | collective-permute-start | bytes 1597448 | tf_op jit(solution)/shard_map/ppermute | solution.py:21
  119.0 14.2 %collective-permute-start.21 = (bf16[208,768]{1,0:T(8,128)(2,1)S(1)}, bf16[208,768]{1,0:T(8,128)(2,1)S(1)}, u32[]{:S(2)}, u32[]{:S(2)}) collective-permute-start(bf16[208,768]{1,0:T(8,128)(2,1)S(1)} %slice_select_fusion.8), channel_id=1, source_target_pairs={{12,0},{0,4},{4,8},{8,12},{13,1},{1,5},{5,9},{9,13},{14,2},{2,6},{... | collective-permute-start | bytes 958472 | tf_op jit(solution)/shard_map/ppermute | solution.py:21
  131.7 14.8 %collective-permute-start.28 = (bf16[208,1280]{1,0:T(8,128)(2,1)}, bf16[208,1280]{1,0:T(8,128)(2,1)}, u32[]{:S(2)}, u32[]{:S(2)}) collective-permute-start(bf16[208,1280]{1,0:T(8,128)(2,1)} %collective-permute-done.23.refs_6_), channel_id=1, source_target_pairs={{16,0},{0,16},{17,1},{1,17},{18,2},{2,18},{19,3},{3,19},{20,4},{4,... | collective-permute-start | bytes 1597448 | tf_op jit(solution)/shard_map/ppermute | solution.py:21
  137.8 18.9 %collective-permute-start.27 = (bf16[208,1536]{1,0:T(8,128)(2,1)S(1)}, bf16[208,1536]{1,0:T(8,128)(2,1)S(1)}, u32[]{:S(2)}, u32[]{:S(2)}) collective-permute-start(bf16[208,1536]{1,0:T(8,128)(2,1)S(1)} %slice.147), channel_id=1, source_target_pairs={{12,0},{0,4},{4,8},{8,12},{13,1},{1,5},{5,9},{9,13},{14,2},{2,6},{... | collective-permute-start | bytes 1916936 | tf_op jit(solution)/shard_map/ppermute | solution.py:21
  (26 other events, 153.3 us)

commit v7 on v6

v7 whole, which is shorter than its diff:
```python
import functools

import jax
import jax.numpy as jnp
from jax import lax
from jax.experimental import pallas as pl
from jax.experimental.pallas import tpu as pltpu
from jax.sharding import PartitionSpec as P

FEATURE_SHARES = (11, 11, 11, 11, 10, 10)
LANE_SHARES = (10, 10, 6, 6)
QUEUE = 2
VMEM = 16 * 1024 * 1024
ANY = pl.BlockSpec(memory_space=pl.ANY)


def shifted(block, axis, distance):
    devices = range(lax.axis_size(axis))
    route = [((i - distance) % len(devices), i) for i in devices]
    return lax.ppermute(block, axis, route)


def mate(block):
    return shifted(block, "sub", 1)


def across(block):
    return shifted(block, "groups", 1)


def tied(value, *earlier):
    return lax.optimization_barrier((value, *earlier))[0] if earlier else value


def cuts(total, unit, shares):
    units, whole, done, marks = total // unit, sum(shares), 0, [0]
    for share in shares:
        done += share
        marks.append(units * done // whole * unit)
    marks[-1] = total
    return list(zip(marks[:-1], marks[1:]))


def call(kernel, operands, in_specs, out, out_spec, scratch, aliases):
    return pl.pallas_call(
        kernel,
        in_specs=in_specs,
        out_specs=out_spec,
        out_shape=out,
        scratch_shapes=scratch,
        input_output_aliases=aliases,
        compiler_params=pltpu.CompilerParams(vmem_limit_bytes=VMEM),
        cost_estimate=pl.CostEstimate(flops=1, bytes_accessed=1, transcendentals=0),
    )(*operands)


def products_kernel(sets, groups, spans, before, *refs):
    row_refs, unit_refs, total = refs[:sets], refs[sets : sets + groups * len(spans)], refs[-1]
    out = refs[-2]
    for step, (a, b) in enumerate(spans):
        units = jnp.concatenate(
            [ref[:, : b - a] for ref in unit_refs[step * groups : (step + 1) * groups]], axis=0
        )
        at = 0
        for ref in row_refs:
            spot = slice(at, at + ref.shape[0])
            at += ref.shape[0]
            value = lax.dot_general(
                ref[:, a:b], units, (((1,), (1,)), ((), ())), preferred_element_type=jnp.float32
            )
            if step > 0:
                value += total[spot]
            elif before:
                value += refs[-3][spot]
            if step < len(spans) - 1:
                total[spot] = value
            else:
                out[spot] = value.astype(out.dtype)


def products(row_sets, unit_sets, spans, before=None, out_type=jnp.bfloat16):
    groups = len(unit_sets) // len(spans)
    shape = (
        sum(r.shape[0] for r in row_sets),
        sum(u.shape[0] for u in unit_sets[:groups]),
    )
    operands = (*row_sets, *unit_sets)
    if before is not None:
        operands += (before,)
    whole = pl.BlockSpec(memory_space=pltpu.VMEM)
    return call(
        functools.partial(
            products_kernel, len(row_sets), groups, tuple(spans), before is not None
        ),
        operands,
        [whole] * len(operands),
        jax.ShapeDtypeStruct(shape, out_type),
        whole,
        [pltpu.VMEM(shape, jnp.float32)],
        {},
    )


def blocks_of(parts):
    found = []
    for i, (a, half, own, other) in enumerate(parts):
        arrays = [(0, lanes) for lanes in own] + [(1, lanes) for lanes in other]
        filled = [0, 0]
        for n, (k, lanes) in enumerate(arrays):
            for lane in range(0, lanes, 512):
                size = min(512, lanes - lane)
                turn = half - 2 * k * half if other else 0
                found.append((i, n, lane, size, (a + k * half + filled[k] + lane, turn)))
            filled[k] += lanes
    return found


def output_kernel(parts, side_ref, *refs):
    hidden, down = refs[:4], refs[4]
    arrived, at = [], 5
    for _, _, own, other in parts:
        count = len(own) + len(other)
        arrived.append((refs[at : at + count], refs[at + count : at + 2 * count]))
        at += 2 * count
    out, result, sems = refs[-3:]
    side, core = side_ref[0], side_ref[1]
    share = down.shape[0] // 2
    shares = [pl.ds(pl.multiple_of(c * share, 16), share) for c in (core, 1 - core)]
    stores, at = [], 0
    for n, (i, array, lane, size, (fixed, turn)) in enumerate(blocks_of(parts)):
        column = pl.ds(pl.multiple_of(fixed + side * turn, 128), size)
        spot = pl.ds(at, size)
        at += size
        total = None
        for m in range(4):
            if m < 2:
                weight = down[shares[m], column]
            else:
                weight = arrived[i][m - 2][array][:, lane : lane + size]
            term = jnp.dot(hidden[m][...], weight, preferred_element_type=jnp.float32)
            total = term if total is None else total + term
        result[:, spot] = total.astype(result.dtype)
        stores.append(
            pltpu.make_async_copy(result.at[:, spot], out.at[:, column], sems.at[n])
        )
        stores[-1].start()
    for copy in stores:
        copy.wait()


def output_part(result, parts, side, hidden, down, arrived):
    rows, width = hidden[0].shape[0], down.shape[1]
    lanes = sum(sum(own) + sum(other) for _, _, own, other in parts)
    operands = [side, *hidden, down, *arrived]
    in_specs = (
        [pl.BlockSpec(memory_space=pltpu.SMEM)]
        + [pl.BlockSpec(memory_space=pltpu.VMEM)] * (5 + len(arrived))
    )
    aliases = {}
    if result is not None:
        aliases = {len(operands): 0}
        operands.append(result)
        in_specs.append(ANY)
    return call(
        functools.partial(output_kernel, parts),
        operands,
        in_specs,
        jax.ShapeDtypeStruct((rows, width), jnp.bfloat16),
        ANY,
        [
            pltpu.VMEM((rows, lanes), jnp.bfloat16),
            pltpu.SemaphoreType.DMA((len(blocks_of(parts)),)),
        ],
        aliases,
    )


def over_slices(partial_value):
    return [
        shifted(partial_value, "tensor", distance)
        for distance in range(1, lax.axis_size("tensor"))
    ]


def summed(partial_value, sent):
    total = partial_value.astype(jnp.float32)
    for block in sent:
        total = total + block.astype(jnp.float32)
    return total


def gated(gate, up):
    return (jax.nn.silu(gate) * up).astype(jnp.bfloat16)


def on_device(tokens, gate_weight, up_weight, down_weight):
    units, width = gate_weight.shape
    rows = tokens.shape[0]
    group = lax.axis_index("groups").astype(jnp.int32)
    first = group == 0
    side = jnp.stack([group, lax.axis_index("sub").astype(jnp.int32)])

    spans = cuts(width, 128, FEATURE_SHARES)
    lane_cuts = [(2 * a, 2 * b) for a, b in cuts(width // 2, 128, LANE_SHARES)]
    count = len(spans)
    total_count = count + len(lane_cuts)
    last = total_count - 1

    def piece(i, *after):
        if i < count:
            a, b = spans[i]
            gate, up = gate_weight, up_weight
            if after:
                gate, up = lax.optimization_barrier((gate, up, *after))[:2]
            return jnp.where(first, gate[:, a:b], up[:, a:b])
        a, b = lane_cuts[i - count]
        mid = (a + b) // 2
        down = tied(down_weight, *after)
        if i == last:
            return down[:, a:b]
        return jnp.where(first, down[:, a:mid], down[:, mid:b])

    pieces = [piece(0)]
    pieces.append(piece(1, pieces[0]))
    pieces += [piece(i, pieces[1]) for i in range(2, total_count)]
    waiting = [shifted(pieces[i], "dp", 1) for i in range(QUEUE)]
    landed, crossed, mates, crossed_mates = [], {}, {}, {}

    def advance(*after):
        i = len(landed)
        held = [*after, *landed[-1:]]
        held += [crossed[j] for j in range(count) if j + 2 == i]
        block = tied(waiting[i], *held)
        landed.append(block)
        if i < last:
            crossed[i] = across(block)
        if i >= count:
            mates[i] = mate(block)
        if i + QUEUE < total_count:
            waiting.append(shifted(tied(pieces[i + QUEUE], block), "dp", 1))
        return block

    def pass_on(n, *after):
        i = count + n
        crossed[i] = tied(crossed[i], *after)
        crossed_mates[i] = mate(crossed[i])
        return crossed[i]

    def local(partial_value, sent):
        pre = summed(partial_value, sent)
        return gated(pre[:, :units], pre[:, units:])

    def batch(lo, hi, now, before=None, out_type=jnp.float32):
        held = [block for i in range(lo, hi) for block in (landed[i], crossed[i])]
        held = lax.optimization_barrier((*held, now))[:-1]
        return products([tokens, tokens_mate], held, spans[lo:hi], before, out_type)

    def activated(partial_value, sent):
        pre = summed(partial_value, sent)
        half = pre.shape[1] // 2
        left, right = pre[:, :half], pre[:, half:]
        return gated(jnp.where(first, left, right), jnp.where(first, right, left))

    tokens_mate = mate(tied(tokens, pieces[0]))
    down_here = lax.all_gather(tied(down_weight, pieces[1]), "sub", axis=0, tiled=True)

    def own_span(rows):
        return products([rows], [gate_weight, up_weight], [(0, width)])

    mine = own_span(tokens)
    now = advance(mine, *pieces[2:])
    theirs = own_span(tied(tokens_mate, now))
    value = jnp.concatenate([mine, theirs], axis=0)
    now = advance(value)
    sent = over_slices(value)
    now = advance()
    now = advance()
    here = local(value, [tied(block, now) for block in sent])
    here_mate = mate(here[rows:])
    here = here[:rows]
    value = batch(0, 2, now)
    now = advance(value, here)
    now = advance(here_mate)
    value = batch(2, 4, now, value)
    now = advance(value)
    value = batch(4, count, now, value, jnp.bfloat16)
    halves = [value[:rows], value[rows:]]
    sent = [over_slices(half) for half in halves]
    now = advance(value)
    now = pass_on(0, now)
    now = advance(now)
    there, given = (
        activated(half, [tied(block, now) for block in blocks])
        for half, blocks in zip(halves, sent)
    )
    there_mate = mate(given)

    def write(result, *which):
        parts, arrived = [], []
        for n in which:
            i = count + n
            a, b = lane_cuts[n]
            if i == last:
                parts.append((a, (b - a) // 2, (b - a,), ()))
                arrived += [landed[i], mates[i]]
            else:
                half = (b - a) // 2
                parts.append((a, half, (half,), (half,)))
                arrived += [landed[i], crossed[i], mates[i], crossed_mates[i]]
        return output_part(
            result,
            tuple(parts),
            side,
            [here, here_mate, there, there_mate],
            down_here,
            arrived,
        )

    result = write(None, 0)
    pass_on(1, result)
    result = write(result, 1)
    now = advance(result)
    result = write(result, 3)
    pass_on(2, now)
    return write(result, 2)


def solution(mesh):
    return jax.shard_map(
        on_device,
        mesh=mesh,
        in_specs=(
            P(("groups", "dp", "sub"), "tensor"),
            P(("dp", "sub"), "tensor"),
            P(("dp", "sub"), "tensor"),
            P(("dp", "sub"), "tensor"),
        ),
        out_specs=P(("groups", "dp", "sub"), "tensor"),
        check_vma=False,
    )
```

time: 169 us -> 161 us (0.953)
  Pallas kernels: 49.5 us -> 35.5 us
  between operations: 0.55 us -> 13.7 us
  starting transfers between devices: 38.1 us -> 25.4 us
  local copies, waits for them, and re-layouts: 2.87 us -> 15.1 us
  waiting for transfers between devices: 66.4 us -> 55.5 us
  other arithmetic: 10.7 us -> 15.3 us
    pallas_call x7 -> x9, Pallas kernels: 49.5 us -> 35.5 us  [call(): pl.pallas_call(kernel, in_specs=in_specs, out_specs=out_spec, out_shape=o...]
    ppermute x39 -> x32, starting transfers between devices: 38.1 us -> 25.4 us  [shifted(): return lax.ppermute(block, axis, route)]
    ppermute x39 -> x32, waiting for transfers between devices: 66.4 us -> 55.5 us  [shifted(): return lax.ppermute(block, axis, route)]
    unnamed x22 -> x26, local copies, waits for them, and re-layouts: 1.67 us -> 9.14 us
    concatenate x0 -> x1, local copies, waits for them, and re-layouts: none -> 2.13 us  [on_device(): value = jnp.concatenate([mine, theirs], axis=0)]
    optimization_barrier x0 -> x1, local copies, waits for them, and re-layouts: none -> 2.12 us  [tied(): return lax.optimization_barrier((value, *earlier))[0] if earlier else value]
    select_n x2, other arithmetic: 1.13 us -> 3.05 us  [piece(): return jnp.where(first, down[:, a:mid], down[:, mid:b])]
  transfers between devices with their start and end apart: 39 -> 33, of which waited for: 16 -> 12; matrix products, arithmetic and copies ran while one was open for 6% -> 12% of each run, Pallas kernels for 25% -> 20%
where the time goes in v7:
time: 161 us
  waiting for transfers between devices  55.5 us (34%)
  Pallas kernels  35.5 us (22%)
  starting transfers between devices  25.4 us (16%)
  other arithmetic  15.3 us (10%)
  local copies, waits for them, and re-layouts  15.1 us (9%)
  between operations  13.7 us (9%)
    ppermute x32, waiting for transfers between devices, shifted(): return lax.ppermute(block, axis, route)  55.5 us
    pallas_call x9, Pallas kernels, call(): pl.pallas_call(kernel, in_specs=in_specs, out_specs=out_spec, out_shape=o...  35.5 us
    ppermute x32, starting transfers between devices, shifted(): return lax.ppermute(block, axis, route)  25.4 us
    unnamed x26, local copies, waits for them, and re-layouts  9.14 us
    select_n x4, other arithmetic, piece(): return jnp.where(first, gate[:, a:b], up[:, a:b])  8.14 us
  transfers between devices with their start and end apart: 33, of which 12 were waited for; matrix products, arithmetic and copies ran while one was open for 12% of the time, Pallas kernels for 20%

profile of v7, /device:TPU:0, one launch (start us, length us, event | category | flops | bytes accessed | tf_op | source)
XLA Modules:
  0.0 160.7 jit_solution(12918093610351103508)
XLA Ops:
  9.7 2.6 %collective-permute-start.1 = (bf16[208,1408]{1,0:T(8,128)(2,1)S(1)}, bf16[208,1408]{1,0:T(8,128)(2,1)S(1)}, u32[]{:S(2)}, u32[]{:S(2)}) collective-permute-start(bf16[208,1408]{1,0:T(8,128)(2,1)S(1)} %slice_select_fusion.3), channel_id=1, source_target_pairs={{12,0},{0,4},{4,8},{8,12},{13,1},{1,5},{5,9},{9,13},{14,2},{2,6},{... | collective-permute-start | bytes 1757192 | tf_op jit(solution)/shard_map/ppermute | solution.py:20
  14.0 2.7 %slice_select_fusion = (bf16[208,1408]{1,0:T(8,128)(2,1)}, bf16[208,1408]{1,0:T(8,128)(2,1)}) fusion(bf16[208,8192]{1,0:T(8,128)(2,1)} %refs_2_.3, bf16[208,8192]{1,0:T(8,128)(2,1)} %refs_1_.3, pred[]{:T(512)S(6)} %eq.3), kind=kLoop, calls=%fused_computation.6 | loop fusion | flops 585728 | bytes 3514369 | tf_op jit(solution)/shard_map/jit(_where)/select_n | solution.py:215
  16.7 2.8 %slice_select_fusion.6 = (bf16[208,1280]{1,0:T(8,128)(2,1)}, bf16[208,1280]{1,0:T(8,128)(2,1)}) fusion(bf16[208,8192]{1,0:T(8,128)(2,1)} %refs_2_.3, bf16[208,8192]{1,0:T(8,128)(2,1)} %refs_1_.3, pred[]{:T(512)S(6)} %eq.3), kind=kLoop, calls=%fused_computation.12 | loop fusion | flops 532480 | bytes 3194881 | tf_op jit(solution)/shard_map/jit(_where)/select_n | solution.py:215
  21.4 2.6 %copy-done.3 = bf16[208,8192]{1,0:T(8,128)(2,1)S(1)} copy-done((bf16[208,8192]{1,0:T(8,128)(2,1)S(1)}, bf16[208,8192]{1,0:T(8,128)(2,1)}, u32[]{:S(2)}) %copy-start.3) | copy-done | bytes 3407896
  24.0 2.9 %shard_map.46 = bf16[320,416]{1,0:T(8,128)(2,1)S(1)} custom-call(bf16[320,8192]{1,0:T(8,128)(2,1)S(1)} %bitcast.3, bf16[208,8192]{1,0:T(8,128)(2,1)S(1)} %copy-done.2, bf16[208,8192]{1,0:T(8,128)(2,1)S(1)} %copy-done.3), custom_call_target="tpu_custom_call" | custom-call | flops 1 | bytes 1 | tf_op jit(solution)/shard_map/pallas_call | solution.py:45
  32.0 5.4 %shard_map.47 = bf16[320,416]{1,0:T(8,128)(2,1)S(1)} custom-call(bf16[320,8192]{1,0:T(8,128)(2,1)} %collective-permute-done.refs_0_.refs_1_, bf16[208,8192]{1,0:T(8,128)(2,1)S(1)} %copy-done.2, bf16[208,8192]{1,0:T(8,128)(2,1)S(1)} %copy-done.4), custom_call_target="tpu_custom_call" | custom-call | flops 1 | bytes 1 | tf_op jit(solution)/shard_map/pallas_call | solution.py:45
  38.3 2.9 %collective-permute-done.3.refs_4_ = bf16[208,1408]{1,0:T(8,128)(2,1)} collective-permute-done((bf16[208,1408]{1,0:T(8,128)(2,1)S(1)}, bf16[208,1408]{1,0:T(8,128)(2,1)}, u32[]{:S(2)}, u32[]{:S(2)}) %collective-permute-start.3) | collective-permute-done | bytes 585760 | tf_op jit(solution)/shard_map/ppermute | solution.py:20
  46.4 7.2 %collective-permute-done.5.refs_2_ = bf16[208,1408]{1,0:T(8,128)(2,1)S(1)} collective-permute-done((bf16[208,1408]{1,0:T(8,128)(2,1)}, bf16[208,1408]{1,0:T(8,128)(2,1)S(1)}, u32[]{:S(2)}, u32[]{:S(2)}) %collective-permute-start.5) | collective-permute-done | bytes 585760 | tf_op jit(solution)/shard_map/ppermute | solution.py:20
  55.3 10.9 %collective-permute-done.4.refs_4_ = bf16[208,1408]{1,0:T(8,128)(2,1)S(1)} collective-permute-done((bf16[208,1408]{1,0:T(8,128)(2,1)}, bf16[208,1408]{1,0:T(8,128)(2,1)S(1)}, u32[]{:S(2)}, u32[]{:S(2)}) %collective-permute-start.4) | collective-permute-done | bytes 585760 | tf_op jit(solution)/shard_map/ppermute | solution.py:20
  71.7 2.5 %copy-done.1 = bf16[320,8192]{1,0:T(8,128)(2,1)S(1)} copy-done((bf16[320,8192]{1,0:T(8,128)(2,1)S(1)}, bf16[320,8192]{1,0:T(8,128)(2,1)}, u32[]{:S(2)}) %copy-start.1) | copy-done | bytes 5242904
  75.2 5.0 %shard_map.48.refs_6_ = f32[640,416]{1,0:T(8,128)S(1)} custom-call(bf16[320,8192]{1,0:T(8,128)(2,1)S(1)} %copy-done.1, bf16[320,8192]{1,0:T(8,128)(2,1)} %collective-permute-done.refs_0_.refs_1_, bf16[208,1408]{1,0:T(8,128)(2,1)S(1)} %copy-done.6, bf16[208,1408]{1,0:T(8,128)(2,1)S(1)} %copy-done.8, bf16[208,1408]{1,0:T(8,128)(2,1)} %collective-permute-done.3.refs_4_, ...), custom_call_target="tpu_custom_call" | custom-call | flops 1 | bytes 1 | tf_op jit(solution)/shard_map/pallas_call | solution.py:45
  82.2 6.8 %collective-permute-done.12.refs_4_ = bf16[208,1280]{1,0:T(8,128)(2,1)S(1)} collective-permute-done((bf16[208,1280]{1,0:T(8,128)(2,1)}, bf16[208,1280]{1,0:T(8,128)(2,1)S(1)}, u32[]{:S(2)}, u32[]{:S(2)}) %collective-permute-start.12) | collective-permute-done | bytes 532512 | tf_op jit(solution)/shard_map/ppermute | solution.py:20
  90.6 4.8 %shard_map.49.refs_6_ = f32[640,416]{1,0:T(8,128)S(1)} custom-call(bf16[320,8192]{1,0:T(8,128)(2,1)S(1)} %copy-done.1, bf16[320,8192]{1,0:T(8,128)(2,1)} %collective-permute-done.refs_0_.refs_1_, bf16[208,1408]{1,0:T(8,128)(2,1)S(1)} %collective-permute-done.5.refs_2_, bf16[208,1408]{1,0:T(8,128)(2,1)S(1)} %collective-permute-done.10.refs_3_, ...), custom_call_target="tpu_custom_call" | custom-call | flops 1 | bytes 1 | tf_op jit(solution)/shard_map/pallas_call | solution.py:45
  95.5 5.0 %collective-permute-done.15.refs_5_ = bf16[208,1280]{1,0:T(8,128)(2,1)} collective-permute-done((bf16[208,1280]{1,0:T(8,128)(2,1)S(1)}, bf16[208,1280]{1,0:T(8,128)(2,1)}, u32[]{:S(2)}, u32[]{:S(2)}) %collective-permute-start.15) | collective-permute-done | bytes 532512 | tf_op jit(solution)/shard_map/ppermute | solution.py:20
  102.2 6.0 %collective-permute-done.14.refs_5_ = bf16[208,1280]{1,0:T(8,128)(2,1)S(1)} collective-permute-done((bf16[208,1280]{1,0:T(8,128)(2,1)S(1)}, bf16[208,1280]{1,0:T(8,128)(2,1)S(1)}, u32[]{:S(2)}, u32[]{:S(2)}) %collective-permute-start.14) | collective-permute-done | bytes 532512 | tf_op jit(solution)/shard_map/ppermute | solution.py:20
  108.2 4.5 %shard_map.50 = bf16[640,416]{1,0:T(8,128)(2,1)S(1)} custom-call(bf16[320,8192]{1,0:T(8,128)(2,1)S(1)} %copy-done.1, bf16[320,8192]{1,0:T(8,128)(2,1)} %collective-permute-done.refs_0_.refs_1_, bf16[208,1280]{1,0:T(8,128)(2,1)} %collective-permute-done.9.refs_2_, bf16[208,1280]{1,0:T(8,128)(2,1)S(1)} %collective-permute-done.11.refs_3_, ...), custom_call_target="tpu_custom_call" | custom-call | flops 1 | bytes 1 | tf_op jit(solution)/shard_map/pallas_call | solution.py:45
  115.6 3.3 %collective-permute-done.18.refs_6_ = bf16[208,1280]{1,0:T(8,128)(2,1)S(1)} collective-permute-done((bf16[208,1280]{1,0:T(8,128)(2,1)}, bf16[208,1280]{1,0:T(8,128)(2,1)S(1)}, u32[]{:S(2)}, u32[]{:S(2)}) %collective-permute-start.18) | collective-permute-done | bytes 532512 | tf_op jit(solution)/shard_map/ppermute | solution.py:20
  119.4 4.8 %collective-permute-done.16 = bf16[320,416]{1,0:T(8,128)(2,1)} collective-permute-done((bf16[320,416]{1,0:T(8,128)(2,1)S(1)}, bf16[320,416]{1,0:T(8,128)(2,1)}, u32[]{:S(2)}, u32[]{:S(2)}) %collective-permute-start.16) | collective-permute-done | bytes 266272 | tf_op jit(solution)/shard_map/ppermute | solution.py:20
  125.8 3.2 %collective-permute-done.20 = bf16[320,416]{1,0:T(8,128)(2,1)} collective-permute-done((bf16[320,416]{1,0:T(8,128)(2,1)}, bf16[320,416]{1,0:T(8,128)(2,1)}, u32[]{:S(2)}, u32[]{:S(2)}) %collective-permute-start.20) | collective-permute-done | bytes 266272 | tf_op jit(solution)/shard_map/ppermute | solution.py:20
  131.9 2.9 %copy-done = bf16[416,8192]{1,0:T(8,128)(2,1)S(1)} copy-done((bf16[416,8192]{1,0:T(8,128)(2,1)S(1)}, bf16[416,8192]{1,0:T(8,128)(2,1)}, u32[]{:S(2)}) %copy-start) | copy-done | bytes 6815768
  134.8 3.9 %shard_map.51.refs_9_ = bf16[320,8192]{1,0:T(8,128)(2,1)} custom-call(s32[2]{0:T(128)S(1)} %pad_add_fusion.side_ref, bf16[320,208]{1,0:T(8,128)(2,1)S(1)} %get-tuple-element.102.refs_0_, bf16[320,208]{1,0:T(8,128)(2,1)S(1)} %collective-permute-done.8.refs_1_, bf16[320,208]{1,0:T(8,128)(2,1)S(1)} %multiply_convert_fusion.1.refs_2_, ...), custom_call_target="tpu_custom_call" | custom-call | flops 1 | bytes 1 | tf_op jit(solution)/shard_map/pallas_call | solution.py:45
  140.7 3.9 %shard_map.52.refs_7_ = bf16[320,8192]{1,0:T(8,128)(2,1)} custom-call(s32[2]{0:T(128)S(1)} %pad_add_fusion.side_ref, bf16[320,208]{1,0:T(8,128)(2,1)S(1)} %get-tuple-element.102.refs_0_, bf16[320,208]{1,0:T(8,128)(2,1)S(1)} %collective-permute-done.8.refs_1_, bf16[320,208]{1,0:T(8,128)(2,1)S(1)} %multiply_convert_fusion.1.refs_2_, ...), custom_call_target="tpu_custom_call", output_to_operand_aliasing={{}: (10, {})} | custom-call | flops 1 | bytes 1 | tf_op jit(solution)/shard_map/pallas_call | solution.py:45
  145.2 3.5 %collective-permute-done.22.refs_6_ = bf16[208,768]{1,0:T(8,128)(2,1)S(1)} collective-permute-done((bf16[208,768]{1,0:T(8,128)(2,1)S(1)}, bf16[208,768]{1,0:T(8,128)(2,1)S(1)}, u32[]{:S(2)}, u32[]{:S(2)}) %collective-permute-start.22) | collective-permute-done | bytes 319520 | tf_op jit(solution)/shard_map/ppermute | solution.py:20
  151.3 2.5 %shard_map.54 = bf16[320,8192]{1,0:T(8,128)(2,1)} custom-call(s32[2]{0:T(128)S(1)} %pad_add_fusion.side_ref, bf16[320,208]{1,0:T(8,128)(2,1)S(1)} %get-tuple-element.102.refs_0_, bf16[320,208]{1,0:T(8,128)(2,1)S(1)} %collective-permute-done.8.refs_1_, bf16[320,208]{1,0:T(8,128)(2,1)S(1)} %multiply_convert_fusion.1.refs_2_, ...), custom_call_target="tpu_custom_call", output_to_operand_aliasing={{}: (10, {})} | custom-call | flops 1 | bytes 1 | tf_op jit(solution)/shard_map/pallas_call | solution.py:45
  (97 shorter events, 44.1 us)
Async XLA Ops:
  6.5 124.7 %all-gather.2.cloned.1.call-start = ((), (), s32[]{:S(2)}) async-start(), calls=%async_computation | async-start | bytes 10223616 | tf_op jit(solution)/shard_map/all_gather | solution.py:265
  7.8 24.1 %collective-permute-start = (bf16[320,8192]{1,0:T(8,128)(2,1)}, bf16[320,8192]{1,0:T(8,128)(2,1)}, u32[]{:S(2)}, u32[]{:S(2)}) collective-permute-start(bf16[320,8192]{1,0:T(8,128)(2,1)} %refs_0_.7), channel_id=1, source_target_pairs={{1,0},{0,1},{3,2},{2,3},{5,4},{4,5},{7,6},{6,7},{9,8},{8,9},{11,10... | collective-permute-start | bytes 15728648 | tf_op jit(solution)/shard_map/ppermute | solution.py:20
  9.7 19.3 %collective-permute-start.1 = (bf16[208,1408]{1,0:T(8,128)(2,1)S(1)}, bf16[208,1408]{1,0:T(8,128)(2,1)S(1)}, u32[]{:S(2)}, u32[]{:S(2)}) collective-permute-start(bf16[208,1408]{1,0:T(8,128)(2,1)S(1)} %slice_select_fusion.3), channel_id=1, source_target_pairs={{12,0},{0,4},{4,8},{8,12},{13,1},{1,5},{5,9},{9,13},{14,2},{2,6},{... | collective-permute-start | bytes 1757192 | tf_op jit(solution)/shard_map/ppermute | solution.py:20
  12.4 28.8 %collective-permute-start.3 = (bf16[208,1408]{1,0:T(8,128)(2,1)S(1)}, bf16[208,1408]{1,0:T(8,128)(2,1)}, u32[]{:S(2)}, u32[]{:S(2)}) collective-permute-start(bf16[208,1408]{1,0:T(8,128)(2,1)S(1)} %slice_select_fusion.2), channel_id=1, source_target_pairs={{12,0},{0,4},{4,8},{8,12},{13,1},{1,5},{5,9},{9,13},{14,2},{2,6},{... | collective-permute-start | bytes 1757192 | tf_op jit(solution)/shard_map/ppermute | solution.py:20
  29.0 24.6 %collective-permute-start.6 = (bf16[208,1408]{1,0:T(8,128)(2,1)S(1)}, bf16[208,1408]{1,0:T(8,128)(2,1)S(1)}, u32[]{:S(2)}, u32[]{:S(2)}) collective-permute-start(bf16[208,1408]{1,0:T(8,128)(2,1)S(1)} %collective-permute-done.1.refs_2_), channel_id=1, source_target_pairs={{16,0},{0,16},{17,1},{1,17},{18,2},{2,18},{19,3},{3,19},{20,4},{4,... | collective-permute-start | bytes 1757192 | tf_op jit(solution)/shard_map/ppermute | solution.py:20
  30.4 23.3 %collective-permute-start.5 = (bf16[208,1408]{1,0:T(8,128)(2,1)}, bf16[208,1408]{1,0:T(8,128)(2,1)S(1)}, u32[]{:S(2)}, u32[]{:S(2)}) collective-permute-start(bf16[208,1408]{1,0:T(8,128)(2,1)} %get-tuple-element.58), channel_id=1, source_target_pairs={{12,0},{0,4},{4,8},{8,12},{13,1},{1,5},{5,9},{9,13},{14,2},{2,6},{... | collective-permute-start | bytes 1757192 | tf_op jit(solution)/shard_map/ppermute | solution.py:20
  41.2 25.0 %collective-permute-start.4 = (bf16[208,1408]{1,0:T(8,128)(2,1)}, bf16[208,1408]{1,0:T(8,128)(2,1)S(1)}, u32[]{:S(2)}, u32[]{:S(2)}) collective-permute-start(bf16[208,1408]{1,0:T(8,128)(2,1)} %get-tuple-element.57), channel_id=1, source_target_pairs={{12,0},{0,4},{4,8},{8,12},{13,1},{1,5},{5,9},{9,13},{14,2},{2,6},{... | collective-permute-start | bytes 1757192 | tf_op jit(solution)/shard_map/ppermute | solution.py:20
  41.2 25.0 %collective-permute-start.7 = (bf16[208,1408]{1,0:T(8,128)(2,1)}, bf16[208,1408]{1,0:T(8,128)(2,1)}, u32[]{:S(2)}, u32[]{:S(2)}) collective-permute-start(bf16[208,1408]{1,0:T(8,128)(2,1)} %collective-permute-done.3.refs_4_), channel_id=1, source_target_pairs={{16,0},{0,16},{17,1},{1,17},{18,2},{2,18},{19,3},{3,19},{20,4},{4,... | collective-permute-start | bytes 1757192 | tf_op jit(solution)/shard_map/ppermute | solution.py:20
  45.0 22.9 %collective-permute-start.2 = (bf16[640,416]{0,1:T(8,128)(2,1)}, bf16[640,416]{0,1:T(8,128)(2,1)}, u32[]{:S(2)}, u32[]{:S(2)}) collective-permute-start(bf16[640,416]{0,1:T(8,128)(2,1)} %copy.8), channel_id=1, source_target_pairs={{2,0},{0,2},{3,1},{1,3},{6,4},{4,6},{7,5},{5,7},{10,8},{8,10},{11,... | collective-permute-start | bytes 1597448 | tf_op jit(solution)/shard_map/ppermute | solution.py:20
  53.6 26.7 %collective-permute-start.10 = (bf16[208,1408]{1,0:T(8,128)(2,1)S(1)}, bf16[208,1408]{1,0:T(8,128)(2,1)S(1)}, u32[]{:S(2)}, u32[]{:S(2)}) collective-permute-start(bf16[208,1408]{1,0:T(8,128)(2,1)S(1)} %collective-permute-done.5.refs_2_), channel_id=1, source_target_pairs={{16,0},{0,16},{17,1},{1,17},{18,2},{2,18},{19,3},{3,19},{20,4},{4,... | collective-permute-start | bytes 1757192 | tf_op jit(solution)/shard_map/ppermute | solution.py:20
  55.3 25.0 %collective-permute-start.9 = (bf16[208,1280]{1,0:T(8,128)(2,1)}, bf16[208,1280]{1,0:T(8,128)(2,1)}, u32[]{:S(2)}, u32[]{:S(2)}) collective-permute-start(bf16[208,1280]{1,0:T(8,128)(2,1)} %get-tuple-element.62), channel_id=1, source_target_pairs={{12,0},{0,4},{4,8},{8,12},{13,1},{1,5},{5,9},{9,13},{14,2},{2,6},{... | collective-permute-start | bytes 1597448 | tf_op jit(solution)/shard_map/ppermute | solution.py:20
  66.2 22.8 %collective-permute-start.13 = (bf16[208,1408]{1,0:T(8,128)(2,1)S(1)}, bf16[208,1408]{1,0:T(8,128)(2,1)}, u32[]{:S(2)}, u32[]{:S(2)}) collective-permute-start(bf16[208,1408]{1,0:T(8,128)(2,1)S(1)} %collective-permute-done.4.refs_4_), channel_id=1, source_target_pairs={{16,0},{0,16},{17,1},{1,17},{18,2},{2,18},{19,3},{3,19},{20,4},{4,... | collective-permute-start | bytes 1757192 | tf_op jit(solution)/shard_map/ppermute | solution.py:20
  69.9 19.0 %collective-permute-start.12 = (bf16[208,1280]{1,0:T(8,128)(2,1)}, bf16[208,1280]{1,0:T(8,128)(2,1)S(1)}, u32[]{:S(2)}, u32[]{:S(2)}) collective-permute-start(bf16[208,1280]{1,0:T(8,128)(2,1)} %get-tuple-element.68), channel_id=1, source_target_pairs={{12,0},{0,4},{4,8},{8,12},{13,1},{1,5},{5,9},{9,13},{14,2},{2,6},{... | collective-permute-start | bytes 1597448 | tf_op jit(solution)/shard_map/ppermute | solution.py:20
  80.3 20.2 %collective-permute-start.15 = (bf16[208,1280]{1,0:T(8,128)(2,1)S(1)}, bf16[208,1280]{1,0:T(8,128)(2,1)}, u32[]{:S(2)}, u32[]{:S(2)}) collective-permute-start(bf16[208,1280]{1,0:T(8,128)(2,1)S(1)} %copy-done.10), channel_id=1, source_target_pairs={{12,0},{0,4},{4,8},{8,12},{13,1},{1,5},{5,9},{9,13},{14,2},{2,6},{... | collective-permute-start | bytes 1597448 | tf_op jit(solution)/shard_map/ppermute | solution.py:20
  81.6 18.9 %collective-permute-start.11 = (bf16[208,1280]{1,0:T(8,128)(2,1)}, bf16[208,1280]{1,0:T(8,128)(2,1)S(1)}, u32[]{:S(2)}, u32[]{:S(2)}) collective-permute-start(bf16[208,1280]{1,0:T(8,128)(2,1)} %collective-permute-done.9.refs_2_), channel_id=1, source_target_pairs={{16,0},{0,16},{17,1},{1,17},{18,2},{2,18},{19,3},{3,19},{20,4},{4,... | collective-permute-start | bytes 1597448 | tf_op jit(solution)/shard_map/ppermute | solution.py:20
  89.0 19.2 %collective-permute-start.14 = (bf16[208,1280]{1,0:T(8,128)(2,1)S(1)}, bf16[208,1280]{1,0:T(8,128)(2,1)S(1)}, u32[]{:S(2)}, u32[]{:S(2)}) collective-permute-start(bf16[208,1280]{1,0:T(8,128)(2,1)S(1)} %collective-permute-done.12.refs_4_), channel_id=1, source_target_pairs={{16,0},{0,16},{17,1},{1,17},{18,2},{2,18},{19,3},{3,19},{20,4},{4,... | collective-permute-start | bytes 1597448 | tf_op jit(solution)/shard_map/ppermute | solution.py:20
  90.6 24.9 %collective-permute-start.19 = (bf16[208,1280]{1,0:T(8,128)(2,1)}, bf16[208,1280]{1,0:T(8,128)(2,1)}, u32[]{:S(2)}, u32[]{:S(2)}) collective-permute-start(bf16[208,1280]{1,0:T(8,128)(2,1)} %get-tuple-element.81), channel_id=1, source_target_pairs={{12,0},{0,4},{4,8},{8,12},{13,1},{1,5},{5,9},{9,13},{14,2},{2,6},{... | collective-permute-start | bytes 1597448 | tf_op jit(solution)/shard_map/ppermute | solution.py:20
  100.5 18.4 %collective-permute-start.18 = (bf16[208,1280]{1,0:T(8,128)(2,1)}, bf16[208,1280]{1,0:T(8,128)(2,1)S(1)}, u32[]{:S(2)}, u32[]{:S(2)}) collective-permute-start(bf16[208,1280]{1,0:T(8,128)(2,1)} %collective-permute-done.15.refs_5_), channel_id=1, source_target_pairs={{16,0},{0,16},{17,1},{1,17},{18,2},{2,18},{19,3},{3,19},{20,4},{4,... | collective-permute-start | bytes 1597448 | tf_op jit(solution)/shard_map/ppermute | solution.py:20
  102.2 17.2 %collective-permute-start.17 = (bf16[208,768]{1,0:T(8,128)(2,1)}, bf16[208,768]{1,0:T(8,128)(2,1)S(1)}, u32[]{:S(2)}, u32[]{:S(2)}) collective-permute-start(bf16[208,768]{1,0:T(8,128)(2,1)} %slice_select_fusion.8), channel_id=1, source_target_pairs={{12,0},{0,4},{4,8},{8,12},{13,1},{1,5},{5,9},{9,13},{14,2},{2,6},{... | collective-permute-start | bytes 958472 | tf_op jit(solution)/shard_map/ppermute | solution.py:20
  114.9 14.0 %collective-permute-start.20 = (bf16[320,416]{1,0:T(8,128)(2,1)}, bf16[320,416]{1,0:T(8,128)(2,1)}, u32[]{:S(2)}, u32[]{:S(2)}) collective-permute-start(bf16[320,416]{1,0:T(8,128)(2,1)} %get-tuple-element.99), channel_id=1, source_target_pairs={{2,0},{0,2},{3,1},{1,3},{6,4},{4,6},{7,5},{5,7},{10,8},{8,10},{11,... | collective-permute-start | bytes 798728 | tf_op jit(solution)/shard_map/ppermute | solution.py:20
  115.6 15.1 %collective-permute-start.25 = (bf16[208,1280]{1,0:T(8,128)(2,1)}, bf16[208,1280]{1,0:T(8,128)(2,1)S(1)}, u32[]{:S(2)}, u32[]{:S(2)}) collective-permute-start(bf16[208,1280]{1,0:T(8,128)(2,1)} %collective-permute-done.15.refs_5_), channel_id=1, source_target_pairs={{1,0},{0,1},{3,2},{2,3},{5,4},{4,5},{7,6},{6,7},{9,8},{8,9},{11,10... | collective-permute-start | bytes 1597448 | tf_op jit(solution)/shard_map/ppermute | solution.py:20
  118.9 19.8 %collective-permute-start.24 = (bf16[208,1280]{1,0:T(8,128)(2,1)}, bf16[208,1280]{1,0:T(8,128)(2,1)S(1)}, u32[]{:S(2)}, u32[]{:S(2)}) collective-permute-start(bf16[208,1280]{1,0:T(8,128)(2,1)} %collective-permute-done.19.refs_5_), channel_id=1, source_target_pairs={{16,0},{0,16},{17,1},{1,17},{18,2},{2,18},{19,3},{3,19},{20,4},{4,... | collective-permute-start | bytes 1597448 | tf_op jit(solution)/shard_map/ppermute | solution.py:20
  119.4 12.5 %collective-permute-start.26 = (bf16[208,1280]{1,0:T(8,128)(2,1)S(1)}, bf16[208,1280]{1,0:T(8,128)(2,1)}, u32[]{:S(2)}, u32[]{:S(2)}) collective-permute-start(bf16[208,1280]{1,0:T(8,128)(2,1)S(1)} %collective-permute-done.18.refs_6_), channel_id=1, source_target_pairs={{1,0},{0,1},{3,2},{2,3},{5,4},{4,5},{7,6},{6,7},{9,8},{8,9},{11,10... | collective-permute-start | bytes 1597448 | tf_op jit(solution)/shard_map/ppermute | solution.py:20
  124.2 20.4 %collective-permute-start.23 = (bf16[208,1536]{1,0:T(8,128)(2,1)}, bf16[208,1536]{1,0:T(8,128)(2,1)S(1)}, u32[]{:S(2)}, u32[]{:S(2)}) collective-permute-start(bf16[208,1536]{1,0:T(8,128)(2,1)} %slice.105), channel_id=1, source_target_pairs={{12,0},{0,4},{4,8},{8,12},{13,1},{1,5},{5,9},{9,13},{14,2},{2,6},{... | collective-permute-start | bytes 1916936 | tf_op jit(solution)/shard_map/ppermute | solution.py:20
  (22 other events, 141.3 us)
Sparse Core Ops, SparseCore 0:
  9.8 19.9 all-gather.1

commit v8 on v7

--- a/solution.py
+++ b/solution.py
@@ -8,7 +8,7 @@
 from jax.sharding import PartitionSpec as P
 
 FEATURE_SHARES = (11, 11, 11, 11, 10, 10)
-LANE_SHARES = (10, 10, 6, 6)
+LANE_SHARES = (12, 12, 8)
 QUEUE = 2
 VMEM = 16 * 1024 * 1024
 ANY = pl.BlockSpec(memory_space=pl.ANY)
@@ -116,16 +116,14 @@
 
 
 def output_kernel(parts, side_ref, *refs):
-    hidden, down = refs[:4], refs[4]
-    arrived, at = [], 5
+    hidden, down = refs[:4], refs[4:6]
+    arrived, at = [], 6
     for _, _, own, other in parts:
         count = len(own) + len(other)
         arrived.append((refs[at : at + count], refs[at + count : at + 2 * count]))
         at += 2 * count
     out, result, sems = refs[-3:]
-    side, core = side_ref[0], side_ref[1]
-    share = down.shape[0] // 2
-    shares = [pl.ds(pl.multiple_of(c * share, 16), share) for c in (core, 1 - core)]
+    side = side_ref[0]
     stores, at = [], 0
     for n, (i, array, lane, size, (fixed, turn)) in enumerate(blocks_of(parts)):
         column = pl.ds(pl.multiple_of(fixed + side * turn, 128), size)
@@ -134,7 +132,7 @@
         total = None
         for m in range(4):
             if m < 2:
-                weight = down[shares[m], column]
+                weight = down[m][:, column]
             else:
                 weight = arrived[i][m - 2][array][:, lane : lane + size]
             term = jnp.dot(hidden[m][...], weight, preferred_element_type=jnp.float32)
@@ -149,12 +147,12 @@
 
 
 def output_part(result, parts, side, hidden, down, arrived):
-    rows, width = hidden[0].shape[0], down.shape[1]
+    rows, width = hidden[0].shape[0], down[0].shape[1]
     lanes = sum(sum(own) + sum(other) for _, _, own, other in parts)
-    operands = [side, *hidden, down, *arrived]
+    operands = [side, *hidden, *down, *arrived]
     in_specs = (
         [pl.BlockSpec(memory_space=pltpu.SMEM)]
-        + [pl.BlockSpec(memory_space=pltpu.VMEM)] * (5 + len(arrived))
+        + [pl.BlockSpec(memory_space=pltpu.VMEM)] * (6 + len(arrived))
     )
     aliases = {}
     if result is not None:
@@ -198,7 +196,7 @@
     rows = tokens.shape[0]
     group = lax.axis_index("groups").astype(jnp.int32)
     first = group == 0
-    side = jnp.stack([group, lax.axis_index("sub").astype(jnp.int32)])
+    side = group.reshape(1)
 
     spans = cuts(width, 128, FEATURE_SHARES)
     lane_cuts = [(2 * a, 2 * b) for a, b in cuts(width // 2, 128, LANE_SHARES)]
@@ -234,17 +232,18 @@
         landed.append(block)
         if i < last:
             crossed[i] = across(block)
-        if i >= count:
-            mates[i] = mate(block)
         if i + QUEUE < total_count:
             waiting.append(shifted(tied(pieces[i + QUEUE], block), "dp", 1))
         return block
 
     def pass_on(n, *after):
         i = count + n
-        crossed[i] = tied(crossed[i], *after)
-        crossed_mates[i] = mate(crossed[i])
-        return crossed[i]
+        held = [tied(landed[i], *after)]
+        if i < last:
+            held.append(tied(crossed[i], *after))
+        mates[i], *rest = [mate(block) for block in held]
+        if rest:
+            crossed_mates[i] = rest[0]
 
     def local(partial_value, sent):
         pre = summed(partial_value, sent)
@@ -262,15 +261,12 @@
         return gated(jnp.where(first, left, right), jnp.where(first, right, left))
 
     tokens_mate = mate(tied(tokens, pieces[0]))
-    down_here = lax.all_gather(tied(down_weight, pieces[1]), "sub", axis=0, tiled=True)
-
-    def own_span(rows):
-        return products([rows], [gate_weight, up_weight], [(0, width)])
-
-    mine = own_span(tokens)
-    now = advance(mine, *pieces[2:])
-    theirs = own_span(tied(tokens_mate, now))
-    value = jnp.concatenate([mine, theirs], axis=0)
+    down_mate = mate(tied(down_weight, pieces[1]))
+    advance(*pieces[2:])
+    now = advance(tokens_mate, down_mate)
+    value = products(
+        [tied(tokens, now), tokens_mate], [gate_weight, up_weight], [(0, width)]
+    )
     now = advance(value)
     sent = over_slices(value)
     now = advance()
@@ -280,15 +276,13 @@
     here = here[:rows]
     value = batch(0, 2, now)
     now = advance(value, here)
-    now = advance(here_mate)
-    value = batch(2, 4, now, value)
-    now = advance(value)
-    value = batch(4, count, now, value, jnp.bfloat16)
+    value = batch(2, count - 1, now, value)
+    now = advance(value, here_mate)
+    value = batch(count - 1, count, now, value, jnp.bfloat16)
     halves = [value[:rows], value[rows:]]
     sent = [over_slices(half) for half in halves]
     now = advance(value)
-    now = pass_on(0, now)
-    now = advance(now)
+    pass_on(0, now)
     there, given = (
         activated(half, [tied(block, now) for block in blocks])
         for half, blocks in zip(halves, sent)
@@ -312,16 +306,15 @@
             tuple(parts),
             side,
             [here, here_mate, there, there_mate],
-            down_here,
+            [down_weight, down_mate],
             arrived,
         )
 
     result = write(None, 0)
     pass_on(1, result)
+    now = advance(result)
+    pass_on(2, now)
     result = write(result, 1)
-    now = advance(result)
-    result = write(result, 3)
-    pass_on(2, now)
     return write(result, 2)
 
 

time: 161 us -> 143 us (0.89)
  between operations: 13.7 us -> 0.42 us
  Pallas kernels: 35.5 us -> 24.3 us
  waiting for transfers between devices: 55.5 us -> 63.2 us
  other arithmetic: 15.3 us -> 11.7 us
  local copies, waits for them, and re-layouts: 15.1 us -> 16.8 us
    pallas_call x9 -> x7, Pallas kernels: 35.5 us -> 24.3 us  [call(): pl.pallas_call(kernel, in_specs=in_specs, out_specs=out_spec, out_shape=o...]
    ppermute x32 -> x29, waiting for transfers between devices: 55.5 us -> 63.2 us  [shifted(): return lax.ppermute(block, axis, route)]
    unnamed x26 -> x34, local copies, waits for them, and re-layouts: 9.14 us -> 11.4 us
    pallas_call x0 -> x1, local copies, waits for them, and re-layouts: none -> 2.15 us  [call(): pl.pallas_call(kernel, in_specs=in_specs, out_specs=out_spec, out_shape=o...]
    concatenate x1 -> x0, local copies, waits for them, and re-layouts: 2.13 us -> none  [on_device(): value = jnp.concatenate([mine, theirs], axis=0)]
    select_n x2 -> x1, other arithmetic: 3.05 us -> 1.2 us  [piece(): return jnp.where(first, down[:, a:mid], down[:, mid:b])]
    ppermute x32 -> x29, starting transfers between devices: 25.4 us -> 26.6 us  [shifted(): return lax.ppermute(block, axis, route)]
  transfers between devices with their start and end apart: 33 -> 29, of which waited for: 12 -> 12; matrix products, arithmetic and copies ran while one was open for 12% -> 11% of each run, Pallas kernels for 20% -> 15%
where the time goes in v8:
time: 143 us
  waiting for transfers between devices  63.2 us (44%)
  starting transfers between devices  26.6 us (19%)
  Pallas kernels  24.3 us (17%)
  local copies, waits for them, and re-layouts  16.8 us (12%)
  other arithmetic  11.7 us (8%)
    ppermute x29, waiting for transfers between devices, shifted(): return lax.ppermute(block, axis, route)  63.2 us
    ppermute x29, starting transfers between devices, shifted(): return lax.ppermute(block, axis, route)  26.6 us
    pallas_call x7, Pallas kernels, call(): pl.pallas_call(kernel, in_specs=in_specs, out_specs=out_spec, out_shape=o...  24.3 us
    unnamed x34, local copies, waits for them, and re-layouts  11.4 us
    select_n x4, other arithmetic, piece(): return jnp.where(first, gate[:, a:b], up[:, a:b])  8.25 us
  transfers between devices with their start and end apart: 29, of which 12 were waited for; matrix products, arithmetic and copies ran while one was open for 11% of the time, Pallas kernels for 15%

profile of v8, /device:TPU:0, one launch (start us, length us, event | category | flops | bytes accessed | tf_op | source)
XLA Modules:
  0.0 143.0 jit_solution(10110372959814833974)
XLA Ops:
  4.2 2.6 %collective-permute-start.3 = (bf16[208,1408]{1,0:T(8,128)(2,1)S(1)}, bf16[208,1408]{1,0:T(8,128)(2,1)S(1)}, u32[]{:S(2)}, u32[]{:S(2)}) collective-permute-start(bf16[208,1408]{1,0:T(8,128)(2,1)S(1)} %slice_select_fusion.5), channel_id=1, source_target_pairs={{12,0},{0,4},{4,8},{8,12},{13,1},{1,5},{5,9},{9,13},{14,2},{2,6},{... | collective-permute-start | bytes 1757192 | tf_op jit(solution)/shard_map/ppermute | solution.py:20
  8.4 2.7 %slice_select_fusion.2 = (bf16[208,1408]{1,0:T(8,128)(2,1)}, bf16[208,1408]{1,0:T(8,128)(2,1)S(1)}) fusion(bf16[208,8192]{1,0:T(8,128)(2,1)} %refs_3_.1, bf16[208,8192]{1,0:T(8,128)(2,1)} %refs_2_.1, pred[]{:T(512)S(6)} %eq.3), kind=kLoop, calls=%fused_computation.7 | loop fusion | flops 585728 | bytes 3514369 | tf_op jit(solution)/shard_map/jit(_where)/select_n | solution.py:213
  11.0 2.5 %slice_select_fusion.6 = (bf16[208,1280]{1,0:T(8,128)(2,1)}, bf16[208,1280]{1,0:T(8,128)(2,1)}) fusion(bf16[208,8192]{1,0:T(8,128)(2,1)} %refs_3_.1, bf16[208,8192]{1,0:T(8,128)(2,1)S(1)} %copy-done.6, pred[]{:T(512)S(6)} %eq.3), kind=kLoop, calls=%fused_computation.11 | loop fusion | flops 532480 | bytes 3194881 | tf_op jit(solution)/shard_map/jit(_where)/select_n | solution.py:213
  15.7 7.2 %collective-permute-done.3.refs_2_ = bf16[208,1408]{1,0:T(8,128)(2,1)S(1)} collective-permute-done((bf16[208,1408]{1,0:T(8,128)(2,1)S(1)}, bf16[208,1408]{1,0:T(8,128)(2,1)S(1)}, u32[]{:S(2)}, u32[]{:S(2)}) %collective-permute-start.3) | collective-permute-done | bytes 585760 | tf_op jit(solution)/shard_map/ppermute | solution.py:20
  25.4 10.2 %collective-permute-done.refs_4_ = bf16[208,1408]{1,0:T(8,128)(2,1)} collective-permute-done((bf16[208,1408]{1,0:T(8,128)(2,1)S(1)}, bf16[208,1408]{1,0:T(8,128)(2,1)}, u32[]{:S(2)}, u32[]{:S(2)}) %collective-permute-start) | collective-permute-done | bytes 585760 | tf_op jit(solution)/shard_map/ppermute | solution.py:20
  39.0 5.6 %shard_map.46 = bf16[640,416]{1,0:T(8,128)(2,1)S(1)} custom-call(bf16[320,8192]{1,0:T(8,128)(2,1)S(1)} %bitcast.2, bf16[320,8192]{1,0:T(8,128)(2,1)S(1)} %collective-permute-done.1.refs_1_, bf16[208,8192]{1,0:T(8,128)(2,1)S(1)} %copy-done.6, bf16[208,8192]{1,0:T(8,128)(2,1)S(1)} %copy-done.7), custom_call_target="tpu_custom_call" | custom-call | flops 1 | bytes 1 | tf_op jit(solution)/shard_map/pallas_call | solution.py:45
  45.5 2.6 %collective-permute-done.5.refs_2_ = bf16[208,1408]{1,0:T(8,128)(2,1)} collective-permute-done((bf16[208,1408]{1,0:T(8,128)(2,1)S(1)}, bf16[208,1408]{1,0:T(8,128)(2,1)}, u32[]{:S(2)}, u32[]{:S(2)}) %collective-permute-start.5) | collective-permute-done | bytes 585760 | tf_op jit(solution)/shard_map/ppermute | solution.py:20
  50.6 2.1 %copy.7 = bf16[640,416]{0,1:T(8,128)(2,1)} copy(bf16[640,416]{1,0:T(8,128)(2,1)} %copy-done.8) | data formatting | bytes 1064960 | tf_op jit(solution)/shard_map/pallas_call | solution.py:45
  54.2 6.4 %collective-permute-done.8.refs_4_ = bf16[208,1408]{1,0:T(8,128)(2,1)} collective-permute-done((bf16[208,1408]{1,0:T(8,128)(2,1)}, bf16[208,1408]{1,0:T(8,128)(2,1)}, u32[]{:S(2)}, u32[]{:S(2)}) %collective-permute-start.8) | collective-permute-done | bytes 585760 | tf_op jit(solution)/shard_map/ppermute | solution.py:20
  62.3 9.5 %collective-permute-done.7.refs_6_ = bf16[208,1280]{1,0:T(8,128)(2,1)} collective-permute-done((bf16[208,1280]{1,0:T(8,128)(2,1)}, bf16[208,1280]{1,0:T(8,128)(2,1)}, u32[]{:S(2)}, u32[]{:S(2)}) %collective-permute-start.7) | collective-permute-done | bytes 532512 | tf_op jit(solution)/shard_map/ppermute | solution.py:20
  73.4 2.1 %copy.8 = bf16[640,416]{1,0:T(8,128)(2,1)} copy(bf16[640,416]{0,1:T(8,128)(2,1)} %collective-permute-done.4) | data formatting | bytes 1064960 | tf_op jit(solution)/shard_map/optimization_barrier | solution.py:32
  78.3 2.5 %copy-done = bf16[320,8192]{1,0:T(8,128)(2,1)S(1)} copy-done((bf16[320,8192]{1,0:T(8,128)(2,1)S(1)}, bf16[320,8192]{1,0:T(8,128)(2,1)}, u32[]{:S(2)}) %copy-start) | copy-done | bytes 5242904
  80.8 2.5 %copy-done.2 = bf16[320,8192]{1,0:T(8,128)(2,1)S(1)} copy-done((bf16[320,8192]{1,0:T(8,128)(2,1)S(1)}, bf16[320,8192]{1,0:T(8,128)(2,1)}, u32[]{:S(2)}) %copy-start.2) | copy-done | bytes 5242904
  85.4 3.5 %shard_map.47.refs_8_ = f32[640,416]{1,0:T(8,128)S(1)} custom-call(bf16[320,8192]{1,0:T(8,128)(2,1)S(1)} %copy-done, bf16[320,8192]{1,0:T(8,128)(2,1)S(1)} %copy-done.2, bf16[208,1408]{1,0:T(8,128)(2,1)S(1)} %copy-done.10, bf16[208,1408]{1,0:T(8,128)(2,1)S(1)} %copy-done.12, bf16[208,1408]{1,0:T(8,128)(2,1)} %collective-permute-done.refs_4_, ...), custom_call_target="tpu_custom_call" | custom-call | flops 1 | bytes 1 | tf_op jit(solution)/shard_map/pallas_call | solution.py:45
  91.4 5.0 %shard_map.48.refs_4_ = f32[640,416]{1,0:T(8,128)S(1)} custom-call(bf16[320,8192]{1,0:T(8,128)(2,1)S(1)} %copy-done, bf16[320,8192]{1,0:T(8,128)(2,1)S(1)} %copy-done.2, bf16[208,1408]{1,0:T(8,128)(2,1)} %collective-permute-done.5.refs_2_, bf16[208,1408]{1,0:T(8,128)(2,1)} %collective-permute-done.10.refs_3_, ...), custom_call_target="tpu_custom_call" | custom-call | flops 1 | bytes 1 | tf_op jit(solution)/shard_map/pallas_call | solution.py:45
  96.4 6.1 %collective-permute-done.15.refs_6_ = bf16[208,1536]{1,0:T(8,128)(2,1)S(1)} collective-permute-done((bf16[208,1536]{1,0:T(8,128)(2,1)}, bf16[208,1536]{1,0:T(8,128)(2,1)S(1)}, u32[]{:S(2)}, u32[]{:S(2)}) %collective-permute-start.15) | collective-permute-done | bytes 639008 | tf_op jit(solution)/shard_map/ppermute | solution.py:20
  104.1 2.1 %shard_map.49 = bf16[640,416]{1,0:T(8,128)(2,1)S(1)} custom-call(bf16[320,8192]{1,0:T(8,128)(2,1)S(1)} %copy-done, bf16[320,8192]{1,0:T(8,128)(2,1)S(1)} %copy-done.2, bf16[208,1280]{1,0:T(8,128)(2,1)} %collective-permute-done.12.refs_2_, bf16[208,1280]{1,0:T(8,128)(2,1)S(1)} %collective-permute-done.14.refs_3_, f32[640,416]{1,0:T(8,128)S(1)} %shard_map.48.refs_4_), custom_call_target="tpu_custom_call" | custom-call | flops 1 | bytes 1 | tf_op jit(solution)/shard_map/pallas_call | solution.py:45
  108.3 1.9 %collective-permute-start.21 = (bf16[208,2048]{1,0:T(8,128)(2,1)S(1)}, bf16[208,2048]{1,0:T(8,128)(2,1)S(1)}, u32[]{:S(2)}, u32[]{:S(2)}) collective-permute-start(bf16[208,2048]{1,0:T(8,128)(2,1)S(1)} %copy-done.13), channel_id=1, source_target_pairs={{12,0},{0,4},{4,8},{8,12},{13,1},{1,5},{5,9},{9,13},{14,2},{2,6},{... | collective-permute-start | bytes 2555912 | tf_op jit(solution)/shard_map/ppermute | solution.py:20
  110.2 6.0 %collective-permute-done.18.refs_6_ = bf16[208,1536]{1,0:T(8,128)(2,1)S(1)} collective-permute-done((bf16[208,1536]{1,0:T(8,128)(2,1)S(1)}, bf16[208,1536]{1,0:T(8,128)(2,1)S(1)}, u32[]{:S(2)}, u32[]{:S(2)}) %collective-permute-start.18) | collective-permute-done | bytes 639008 | tf_op jit(solution)/shard_map/ppermute | solution.py:20
  122.0 3.0 %shard_map.50.refs_10_ = bf16[320,8192]{1,0:T(8,128)(2,1)} custom-call(s32[1]{0:T(128)} %bitcast.side_ref, bf16[320,208]{1,0:T(8,128)(2,1)S(1)} %get-tuple-element.102.refs_0_, bf16[320,208]{1,0:T(8,128)(2,1)S(1)} %collective-permute-done.11.refs_1_, bf16[320,208]{1,0:T(8,128)(2,1)S(1)} %multiply_convert_fusion.1.refs_2_, ...), custom_call_target="tpu_custom_call" | custom-call | flops 1 | bytes 1 | tf_op jit(solution)/shard_map/pallas_call | solution.py:45
  125.0 8.3 %collective-permute-done.21.refs_6_ = bf16[208,2048]{1,0:T(8,128)(2,1)S(1)} collective-permute-done((bf16[208,2048]{1,0:T(8,128)(2,1)S(1)}, bf16[208,2048]{1,0:T(8,128)(2,1)S(1)}, u32[]{:S(2)}, u32[]{:S(2)}) %collective-permute-start.21) | collective-permute-done | bytes 852000 | tf_op jit(solution)/shard_map/ppermute | solution.py:20
  133.9 2.8 %collective-permute-done.28.refs_9_ = bf16[208,1536]{1,0:T(8,128)(2,1)S(1)} collective-permute-done((bf16[208,1536]{1,0:T(8,128)(2,1)S(1)}, bf16[208,1536]{1,0:T(8,128)(2,1)S(1)}, u32[]{:S(2)}, u32[]{:S(2)}) %collective-permute-start.28) | collective-permute-done | bytes 639008 | tf_op jit(solution)/shard_map/ppermute | solution.py:20
  137.6 3.0 %shard_map.51.refs_8_ = bf16[320,8192]{1,0:T(8,128)(2,1)} custom-call(s32[1]{0:T(128)} %bitcast.side_ref, bf16[320,208]{1,0:T(8,128)(2,1)S(1)} %get-tuple-element.102.refs_0_, bf16[320,208]{1,0:T(8,128)(2,1)S(1)} %collective-permute-done.11.refs_1_, bf16[320,208]{1,0:T(8,128)(2,1)S(1)} %multiply_convert_fusion.1.refs_2_, ...), custom_call_target="tpu_custom_call", output_to_operand_aliasing={{}: (11, {})} | custom-call | flops 1 | bytes 1 | tf_op jit(solution)/shard_map/pallas_call | solution.py:45
  140.5 2.3 %shard_map.52 = bf16[320,8192]{1,0:T(8,128)(2,1)} custom-call(s32[1]{0:T(128)} %bitcast.side_ref, bf16[320,208]{1,0:T(8,128)(2,1)S(1)} %get-tuple-element.102.refs_0_, bf16[320,208]{1,0:T(8,128)(2,1)S(1)} %collective-permute-done.11.refs_1_, bf16[320,208]{1,0:T(8,128)(2,1)S(1)} %multiply_convert_fusion.1.refs_2_, ...), custom_call_target="tpu_custom_call", output_to_operand_aliasing={{}: (9, {})} | custom-call | flops 1 | bytes 1 | tf_op jit(solution)/shard_map/pallas_call | solution.py:45
  (91 shorter events, 40.3 us)
Async XLA Ops:
  1.5 35.9 %collective-permute-start.1 = (bf16[320,8192]{1,0:T(8,128)(2,1)}, bf16[320,8192]{1,0:T(8,128)(2,1)S(1)}, u32[]{:S(2)}, u32[]{:S(2)}) collective-permute-start(bf16[320,8192]{1,0:T(8,128)(2,1)} %refs_0_.6), channel_id=1, source_target_pairs={{1,0},{0,1},{3,2},{2,3},{5,4},{4,5},{7,6},{6,7},{9,8},{8,9},{11,10... | collective-permute-start | bytes 15728648 | tf_op jit(solution)/shard_map/ppermute | solution.py:20
  3.7 31.9 %collective-permute-start.2 = (bf16[208,8192]{1,0:T(8,128)(2,1)S(1)}, bf16[208,8192]{1,0:T(8,128)(2,1)S(1)}, u32[]{:S(2)}, u32[]{:S(2)}) collective-permute-start(bf16[208,8192]{1,0:T(8,128)(2,1)S(1)} %copy-done.3), channel_id=1, source_target_pairs={{1,0},{0,1},{3,2},{2,3},{5,4},{4,5},{7,6},{6,7},{9,8},{8,9},{11,10... | collective-permute-start | bytes 10223624 | tf_op jit(solution)/shard_map/ppermute | solution.py:20
  4.2 18.7 %collective-permute-start.3 = (bf16[208,1408]{1,0:T(8,128)(2,1)S(1)}, bf16[208,1408]{1,0:T(8,128)(2,1)S(1)}, u32[]{:S(2)}, u32[]{:S(2)}) collective-permute-start(bf16[208,1408]{1,0:T(8,128)(2,1)S(1)} %slice_select_fusion.5), channel_id=1, source_target_pairs={{12,0},{0,4},{4,8},{8,12},{13,1},{1,5},{5,9},{9,13},{14,2},{2,6},{... | collective-permute-start | bytes 1757192 | tf_op jit(solution)/shard_map/ppermute | solution.py:20
  6.8 28.8 %collective-permute-start = (bf16[208,1408]{1,0:T(8,128)(2,1)S(1)}, bf16[208,1408]{1,0:T(8,128)(2,1)}, u32[]{:S(2)}, u32[]{:S(2)}) collective-permute-start(bf16[208,1408]{1,0:T(8,128)(2,1)S(1)} %slice_select_fusion.4), channel_id=1, source_target_pairs={{12,0},{0,4},{4,8},{8,12},{13,1},{1,5},{5,9},{9,13},{14,2},{2,6},{... | collective-permute-start | bytes 1757192 | tf_op jit(solution)/shard_map/ppermute | solution.py:20
  22.9 25.2 %collective-permute-start.5 = (bf16[208,1408]{1,0:T(8,128)(2,1)S(1)}, bf16[208,1408]{1,0:T(8,128)(2,1)}, u32[]{:S(2)}, u32[]{:S(2)}) collective-permute-start(bf16[208,1408]{1,0:T(8,128)(2,1)S(1)} %get-tuple-element.57), channel_id=1, source_target_pairs={{12,0},{0,4},{4,8},{8,12},{13,1},{1,5},{5,9},{9,13},{14,2},{2,6},{... | collective-permute-start | bytes 1757192 | tf_op jit(solution)/shard_map/ppermute | solution.py:20
  22.9 25.2 %collective-permute-start.6 = (bf16[208,1408]{1,0:T(8,128)(2,1)S(1)}, bf16[208,1408]{1,0:T(8,128)(2,1)S(1)}, u32[]{:S(2)}, u32[]{:S(2)}) collective-permute-start(bf16[208,1408]{1,0:T(8,128)(2,1)S(1)} %collective-permute-done.3.refs_2_), channel_id=1, source_target_pairs={{16,0},{0,16},{17,1},{1,17},{18,2},{2,18},{19,3},{3,19},{20,4},{4,... | collective-permute-start | bytes 1757192 | tf_op jit(solution)/shard_map/ppermute | solution.py:20
  37.3 23.3 %collective-permute-start.9 = (bf16[208,1408]{1,0:T(8,128)(2,1)}, bf16[208,1408]{1,0:T(8,128)(2,1)}, u32[]{:S(2)}, u32[]{:S(2)}) collective-permute-start(bf16[208,1408]{1,0:T(8,128)(2,1)} %collective-permute-done.refs_4_), channel_id=1, source_target_pairs={{16,0},{0,16},{17,1},{1,17},{18,2},{2,18},{19,3},{3,19},{20,4},{4,... | collective-permute-start | bytes 1757192 | tf_op jit(solution)/shard_map/ppermute | solution.py:20
  39.0 21.7 %collective-permute-start.8 = (bf16[208,1408]{1,0:T(8,128)(2,1)}, bf16[208,1408]{1,0:T(8,128)(2,1)}, u32[]{:S(2)}, u32[]{:S(2)}) collective-permute-start(bf16[208,1408]{1,0:T(8,128)(2,1)} %get-tuple-element.60), channel_id=1, source_target_pairs={{12,0},{0,4},{4,8},{8,12},{13,1},{1,5},{5,9},{9,13},{14,2},{2,6},{... | collective-permute-start | bytes 1757192 | tf_op jit(solution)/shard_map/ppermute | solution.py:20
  48.9 22.9 %collective-permute-start.10 = (bf16[208,1408]{1,0:T(8,128)(2,1)}, bf16[208,1408]{1,0:T(8,128)(2,1)}, u32[]{:S(2)}, u32[]{:S(2)}) collective-permute-start(bf16[208,1408]{1,0:T(8,128)(2,1)} %collective-permute-done.5.refs_2_), channel_id=1, source_target_pairs={{16,0},{0,16},{17,1},{1,17},{18,2},{2,18},{19,3},{3,19},{20,4},{4,... | collective-permute-start | bytes 1757192 | tf_op jit(solution)/shard_map/ppermute | solution.py:20
  50.6 21.2 %collective-permute-start.7 = (bf16[208,1280]{1,0:T(8,128)(2,1)}, bf16[208,1280]{1,0:T(8,128)(2,1)}, u32[]{:S(2)}, u32[]{:S(2)}) collective-permute-start(bf16[208,1280]{1,0:T(8,128)(2,1)} %get-tuple-element.59), channel_id=1, source_target_pairs={{12,0},{0,4},{4,8},{8,12},{13,1},{1,5},{5,9},{9,13},{14,2},{2,6},{... | collective-permute-start | bytes 1597448 | tf_op jit(solution)/shard_map/ppermute | solution.py:20
  52.7 20.6 %collective-permute-start.4 = (bf16[640,416]{0,1:T(8,128)(2,1)}, bf16[640,416]{0,1:T(8,128)(2,1)}, u32[]{:S(2)}, u32[]{:S(2)}) collective-permute-start(bf16[640,416]{0,1:T(8,128)(2,1)} %copy.7), channel_id=1, source_target_pairs={{2,0},{0,2},{3,1},{1,3},{6,4},{4,6},{7,5},{5,7},{10,8},{8,10},{11,... | collective-permute-start | bytes 1597448 | tf_op jit(solution)/shard_map/ppermute | solution.py:20
  60.7 28.6 %collective-permute-start.13 = (bf16[208,1408]{1,0:T(8,128)(2,1)}, bf16[208,1408]{1,0:T(8,128)(2,1)}, u32[]{:S(2)}, u32[]{:S(2)}) collective-permute-start(bf16[208,1408]{1,0:T(8,128)(2,1)} %collective-permute-done.8.refs_4_), channel_id=1, source_target_pairs={{16,0},{0,16},{17,1},{1,17},{18,2},{2,18},{19,3},{3,19},{20,4},{4,... | collective-permute-start | bytes 1757192 | tf_op jit(solution)/shard_map/ppermute | solution.py:20
  71.8 17.4 %collective-permute-start.12 = (bf16[208,1280]{1,0:T(8,128)(2,1)}, bf16[208,1280]{1,0:T(8,128)(2,1)}, u32[]{:S(2)}, u32[]{:S(2)}) collective-permute-start(bf16[208,1280]{1,0:T(8,128)(2,1)} %get-tuple-element.64), channel_id=1, source_target_pairs={{12,0},{0,4},{4,8},{8,12},{13,1},{1,5},{5,9},{9,13},{14,2},{2,6},{... | collective-permute-start | bytes 1597448 | tf_op jit(solution)/shard_map/ppermute | solution.py:20
  71.8 18.6 %collective-permute-start.16 = (bf16[208,1280]{1,0:T(8,128)(2,1)}, bf16[208,1280]{1,0:T(8,128)(2,1)}, u32[]{:S(2)}, u32[]{:S(2)}) collective-permute-start(bf16[208,1280]{1,0:T(8,128)(2,1)} %collective-permute-done.7.refs_6_), channel_id=1, source_target_pairs={{16,0},{0,16},{17,1},{1,17},{18,2},{2,18},{19,3},{3,19},{20,4},{4,... | collective-permute-start | bytes 1597448 | tf_op jit(solution)/shard_map/ppermute | solution.py:20
  77.0 25.5 %collective-permute-start.15 = (bf16[208,1536]{1,0:T(8,128)(2,1)}, bf16[208,1536]{1,0:T(8,128)(2,1)S(1)}, u32[]{:S(2)}, u32[]{:S(2)}) collective-permute-start(bf16[208,1536]{1,0:T(8,128)(2,1)} %get-tuple-element.70), channel_id=1, source_target_pairs={{12,0},{0,4},{4,8},{8,12},{13,1},{1,5},{5,9},{9,13},{14,2},{2,6},{... | collective-permute-start | bytes 1916936 | tf_op jit(solution)/shard_map/ppermute | solution.py:20
  89.2 14.8 %collective-permute-start.14 = (bf16[208,1280]{1,0:T(8,128)(2,1)}, bf16[208,1280]{1,0:T(8,128)(2,1)S(1)}, u32[]{:S(2)}, u32[]{:S(2)}) collective-permute-start(bf16[208,1280]{1,0:T(8,128)(2,1)} %collective-permute-done.12.refs_2_), channel_id=1, source_target_pairs={{16,0},{0,16},{17,1},{1,17},{18,2},{2,18},{19,3},{3,19},{20,4},{4,... | collective-permute-start | bytes 1597448 | tf_op jit(solution)/shard_map/ppermute | solution.py:20
  90.5 6.0 %collective-permute-start.11 = (bf16[320,208]{1,0:T(8,128)(2,1)S(1)}, bf16[320,208]{1,0:T(8,128)(2,1)S(1)}, u32[]{:S(2)}, u32[]{:S(2)}) collective-permute-start(bf16[320,208]{1,0:T(8,128)(2,1)S(1)} %get-tuple-element.101), channel_id=1, source_target_pairs={{1,0},{0,1},{3,2},{2,3},{5,4},{4,5},{7,6},{6,7},{9,8},{8,9},{11,10... | collective-permute-start | bytes 399368 | tf_op jit(solution)/shard_map/ppermute | solution.py:20
  90.5 25.7 %collective-permute-start.18 = (bf16[208,1536]{1,0:T(8,128)(2,1)S(1)}, bf16[208,1536]{1,0:T(8,128)(2,1)S(1)}, u32[]{:S(2)}, u32[]{:S(2)}) collective-permute-start(bf16[208,1536]{1,0:T(8,128)(2,1)S(1)} %copy-done.14), channel_id=1, source_target_pairs={{12,0},{0,4},{4,8},{8,12},{13,1},{1,5},{5,9},{9,13},{14,2},{2,6},{... | collective-permute-start | bytes 1916936 | tf_op jit(solution)/shard_map/ppermute | solution.py:20
  102.5 15.2 %collective-permute-start.22 = (bf16[208,1536]{1,0:T(8,128)(2,1)S(1)}, bf16[208,1536]{1,0:T(8,128)(2,1)S(1)}, u32[]{:S(2)}, u32[]{:S(2)}) collective-permute-start(bf16[208,1536]{1,0:T(8,128)(2,1)S(1)} %collective-permute-done.15.refs_6_), channel_id=1, source_target_pairs={{16,0},{0,16},{17,1},{1,17},{18,2},{2,18},{19,3},{3,19},{20,4},{4,... | collective-permute-start | bytes 1916936 | tf_op jit(solution)/shard_map/ppermute | solution.py:20
  106.2 11.6 %collective-permute-start.17 = (bf16[320,416]{1,0:T(8,128)(2,1)S(1)}, bf16[320,416]{1,0:T(8,128)(2,1)S(1)}, u32[]{:S(2)}, u32[]{:S(2)}) collective-permute-start(bf16[320,416]{1,0:T(8,128)(2,1)S(1)} %get-tuple-element.100), channel_id=1, source_target_pairs={{2,0},{0,2},{3,1},{1,3},{6,4},{4,6},{7,5},{5,7},{10,8},{8,10},{11,... | collective-permute-start | bytes 798728 | tf_op jit(solution)/shard_map/ppermute | solution.py:20
  107.7 12.4 %collective-permute-start.19 = (bf16[320,416]{1,0:T(8,128)(2,1)S(1)}, bf16[320,416]{1,0:T(8,128)(2,1)S(1)}, u32[]{:S(2)}, u32[]{:S(2)}) collective-permute-start(bf16[320,416]{1,0:T(8,128)(2,1)S(1)} %get-tuple-element.99), channel_id=1, source_target_pairs={{2,0},{0,2},{3,1},{1,3},{6,4},{4,6},{7,5},{5,7},{10,8},{8,10},{11,... | collective-permute-start | bytes 798728 | tf_op jit(solution)/shard_map/ppermute | solution.py:20
  108.3 25.1 %collective-permute-start.21 = (bf16[208,2048]{1,0:T(8,128)(2,1)S(1)}, bf16[208,2048]{1,0:T(8,128)(2,1)S(1)}, u32[]{:S(2)}, u32[]{:S(2)}) collective-permute-start(bf16[208,2048]{1,0:T(8,128)(2,1)S(1)} %copy-done.13), channel_id=1, source_target_pairs={{12,0},{0,4},{4,8},{8,12},{13,1},{1,5},{5,9},{9,13},{14,2},{2,6},{... | collective-permute-start | bytes 2555912 | tf_op jit(solution)/shard_map/ppermute | solution.py:20
  116.2 17.1 %collective-permute-start.26 = (bf16[208,1536]{1,0:T(8,128)(2,1)S(1)}, bf16[208,1536]{1,0:T(8,128)(2,1)S(1)}, u32[]{:S(2)}, u32[]{:S(2)}) collective-permute-start(bf16[208,1536]{1,0:T(8,128)(2,1)S(1)} %collective-permute-done.18.refs_6_), channel_id=1, source_target_pairs={{16,0},{0,16},{17,1},{1,17},{18,2},{2,18},{19,3},{3,19},{20,4},{4,... | collective-permute-start | bytes 1916936 | tf_op jit(solution)/shard_map/ppermute | solution.py:20
  133.3 7.2 %collective-permute-start.25 = (bf16[208,2048]{1,0:T(8,128)(2,1)S(1)}, bf16[208,2048]{1,0:T(8,128)(2,1)S(1)}, u32[]{:S(2)}, u32[]{:S(2)}) collective-permute-start(bf16[208,2048]{1,0:T(8,128)(2,1)S(1)} %collective-permute-done.21.refs_6_), channel_id=1, source_target_pairs={{1,0},{0,1},{3,2},{2,3},{5,4},{4,5},{7,6},{6,7},{9,8},{8,9},{11,10... | collective-permute-start | bytes 2555912 | tf_op jit(solution)/shard_map/ppermute | solution.py:20
  (22 other events, 167.3 us)

commit v9 on v8

--- a/solution.py
+++ b/solution.py
@@ -8,7 +8,7 @@
 from jax.sharding import PartitionSpec as P
 
 FEATURE_SHARES = (11, 11, 11, 11, 10, 10)
-LANE_SHARES = (12, 12, 8)
+LANE_SHARES = (10, 9, 7, 6)
 QUEUE = 2
 VMEM = 16 * 1024 * 1024
 ANY = pl.BlockSpec(memory_space=pl.ANY)
@@ -103,29 +103,20 @@
 
 def blocks_of(parts):
     found = []
-    for i, (a, half, own, other) in enumerate(parts):
-        arrays = [(0, lanes) for lanes in own] + [(1, lanes) for lanes in other]
-        filled = [0, 0]
-        for n, (k, lanes) in enumerate(arrays):
-            for lane in range(0, lanes, 512):
-                size = min(512, lanes - lane)
-                turn = half - 2 * k * half if other else 0
-                found.append((i, n, lane, size, (a + k * half + filled[k] + lane, turn)))
-            filled[k] += lanes
+    for i, (a, lanes, half, others) in enumerate(parts):
+        for lane in range(0, lanes, 512):
+            size = min(512, lanes - lane)
+            fixed = a + lane + (half if others else 0)
+            found.append((i, lane, size, (fixed, -half if others else half)))
     return found
 
 
 def output_kernel(parts, side_ref, *refs):
-    hidden, down = refs[:4], refs[4:6]
-    arrived, at = [], 6
-    for _, _, own, other in parts:
-        count = len(own) + len(other)
-        arrived.append((refs[at : at + count], refs[at + count : at + 2 * count]))
-        at += 2 * count
+    hidden, down, arrived = refs[:4], refs[4:6], refs[6 : 6 + 2 * len(parts)]
     out, result, sems = refs[-3:]
     side = side_ref[0]
     stores, at = [], 0
-    for n, (i, array, lane, size, (fixed, turn)) in enumerate(blocks_of(parts)):
+    for n, (i, lane, size, (fixed, turn)) in enumerate(blocks_of(parts)):
         column = pl.ds(pl.multiple_of(fixed + side * turn, 128), size)
         spot = pl.ds(at, size)
         at += size
@@ -134,7 +125,7 @@
             if m < 2:
                 weight = down[m][:, column]
             else:
-                weight = arrived[i][m - 2][array][:, lane : lane + size]
+                weight = arrived[2 * i + m - 2][:, lane : lane + size]
             term = jnp.dot(hidden[m][...], weight, preferred_element_type=jnp.float32)
             total = term if total is None else total + term
         result[:, spot] = total.astype(result.dtype)
@@ -148,7 +139,7 @@
 
 def output_part(result, parts, side, hidden, down, arrived):
     rows, width = hidden[0].shape[0], down[0].shape[1]
-    lanes = sum(sum(own) + sum(other) for _, _, own, other in parts)
+    lanes = sum(part[1] for part in parts)
     operands = [side, *hidden, *down, *arrived]
     in_specs = (
         [pl.BlockSpec(memory_space=pltpu.SMEM)]
@@ -236,14 +227,11 @@
             waiting.append(shifted(tied(pieces[i + QUEUE], block), "dp", 1))
         return block
 
-    def pass_on(n, *after):
-        i = count + n
-        held = [tied(landed[i], *after)]
-        if i < last:
-            held.append(tied(crossed[i], *after))
-        mates[i], *rest = [mate(block) for block in held]
-        if rest:
-            crossed_mates[i] = rest[0]
+    def pass_own(n, *after):
+        mates[n] = mate(tied(landed[count + n], *after))
+
+    def pass_other(n, *after):
+        crossed_mates[n] = mate(tied(crossed[count + n], *after))
 
     def local(partial_value, sent):
         pre = summed(partial_value, sent)
@@ -264,43 +252,48 @@
     down_mate = mate(tied(down_weight, pieces[1]))
     advance(*pieces[2:])
     now = advance(tokens_mate, down_mate)
-    value = products(
+    own_value = products(
         [tied(tokens, now), tokens_mate], [gate_weight, up_weight], [(0, width)]
     )
+    now = advance(own_value)
+    own_sent = over_slices(own_value)
+    now = advance()
+    value = batch(0, 2, now)
     now = advance(value)
-    sent = over_slices(value)
-    now = advance()
-    now = advance()
-    here = local(value, [tied(block, now) for block in sent])
+    here = local(own_value, [tied(block, now) for block in own_sent])
     here_mate = mate(here[rows:])
     here = here[:rows]
-    value = batch(0, 2, now)
-    now = advance(value, here)
+    now = advance(here)
     value = batch(2, count - 1, now, value)
     now = advance(value, here_mate)
     value = batch(count - 1, count, now, value, jnp.bfloat16)
     halves = [value[:rows], value[rows:]]
     sent = [over_slices(half) for half in halves]
     now = advance(value)
-    pass_on(0, now)
+    pass_own(0, now)
+    now = advance(crossed[count])
+    pass_own(1, now)
+    pass_other(0, now)
     there, given = (
         activated(half, [tied(block, now) for block in blocks])
         for half, blocks in zip(halves, sent)
     )
-    there_mate = mate(given)
+    there_mate = tied(mate(given), crossed[count + 1])
 
     def write(result, *which):
         parts, arrived = [], []
-        for n in which:
-            i = count + n
+        for n, others in which:
             a, b = lane_cuts[n]
-            if i == last:
-                parts.append((a, (b - a) // 2, (b - a,), ()))
-                arrived += [landed[i], mates[i]]
+            half = (b - a) // 2
+            if count + n == last:
+                parts.append((a, b - a, 0, False))
+                arrived += [landed[last], mates[n]]
+            elif others:
+                parts.append((a, half, half, True))
+                arrived += [crossed[count + n], crossed_mates[n]]
             else:
-                half = (b - a) // 2
-                parts.append((a, half, (half,), (half,)))
-                arrived += [landed[i], crossed[i], mates[i], crossed_mates[i]]
+                parts.append((a, half, half, False))
+                arrived += [landed[count + n], mates[n]]
         return output_part(
             result,
             tuple(parts),
@@ -310,12 +303,15 @@
             arrived,
         )
 
-    result = write(None, 0)
-    pass_on(1, result)
+    result = write(None, (0, False), (0, True), (1, False))
+    pass_own(2, result)
+    pass_other(1, result)
     now = advance(result)
-    pass_on(2, now)
-    result = write(result, 1)
-    return write(result, 2)
+    pass_own(3, now)
+    pass_other(2, now)
+    result = write(result, (2, False), (1, True))
+    result = write(result, (3, False))
+    return write(result, (2, True))
 
 
 def solution(mesh):

time: 143 us -> 156 us (1.091)
  waiting for transfers between devices: 63.2 us -> 69.3 us
  local copies, waits for them, and re-layouts: 16.8 us -> 22.7 us
  other arithmetic: 11.7 us -> 13.7 us
  starting transfers between devices: 26.6 us -> 24.6 us
    ppermute x29 -> x33, waiting for transfers between devices: 63.2 us -> 69.3 us  [shifted(): return lax.ppermute(block, axis, route)]
    unnamed x34 -> x44, local copies, waits for them, and re-layouts: 11.4 us -> 17.5 us
    ppermute x29 -> x33, starting transfers between devices: 26.6 us -> 24.6 us  [shifted(): return lax.ppermute(block, axis, route)]
    pallas_call x7 -> x8, Pallas kernels: 24.3 us -> 24.7 us  [call(): pl.pallas_call(kernel, in_specs=in_specs, out_specs=out_spec, out_shape=o...]
  transfers between devices with their start and end apart: 29 -> 33, of which waited for: 12 -> 11; matrix products, arithmetic and copies ran while one was open for 11% -> 11% of each run, Pallas kernels for 15% -> 15%
where the time goes in v9:
time: 156 us
  waiting for transfers between devices  69.3 us (44%)
  Pallas kernels  24.7 us (16%)
  starting transfers between devices  24.6 us (16%)
  local copies, waits for them, and re-layouts  22.7 us (15%)
  other arithmetic  13.7 us (9%)
    ppermute x33, waiting for transfers between devices, shifted(): return lax.ppermute(block, axis, route)  69.3 us
    pallas_call x8, Pallas kernels, call(): pl.pallas_call(kernel, in_specs=in_specs, out_specs=out_spec, out_shape=o...  24.7 us
    ppermute x33, starting transfers between devices, shifted(): return lax.ppermute(block, axis, route)  24.6 us
    unnamed x44, local copies, waits for them, and re-layouts  17.5 us
    select_n x4, other arithmetic, piece(): return jnp.where(first, gate[:, a:b], up[:, a:b])  8.87 us
  transfers between devices with their start and end apart: 33, of which 11 were waited for; matrix products, arithmetic and copies ran while one was open for 11% of the time, Pallas kernels for 15%

profile of v9, /device:TPU:0, one launch (start us, length us, event | category | flops | bytes accessed | tf_op | source)
XLA Modules:
  0.0 155.6 jit_solution(16254014190693962029)
XLA Ops:
  4.2 2.6 %collective-permute-start.3 = (bf16[208,1408]{1,0:T(8,128)(2,1)S(1)}, bf16[208,1408]{1,0:T(8,128)(2,1)S(1)}, u32[]{:S(2)}, u32[]{:S(2)}) collective-permute-start(bf16[208,1408]{1,0:T(8,128)(2,1)S(1)} %slice_select_fusion.3), channel_id=1, source_target_pairs={{12,0},{0,4},{4,8},{8,12},{13,1},{1,5},{5,9},{9,13},{14,2},{2,6},{... | collective-permute-start | bytes 1757192 | tf_op jit(solution)/shard_map/ppermute | solution.py:20
  9.3 2.7 %slice_select_fusion = (bf16[208,1408]{1,0:T(8,128)(2,1)}, bf16[208,1408]{1,0:T(8,128)(2,1)S(1)}) fusion(bf16[208,8192]{1,0:T(8,128)(2,1)} %refs_3_.1, bf16[208,8192]{1,0:T(8,128)(2,1)} %refs_2_.1, pred[]{:T(512)S(6)} %eq.3), kind=kLoop, calls=%fused_computation.5 | loop fusion | flops 585728 | bytes 3514369 | tf_op jit(solution)/shard_map/jit(_where)/select_n | solution.py:204
  11.9 2.9 %slice_select_fusion.5 = (bf16[208,1280]{1,0:T(8,128)(2,1)}, bf16[208,1280]{1,0:T(8,128)(2,1)}) fusion(bf16[208,8192]{1,0:T(8,128)(2,1)} %refs_3_.1, bf16[208,8192]{1,0:T(8,128)(2,1)} %refs_2_.1, pred[]{:T(512)S(6)} %eq.3), kind=kLoop, calls=%fused_computation.10 | loop fusion | flops 532480 | bytes 3194881 | tf_op jit(solution)/shard_map/jit(_where)/select_n | solution.py:204
  17.3 5.6 %collective-permute-done.3.refs_2_ = bf16[208,1408]{1,0:T(8,128)(2,1)S(1)} collective-permute-done((bf16[208,1408]{1,0:T(8,128)(2,1)S(1)}, bf16[208,1408]{1,0:T(8,128)(2,1)S(1)}, u32[]{:S(2)}, u32[]{:S(2)}) %collective-permute-start.3) | collective-permute-done | bytes 585760 | tf_op jit(solution)/shard_map/ppermute | solution.py:20
  25.4 10.2 %collective-permute-done.refs_4_ = bf16[208,1408]{1,0:T(8,128)(2,1)} collective-permute-done((bf16[208,1408]{1,0:T(8,128)(2,1)S(1)}, bf16[208,1408]{1,0:T(8,128)(2,1)}, u32[]{:S(2)}, u32[]{:S(2)}) %collective-permute-start) | collective-permute-done | bytes 585760 | tf_op jit(solution)/shard_map/ppermute | solution.py:20
  39.2 5.6 %shard_map.46 = bf16[640,416]{1,0:T(8,128)(2,1)S(1)} custom-call(bf16[320,8192]{1,0:T(8,128)(2,1)S(1)} %bitcast.2, bf16[320,8192]{1,0:T(8,128)(2,1)S(1)} %collective-permute-done.1.refs_1_, bf16[208,8192]{1,0:T(8,128)(2,1)S(1)} %copy-done.8, bf16[208,8192]{1,0:T(8,128)(2,1)S(1)} %copy-done.9), custom_call_target="tpu_custom_call" | custom-call | flops 1 | bytes 1 | tf_op jit(solution)/shard_map/pallas_call | solution.py:45
  45.6 2.5 %collective-permute-done.5.refs_2_ = bf16[208,1408]{1,0:T(8,128)(2,1)} collective-permute-done((bf16[208,1408]{1,0:T(8,128)(2,1)S(1)}, bf16[208,1408]{1,0:T(8,128)(2,1)}, u32[]{:S(2)}, u32[]{:S(2)}) %collective-permute-start.5) | collective-permute-done | bytes 585760 | tf_op jit(solution)/shard_map/ppermute | solution.py:20
  50.6 2.1 %copy.8 = bf16[640,416]{0,1:T(8,128)(2,1)} copy(bf16[640,416]{1,0:T(8,128)(2,1)} %copy-done.10) | data formatting | bytes 1064960 | tf_op jit(solution)/shard_map/pallas_call | solution.py:45
  54.3 6.4 %collective-permute-done.9.refs_4_ = bf16[208,1408]{1,0:T(8,128)(2,1)} collective-permute-done((bf16[208,1408]{1,0:T(8,128)(2,1)}, bf16[208,1408]{1,0:T(8,128)(2,1)}, u32[]{:S(2)}, u32[]{:S(2)}) %collective-permute-start.9) | collective-permute-done | bytes 585760 | tf_op jit(solution)/shard_map/ppermute | solution.py:20
  62.4 2.5 %copy-done.1 = bf16[320,8192]{1,0:T(8,128)(2,1)S(1)} copy-done((bf16[320,8192]{1,0:T(8,128)(2,1)S(1)}, bf16[320,8192]{1,0:T(8,128)(2,1)}, u32[]{:S(2)}) %copy-start.1) | copy-done | bytes 5242904
  64.9 2.5 %copy-done.4 = bf16[320,8192]{1,0:T(8,128)(2,1)S(1)} copy-done((bf16[320,8192]{1,0:T(8,128)(2,1)S(1)}, bf16[320,8192]{1,0:T(8,128)(2,1)}, u32[]{:S(2)}) %copy-start.4) | copy-done | bytes 5242904
  69.5 3.5 %shard_map.47.refs_8_ = f32[640,416]{1,0:T(8,128)S(1)} custom-call(bf16[320,8192]{1,0:T(8,128)(2,1)S(1)} %copy-done.1, bf16[320,8192]{1,0:T(8,128)(2,1)S(1)} %copy-done.4, bf16[208,1408]{1,0:T(8,128)(2,1)S(1)} %copy-done.14, bf16[208,1408]{1,0:T(8,128)(2,1)S(1)} %copy-done.16, bf16[208,1408]{1,0:T(8,128)(2,1)} %collective-permute-done.refs_4_, ...), custom_call_target="tpu_custom_call" | custom-call | flops 1 | bytes 1 | tf_op jit(solution)/shard_map/pallas_call | solution.py:45
  74.4 2.1 %copy.9 = bf16[640,416]{1,0:T(8,128)(2,1)} copy(bf16[640,416]{0,1:T(8,128)(2,1)} %collective-permute-done.4) | data formatting | bytes 1064960 | tf_op jit(solution)/shard_map/optimization_barrier | solution.py:32
  79.8 13.7 %collective-permute-done.12.refs_2_ = bf16[208,1280]{1,0:T(8,128)(2,1)S(1)} collective-permute-done((bf16[208,1280]{1,0:T(8,128)(2,1)}, bf16[208,1280]{1,0:T(8,128)(2,1)S(1)}, u32[]{:S(2)}, u32[]{:S(2)}) %collective-permute-start.12) | collective-permute-done | bytes 532512 | tf_op jit(solution)/shard_map/ppermute | solution.py:20
  95.2 2.5 %copy-done.2 = bf16[320,8192]{1,0:T(8,128)(2,1)S(1)} copy-done((bf16[320,8192]{1,0:T(8,128)(2,1)S(1)}, bf16[320,8192]{1,0:T(8,128)(2,1)}, u32[]{:S(2)}) %copy-start.2) | copy-done | bytes 5242904
  97.7 2.5 %copy-done.5 = bf16[320,8192]{1,0:T(8,128)(2,1)S(1)} copy-done((bf16[320,8192]{1,0:T(8,128)(2,1)S(1)}, bf16[320,8192]{1,0:T(8,128)(2,1)}, u32[]{:S(2)}) %copy-start.5) | copy-done | bytes 5242904
  100.2 5.0 %shard_map.48.refs_4_ = f32[640,416]{1,0:T(8,128)S(1)} custom-call(bf16[320,8192]{1,0:T(8,128)(2,1)S(1)} %copy-done.2, bf16[320,8192]{1,0:T(8,128)(2,1)S(1)} %copy-done.5, bf16[208,1408]{1,0:T(8,128)(2,1)} %collective-permute-done.5.refs_2_, bf16[208,1408]{1,0:T(8,128)(2,1)} %collective-permute-done.10.refs_3_, ...), custom_call_target="tpu_custom_call" | custom-call | flops 1 | bytes 1 | tf_op jit(solution)/shard_map/pallas_call | solution.py:45
  109.2 12.1 %collective-permute-done.20.refs_10_ = bf16[208,1152]{1,0:T(8,128)(2,1)S(1)} collective-permute-done((bf16[208,1152]{1,0:T(8,128)(2,1)S(1)}, bf16[208,1152]{1,0:T(8,128)(2,1)S(1)}, u32[]{:S(2)}, u32[]{:S(2)}) %collective-permute-start.20) | collective-permute-done | bytes 479264 | tf_op jit(solution)/shard_map/ppermute | solution.py:20
  123.0 5.6 %collective-permute-done.18.refs_6_ = bf16[208,896]{1,0:T(8,128)(2,1)S(1)} collective-permute-done((bf16[208,896]{1,0:T(8,128)(2,1)S(1)}, bf16[208,896]{1,0:T(8,128)(2,1)S(1)}, u32[]{:S(2)}, u32[]{:S(2)}) %collective-permute-start.18) | collective-permute-done | bytes 372768 | tf_op jit(solution)/shard_map/ppermute | solution.py:20
  130.6 2.3 %collective-permute-done.23.refs_8_ = bf16[208,1152]{1,0:T(8,128)(2,1)S(1)} collective-permute-done((bf16[208,1152]{1,0:T(8,128)(2,1)S(1)}, bf16[208,1152]{1,0:T(8,128)(2,1)S(1)}, u32[]{:S(2)}, u32[]{:S(2)}) %collective-permute-start.23) | collective-permute-done | bytes 479264 | tf_op jit(solution)/shard_map/ppermute | solution.py:20
  134.7 3.6 %shard_map.50.refs_10_ = bf16[320,8192]{1,0:T(8,128)(2,1)} custom-call(s32[1]{0:T(128)} %bitcast.side_ref, bf16[320,208]{1,0:T(8,128)(2,1)S(1)} %get-tuple-element.110.refs_0_, bf16[320,208]{1,0:T(8,128)(2,1)S(1)} %collective-permute-done.11.refs_1_, bf16[320,208]{1,0:T(8,128)(2,1)S(1)} %multiply_convert_fusion.1.refs_2_, ...), custom_call_target="tpu_custom_call" | custom-call | flops 1 | bytes 1 | tf_op jit(solution)/shard_map/pallas_call | solution.py:45
  138.4 7.7 %collective-permute-done.25.refs_6_ = bf16[208,1536]{1,0:T(8,128)(2,1)S(1)} collective-permute-done((bf16[208,1536]{1,0:T(8,128)(2,1)S(1)}, bf16[208,1536]{1,0:T(8,128)(2,1)S(1)}, u32[]{:S(2)}, u32[]{:S(2)}) %collective-permute-start.25) | collective-permute-done | bytes 639008 | tf_op jit(solution)/shard_map/ppermute | solution.py:20
  147.1 2.3 %collective-permute-done.31.refs_7_ = bf16[208,896]{1,0:T(8,128)(2,1)S(1)} collective-permute-done((bf16[208,896]{1,0:T(8,128)(2,1)S(1)}, bf16[208,896]{1,0:T(8,128)(2,1)S(1)}, u32[]{:S(2)}, u32[]{:S(2)}) %collective-permute-start.31) | collective-permute-done | bytes 372768 | tf_op jit(solution)/shard_map/ppermute | solution.py:20
  149.4 2.6 %shard_map.51.refs_8_ = bf16[320,8192]{1,0:T(8,128)(2,1)} custom-call(s32[1]{0:T(128)} %bitcast.side_ref, bf16[320,208]{1,0:T(8,128)(2,1)S(1)} %get-tuple-element.110.refs_0_, bf16[320,208]{1,0:T(8,128)(2,1)S(1)} %collective-permute-done.11.refs_1_, bf16[320,208]{1,0:T(8,128)(2,1)S(1)} %multiply_convert_fusion.1.refs_2_, ...), custom_call_target="tpu_custom_call", output_to_operand_aliasing={{}: (11, {})} | custom-call | flops 1 | bytes 1 | tf_op jit(solution)/shard_map/pallas_call | solution.py:45
  (112 shorter events, 44.1 us)
Async XLA Ops:
  1.5 35.9 %collective-permute-start.1 = (bf16[320,8192]{1,0:T(8,128)(2,1)}, bf16[320,8192]{1,0:T(8,128)(2,1)S(1)}, u32[]{:S(2)}, u32[]{:S(2)}) collective-permute-start(bf16[320,8192]{1,0:T(8,128)(2,1)} %refs_0_.6), channel_id=1, source_target_pairs={{1,0},{0,1},{3,2},{2,3},{5,4},{4,5},{7,6},{6,7},{9,8},{8,9},{11,10... | collective-permute-start | bytes 15728648 | tf_op jit(solution)/shard_map/ppermute | solution.py:20
  3.9 31.7 %collective-permute-start.2 = (bf16[208,8192]{1,0:T(8,128)(2,1)S(1)}, bf16[208,8192]{1,0:T(8,128)(2,1)S(1)}, u32[]{:S(2)}, u32[]{:S(2)}) collective-permute-start(bf16[208,8192]{1,0:T(8,128)(2,1)S(1)} %copy-done), channel_id=1, source_target_pairs={{1,0},{0,1},{3,2},{2,3},{5,4},{4,5},{7,6},{6,7},{9,8},{8,9},{11,10... | collective-permute-start | bytes 10223624 | tf_op jit(solution)/shard_map/ppermute | solution.py:20
  4.2 18.8 %collective-permute-start.3 = (bf16[208,1408]{1,0:T(8,128)(2,1)S(1)}, bf16[208,1408]{1,0:T(8,128)(2,1)S(1)}, u32[]{:S(2)}, u32[]{:S(2)}) collective-permute-start(bf16[208,1408]{1,0:T(8,128)(2,1)S(1)} %slice_select_fusion.3), channel_id=1, source_target_pairs={{12,0},{0,4},{4,8},{8,12},{13,1},{1,5},{5,9},{9,13},{14,2},{2,6},{... | collective-permute-start | bytes 1757192 | tf_op jit(solution)/shard_map/ppermute | solution.py:20
  6.8 28.8 %collective-permute-start = (bf16[208,1408]{1,0:T(8,128)(2,1)S(1)}, bf16[208,1408]{1,0:T(8,128)(2,1)}, u32[]{:S(2)}, u32[]{:S(2)}) collective-permute-start(bf16[208,1408]{1,0:T(8,128)(2,1)S(1)} %slice_select_fusion.2), channel_id=1, source_target_pairs={{12,0},{0,4},{4,8},{8,12},{13,1},{1,5},{5,9},{9,13},{14,2},{2,6},{... | collective-permute-start | bytes 1757192 | tf_op jit(solution)/shard_map/ppermute | solution.py:20
  22.9 25.2 %collective-permute-start.5 = (bf16[208,1408]{1,0:T(8,128)(2,1)S(1)}, bf16[208,1408]{1,0:T(8,128)(2,1)}, u32[]{:S(2)}, u32[]{:S(2)}) collective-permute-start(bf16[208,1408]{1,0:T(8,128)(2,1)S(1)} %get-tuple-element.62), channel_id=1, source_target_pairs={{12,0},{0,4},{4,8},{8,12},{13,1},{1,5},{5,9},{9,13},{14,2},{2,6},{... | collective-permute-start | bytes 1757192 | tf_op jit(solution)/shard_map/ppermute | solution.py:20
  22.9 25.2 %collective-permute-start.6 = (bf16[208,1408]{1,0:T(8,128)(2,1)S(1)}, bf16[208,1408]{1,0:T(8,128)(2,1)S(1)}, u32[]{:S(2)}, u32[]{:S(2)}) collective-permute-start(bf16[208,1408]{1,0:T(8,128)(2,1)S(1)} %collective-permute-done.3.refs_2_), channel_id=1, source_target_pairs={{16,0},{0,16},{17,1},{1,17},{18,2},{2,18},{19,3},{3,19},{20,4},{4,... | collective-permute-start | bytes 1757192 | tf_op jit(solution)/shard_map/ppermute | solution.py:20
  37.4 23.3 %collective-permute-start.9 = (bf16[208,1408]{1,0:T(8,128)(2,1)}, bf16[208,1408]{1,0:T(8,128)(2,1)}, u32[]{:S(2)}, u32[]{:S(2)}) collective-permute-start(bf16[208,1408]{1,0:T(8,128)(2,1)} %get-tuple-element.65), channel_id=1, source_target_pairs={{12,0},{0,4},{4,8},{8,12},{13,1},{1,5},{5,9},{9,13},{14,2},{2,6},{... | collective-permute-start | bytes 1757192 | tf_op jit(solution)/shard_map/ppermute | solution.py:20
  37.4 23.3 %collective-permute-start.8 = (bf16[208,1408]{1,0:T(8,128)(2,1)}, bf16[208,1408]{1,0:T(8,128)(2,1)}, u32[]{:S(2)}, u32[]{:S(2)}) collective-permute-start(bf16[208,1408]{1,0:T(8,128)(2,1)} %collective-permute-done.refs_4_), channel_id=1, source_target_pairs={{16,0},{0,16},{17,1},{1,17},{18,2},{2,18},{19,3},{3,19},{20,4},{4,... | collective-permute-start | bytes 1757192 | tf_op jit(solution)/shard_map/ppermute | solution.py:20
  49.0 25.0 %collective-permute-start.10 = (bf16[208,1408]{1,0:T(8,128)(2,1)}, bf16[208,1408]{1,0:T(8,128)(2,1)}, u32[]{:S(2)}, u32[]{:S(2)}) collective-permute-start(bf16[208,1408]{1,0:T(8,128)(2,1)} %collective-permute-done.5.refs_2_), channel_id=1, source_target_pairs={{16,0},{0,16},{17,1},{1,17},{18,2},{2,18},{19,3},{3,19},{20,4},{4,... | collective-permute-start | bytes 1757192 | tf_op jit(solution)/shard_map/ppermute | solution.py:20
  50.6 23.4 %collective-permute-start.7 = (bf16[208,1280]{1,0:T(8,128)(2,1)}, bf16[208,1280]{1,0:T(8,128)(2,1)}, u32[]{:S(2)}, u32[]{:S(2)}) collective-permute-start(bf16[208,1280]{1,0:T(8,128)(2,1)} %get-tuple-element.64), channel_id=1, source_target_pairs={{12,0},{0,4},{4,8},{8,12},{13,1},{1,5},{5,9},{9,13},{14,2},{2,6},{... | collective-permute-start | bytes 1597448 | tf_op jit(solution)/shard_map/ppermute | solution.py:20
  52.8 21.6 %collective-permute-start.4 = (bf16[640,416]{0,1:T(8,128)(2,1)}, bf16[640,416]{0,1:T(8,128)(2,1)}, u32[]{:S(2)}, u32[]{:S(2)}) collective-permute-start(bf16[640,416]{0,1:T(8,128)(2,1)} %copy.8), channel_id=1, source_target_pairs={{2,0},{0,2},{3,1},{1,3},{6,4},{4,6},{7,5},{5,7},{10,8},{8,10},{11,... | collective-permute-start | bytes 1597448 | tf_op jit(solution)/shard_map/ppermute | solution.py:20
  60.7 32.8 %collective-permute-start.13 = (bf16[208,1408]{1,0:T(8,128)(2,1)}, bf16[208,1408]{1,0:T(8,128)(2,1)}, u32[]{:S(2)}, u32[]{:S(2)}) collective-permute-start(bf16[208,1408]{1,0:T(8,128)(2,1)} %collective-permute-done.9.refs_4_), channel_id=1, source_target_pairs={{16,0},{0,16},{17,1},{1,17},{18,2},{2,18},{19,3},{3,19},{20,4},{4,... | collective-permute-start | bytes 1757192 | tf_op jit(solution)/shard_map/ppermute | solution.py:20
  74.0 21.2 %collective-permute-start.16 = (bf16[208,1280]{1,0:T(8,128)(2,1)}, bf16[208,1280]{1,0:T(8,128)(2,1)}, u32[]{:S(2)}, u32[]{:S(2)}) collective-permute-start(bf16[208,1280]{1,0:T(8,128)(2,1)} %collective-permute-done.7.refs_6_), channel_id=1, source_target_pairs={{16,0},{0,16},{17,1},{1,17},{18,2},{2,18},{19,3},{3,19},{20,4},{4,... | collective-permute-start | bytes 1597448 | tf_op jit(solution)/shard_map/ppermute | solution.py:20
  76.5 17.0 %collective-permute-start.12 = (bf16[208,1280]{1,0:T(8,128)(2,1)}, bf16[208,1280]{1,0:T(8,128)(2,1)S(1)}, u32[]{:S(2)}, u32[]{:S(2)}) collective-permute-start(bf16[208,1280]{1,0:T(8,128)(2,1)} %get-tuple-element.73), channel_id=1, source_target_pairs={{12,0},{0,4},{4,8},{8,12},{13,1},{1,5},{5,9},{9,13},{14,2},{2,6},{... | collective-permute-start | bytes 1597448 | tf_op jit(solution)/shard_map/ppermute | solution.py:20
  78.1 27.2 %collective-permute-start.15 = (bf16[208,1280]{1,0:T(8,128)(2,1)}, bf16[208,1280]{1,0:T(8,128)(2,1)S(1)}, u32[]{:S(2)}, u32[]{:S(2)}) collective-permute-start(bf16[208,1280]{1,0:T(8,128)(2,1)} %slice_select_fusion.4), channel_id=1, source_target_pairs={{12,0},{0,4},{4,8},{8,12},{13,1},{1,5},{5,9},{9,13},{14,2},{2,6},{... | collective-permute-start | bytes 1597448 | tf_op jit(solution)/shard_map/ppermute | solution.py:20
  93.5 12.4 %collective-permute-start.14 = (bf16[208,1280]{1,0:T(8,128)(2,1)S(1)}, bf16[208,1280]{1,0:T(8,128)(2,1)S(1)}, u32[]{:S(2)}, u32[]{:S(2)}) collective-permute-start(bf16[208,1280]{1,0:T(8,128)(2,1)S(1)} %collective-permute-done.12.refs_2_), channel_id=1, source_target_pairs={{16,0},{0,16},{17,1},{1,17},{18,2},{2,18},{19,3},{3,19},{20,4},{4,... | collective-permute-start | bytes 1597448 | tf_op jit(solution)/shard_map/ppermute | solution.py:20
  105.3 23.3 %collective-permute-start.19 = (bf16[208,1280]{1,0:T(8,128)(2,1)S(1)}, bf16[208,1280]{1,0:T(8,128)(2,1)S(1)}, u32[]{:S(2)}, u32[]{:S(2)}) collective-permute-start(bf16[208,1280]{1,0:T(8,128)(2,1)S(1)} %collective-permute-done.15.refs_6_), channel_id=1, source_target_pairs={{16,0},{0,16},{17,1},{1,17},{18,2},{2,18},{19,3},{3,19},{20,4},{4,... | collective-permute-start | bytes 1597448 | tf_op jit(solution)/shard_map/ppermute | solution.py:20
  105.7 15.6 %collective-permute-start.20 = (bf16[208,1152]{1,0:T(8,128)(2,1)S(1)}, bf16[208,1152]{1,0:T(8,128)(2,1)S(1)}, u32[]{:S(2)}, u32[]{:S(2)}) collective-permute-start(bf16[208,1152]{1,0:T(8,128)(2,1)S(1)} %copy-done.18), channel_id=1, source_target_pairs={{12,0},{0,4},{4,8},{8,12},{13,1},{1,5},{5,9},{9,13},{14,2},{2,6},{... | collective-permute-start | bytes 1437704 | tf_op jit(solution)/shard_map/ppermute | solution.py:20
  105.7 22.9 %collective-permute-start.18 = (bf16[208,896]{1,0:T(8,128)(2,1)S(1)}, bf16[208,896]{1,0:T(8,128)(2,1)S(1)}, u32[]{:S(2)}, u32[]{:S(2)}) collective-permute-start(bf16[208,896]{1,0:T(8,128)(2,1)S(1)} %copy-done.19), channel_id=1, source_target_pairs={{12,0},{0,4},{4,8},{8,12},{13,1},{1,5},{5,9},{9,13},{14,2},{2,6},{... | collective-permute-start | bytes 1118216 | tf_op jit(solution)/shard_map/ppermute | solution.py:20
  107.1 21.5 %collective-permute-start.17 = (bf16[320,416]{1,0:T(8,128)(2,1)S(1)}, bf16[320,416]{1,0:T(8,128)(2,1)S(1)}, u32[]{:S(2)}, u32[]{:S(2)}) collective-permute-start(bf16[320,416]{1,0:T(8,128)(2,1)S(1)} %get-tuple-element.108), channel_id=1, source_target_pairs={{2,0},{0,2},{3,1},{1,3},{6,4},{4,6},{7,5},{5,7},{10,8},{8,10},{11,... | collective-permute-start | bytes 798728 | tf_op jit(solution)/shard_map/ppermute | solution.py:20
  108.8 19.8 %collective-permute-start.21 = (bf16[320,416]{1,0:T(8,128)(2,1)S(1)}, bf16[320,416]{1,0:T(8,128)(2,1)S(1)}, u32[]{:S(2)}, u32[]{:S(2)}) collective-permute-start(bf16[320,416]{1,0:T(8,128)(2,1)S(1)} %get-tuple-element.107), channel_id=1, source_target_pairs={{2,0},{0,2},{3,1},{1,3},{6,4},{4,6},{7,5},{5,7},{10,8},{8,10},{11,... | collective-permute-start | bytes 798728 | tf_op jit(solution)/shard_map/ppermute | solution.py:20
  121.3 11.6 %collective-permute-start.23 = (bf16[208,1152]{1,0:T(8,128)(2,1)S(1)}, bf16[208,1152]{1,0:T(8,128)(2,1)S(1)}, u32[]{:S(2)}, u32[]{:S(2)}) collective-permute-start(bf16[208,1152]{1,0:T(8,128)(2,1)S(1)} %collective-permute-done.20.refs_10_), channel_id=1, source_target_pairs={{16,0},{0,16},{17,1},{1,17},{18,2},{2,18},{19,3},{3,19},{20,4},{4,... | collective-permute-start | bytes 1437704 | tf_op jit(solution)/shard_map/ppermute | solution.py:20
  128.6 17.5 %collective-permute-start.25 = (bf16[208,1536]{1,0:T(8,128)(2,1)S(1)}, bf16[208,1536]{1,0:T(8,128)(2,1)S(1)}, u32[]{:S(2)}, u32[]{:S(2)}) collective-permute-start(bf16[208,1536]{1,0:T(8,128)(2,1)S(1)} %copy-done.17), channel_id=1, source_target_pairs={{12,0},{0,4},{4,8},{8,12},{13,1},{1,5},{5,9},{9,13},{14,2},{2,6},{... | collective-permute-start | bytes 1916936 | tf_op jit(solution)/shard_map/ppermute | solution.py:20
  132.9 13.7 %collective-permute-start.24 = (bf16[208,896]{1,0:T(8,128)(2,1)S(1)}, bf16[208,896]{1,0:T(8,128)(2,1)S(1)}, u32[]{:S(2)}, u32[]{:S(2)}) collective-permute-start(bf16[208,896]{1,0:T(8,128)(2,1)S(1)} %collective-permute-done.18.refs_6_), channel_id=1, source_target_pairs={{16,0},{0,16},{17,1},{1,17},{18,2},{2,18},{19,3},{3,19},{20,4},{4,... | collective-permute-start | bytes 1118216 | tf_op jit(solution)/shard_map/ppermute | solution.py:20
  (31 other events, 278.8 us)

commit v10 on v8

--- a/solution.py
+++ b/solution.py
@@ -7,7 +7,7 @@
 from jax.experimental.pallas import tpu as pltpu
 from jax.sharding import PartitionSpec as P
 
-FEATURE_SHARES = (11, 11, 11, 11, 10, 10)
+FEATURE_SHARES = (1,) * 8
 LANE_SHARES = (12, 12, 8)
 QUEUE = 2
 VMEM = 16 * 1024 * 1024
@@ -54,31 +54,56 @@
     )(*operands)
 
 
-def products_kernel(sets, groups, spans, before, *refs):
-    row_refs, unit_refs, total = refs[:sets], refs[sets : sets + groups * len(spans)], refs[-1]
-    out = refs[-2]
+def products_kernel(sets, groups, spans, before, held, *refs):
+    row_refs, unit_refs = refs[:sets], refs[sets : sets + groups * len(spans)]
+    extra = 3 if held else 1
+    out, total = refs[-1 - extra], refs[-extra]
+    copies = []
+    if held:
+        rows, sems = refs[-2:]
+        width = 0
+        for step, (a, b) in enumerate(spans):
+            at = 0
+            for i, ref in enumerate(row_refs):
+                copies.append(
+                    pltpu.make_async_copy(
+                        ref.at[:, a:b],
+                        rows.at[at : at + ref.shape[0], width : width + b - a],
+                        sems.at[step, i],
+                    )
+                )
+                copies[-1].start()
+                at += ref.shape[0]
+            width += b - a
+    width = 0
     for step, (a, b) in enumerate(spans):
         units = jnp.concatenate(
             [ref[:, : b - a] for ref in unit_refs[step * groups : (step + 1) * groups]], axis=0
         )
         at = 0
-        for ref in row_refs:
+        for i, ref in enumerate(row_refs):
             spot = slice(at, at + ref.shape[0])
             at += ref.shape[0]
+            if held:
+                copies[step * sets + i].wait()
+                block = rows[spot, width : width + b - a]
+            else:
+                block = ref[:, a:b]
             value = lax.dot_general(
-                ref[:, a:b], units, (((1,), (1,)), ((), ())), preferred_element_type=jnp.float32
+                block, units, (((1,), (1,)), ((), ())), preferred_element_type=jnp.float32
             )
             if step > 0:
                 value += total[spot]
             elif before:
-                value += refs[-3][spot]
+                value += refs[-2 - extra][spot]
             if step < len(spans) - 1:
                 total[spot] = value
             else:
                 out[spot] = value.astype(out.dtype)
-
-
-def products(row_sets, unit_sets, spans, before=None, out_type=jnp.bfloat16):
+        width += b - a
+
+
+def products(row_sets, unit_sets, spans, before=None, out_type=jnp.bfloat16, held=False):
     groups = len(unit_sets) // len(spans)
     shape = (
         sum(r.shape[0] for r in row_sets),
@@ -88,15 +113,22 @@
     if before is not None:
         operands += (before,)
     whole = pl.BlockSpec(memory_space=pltpu.VMEM)
+    scratch = [pltpu.VMEM(shape, jnp.float32)]
+    if held:
+        scratch += [
+            pltpu.VMEM((shape[0], sum(b - a for a, b in spans)), jnp.bfloat16),
+            pltpu.SemaphoreType.DMA((len(spans), len(row_sets))),
+        ]
     return call(
         functools.partial(
-            products_kernel, len(row_sets), groups, tuple(spans), before is not None
+            products_kernel, len(row_sets), groups, tuple(spans), before is not None, held
         ),
         operands,
-        [whole] * len(operands),
+        [ANY if held else whole] * len(row_sets)
+        + [whole] * (len(operands) - len(row_sets)),
         jax.ShapeDtypeStruct(shape, out_type),
         whole,
-        [pltpu.VMEM(shape, jnp.float32)],
+        scratch,
         {},
     )
 
@@ -236,14 +268,11 @@
             waiting.append(shifted(tied(pieces[i + QUEUE], block), "dp", 1))
         return block
 
-    def pass_on(n, *after):
-        i = count + n
-        held = [tied(landed[i], *after)]
-        if i < last:
-            held.append(tied(crossed[i], *after))
-        mates[i], *rest = [mate(block) for block in held]
-        if rest:
-            crossed_mates[i] = rest[0]
+    def pass_own(n, *after):
+        mates[count + n] = mate(tied(landed[count + n], *after))
+
+    def pass_other(n, *after):
+        crossed_mates[count + n] = mate(tied(crossed[count + n], *after))
 
     def local(partial_value, sent):
         pre = summed(partial_value, sent)
@@ -252,7 +281,7 @@
     def batch(lo, hi, now, before=None, out_type=jnp.float32):
         held = [block for i in range(lo, hi) for block in (landed[i], crossed[i])]
         held = lax.optimization_barrier((*held, now))[:-1]
-        return products([tokens, tokens_mate], held, spans[lo:hi], before, out_type)
+        return products([tokens, tokens_mate], held, spans[lo:hi], before, out_type, True)
 
     def activated(partial_value, sent):
         pre = summed(partial_value, sent)
@@ -263,26 +292,29 @@
     tokens_mate = mate(tied(tokens, pieces[0]))
     down_mate = mate(tied(down_weight, pieces[1]))
     advance(*pieces[2:])
+    advance()
     now = advance(tokens_mate, down_mate)
-    value = products(
+    own_value = products(
         [tied(tokens, now), tokens_mate], [gate_weight, up_weight], [(0, width)]
     )
+    now = advance(own_value)
+    own_sent = over_slices(own_value)
+    advance()
+    now = advance()
+    value = batch(0, 4, now)
     now = advance(value)
-    sent = over_slices(value)
-    now = advance()
-    now = advance()
-    here = local(value, [tied(block, now) for block in sent])
+    here = local(own_value, [tied(block, now) for block in own_sent])
     here_mate = mate(here[rows:])
     here = here[:rows]
-    value = batch(0, 2, now)
-    now = advance(value, here)
-    value = batch(2, count - 1, now, value)
+    now = advance(here)
+    value = batch(4, count - 1, now, value)
     now = advance(value, here_mate)
     value = batch(count - 1, count, now, value, jnp.bfloat16)
     halves = [value[:rows], value[rows:]]
     sent = [over_slices(half) for half in halves]
     now = advance(value)
-    pass_on(0, now)
+    pass_own(0, now)
+    pass_other(0, now)
     there, given = (
         activated(half, [tied(block, now) for block in blocks])
         for half, blocks in zip(halves, sent)
@@ -311,9 +343,10 @@
         )
 
     result = write(None, 0)
-    pass_on(1, result)
-    now = advance(result)
-    pass_on(2, now)
+    pass_own(1, result)
+    pass_other(1, result)
+    now = advance(result, crossed[count + 1])
+    pass_own(2, now)
     result = write(result, 1)
     return write(result, 2)
 

time: 143 us -> 148 us (1.035)
  waiting for transfers between devices: 63.2 us -> 48.7 us
  local copies, waits for them, and re-layouts: 16.8 us -> 29 us
  starting transfers between devices: 26.6 us -> 31.9 us
  Pallas kernels: 24.3 us -> 27.7 us
  other arithmetic: 11.7 us -> 9.92 us
    ppermute x29 -> x33, waiting for transfers between devices: 63.2 us -> 48.7 us  [shifted(): return lax.ppermute(block, axis, route)]
    unnamed x34 -> x46, local copies, waits for them, and re-layouts: 11.4 us -> 22.4 us
    ppermute x29 -> x33, starting transfers between devices: 26.6 us -> 31.9 us  [shifted(): return lax.ppermute(block, axis, route)]
    pallas_call x7, Pallas kernels: 24.3 us -> 27.7 us  [call(): pl.pallas_call(kernel, in_specs=in_specs, out_specs=out_spec, out_shape=o...]
    select_n x4 -> x3, other arithmetic: 8.25 us -> 6.37 us  [piece(): return jnp.where(first, gate[:, a:b], up[:, a:b])]
  transfers between devices with their start and end apart: 29 -> 33, of which waited for: 12 -> 12; matrix products, arithmetic and copies ran while one was open for 11% -> 10% of each run, Pallas kernels for 15% -> 17%
where the time goes in v10:
time: 148 us
  waiting for transfers between devices  48.7 us (33%)
  starting transfers between devices  31.9 us (22%)
  local copies, waits for them, and re-layouts  29 us (20%)
  Pallas kernels  27.7 us (19%)
  other arithmetic  9.92 us (7%)
    ppermute x33, waiting for transfers between devices, shifted(): return lax.ppermute(block, axis, route)  48.7 us
    ppermute x33, starting transfers between devices, shifted(): return lax.ppermute(block, axis, route)  31.9 us
    pallas_call x7, Pallas kernels, call(): pl.pallas_call(kernel, in_specs=in_specs, out_specs=out_spec, out_shape=o...  27.7 us
    unnamed x46, local copies, waits for them, and re-layouts  22.4 us
    select_n x3, other arithmetic, piece(): return jnp.where(first, gate[:, a:b], up[:, a:b])  6.37 us
  transfers between devices with their start and end apart: 33, of which 12 were waited for; matrix products, arithmetic and copies ran while one was open for 10% of the time, Pallas kernels for 17%

profile of v10, /device:TPU:0, one launch (start us, length us, event | category | flops | bytes accessed | tf_op | source)
XLA Modules:
  0.0 147.7 jit_solution(1743824449265385269)
XLA Ops:
  3.0 3.0 %collective-permute-start = (bf16[208,1024]{1,0:T(8,128)(2,1)S(1)}, bf16[208,1024]{1,0:T(8,128)(2,1)S(1)}, u32[]{:S(2)}, u32[]{:S(2)}) collective-permute-start(bf16[208,1024]{1,0:T(8,128)(2,1)S(1)} %slice_select_fusion.9), channel_id=1, source_target_pairs={{12,0},{0,4},{4,8},{8,12},{13,1},{1,5},{5,9},{9,13},{14,2},{2,6},{... | collective-permute-start | bytes 1277960 | tf_op jit(solution)/shard_map/ppermute | solution.py:20
  7.6 2.3 %slice.113 = bf16[208,2048]{1,0:T(8,128)(2,1)} slice(bf16[208,8192]{1,0:T(8,128)(2,1)} %refs_4_.5), slice={[0:208], [6144:8192]} | slice | bytes 1703936 | tf_op jit(solution)/shard_map/slice | solution.py:250
  9.9 4.0 %slice_select_fusion.2 = (bf16[208,1024]{1,0:T(8,128)(2,1)}, bf16[208,1024]{1,0:T(8,128)(2,1)}, bf16[208,1024]{1,0:T(8,128)(2,1)}, bf16[208,1024]{1,0:T(8,128)(2...) fusion(bf16[208,8192]{1,0:T(8,128)(2,1)} %refs_3_.1, bf16[208,8192]{1,0:T(8,128)(2,1)} %refs_2_.1, pred[]{:T(512)S(6)} %eq.3), kind=kLoop, calls=%fused_computation.7 | loop fusion | flops 1277952 | bytes 7667713 | tf_op jit(solution)/shard_map/jit(_where)/select_n | solution.py:245
  15.1 3.6 %collective-permute-done.refs_2_ = bf16[208,1024]{1,0:T(8,128)(2,1)S(1)} collective-permute-done((bf16[208,1024]{1,0:T(8,128)(2,1)S(1)}, bf16[208,1024]{1,0:T(8,128)(2,1)S(1)}, u32[]{:S(2)}, u32[]{:S(2)}) %collective-permute-start) | collective-permute-done | bytes 426016 | tf_op jit(solution)/shard_map/ppermute | solution.py:20
  21.2 6.7 %collective-permute-done.4.refs_4_ = bf16[208,1024]{1,0:T(8,128)(2,1)} collective-permute-done((bf16[208,1024]{1,0:T(8,128)(2,1)S(1)}, bf16[208,1024]{1,0:T(8,128)(2,1)}, u32[]{:S(2)}, u32[]{:S(2)}) %collective-permute-start.4) | collective-permute-done | bytes 426016 | tf_op jit(solution)/shard_map/ppermute | solution.py:20
  27.9 9.1 %collective-permute-done.1.refs_6_ = bf16[208,1024]{1,0:T(8,128)(2,1)} collective-permute-done((bf16[208,1024]{1,0:T(8,128)(2,1)S(1)}, bf16[208,1024]{1,0:T(8,128)(2,1)}, u32[]{:S(2)}, u32[]{:S(2)}) %collective-permute-start.1) | collective-permute-done | bytes 426016 | tf_op jit(solution)/shard_map/ppermute | solution.py:20
  43.6 5.6 %shard_map.46 = bf16[640,416]{1,0:T(8,128)(2,1)S(1)} custom-call(bf16[320,8192]{1,0:T(8,128)(2,1)S(1)} %bitcast.2, bf16[320,8192]{1,0:T(8,128)(2,1)S(1)} %collective-permute-done.2.refs_1_, bf16[208,8192]{1,0:T(8,128)(2,1)S(1)} %copy-done.8, bf16[208,8192]{1,0:T(8,128)(2,1)S(1)} %copy-done.9), custom_call_target="tpu_custom_call" | custom-call | flops 1 | bytes 1 | tf_op jit(solution)/shard_map/pallas_call | solution.py:45
  49.2 2.3 %copy-done.2 = bf16[320,8192]{1,0:T(8,128)(2,1)} copy-done((bf16[320,8192]{1,0:T(8,128)(2,1)}, bf16[320,8192]{1,0:T(8,128)(2,1)S(1)}, u32[]{:S(2)}) %copy-start.2) | copy-done | bytes 5242904
  61.2 9.9 %collective-permute-done.13.refs_4_ = bf16[208,1024]{1,0:T(8,128)(2,1)} collective-permute-done((bf16[208,1024]{1,0:T(8,128)(2,1)}, bf16[208,1024]{1,0:T(8,128)(2,1)}, u32[]{:S(2)}, u32[]{:S(2)}) %collective-permute-start.13) | collective-permute-done | bytes 426016 | tf_op jit(solution)/shard_map/ppermute | solution.py:20
  73.7 2.5 %copy-done = bf16[320,8192]{1,0:T(8,128)(2,1)S(1)} copy-done((bf16[320,8192]{1,0:T(8,128)(2,1)S(1)}, bf16[320,8192]{1,0:T(8,128)(2,1)}, u32[]{:S(2)}) %copy-start) | copy-done | bytes 5242904
  76.2 2.5 %copy-done.3 = bf16[320,8192]{1,0:T(8,128)(2,1)S(1)} copy-done((bf16[320,8192]{1,0:T(8,128)(2,1)S(1)}, bf16[320,8192]{1,0:T(8,128)(2,1)}, u32[]{:S(2)}) %copy-start.3) | copy-done | bytes 5242904
  80.7 6.5 %shard_map.47.refs_8_ = f32[640,416]{1,0:T(8,128)S(1)} custom-call(bf16[320,8192]{1,0:T(8,128)(2,1)S(1)} %copy-done, bf16[320,8192]{1,0:T(8,128)(2,1)S(1)} %copy-done.3, bf16[208,1024]{1,0:T(8,128)(2,1)S(1)} %copy-done.16, bf16[208,1024]{1,0:T(8,128)(2,1)S(1)} %copy-done.18, bf16[208,1024]{1,0:T(8,128)(2,1)} %collective-permute-done.4.refs_4_, ...), custom_call_target="tpu_custom_call" | custom-call | flops 1 | bytes 1 | tf_op jit(solution)/shard_map/pallas_call | solution.py:45
  99.0 2.5 %copy-done.1 = bf16[320,8192]{1,0:T(8,128)(2,1)S(1)} copy-done((bf16[320,8192]{1,0:T(8,128)(2,1)S(1)}, bf16[320,8192]{1,0:T(8,128)(2,1)}, u32[]{:S(2)}) %copy-start.1) | copy-done | bytes 5242904
  101.5 2.5 %copy-done.4 = bf16[320,8192]{1,0:T(8,128)(2,1)S(1)} copy-done((bf16[320,8192]{1,0:T(8,128)(2,1)S(1)}, bf16[320,8192]{1,0:T(8,128)(2,1)}, u32[]{:S(2)}) %copy-start.4) | copy-done | bytes 5242904
  104.0 5.2 %shard_map.48.refs_4_ = f32[640,416]{1,0:T(8,128)S(1)} custom-call(bf16[320,8192]{1,0:T(8,128)(2,1)S(1)} %copy-done.1, bf16[320,8192]{1,0:T(8,128)(2,1)S(1)} %copy-done.4, bf16[208,1024]{1,0:T(8,128)(2,1)} %collective-permute-done.7.refs_2_, bf16[208,1024]{1,0:T(8,128)(2,1)S(1)} %copy-done.14, bf16[208,1024]{1,0:T(8,128)(2,1)} %collective-permute-done.13.refs_4_, ...), custom_call_target="tpu_custom_call" | custom-call | flops 1 | bytes 1 | tf_op jit(solution)/shard_map/pallas_call | solution.py:45
  109.4 2.5 %collective-permute-start.26 = (bf16[208,1536]{1,0:T(8,128)(2,1)S(1)}, bf16[208,1536]{1,0:T(8,128)(2,1)S(1)}, u32[]{:S(2)}, u32[]{:S(2)}) collective-permute-start(bf16[208,1536]{1,0:T(8,128)(2,1)S(1)} %collective-permute-done.19.refs_6_), channel_id=1, source_target_pairs={{16,0},{0,16},{17,1},{1,17},{18,2},{2,18},{19,3},{3,19},{20,4},{4,... | collective-permute-start | bytes 1916936 | tf_op jit(solution)/shard_map/ppermute | solution.py:20
  111.9 2.3 %shard_map.49 = bf16[640,416]{1,0:T(8,128)(2,1)S(1)} custom-call(bf16[320,8192]{1,0:T(8,128)(2,1)S(1)} %copy-done.1, bf16[320,8192]{1,0:T(8,128)(2,1)S(1)} %copy-done.4, bf16[208,1024]{1,0:T(8,128)(2,1)} %collective-permute-done.16.refs_2_, bf16[208,1024]{1,0:T(8,128)(2,1)S(1)} %collective-permute-done.18.refs_3_, f32[640,416]{1,0:T(8,128)S(1)} %shard_map.48.refs_4_), custom_call_target="tpu_custom_call" | custom-call | flops 1 | bytes 1 | tf_op jit(solution)/shard_map/pallas_call | solution.py:45
  118.4 4.0 %collective-permute-done.22.refs_6_ = bf16[208,1536]{1,0:T(8,128)(2,1)S(1)} collective-permute-done((bf16[208,1536]{1,0:T(8,128)(2,1)S(1)}, bf16[208,1536]{1,0:T(8,128)(2,1)S(1)}, u32[]{:S(2)}, u32[]{:S(2)}) %collective-permute-start.22) | collective-permute-done | bytes 639008 | tf_op jit(solution)/shard_map/ppermute | solution.py:20
  123.9 3.4 %collective-permute-done.23 = bf16[320,416]{1,0:T(8,128)(2,1)S(1)} collective-permute-done((bf16[320,416]{1,0:T(8,128)(2,1)S(1)}, bf16[320,416]{1,0:T(8,128)(2,1)S(1)}, u32[]{:S(2)}, u32[]{:S(2)}) %collective-permute-start.23) | collective-permute-done | bytes 266272 | tf_op jit(solution)/shard_map/ppermute | solution.py:20
  129.7 3.0 %shard_map.50.refs_10_ = bf16[320,8192]{1,0:T(8,128)(2,1)} custom-call(s32[1]{0:T(128)} %bitcast.side_ref, bf16[320,208]{1,0:T(8,128)(2,1)S(1)} %get-tuple-element.120.refs_0_, bf16[320,208]{1,0:T(8,128)(2,1)S(1)} %collective-permute-done.15.refs_1_, bf16[320,208]{1,0:T(8,128)(2,1)S(1)} %multiply_convert_fusion.1.refs_2_, ...), custom_call_target="tpu_custom_call" | custom-call | flops 1 | bytes 1 | tf_op jit(solution)/shard_map/pallas_call | solution.py:45
  132.7 5.4 %collective-permute-done.29.refs_7_ = bf16[208,1536]{1,0:T(8,128)(2,1)S(1)} collective-permute-done((bf16[208,1536]{1,0:T(8,128)(2,1)S(1)}, bf16[208,1536]{1,0:T(8,128)(2,1)S(1)}, u32[]{:S(2)}, u32[]{:S(2)}) %collective-permute-start.29) | collective-permute-done | bytes 639008 | tf_op jit(solution)/shard_map/ppermute | solution.py:20
  138.6 2.8 %collective-permute-done.32.refs_9_ = bf16[208,1536]{1,0:T(8,128)(2,1)S(1)} collective-permute-done((bf16[208,1536]{1,0:T(8,128)(2,1)S(1)}, bf16[208,1536]{1,0:T(8,128)(2,1)S(1)}, u32[]{:S(2)}, u32[]{:S(2)}) %collective-permute-start.32) | collective-permute-done | bytes 639008 | tf_op jit(solution)/shard_map/ppermute | solution.py:20
  142.3 3.0 %shard_map.51.refs_8_ = bf16[320,8192]{1,0:T(8,128)(2,1)} custom-call(s32[1]{0:T(128)} %bitcast.side_ref, bf16[320,208]{1,0:T(8,128)(2,1)S(1)} %get-tuple-element.120.refs_0_, bf16[320,208]{1,0:T(8,128)(2,1)S(1)} %collective-permute-done.15.refs_1_, bf16[320,208]{1,0:T(8,128)(2,1)S(1)} %multiply_convert_fusion.1.refs_2_, ...), custom_call_target="tpu_custom_call", output_to_operand_aliasing={{}: (11, {})} | custom-call | flops 1 | bytes 1 | tf_op jit(solution)/shard_map/pallas_call | solution.py:45
  145.3 2.3 %shard_map.52 = bf16[320,8192]{1,0:T(8,128)(2,1)} custom-call(s32[1]{0:T(128)} %bitcast.side_ref, bf16[320,208]{1,0:T(8,128)(2,1)S(1)} %get-tuple-element.120.refs_0_, bf16[320,208]{1,0:T(8,128)(2,1)S(1)} %collective-permute-done.15.refs_1_, bf16[320,208]{1,0:T(8,128)(2,1)S(1)} %multiply_convert_fusion.1.refs_2_, ...), custom_call_target="tpu_custom_call", output_to_operand_aliasing={{}: (9, {})} | custom-call | flops 1 | bytes 1 | tf_op jit(solution)/shard_map/pallas_call | solution.py:45
  (110 shorter events, 50.6 us)
Async XLA Ops:
  1.2 40.2 %collective-permute-start.2 = (bf16[320,8192]{1,0:T(8,128)(2,1)}, bf16[320,8192]{1,0:T(8,128)(2,1)S(1)}, u32[]{:S(2)}, u32[]{:S(2)}) collective-permute-start(bf16[320,8192]{1,0:T(8,128)(2,1)} %refs_0_.6), channel_id=1, source_target_pairs={{1,0},{0,1},{3,2},{2,3},{5,4},{4,5},{7,6},{6,7},{9,8},{8,9},{11,10... | collective-permute-start | bytes 15728648 | tf_op jit(solution)/shard_map/ppermute | solution.py:20
  2.9 36.7 %collective-permute-start.3 = (bf16[208,8192]{1,0:T(8,128)(2,1)}, bf16[208,8192]{1,0:T(8,128)(2,1)S(1)}, u32[]{:S(2)}, u32[]{:S(2)}) collective-permute-start(bf16[208,8192]{1,0:T(8,128)(2,1)} %refs_4_.5), channel_id=1, source_target_pairs={{1,0},{0,1},{3,2},{2,3},{5,4},{4,5},{7,6},{6,7},{9,8},{8,9},{11,10... | collective-permute-start | bytes 10223624 | tf_op jit(solution)/shard_map/ppermute | solution.py:20
  3.0 15.7 %collective-permute-start = (bf16[208,1024]{1,0:T(8,128)(2,1)S(1)}, bf16[208,1024]{1,0:T(8,128)(2,1)S(1)}, u32[]{:S(2)}, u32[]{:S(2)}) collective-permute-start(bf16[208,1024]{1,0:T(8,128)(2,1)S(1)} %slice_select_fusion.9), channel_id=1, source_target_pairs={{12,0},{0,4},{4,8},{8,12},{13,1},{1,5},{5,9},{9,13},{14,2},{2,6},{... | collective-permute-start | bytes 1277960 | tf_op jit(solution)/shard_map/ppermute | solution.py:20
  6.0 21.9 %collective-permute-start.4 = (bf16[208,1024]{1,0:T(8,128)(2,1)S(1)}, bf16[208,1024]{1,0:T(8,128)(2,1)}, u32[]{:S(2)}, u32[]{:S(2)}) collective-permute-start(bf16[208,1024]{1,0:T(8,128)(2,1)S(1)} %slice_select_fusion.8), channel_id=1, source_target_pairs={{12,0},{0,4},{4,8},{8,12},{13,1},{1,5},{5,9},{9,13},{14,2},{2,6},{... | collective-permute-start | bytes 1277960 | tf_op jit(solution)/shard_map/ppermute | solution.py:20
  18.7 18.4 %collective-permute-start.1 = (bf16[208,1024]{1,0:T(8,128)(2,1)S(1)}, bf16[208,1024]{1,0:T(8,128)(2,1)}, u32[]{:S(2)}, u32[]{:S(2)}) collective-permute-start(bf16[208,1024]{1,0:T(8,128)(2,1)S(1)} %get-tuple-element.62), channel_id=1, source_target_pairs={{12,0},{0,4},{4,8},{8,12},{13,1},{1,5},{5,9},{9,13},{14,2},{2,6},{... | collective-permute-start | bytes 1277960 | tf_op jit(solution)/shard_map/ppermute | solution.py:20
  18.7 20.1 %collective-permute-start.5 = (bf16[208,1024]{1,0:T(8,128)(2,1)S(1)}, bf16[208,1024]{1,0:T(8,128)(2,1)S(1)}, u32[]{:S(2)}, u32[]{:S(2)}) collective-permute-start(bf16[208,1024]{1,0:T(8,128)(2,1)S(1)} %collective-permute-done.refs_2_), channel_id=1, source_target_pairs={{16,0},{0,16},{17,1},{1,17},{18,2},{2,18},{19,3},{3,19},{20,4},{4,... | collective-permute-start | bytes 1277960 | tf_op jit(solution)/shard_map/ppermute | solution.py:20
  27.9 28.3 %collective-permute-start.8 = (bf16[208,1024]{1,0:T(8,128)(2,1)}, bf16[208,1024]{1,0:T(8,128)(2,1)}, u32[]{:S(2)}, u32[]{:S(2)}) collective-permute-start(bf16[208,1024]{1,0:T(8,128)(2,1)} %get-tuple-element.68), channel_id=1, source_target_pairs={{12,0},{0,4},{4,8},{8,12},{13,1},{1,5},{5,9},{9,13},{14,2},{2,6},{... | collective-permute-start | bytes 1277960 | tf_op jit(solution)/shard_map/ppermute | solution.py:20
  37.0 19.2 %collective-permute-start.9 = (bf16[208,1024]{1,0:T(8,128)(2,1)}, bf16[208,1024]{1,0:T(8,128)(2,1)}, u32[]{:S(2)}, u32[]{:S(2)}) collective-permute-start(bf16[208,1024]{1,0:T(8,128)(2,1)} %collective-permute-done.4.refs_4_), channel_id=1, source_target_pairs={{16,0},{0,16},{17,1},{1,17},{18,2},{2,18},{19,3},{3,19},{20,4},{4,... | collective-permute-start | bytes 1277960 | tf_op jit(solution)/shard_map/ppermute | solution.py:20
  41.4 17.8 %collective-permute-start.7 = (bf16[208,1024]{1,0:T(8,128)(2,1)}, bf16[208,1024]{1,0:T(8,128)(2,1)}, u32[]{:S(2)}, u32[]{:S(2)}) collective-permute-start(bf16[208,1024]{1,0:T(8,128)(2,1)} %get-tuple-element.67), channel_id=1, source_target_pairs={{12,0},{0,4},{4,8},{8,12},{13,1},{1,5},{5,9},{9,13},{14,2},{2,6},{... | collective-permute-start | bytes 1277960 | tf_op jit(solution)/shard_map/ppermute | solution.py:20
  41.4 17.8 %collective-permute-start.10 = (bf16[208,1024]{1,0:T(8,128)(2,1)}, bf16[208,1024]{1,0:T(8,128)(2,1)}, u32[]{:S(2)}, u32[]{:S(2)}) collective-permute-start(bf16[208,1024]{1,0:T(8,128)(2,1)} %collective-permute-done.1.refs_6_), channel_id=1, source_target_pairs={{16,0},{0,16},{17,1},{1,17},{18,2},{2,18},{19,3},{3,19},{20,4},{4,... | collective-permute-start | bytes 1277960 | tf_op jit(solution)/shard_map/ppermute | solution.py:20
  54.5 35.0 %collective-permute-start.6 = (bf16[640,416]{0,1:T(8,128)(2,1)}, bf16[640,416]{0,1:T(8,128)(2,1)}, u32[]{:S(2)}, u32[]{:S(2)}) collective-permute-start(bf16[640,416]{0,1:T(8,128)(2,1)} %copy.7), channel_id=1, source_target_pairs={{2,0},{0,2},{3,1},{1,3},{6,4},{4,6},{7,5},{5,7},{10,8},{8,10},{11,... | collective-permute-start | bytes 1597448 | tf_op jit(solution)/shard_map/ppermute | solution.py:20
  56.3 14.9 %collective-permute-start.13 = (bf16[208,1024]{1,0:T(8,128)(2,1)}, bf16[208,1024]{1,0:T(8,128)(2,1)}, u32[]{:S(2)}, u32[]{:S(2)}) collective-permute-start(bf16[208,1024]{1,0:T(8,128)(2,1)} %get-tuple-element.72), channel_id=1, source_target_pairs={{12,0},{0,4},{4,8},{8,12},{13,1},{1,5},{5,9},{9,13},{14,2},{2,6},{... | collective-permute-start | bytes 1277960 | tf_op jit(solution)/shard_map/ppermute | solution.py:20
  57.6 13.5 %collective-permute-start.12 = (bf16[208,1024]{1,0:T(8,128)(2,1)}, bf16[208,1024]{1,0:T(8,128)(2,1)S(1)}, u32[]{:S(2)}, u32[]{:S(2)}) collective-permute-start(bf16[208,1024]{1,0:T(8,128)(2,1)} %collective-permute-done.8.refs_8_), channel_id=1, source_target_pairs={{16,0},{0,16},{17,1},{1,17},{18,2},{2,18},{19,3},{3,19},{20,4},{4,... | collective-permute-start | bytes 1277960 | tf_op jit(solution)/shard_map/ppermute | solution.py:20
  59.2 29.2 %collective-permute-start.11 = (bf16[208,1024]{1,0:T(8,128)(2,1)}, bf16[208,1024]{1,0:T(8,128)(2,1)}, u32[]{:S(2)}, u32[]{:S(2)}) collective-permute-start(bf16[208,1024]{1,0:T(8,128)(2,1)} %get-tuple-element.71), channel_id=1, source_target_pairs={{12,0},{0,4},{4,8},{8,12},{13,1},{1,5},{5,9},{9,13},{14,2},{2,6},{... | collective-permute-start | bytes 1277960 | tf_op jit(solution)/shard_map/ppermute | solution.py:20
  60.7 27.6 %collective-permute-start.14 = (bf16[208,1024]{1,0:T(8,128)(2,1)}, bf16[208,1024]{1,0:T(8,128)(2,1)S(1)}, u32[]{:S(2)}, u32[]{:S(2)}) collective-permute-start(bf16[208,1024]{1,0:T(8,128)(2,1)} %collective-permute-done.7.refs_2_), channel_id=1, source_target_pairs={{16,0},{0,16},{17,1},{1,17},{18,2},{2,18},{19,3},{3,19},{20,4},{4,... | collective-permute-start | bytes 1277960 | tf_op jit(solution)/shard_map/ppermute | solution.py:20
  71.1 24.6 %collective-permute-start.17 = (bf16[208,1024]{1,0:T(8,128)(2,1)}, bf16[208,1024]{1,0:T(8,128)(2,1)}, u32[]{:S(2)}, u32[]{:S(2)}) collective-permute-start(bf16[208,1024]{1,0:T(8,128)(2,1)} %collective-permute-done.13.refs_4_), channel_id=1, source_target_pairs={{16,0},{0,16},{17,1},{1,17},{18,2},{2,18},{19,3},{3,19},{20,4},{4,... | collective-permute-start | bytes 1277960 | tf_op jit(solution)/shard_map/ppermute | solution.py:20
  72.7 23.0 %collective-permute-start.16 = (bf16[208,1024]{1,0:T(8,128)(2,1)}, bf16[208,1024]{1,0:T(8,128)(2,1)}, u32[]{:S(2)}, u32[]{:S(2)}) collective-permute-start(bf16[208,1024]{1,0:T(8,128)(2,1)} %get-tuple-element.84), channel_id=1, source_target_pairs={{12,0},{0,4},{4,8},{8,12},{13,1},{1,5},{5,9},{9,13},{14,2},{2,6},{... | collective-permute-start | bytes 1277960 | tf_op jit(solution)/shard_map/ppermute | solution.py:20
  93.3 16.0 %collective-permute-start.19 = (bf16[208,1536]{1,0:T(8,128)(2,1)}, bf16[208,1536]{1,0:T(8,128)(2,1)S(1)}, u32[]{:S(2)}, u32[]{:S(2)}) collective-permute-start(bf16[208,1536]{1,0:T(8,128)(2,1)} %get-tuple-element.86), channel_id=1, source_target_pairs={{12,0},{0,4},{4,8},{8,12},{13,1},{1,5},{5,9},{9,13},{14,2},{2,6},{... | collective-permute-start | bytes 1916936 | tf_op jit(solution)/shard_map/ppermute | solution.py:20
  95.7 16.2 %collective-permute-start.18 = (bf16[208,1024]{1,0:T(8,128)(2,1)}, bf16[208,1024]{1,0:T(8,128)(2,1)S(1)}, u32[]{:S(2)}, u32[]{:S(2)}) collective-permute-start(bf16[208,1024]{1,0:T(8,128)(2,1)} %collective-permute-done.16.refs_2_), channel_id=1, source_target_pairs={{16,0},{0,16},{17,1},{1,17},{18,2},{2,18},{19,3},{3,19},{20,4},{4,... | collective-permute-start | bytes 1277960 | tf_op jit(solution)/shard_map/ppermute | solution.py:20
  97.3 25.1 %collective-permute-start.22 = (bf16[208,1536]{1,0:T(8,128)(2,1)S(1)}, bf16[208,1536]{1,0:T(8,128)(2,1)S(1)}, u32[]{:S(2)}, u32[]{:S(2)}) collective-permute-start(bf16[208,1536]{1,0:T(8,128)(2,1)S(1)} %copy-done.20), channel_id=1, source_target_pairs={{12,0},{0,4},{4,8},{8,12},{13,1},{1,5},{5,9},{9,13},{14,2},{2,6},{... | collective-permute-start | bytes 1916936 | tf_op jit(solution)/shard_map/ppermute | solution.py:20
  109.4 18.0 %collective-permute-start.26 = (bf16[208,1536]{1,0:T(8,128)(2,1)S(1)}, bf16[208,1536]{1,0:T(8,128)(2,1)S(1)}, u32[]{:S(2)}, u32[]{:S(2)}) collective-permute-start(bf16[208,1536]{1,0:T(8,128)(2,1)S(1)} %collective-permute-done.19.refs_6_), channel_id=1, source_target_pairs={{16,0},{0,16},{17,1},{1,17},{18,2},{2,18},{19,3},{3,19},{20,4},{4,... | collective-permute-start | bytes 1916936 | tf_op jit(solution)/shard_map/ppermute | solution.py:20
  115.1 12.3 %collective-permute-start.23 = (bf16[320,416]{1,0:T(8,128)(2,1)S(1)}, bf16[320,416]{1,0:T(8,128)(2,1)S(1)}, u32[]{:S(2)}, u32[]{:S(2)}) collective-permute-start(bf16[320,416]{1,0:T(8,128)(2,1)S(1)} %get-tuple-element.117), channel_id=1, source_target_pairs={{2,0},{0,2},{3,1},{1,3},{6,4},{4,6},{7,5},{5,7},{10,8},{8,10},{11,... | collective-permute-start | bytes 798728 | tf_op jit(solution)/shard_map/ppermute | solution.py:20
  116.3 21.7 %collective-permute-start.25 = (bf16[208,2048]{1,0:T(8,128)(2,1)S(1)}, bf16[208,2048]{1,0:T(8,128)(2,1)S(1)}, u32[]{:S(2)}, u32[]{:S(2)}) collective-permute-start(bf16[208,2048]{1,0:T(8,128)(2,1)S(1)} %copy-done.19), channel_id=1, source_target_pairs={{12,0},{0,4},{4,8},{8,12},{13,1},{1,5},{5,9},{9,13},{14,2},{2,6},{... | collective-permute-start | bytes 2555912 | tf_op jit(solution)/shard_map/ppermute | solution.py:20
  122.4 15.7 %collective-permute-start.29 = (bf16[208,1536]{1,0:T(8,128)(2,1)S(1)}, bf16[208,1536]{1,0:T(8,128)(2,1)S(1)}, u32[]{:S(2)}, u32[]{:S(2)}) collective-permute-start(bf16[208,1536]{1,0:T(8,128)(2,1)S(1)} %collective-permute-done.22.refs_6_), channel_id=1, source_target_pairs={{16,0},{0,16},{17,1},{1,17},{18,2},{2,18},{19,3},{3,19},{20,4},{4,... | collective-permute-start | bytes 1916936 | tf_op jit(solution)/shard_map/ppermute | solution.py:20
  (32 other events, 218.4 us)

commit v11 on v8

--- a/solution.py
+++ b/solution.py
@@ -7,9 +7,17 @@
 from jax.experimental.pallas import tpu as pltpu
 from jax.sharding import PartitionSpec as P
 
-FEATURE_SHARES = (11, 11, 11, 11, 10, 10)
-LANE_SHARES = (12, 12, 8)
+FEATURE_SHARES = (1,) * 8
+LANE_SHARES = (10, 12, 10)
 QUEUE = 2
+OWN, OWN_SUM, OWN_MATE = 1, 4, 6
+BATCHES = ((5, 0, 4), (7, 4, 7), (8, 7, 8))
+PASS = (9, 9)
+BEFORE_LAST = (1, 0, 0)
+WHOLE_FIRST = True
+SWAP_WAIT = 2
+SPLIT = False
+HOLD = 1
 VMEM = 16 * 1024 * 1024
 ANY = pl.BlockSpec(memory_space=pl.ANY)
 
@@ -54,15 +62,15 @@
     )(*operands)
 
 
-def products_kernel(sets, groups, spans, before, *refs):
-    row_refs, unit_refs, total = refs[:sets], refs[sets : sets + groups * len(spans)], refs[-1]
-    out = refs[-2]
+def products_kernel(sets, groups, spans, before, outs, *refs):
+    row_refs, unit_refs = refs[:sets], refs[sets : sets + groups * len(spans)]
+    out_refs, total = refs[-1 - outs : -1], refs[-1]
     for step, (a, b) in enumerate(spans):
         units = jnp.concatenate(
             [ref[:, : b - a] for ref in unit_refs[step * groups : (step + 1) * groups]], axis=0
         )
         at = 0
-        for ref in row_refs:
+        for i, ref in enumerate(row_refs):
             spot = slice(at, at + ref.shape[0])
             at += ref.shape[0]
             value = lax.dot_general(
@@ -71,32 +79,71 @@
             if step > 0:
                 value += total[spot]
             elif before:
-                value += refs[-3][spot]
+                value += refs[-2 - outs][spot]
             if step < len(spans) - 1:
                 total[spot] = value
+            elif outs == 1:
+                out_refs[0][spot] = value.astype(out_refs[0].dtype)
             else:
-                out[spot] = value.astype(out.dtype)
-
-
-def products(row_sets, unit_sets, spans, before=None, out_type=jnp.bfloat16):
+                out_refs[i][...] = value.astype(out_refs[i].dtype)
+
+
+WHOLE = pl.BlockSpec(memory_space=pltpu.VMEM)
+
+
+def products(row_sets, unit_sets, spans, before=None, out_type=jnp.bfloat16, split=False):
     groups = len(unit_sets) // len(spans)
-    shape = (
-        sum(r.shape[0] for r in row_sets),
-        sum(u.shape[0] for u in unit_sets[:groups]),
-    )
+    count = sum(u.shape[0] for u in unit_sets[:groups])
+    shape = (sum(r.shape[0] for r in row_sets), count)
+    shapes = [(r.shape[0], count) for r in row_sets] if split else [shape]
     operands = (*row_sets, *unit_sets)
     if before is not None:
         operands += (before,)
-    whole = pl.BlockSpec(memory_space=pltpu.VMEM)
-    return call(
+    found = call(
         functools.partial(
-            products_kernel, len(row_sets), groups, tuple(spans), before is not None
+            products_kernel, len(row_sets), groups, tuple(spans), before is not None, len(shapes)
         ),
         operands,
-        [whole] * len(operands),
-        jax.ShapeDtypeStruct(shape, out_type),
-        whole,
+        [WHOLE] * len(operands),
+        [jax.ShapeDtypeStruct(s, out_type) for s in shapes],
+        [WHOLE] * len(shapes),
         [pltpu.VMEM(shape, jnp.float32)],
+        {},
+    )
+    return found if split else found[0]
+
+
+def activation_kernel(count, turned, side_ref, *refs):
+    terms, outs = refs[:-2], refs[-2:]
+    per = len(terms) // count
+    rows, units = outs[0].shape
+    first = side_ref[0] == 0
+    at = 0
+    for i in range(count):
+        block = terms[i * per : (i + 1) * per]
+        for start in range(0, block[0].shape[0], rows):
+            total = block[0][start : start + rows].astype(jnp.float32)
+            for ref in block[1:]:
+                total += ref[start : start + rows].astype(jnp.float32)
+            gate, up = total[:, :units], total[:, units:]
+            if turned:
+                gate, up = jnp.where(first, gate, up), jnp.where(first, up, gate)
+            outs[at][...] = (gate / (1.0 + jnp.exp(-gate)) * up).astype(outs[at].dtype)
+            at += 1
+
+
+def activated(side, blocks, rows, turned):
+    operands = [side]
+    for value, others in blocks:
+        operands += [value, *others]
+    shape = (rows, blocks[0][0].shape[1] // 2)
+    return call(
+        functools.partial(activation_kernel, len(blocks), turned),
+        operands,
+        [pl.BlockSpec(memory_space=pltpu.SMEM)] + [WHOLE] * (len(operands) - 1),
+        [jax.ShapeDtypeStruct(shape, jnp.bfloat16)] * 2,
+        [WHOLE] * 2,
+        [],
         {},
     )
 
@@ -180,17 +227,6 @@
     ]
 
 
-def summed(partial_value, sent):
-    total = partial_value.astype(jnp.float32)
-    for block in sent:
-        total = total + block.astype(jnp.float32)
-    return total
-
-
-def gated(gate, up):
-    return (jax.nn.silu(gate) * up).astype(jnp.bfloat16)
-
-
 def on_device(tokens, gate_weight, up_weight, down_weight):
     units, width = gate_weight.shape
     rows = tokens.shape[0]
@@ -227,7 +263,7 @@
     def advance(*after):
         i = len(landed)
         held = [*after, *landed[-1:]]
-        held += [crossed[j] for j in range(count) if j + 2 == i]
+        held += [crossed[j] for j in range(count) if j + SWAP_WAIT == i]
         block = tied(waiting[i], *held)
         landed.append(block)
         if i < last:
@@ -236,58 +272,67 @@
             waiting.append(shifted(tied(pieces[i + QUEUE], block), "dp", 1))
         return block
 
-    def pass_on(n, *after):
-        i = count + n
-        held = [tied(landed[i], *after)]
-        if i < last:
-            held.append(tied(crossed[i], *after))
-        mates[i], *rest = [mate(block) for block in held]
-        if rest:
-            crossed_mates[i] = rest[0]
-
-    def local(partial_value, sent):
-        pre = summed(partial_value, sent)
-        return gated(pre[:, :units], pre[:, units:])
-
-    def batch(lo, hi, now, before=None, out_type=jnp.float32):
+    def pass_own(n, *after):
+        mates[count + n] = mate(tied(landed[count + n], *after))
+
+    def pass_other(n, *after):
+        crossed_mates[count + n] = mate(tied(crossed[count + n], *after))
+
+    def batch(lo, hi, now, before=None, last_one=False):
         held = [block for i in range(lo, hi) for block in (landed[i], crossed[i])]
         held = lax.optimization_barrier((*held, now))[:-1]
-        return products([tokens, tokens_mate], held, spans[lo:hi], before, out_type)
-
-    def activated(partial_value, sent):
-        pre = summed(partial_value, sent)
-        half = pre.shape[1] // 2
-        left, right = pre[:, :half], pre[:, half:]
-        return gated(jnp.where(first, left, right), jnp.where(first, right, left))
+        return products(
+            [tokens, tokens_mate],
+            held,
+            spans[lo:hi],
+            before,
+            jnp.bfloat16 if last_one else jnp.float32,
+            last_one and SPLIT,
+        )
 
     tokens_mate = mate(tied(tokens, pieces[0]))
     down_mate = mate(tied(down_weight, pieces[1]))
-    advance(*pieces[2:])
-    now = advance(tokens_mate, down_mate)
-    value = products(
-        [tied(tokens, now), tokens_mate], [gate_weight, up_weight], [(0, width)]
-    )
-    now = advance(value)
-    sent = over_slices(value)
-    now = advance()
-    now = advance()
-    here = local(value, [tied(block, now) for block in sent])
-    here_mate = mate(here[rows:])
-    here = here[:rows]
-    value = batch(0, 2, now)
-    now = advance(value, here)
-    value = batch(2, count - 1, now, value)
-    now = advance(value, here_mate)
-    value = batch(count - 1, count, now, value, jnp.bfloat16)
-    halves = [value[:rows], value[rows:]]
-    sent = [over_slices(half) for half in halves]
-    now = advance(value)
-    pass_on(0, now)
-    there, given = (
-        activated(half, [tied(block, now) for block in blocks])
-        for half, blocks in zip(halves, sent)
+    due = {0: pieces[2:], OWN: [tokens_mate, down_mate]}
+    value = own_value = None
+    for i in range(last):
+        now = advance(*due.get(i, []))
+        after = due.setdefault(i + 1, [])
+        if i == OWN:
+            own_value = products(
+                [tied(tokens, now), tokens_mate], [gate_weight, up_weight], [(0, width)]
+            )
+            own_sent = over_slices(own_value)
+            after.append(own_value)
+        if i == OWN_SUM:
+            here, given = activated(
+                side, [(own_value, [tied(block, now) for block in own_sent])], rows, False
+            )
+            here_mate = mate(given)
+            after.append(here)
+            due.setdefault(OWN_MATE, []).append(here_mate)
+        for stage, lo, hi in BATCHES:
+            if i == stage:
+                value = batch(lo, hi, now, value, hi == count)
+                halves = value if isinstance(value, (list, tuple)) else [value]
+                after += halves
+                if hi == count:
+                    sent = [over_slices(half) for half in halves]
+        if i == PASS[0]:
+            pass_own(0, now)
+        if i == PASS[1]:
+            pass_other(0, now)
+    there, given = activated(
+        side,
+        [
+            (half, [tied(block, now) for block in blocks])
+            for half, blocks in zip(halves, sent)
+        ],
+        rows,
+        True,
     )
     there_mate = mate(given)
+    if HOLD:
+        there_mate = tied(there_mate, crossed[count + 1])
 
     def write(result, *which):
         parts, arrived = [], []
@@ -311,11 +356,14 @@
         )
 
     result = write(None, 0)
-    pass_on(1, result)
-    now = advance(result)
-    pass_on(2, now)
-    result = write(result, 1)
-    return write(result, 2)
+    pass_own(1, result)
+    pass_other(1, result)
+    waits = (crossed[count + 1], mates[count + 1], crossed_mates[count + 1])
+    now = advance(result, *(wait for wait, use in zip(waits, BEFORE_LAST) if use))
+    pass_own(2, now)
+    for n in (2, 1) if WHOLE_FIRST else (1, 2):
+        result = write(result, n)
+    return result
 
 
 def solution(mesh):

time: 143 us -> 144 us (level)
  waiting for transfers between devices: 63.2 us -> 47.5 us
  local copies, waits for them, and re-layouts: 16.8 us -> 31.1 us
  Pallas kernels: 24.3 us -> 28 us
  other arithmetic: 11.7 us -> 10.2 us
    ppermute x29 -> x32, waiting for transfers between devices: 63.2 us -> 47.5 us  [shifted(): return lax.ppermute(block, axis, route)]
    unnamed x34 -> x54, local copies, waits for them, and re-layouts: 11.4 us -> 21.4 us
    pallas_call x7 -> x9, Pallas kernels: 24.3 us -> 28 us  [call(): pl.pallas_call(kernel, in_specs=in_specs, out_specs=out_spec, out_shape=o...]
    pallas_call x1 -> x2, local copies, waits for them, and re-layouts: 2.15 us -> 4.28 us  [call(): pl.pallas_call(kernel, in_specs=in_specs, out_specs=out_spec, out_shape=o...]
    optimization_barrier x1 -> x2, local copies, waits for them, and re-layouts: 2.14 us -> 4.26 us  [tied(): return lax.optimization_barrier((value, *earlier))[0] if earlier else value]
    select_n x1 -> x2, other arithmetic: 1.2 us -> 3.21 us  [piece(): return jnp.where(first, down[:, a:mid], down[:, mid:b])]
    add x2 -> x0, other arithmetic: 1.65 us -> none  [summed(): total = total + block.astype(jnp.float32)]
    select_n x4 -> x3, other arithmetic: 8.25 us -> 6.94 us  [piece(): return jnp.where(first, gate[:, a:b], up[:, a:b])]
  transfers between devices with their start and end apart: 29 -> 32, of which waited for: 12 -> 14; matrix products, arithmetic and copies ran while one was open for 11% -> 13% of each run, Pallas kernels for 15% -> 17%
where the time goes in v11:
time: 144 us
  waiting for transfers between devices  47.5 us (33%)
  local copies, waits for them, and re-layouts  31.1 us (22%)
  Pallas kernels  28 us (19%)
  starting transfers between devices  26.4 us (18%)
  other arithmetic  10.2 us (7%)
    ppermute x32, waiting for transfers between devices, shifted(): return lax.ppermute(block, axis, route)  47.5 us
    pallas_call x9, Pallas kernels, call(): pl.pallas_call(kernel, in_specs=in_specs, out_specs=out_spec, out_shape=o...  28 us
    ppermute x32, starting transfers between devices, shifted(): return lax.ppermute(block, axis, route)  26.4 us
    unnamed x54, local copies, waits for them, and re-layouts  21.4 us
    select_n x3, other arithmetic, piece(): return jnp.where(first, gate[:, a:b], up[:, a:b])  6.94 us
    pallas_call x2, local copies, waits for them, and re-layouts, call(): pl.pallas_call(kernel, in_specs=in_specs, out_specs=out_spec, out_shape=o...  4.28 us
    optimization_barrier x2, local copies, waits for them, and re-layouts, tied(): return lax.optimization_barrier((value, *earlier))[0] if earlier else value  4.26 us
    select_n x2, other arithmetic, piece(): return jnp.where(first, down[:, a:mid], down[:, mid:b])  3.21 us
  transfers between devices with their start and end apart: 32, of which 14 were waited for; matrix products, arithmetic and copies ran while one was open for 13% of the time, Pallas kernels for 17%

profile of v11, /device:TPU:0, one launch (start us, length us, event | category | flops | bytes accessed | tf_op | source)
XLA Modules:
  0.0 143.6 jit_solution(4450927452378102819)
XLA Ops:
  3.2 3.0 %collective-permute-start.3 = (bf16[208,1024]{1,0:T(8,128)(2,1)S(1)}, bf16[208,1024]{1,0:T(8,128)(2,1)S(1)}, u32[]{:S(2)}, u32[]{:S(2)}) collective-permute-start(bf16[208,1024]{1,0:T(8,128)(2,1)S(1)} %slice_select_fusion.9), channel_id=1, source_target_pairs={{12,0},{0,4},{4,8},{8,12},{13,1},{1,5},{5,9},{9,13},{14,2},{2,6},{... | collective-permute-start | bytes 1277960 | tf_op jit(solution)/shard_map/ppermute | solution.py:28
  7.8 2.3 %slice_select_fusion = bf16[208,1536]{1,0:T(8,128)(2,1)} fusion(bf16[208,8192]{1,0:T(8,128)(2,1)} %refs_4_.5, pred[]{:T(512)S(6)} %eq.3), kind=kLoop, calls=%fused_computation | loop fusion | flops 319488 | bytes 1916929 | tf_op jit(solution)/shard_map/jit(_where)/select_n | solution.py:255
  11.0 4.4 %slice_select_fusion.2 = (bf16[208,1024]{1,0:T(8,128)(2,1)}, bf16[208,1024]{1,0:T(8,128)(2,1)}, bf16[208,1024]{1,0:T(8,128)(2,1)}, bf16[208,1024]{1,0:T(8,128)(2...) fusion(bf16[208,8192]{1,0:T(8,128)(2,1)} %refs_3_.1, bf16[208,8192]{1,0:T(8,128)(2,1)} %refs_2_.1, pred[]{:T(512)S(6)} %eq.3), kind=kLoop, calls=%fused_computation.2 | loop fusion | flops 1277952 | bytes 7667713 | tf_op jit(solution)/shard_map/jit(_where)/select_n | solution.py:249
  16.5 2.3 %collective-permute-done.3.refs_2_ = bf16[208,1024]{1,0:T(8,128)(2,1)S(1)} collective-permute-done((bf16[208,1024]{1,0:T(8,128)(2,1)S(1)}, bf16[208,1024]{1,0:T(8,128)(2,1)S(1)}, u32[]{:S(2)}, u32[]{:S(2)}) %collective-permute-start.3) | collective-permute-done | bytes 426016 | tf_op jit(solution)/shard_map/ppermute | solution.py:28
  21.4 6.7 %collective-permute-done.refs_4_ = bf16[208,1024]{1,0:T(8,128)(2,1)} collective-permute-done((bf16[208,1024]{1,0:T(8,128)(2,1)S(1)}, bf16[208,1024]{1,0:T(8,128)(2,1)}, u32[]{:S(2)}, u32[]{:S(2)}) %collective-permute-start) | collective-permute-done | bytes 426016 | tf_op jit(solution)/shard_map/ppermute | solution.py:28
  31.7 5.6 %shard_map.46.refs_0_ = bf16[640,416]{1,0:T(8,128)(2,1)S(1)} custom-call(bf16[320,8192]{1,0:T(8,128)(2,1)S(1)} %bitcast.2, bf16[320,8192]{1,0:T(8,128)(2,1)S(1)} %collective-permute-done.1.refs_1_, bf16[208,8192]{1,0:T(8,128)(2,1)S(1)} %copy-done.6, bf16[208,8192]{1,0:T(8,128)(2,1)S(1)} %copy-done.7), custom_call_target="tpu_custom_call" | custom-call | flops 1 | bytes 1 | tf_op jit(solution)/shard_map/pallas_call | solution.py:53
  40.7 2.1 %copy.7 = bf16[640,416]{0,1:T(8,128)(2,1)} copy(bf16[640,416]{1,0:T(8,128)(2,1)} %copy-done.8) | data formatting | bytes 1064960 | tf_op jit(solution)/shard_map/pallas_call | solution.py:53
  48.1 7.4 %collective-permute-done.7.refs_2_ = bf16[208,1024]{1,0:T(8,128)(2,1)} collective-permute-done((bf16[208,1024]{1,0:T(8,128)(2,1)}, bf16[208,1024]{1,0:T(8,128)(2,1)}, u32[]{:S(2)}, u32[]{:S(2)}) %collective-permute-start.7) | collective-permute-done | bytes 426016 | tf_op jit(solution)/shard_map/ppermute | solution.py:28
  57.2 2.1 %copy.8.refs_1_ = bf16[640,416]{1,0:T(8,128)(2,1)} copy(bf16[640,416]{0,1:T(8,128)(2,1)} %collective-permute-done.4) | data formatting | bytes 1064960 | tf_op jit(solution)/shard_map/optimization_barrier | solution.py:40
  66.4 2.5 %copy-done = bf16[320,8192]{1,0:T(8,128)(2,1)S(1)} copy-done((bf16[320,8192]{1,0:T(8,128)(2,1)S(1)}, bf16[320,8192]{1,0:T(8,128)(2,1)}, u32[]{:S(2)}) %copy-start) | copy-done | bytes 5242904
  68.8 2.5 %copy-done.2 = bf16[320,8192]{1,0:T(8,128)(2,1)S(1)} copy-done((bf16[320,8192]{1,0:T(8,128)(2,1)S(1)}, bf16[320,8192]{1,0:T(8,128)(2,1)}, u32[]{:S(2)}) %copy-start.2) | copy-done | bytes 5242904
  73.3 4.6 %shard_map.48.refs_8_ = f32[640,416]{1,0:T(8,128)S(1)} custom-call(bf16[320,8192]{1,0:T(8,128)(2,1)S(1)} %copy-done, bf16[320,8192]{1,0:T(8,128)(2,1)S(1)} %copy-done.2, bf16[208,1024]{1,0:T(8,128)(2,1)S(1)} %copy-done.21, bf16[208,1024]{1,0:T(8,128)(2,1)S(1)} %copy-done.23, bf16[208,1024]{1,0:T(8,128)(2,1)} %collective-permute-done.refs_4_, ...), custom_call_target="tpu_custom_call" | custom-call | flops 1 | bytes 1 | tf_op jit(solution)/shard_map/pallas_call | solution.py:53
  80.5 2.2 %collective-permute-done.14.refs_2_ = bf16[208,1024]{1,0:T(8,128)(2,1)S(1)} collective-permute-done((bf16[208,1024]{1,0:T(8,128)(2,1)}, bf16[208,1024]{1,0:T(8,128)(2,1)S(1)}, u32[]{:S(2)}, u32[]{:S(2)}) %collective-permute-start.14) | collective-permute-done | bytes 426016 | tf_op jit(solution)/shard_map/ppermute | solution.py:28
  84.5 8.5 %collective-permute-done.20.refs_7_ = bf16[208,1024]{1,0:T(8,128)(2,1)S(1)} collective-permute-done((bf16[208,1024]{1,0:T(8,128)(2,1)}, bf16[208,1024]{1,0:T(8,128)(2,1)S(1)}, u32[]{:S(2)}, u32[]{:S(2)}) %collective-permute-start.20) | collective-permute-done | bytes 426016 | tf_op jit(solution)/shard_map/ppermute | solution.py:28
  93.0 3.6 %shard_map.49.refs_4_ = f32[640,416]{1,0:T(8,128)S(1)} custom-call(bf16[320,8192]{1,0:T(8,128)(2,1)S(1)} %copy-done, bf16[320,8192]{1,0:T(8,128)(2,1)S(1)} %copy-done.2, bf16[208,1024]{1,0:T(8,128)(2,1)} %collective-permute-done.7.refs_2_, bf16[208,1024]{1,0:T(8,128)(2,1)} %collective-permute-done.16.refs_3_, ...), custom_call_target="tpu_custom_call" | custom-call | flops 1 | bytes 1 | tf_op jit(solution)/shard_map/pallas_call | solution.py:53
  98.8 3.4 %collective-permute-done.18.refs_3_ = bf16[208,1024]{1,0:T(8,128)(2,1)S(1)} collective-permute-done((bf16[208,1024]{1,0:T(8,128)(2,1)S(1)}, bf16[208,1024]{1,0:T(8,128)(2,1)S(1)}, u32[]{:S(2)}, u32[]{:S(2)}) %collective-permute-start.18) | collective-permute-done | bytes 426016 | tf_op jit(solution)/shard_map/ppermute | solution.py:28
  103.8 2.1 %copy.9 = bf16[640,416]{0,1:T(8,128)(2,1)} copy(bf16[640,416]{1,0:T(8,128)(2,1)} %copy-done.10) | data formatting | bytes 1064960 | tf_op jit(solution)/shard_map/pallas_call | solution.py:53
  112.2 3.4 %collective-permute-done.21 = bf16[640,416]{0,1:T(8,128)(2,1)} collective-permute-done((bf16[640,416]{0,1:T(8,128)(2,1)}, bf16[640,416]{0,1:T(8,128)(2,1)}, u32[]{:S(2)}, u32[]{:S(2)}) %collective-permute-start.21) | collective-permute-done | bytes 532512 | tf_op jit(solution)/shard_map/ppermute | solution.py:28
  115.5 2.1 %copy.10.refs_1_ = bf16[640,416]{1,0:T(8,128)(2,1)} copy(bf16[640,416]{0,1:T(8,128)(2,1)} %collective-permute-done.21) | data formatting | bytes 1064960 | tf_op jit(solution)/shard_map/optimization_barrier | solution.py:40
  122.1 2.2 %collective-permute-done.24.refs_7_ = bf16[208,1536]{1,0:T(8,128)(2,1)} collective-permute-done((bf16[208,1536]{1,0:T(8,128)(2,1)}, bf16[208,1536]{1,0:T(8,128)(2,1)}, u32[]{:S(2)}, u32[]{:S(2)}) %collective-permute-start.24) | collective-permute-done | bytes 639008 | tf_op jit(solution)/shard_map/ppermute | solution.py:28
  128.1 4.2 %shard_map.52.refs_8_ = bf16[320,8192]{1,0:T(8,128)(2,1)} custom-call(s32[1]{0:T(128)} %bitcast.side_ref, bf16[320,208]{1,0:T(8,128)(2,1)S(1)} %copy-done.15, bf16[320,208]{1,0:T(8,128)(2,1)S(1)} %copy-done.18, bf16[320,208]{1,0:T(8,128)(2,1)S(1)} %get-tuple-element.105.refs_2_, bf16[320,208]{1,0:T(8,128)(2,1)S(1)} %collective-permute-done.23.refs_3_, ...), custom_call_target="tpu_custom_call" | custom-call | flops 1 | bytes 1 | tf_op jit(solution)/shard_map/pallas_call | solution.py:53
  133.0 2.3 %collective-permute-done.31.refs_7_ = bf16[208,2560]{1,0:T(8,128)(2,1)S(1)} collective-permute-done((bf16[208,2560]{1,0:T(8,128)(2,1)}, bf16[208,2560]{1,0:T(8,128)(2,1)S(1)}, u32[]{:S(2)}, u32[]{:S(2)}) %collective-permute-start.31) | collective-permute-done | bytes 1064992 | tf_op jit(solution)/shard_map/ppermute | solution.py:28
  135.3 3.8 %shard_map.53.refs_10_ = bf16[320,8192]{1,0:T(8,128)(2,1)} custom-call(s32[1]{0:T(128)} %bitcast.side_ref, bf16[320,208]{1,0:T(8,128)(2,1)S(1)} %copy-done.15, bf16[320,208]{1,0:T(8,128)(2,1)S(1)} %copy-done.18, bf16[320,208]{1,0:T(8,128)(2,1)S(1)} %get-tuple-element.105.refs_2_, ...), custom_call_target="tpu_custom_call", output_to_operand_aliasing={{}: (9, {})} | custom-call | flops 1 | bytes 1 | tf_op jit(solution)/shard_map/pallas_call | solution.py:53
  139.2 4.3 %shard_map.54 = bf16[320,8192]{1,0:T(8,128)(2,1)} custom-call(s32[1]{0:T(128)} %bitcast.side_ref, bf16[320,208]{1,0:T(8,128)(2,1)S(1)} %copy-done.16, bf16[320,208]{1,0:T(8,128)(2,1)S(1)} %copy-done.19, bf16[320,208]{1,0:T(8,128)(2,1)S(1)} %get-tuple-element.105.refs_2_, ...), custom_call_target="tpu_custom_call", output_to_operand_aliasing={{}: (11, {})} | custom-call | flops 1 | bytes 1 | tf_op jit(solution)/shard_map/pallas_call | solution.py:53
  (114 shorter events, 55.5 us)
Async XLA Ops:
  1.3 28.5 %collective-permute-start.1 = (bf16[320,8192]{1,0:T(8,128)(2,1)}, bf16[320,8192]{1,0:T(8,128)(2,1)S(1)}, u32[]{:S(2)}, u32[]{:S(2)}) collective-permute-start(bf16[320,8192]{1,0:T(8,128)(2,1)} %refs_0_.6), channel_id=1, source_target_pairs={{1,0},{0,1},{3,2},{2,3},{5,4},{4,5},{7,6},{6,7},{9,8},{8,9},{11,10... | collective-permute-start | bytes 15728648 | tf_op jit(solution)/shard_map/ppermute | solution.py:28
  3.0 25.0 %collective-permute-start.2 = (bf16[208,8192]{1,0:T(8,128)(2,1)}, bf16[208,8192]{1,0:T(8,128)(2,1)S(1)}, u32[]{:S(2)}, u32[]{:S(2)}) collective-permute-start(bf16[208,8192]{1,0:T(8,128)(2,1)} %refs_4_.5), channel_id=1, source_target_pairs={{1,0},{0,1},{3,2},{2,3},{5,4},{4,5},{7,6},{6,7},{9,8},{8,9},{11,10... | collective-permute-start | bytes 10223624 | tf_op jit(solution)/shard_map/ppermute | solution.py:28
  3.2 15.7 %collective-permute-start.3 = (bf16[208,1024]{1,0:T(8,128)(2,1)S(1)}, bf16[208,1024]{1,0:T(8,128)(2,1)S(1)}, u32[]{:S(2)}, u32[]{:S(2)}) collective-permute-start(bf16[208,1024]{1,0:T(8,128)(2,1)S(1)} %slice_select_fusion.9), channel_id=1, source_target_pairs={{12,0},{0,4},{4,8},{8,12},{13,1},{1,5},{5,9},{9,13},{14,2},{2,6},{... | collective-permute-start | bytes 1277960 | tf_op jit(solution)/shard_map/ppermute | solution.py:28
  6.2 21.9 %collective-permute-start = (bf16[208,1024]{1,0:T(8,128)(2,1)S(1)}, bf16[208,1024]{1,0:T(8,128)(2,1)}, u32[]{:S(2)}, u32[]{:S(2)}) collective-permute-start(bf16[208,1024]{1,0:T(8,128)(2,1)S(1)} %slice_select_fusion.8), channel_id=1, source_target_pairs={{12,0},{0,4},{4,8},{8,12},{13,1},{1,5},{5,9},{9,13},{14,2},{2,6},{... | collective-permute-start | bytes 1277960 | tf_op jit(solution)/shard_map/ppermute | solution.py:28
  18.8 19.3 %collective-permute-start.5 = (bf16[208,1024]{1,0:T(8,128)(2,1)S(1)}, bf16[208,1024]{1,0:T(8,128)(2,1)}, u32[]{:S(2)}, u32[]{:S(2)}) collective-permute-start(bf16[208,1024]{1,0:T(8,128)(2,1)S(1)} %get-tuple-element.69), channel_id=1, source_target_pairs={{12,0},{0,4},{4,8},{8,12},{13,1},{1,5},{5,9},{9,13},{14,2},{2,6},{... | collective-permute-start | bytes 1277960 | tf_op jit(solution)/shard_map/ppermute | solution.py:28
  18.9 19.3 %collective-permute-start.6 = (bf16[208,1024]{1,0:T(8,128)(2,1)S(1)}, bf16[208,1024]{1,0:T(8,128)(2,1)S(1)}, u32[]{:S(2)}, u32[]{:S(2)}) collective-permute-start(bf16[208,1024]{1,0:T(8,128)(2,1)S(1)} %collective-permute-done.3.refs_2_), channel_id=1, source_target_pairs={{16,0},{0,16},{17,1},{1,17},{18,2},{2,18},{19,3},{3,19},{20,4},{4,... | collective-permute-start | bytes 1277960 | tf_op jit(solution)/shard_map/ppermute | solution.py:28
  29.9 16.5 %collective-permute-start.8 = (bf16[208,1024]{1,0:T(8,128)(2,1)}, bf16[208,1024]{1,0:T(8,128)(2,1)}, u32[]{:S(2)}, u32[]{:S(2)}) collective-permute-start(bf16[208,1024]{1,0:T(8,128)(2,1)} %get-tuple-element.72), channel_id=1, source_target_pairs={{12,0},{0,4},{4,8},{8,12},{13,1},{1,5},{5,9},{9,13},{14,2},{2,6},{... | collective-permute-start | bytes 1277960 | tf_op jit(solution)/shard_map/ppermute | solution.py:28
  29.9 16.4 %collective-permute-start.9 = (bf16[208,1024]{1,0:T(8,128)(2,1)}, bf16[208,1024]{1,0:T(8,128)(2,1)}, u32[]{:S(2)}, u32[]{:S(2)}) collective-permute-start(bf16[208,1024]{1,0:T(8,128)(2,1)} %collective-permute-done.refs_4_), channel_id=1, source_target_pairs={{16,0},{0,16},{17,1},{1,17},{18,2},{2,18},{19,3},{3,19},{20,4},{4,... | collective-permute-start | bytes 1277960 | tf_op jit(solution)/shard_map/ppermute | solution.py:28
  38.9 16.5 %collective-permute-start.7 = (bf16[208,1024]{1,0:T(8,128)(2,1)}, bf16[208,1024]{1,0:T(8,128)(2,1)}, u32[]{:S(2)}, u32[]{:S(2)}) collective-permute-start(bf16[208,1024]{1,0:T(8,128)(2,1)} %get-tuple-element.71), channel_id=1, source_target_pairs={{12,0},{0,4},{4,8},{8,12},{13,1},{1,5},{5,9},{9,13},{14,2},{2,6},{... | collective-permute-start | bytes 1277960 | tf_op jit(solution)/shard_map/ppermute | solution.py:28
  40.2 15.2 %collective-permute-start.10 = (bf16[208,1024]{1,0:T(8,128)(2,1)}, bf16[208,1024]{1,0:T(8,128)(2,1)}, u32[]{:S(2)}, u32[]{:S(2)}) collective-permute-start(bf16[208,1024]{1,0:T(8,128)(2,1)} %collective-permute-done.5.refs_6_), channel_id=1, source_target_pairs={{16,0},{0,16},{17,1},{1,17},{18,2},{2,18},{19,3},{3,19},{20,4},{4,... | collective-permute-start | bytes 1277960 | tf_op jit(solution)/shard_map/ppermute | solution.py:28
  42.9 14.4 %collective-permute-start.4 = (bf16[640,416]{0,1:T(8,128)(2,1)}, bf16[640,416]{0,1:T(8,128)(2,1)}, u32[]{:S(2)}, u32[]{:S(2)}) collective-permute-start(bf16[640,416]{0,1:T(8,128)(2,1)} %copy.7), channel_id=1, source_target_pairs={{2,0},{0,2},{3,1},{1,3},{6,4},{4,6},{7,5},{5,7},{10,8},{8,10},{11,... | collective-permute-start | bytes 1597448 | tf_op jit(solution)/shard_map/ppermute | solution.py:28
  46.3 18.3 %collective-permute-start.12 = (bf16[208,1024]{1,0:T(8,128)(2,1)}, bf16[208,1024]{1,0:T(8,128)(2,1)}, u32[]{:S(2)}, u32[]{:S(2)}) collective-permute-start(bf16[208,1024]{1,0:T(8,128)(2,1)} %get-tuple-element.78), channel_id=1, source_target_pairs={{12,0},{0,4},{4,8},{8,12},{13,1},{1,5},{5,9},{9,13},{14,2},{2,6},{... | collective-permute-start | bytes 1277960 | tf_op jit(solution)/shard_map/ppermute | solution.py:28
  46.4 18.2 %collective-permute-start.13 = (bf16[208,1024]{1,0:T(8,128)(2,1)}, bf16[208,1024]{1,0:T(8,128)(2,1)}, u32[]{:S(2)}, u32[]{:S(2)}) collective-permute-start(bf16[208,1024]{1,0:T(8,128)(2,1)} %collective-permute-done.8.refs_8_), channel_id=1, source_target_pairs={{16,0},{0,16},{17,1},{1,17},{18,2},{2,18},{19,3},{3,19},{20,4},{4,... | collective-permute-start | bytes 1277960 | tf_op jit(solution)/shard_map/ppermute | solution.py:28
  55.5 23.2 %collective-permute-start.15 = (bf16[208,1024]{1,0:T(8,128)(2,1)}, bf16[208,1024]{1,0:T(8,128)(2,1)}, u32[]{:S(2)}, u32[]{:S(2)}) collective-permute-start(bf16[208,1024]{1,0:T(8,128)(2,1)} %get-tuple-element.81), channel_id=1, source_target_pairs={{12,0},{0,4},{4,8},{8,12},{13,1},{1,5},{5,9},{9,13},{14,2},{2,6},{... | collective-permute-start | bytes 1277960 | tf_op jit(solution)/shard_map/ppermute | solution.py:28
  55.5 23.1 %collective-permute-start.16 = (bf16[208,1024]{1,0:T(8,128)(2,1)}, bf16[208,1024]{1,0:T(8,128)(2,1)}, u32[]{:S(2)}, u32[]{:S(2)}) collective-permute-start(bf16[208,1024]{1,0:T(8,128)(2,1)} %collective-permute-done.7.refs_2_), channel_id=1, source_target_pairs={{16,0},{0,16},{17,1},{1,17},{18,2},{2,18},{19,3},{3,19},{20,4},{4,... | collective-permute-start | bytes 1277960 | tf_op jit(solution)/shard_map/ppermute | solution.py:28
  62.5 15.4 %collective-permute-start.11 = (bf16[320,208]{1,0:T(8,128)(2,1)S(1)}, bf16[320,208]{1,0:T(8,128)(2,1)S(1)}, u32[]{:S(2)}, u32[]{:S(2)}) collective-permute-start(bf16[320,208]{1,0:T(8,128)(2,1)S(1)} %get-tuple-element.77), channel_id=1, source_target_pairs={{1,0},{0,1},{3,2},{2,3},{5,4},{4,5},{7,6},{6,7},{9,8},{8,9},{11,10... | collective-permute-start | bytes 399368 | tf_op jit(solution)/shard_map/ppermute | solution.py:28
  64.6 18.1 %collective-permute-start.14 = (bf16[208,1024]{1,0:T(8,128)(2,1)}, bf16[208,1024]{1,0:T(8,128)(2,1)S(1)}, u32[]{:S(2)}, u32[]{:S(2)}) collective-permute-start(bf16[208,1024]{1,0:T(8,128)(2,1)} %get-tuple-element.80), channel_id=1, source_target_pairs={{12,0},{0,4},{4,8},{8,12},{13,1},{1,5},{5,9},{9,13},{14,2},{2,6},{... | collective-permute-start | bytes 1277960 | tf_op jit(solution)/shard_map/ppermute | solution.py:28
  64.6 18.1 %collective-permute-start.17 = (bf16[208,1024]{1,0:T(8,128)(2,1)}, bf16[208,1024]{1,0:T(8,128)(2,1)S(1)}, u32[]{:S(2)}, u32[]{:S(2)}) collective-permute-start(bf16[208,1024]{1,0:T(8,128)(2,1)} %collective-permute-done.12.refs_4_), channel_id=1, source_target_pairs={{16,0},{0,16},{17,1},{1,17},{18,2},{2,18},{19,3},{3,19},{20,4},{4,... | collective-permute-start | bytes 1277960 | tf_op jit(solution)/shard_map/ppermute | solution.py:28
  78.6 18.0 %collective-permute-start.19 = (bf16[208,1280]{1,0:T(8,128)(2,1)S(1)}, bf16[208,1280]{1,0:T(8,128)(2,1)}, u32[]{:S(2)}, u32[]{:S(2)}) collective-permute-start(bf16[208,1280]{1,0:T(8,128)(2,1)S(1)} %copy-done.24), channel_id=1, source_target_pairs={{12,0},{0,4},{4,8},{8,12},{13,1},{1,5},{5,9},{9,13},{14,2},{2,6},{... | collective-permute-start | bytes 1597448 | tf_op jit(solution)/shard_map/ppermute | solution.py:28
  82.7 26.6 %collective-permute-start.22 = (bf16[208,1536]{1,0:T(8,128)(2,1)}, bf16[208,1536]{1,0:T(8,128)(2,1)}, u32[]{:S(2)}, u32[]{:S(2)}) collective-permute-start(bf16[208,1536]{1,0:T(8,128)(2,1)} %slice_select_fusion), channel_id=1, source_target_pairs={{12,0},{0,4},{4,8},{8,12},{13,1},{1,5},{5,9},{9,13},{14,2},{2,6},{... | collective-permute-start | bytes 1916936 | tf_op jit(solution)/shard_map/ppermute | solution.py:28
  82.8 19.4 %collective-permute-start.18 = (bf16[208,1024]{1,0:T(8,128)(2,1)S(1)}, bf16[208,1024]{1,0:T(8,128)(2,1)S(1)}, u32[]{:S(2)}, u32[]{:S(2)}) collective-permute-start(bf16[208,1024]{1,0:T(8,128)(2,1)S(1)} %collective-permute-done.14.refs_2_), channel_id=1, source_target_pairs={{16,0},{0,16},{17,1},{1,17},{18,2},{2,18},{19,3},{3,19},{20,4},{4,... | collective-permute-start | bytes 1277960 | tf_op jit(solution)/shard_map/ppermute | solution.py:28
  96.6 15.1 %collective-permute-start.25 = (bf16[208,1280]{1,0:T(8,128)(2,1)}, bf16[208,1280]{1,0:T(8,128)(2,1)}, u32[]{:S(2)}, u32[]{:S(2)}) collective-permute-start(bf16[208,1280]{1,0:T(8,128)(2,1)} %collective-permute-done.19.refs_6_), channel_id=1, source_target_pairs={{16,0},{0,16},{17,1},{1,17},{18,2},{2,18},{19,3},{3,19},{20,4},{4,... | collective-permute-start | bytes 1597448 | tf_op jit(solution)/shard_map/ppermute | solution.py:28
  97.2 35.1 %collective-permute-start.30 = (bf16[208,2560]{1,0:T(8,128)(2,1)}, bf16[208,2560]{1,0:T(8,128)(2,1)}, u32[]{:S(2)}, u32[]{:S(2)}) collective-permute-start(bf16[208,2560]{1,0:T(8,128)(2,1)} %slice.83), channel_id=1, source_target_pairs={{12,0},{0,4},{4,8},{8,12},{13,1},{1,5},{5,9},{9,13},{14,2},{2,6},{... | collective-permute-start | bytes 3194888 | tf_op jit(solution)/shard_map/ppermute | solution.py:28
  109.3 14.9 %collective-permute-start.24 = (bf16[208,1536]{1,0:T(8,128)(2,1)}, bf16[208,1536]{1,0:T(8,128)(2,1)}, u32[]{:S(2)}, u32[]{:S(2)}) collective-permute-start(bf16[208,1536]{1,0:T(8,128)(2,1)} %collective-permute-done.22.refs_6_), channel_id=1, source_target_pairs={{16,0},{0,16},{17,1},{1,17},{18,2},{2,18},{19,3},{3,19},{20,4},{4,... | collective-permute-start | bytes 1916936 | tf_op jit(solution)/shard_map/ppermute | solution.py:28
  (35 other events, 210.0 us)

commit v12 on v11

--- a/solution.py
+++ b/solution.py
@@ -16,7 +16,6 @@
 BEFORE_LAST = (1, 0, 0)
 WHOLE_FIRST = True
 SWAP_WAIT = 2
-SPLIT = False
 HOLD = 1
 VMEM = 16 * 1024 * 1024
 ANY = pl.BlockSpec(memory_space=pl.ANY)
@@ -62,83 +61,69 @@
     )(*operands)
 
 
-def products_kernel(sets, groups, spans, before, outs, *refs):
+def products_kernel(sets, groups, spans, before, *refs):
     row_refs, unit_refs = refs[:sets], refs[sets : sets + groups * len(spans)]
-    out_refs, total = refs[-1 - outs : -1], refs[-1]
+    out, total = refs[-2:]
     for step, (a, b) in enumerate(spans):
         units = jnp.concatenate(
             [ref[:, : b - a] for ref in unit_refs[step * groups : (step + 1) * groups]], axis=0
         )
-        at = 0
-        for i, ref in enumerate(row_refs):
-            spot = slice(at, at + ref.shape[0])
-            at += ref.shape[0]
-            value = lax.dot_general(
-                ref[:, a:b], units, (((1,), (1,)), ((), ())), preferred_element_type=jnp.float32
-            )
-            if step > 0:
-                value += total[spot]
-            elif before:
-                value += refs[-2 - outs][spot]
-            if step < len(spans) - 1:
-                total[spot] = value
-            elif outs == 1:
-                out_refs[0][spot] = value.astype(out_refs[0].dtype)
-            else:
-                out_refs[i][...] = value.astype(out_refs[i].dtype)
+        rows = jnp.concatenate([ref[:, a:b] for ref in row_refs], axis=0)
+        value = lax.dot_general(
+            units, rows, (((1,), (1,)), ((), ())), preferred_element_type=jnp.float32
+        )
+        if step > 0:
+            value += total[...]
+        elif before:
+            value += refs[-3][...]
+        if step < len(spans) - 1:
+            total[...] = value
+        else:
+            out[...] = value.astype(out.dtype)
 
 
 WHOLE = pl.BlockSpec(memory_space=pltpu.VMEM)
 
 
-def products(row_sets, unit_sets, spans, before=None, out_type=jnp.bfloat16, split=False):
+def products(row_sets, unit_sets, spans, before=None, out_type=jnp.bfloat16):
     groups = len(unit_sets) // len(spans)
-    count = sum(u.shape[0] for u in unit_sets[:groups])
-    shape = (sum(r.shape[0] for r in row_sets), count)
-    shapes = [(r.shape[0], count) for r in row_sets] if split else [shape]
+    shape = (sum(u.shape[0] for u in unit_sets[:groups]), sum(r.shape[0] for r in row_sets))
     operands = (*row_sets, *unit_sets)
     if before is not None:
         operands += (before,)
-    found = call(
+    return call(
         functools.partial(
-            products_kernel, len(row_sets), groups, tuple(spans), before is not None, len(shapes)
+            products_kernel, len(row_sets), groups, tuple(spans), before is not None
         ),
         operands,
         [WHOLE] * len(operands),
-        [jax.ShapeDtypeStruct(s, out_type) for s in shapes],
-        [WHOLE] * len(shapes),
+        jax.ShapeDtypeStruct(shape, out_type),
+        WHOLE,
         [pltpu.VMEM(shape, jnp.float32)],
         {},
     )
-    return found if split else found[0]
-
-
-def activation_kernel(count, turned, side_ref, *refs):
+
+
+def activation_kernel(turned, side_ref, *refs):
     terms, outs = refs[:-2], refs[-2:]
-    per = len(terms) // count
     rows, units = outs[0].shape
-    first = side_ref[0] == 0
-    at = 0
-    for i in range(count):
-        block = terms[i * per : (i + 1) * per]
-        for start in range(0, block[0].shape[0], rows):
-            total = block[0][start : start + rows].astype(jnp.float32)
-            for ref in block[1:]:
-                total += ref[start : start + rows].astype(jnp.float32)
-            gate, up = total[:, :units], total[:, units:]
-            if turned:
-                gate, up = jnp.where(first, gate, up), jnp.where(first, up, gate)
-            outs[at][...] = (gate / (1.0 + jnp.exp(-gate)) * up).astype(outs[at].dtype)
-            at += 1
-
-
-def activated(side, blocks, rows, turned):
-    operands = [side]
-    for value, others in blocks:
-        operands += [value, *others]
-    shape = (rows, blocks[0][0].shape[1] // 2)
+    total = terms[0][...].astype(jnp.float32)
+    for ref in terms[1:]:
+        total += ref[...].astype(jnp.float32)
+    gate, up = total[:units], total[units:]
+    if turned:
+        first = side_ref[0] == 0
+        gate, up = jnp.where(first, gate, up), jnp.where(first, up, gate)
+    hidden = (gate / (1.0 + jnp.exp(-gate)) * up).T
+    for i, out in enumerate(outs):
+        out[...] = hidden[i * rows : (i + 1) * rows].astype(out.dtype)
+
+
+def activated(side, value, others, turned):
+    operands = [side, value, *others]
+    shape = (value.shape[1] // 2, value.shape[0] // 2)
     return call(
-        functools.partial(activation_kernel, len(blocks), turned),
+        functools.partial(activation_kernel, turned),
         operands,
         [pl.BlockSpec(memory_space=pltpu.SMEM)] + [WHOLE] * (len(operands) - 1),
         [jax.ShapeDtypeStruct(shape, jnp.bfloat16)] * 2,
@@ -229,7 +214,6 @@
 
 def on_device(tokens, gate_weight, up_weight, down_weight):
     units, width = gate_weight.shape
-    rows = tokens.shape[0]
     group = lax.axis_index("groups").astype(jnp.int32)
     first = group == 0
     side = group.reshape(1)
@@ -278,17 +262,11 @@
     def pass_other(n, *after):
         crossed_mates[count + n] = mate(tied(crossed[count + n], *after))
 
-    def batch(lo, hi, now, before=None, last_one=False):
+    def batch(lo, hi, now, before=None):
         held = [block for i in range(lo, hi) for block in (landed[i], crossed[i])]
         held = lax.optimization_barrier((*held, now))[:-1]
-        return products(
-            [tokens, tokens_mate],
-            held,
-            spans[lo:hi],
-            before,
-            jnp.bfloat16 if last_one else jnp.float32,
-            last_one and SPLIT,
-        )
+        kind = jnp.bfloat16 if hi == count else jnp.float32
+        return products([tokens, tokens_mate], held, spans[lo:hi], before, kind)
 
     tokens_mate = mate(tied(tokens, pieces[0]))
     down_mate = mate(tied(down_weight, pieces[1]))
@@ -305,31 +283,22 @@
             after.append(own_value)
         if i == OWN_SUM:
             here, given = activated(
-                side, [(own_value, [tied(block, now) for block in own_sent])], rows, False
+                side, own_value, [tied(block, now) for block in own_sent], False
             )
             here_mate = mate(given)
             after.append(here)
             due.setdefault(OWN_MATE, []).append(here_mate)
         for stage, lo, hi in BATCHES:
             if i == stage:
-                value = batch(lo, hi, now, value, hi == count)
-                halves = value if isinstance(value, (list, tuple)) else [value]
-                after += halves
+                value = batch(lo, hi, now, value)
+                after.append(value)
                 if hi == count:
-                    sent = [over_slices(half) for half in halves]
+                    sent = over_slices(value)
         if i == PASS[0]:
             pass_own(0, now)
         if i == PASS[1]:
             pass_other(0, now)
-    there, given = activated(
-        side,
-        [
-            (half, [tied(block, now) for block in blocks])
-            for half, blocks in zip(halves, sent)
-        ],
-        rows,
-        True,
-    )
+    there, given = activated(side, value, [tied(block, now) for block in sent], True)
     there_mate = mate(given)
     if HOLD:
         there_mate = tied(there_mate, crossed[count + 1])

time: 144 us -> 139 us (0.965)
  waiting for transfers between devices: 47.5 us -> 83.6 us
  local copies, waits for them, and re-layouts: 31.1 us -> 0.1 us
  Pallas kernels: 28 us -> 20.4 us
  other arithmetic: 10.2 us -> 6.93 us
    ppermute x32, waiting for transfers between devices: 47.5 us -> 83.6 us  [shifted(): return lax.ppermute(block, axis, route)]
    unnamed x54 -> x10, local copies, waits for them, and re-layouts: 21.4 us -> 0.03 us
    pallas_call x9, Pallas kernels: 28 us -> 20.4 us  [call(): pl.pallas_call(kernel, in_specs=in_specs, out_specs=out_spec, out_shape=o...]
    pallas_call x2 -> x0, local copies, waits for them, and re-layouts: 4.28 us -> none  [call(): pl.pallas_call(kernel, in_specs=in_specs, out_specs=out_spec, out_shape=o...]
    optimization_barrier x2 -> x0, local copies, waits for them, and re-layouts: 4.26 us -> none  [tied(): return lax.optimization_barrier((value, *earlier))[0] if earlier else value]
    select_n x2, other arithmetic: 3.21 us -> 1.55 us  [piece(): return jnp.where(first, down[:, a:mid], down[:, mid:b])]
    select_n x3, other arithmetic: 6.94 us -> 5.38 us  [piece(): return jnp.where(first, gate[:, a:b], up[:, a:b])]
  transfers between devices with their start and end apart: 32 -> 32, of which waited for: 14 -> 14; matrix products, arithmetic and copies ran while one was open for 13% -> 4% of each run, Pallas kernels for 17% -> 13%
where the time goes in v12:
time: 139 us
  waiting for transfers between devices  83.6 us (60%)
  starting transfers between devices  27.2 us (20%)
  Pallas kernels  20.4 us (15%)
  other arithmetic  6.93 us (5%)
    ppermute x32, waiting for transfers between devices, shifted(): return lax.ppermute(block, axis, route)  83.6 us
    ppermute x32, starting transfers between devices, shifted(): return lax.ppermute(block, axis, route)  27.2 us
    pallas_call x9, Pallas kernels, call(): pl.pallas_call(kernel, in_specs=in_specs, out_specs=out_spec, out_shape=o...  20.4 us
    select_n x3, other arithmetic, piece(): return jnp.where(first, gate[:, a:b], up[:, a:b])  5.38 us
  transfers between devices with their start and end apart: 32, of which 14 were waited for; matrix products, arithmetic and copies ran while one was open for 4% of the time, Pallas kernels for 13%

profile of v12, /device:TPU:0, one launch (start us, length us, event | category | flops | bytes accessed | tf_op | source)
XLA Modules:
  0.0 138.6 jit_solution(9312812099934626685)
XLA Ops:
  3.2 3.0 %collective-permute-start.3 = (bf16[208,1024]{1,0:T(8,128)(2,1)S(1)}, bf16[208,1024]{1,0:T(8,128)(2,1)S(1)}, u32[]{:S(2)}, u32[]{:S(2)}) collective-permute-start(bf16[208,1024]{1,0:T(8,128)(2,1)S(1)} %slice_select_fusion.9), channel_id=1, source_target_pairs={{12,0},{0,4},{4,8},{8,12},{13,1},{1,5},{5,9},{9,13},{14,2},{2,6},{... | collective-permute-start | bytes 1277960 | tf_op jit(solution)/shard_map/ppermute | solution.py:27
  9.4 2.9 %slice_select_fusion.2 = (bf16[208,1024]{1,0:T(8,128)(2,1)S(1)}, bf16[208,1024]{1,0:T(8,128)(2,1)S(1)}, bf16[208,1024]{1,0:T(8,128)(2,1)S(1)}, bf16[208,1024]{1,...) fusion(bf16[208,8192]{1,0:T(8,128)(2,1)} %refs_3_.1, bf16[208,8192]{1,0:T(8,128)(2,1)} %refs_2_.1, ...), kind=kLoop, calls=%fused_computation.2 | loop fusion | flops 1277952 | bytes 7667713 | tf_op jit(solution)/shard_map/jit(_where)/select_n | solution.py:233
  12.3 6.5 %collective-permute-done.3.refs_2_ = bf16[208,1024]{1,0:T(8,128)(2,1)S(1)} collective-permute-done((bf16[208,1024]{1,0:T(8,128)(2,1)S(1)}, bf16[208,1024]{1,0:T(8,128)(2,1)S(1)}, u32[]{:S(2)}, u32[]{:S(2)}) %collective-permute-start.3) | collective-permute-done | bytes 426016 | tf_op jit(solution)/shard_map/ppermute | solution.py:27
  20.6 7.4 %collective-permute-done.refs_4_ = bf16[208,1024]{1,0:T(8,128)(2,1)S(1)} collective-permute-done((bf16[208,1024]{1,0:T(8,128)(2,1)S(1)}, bf16[208,1024]{1,0:T(8,128)(2,1)S(1)}, u32[]{:S(2)}, u32[]{:S(2)}) %collective-permute-start) | collective-permute-done | bytes 426016 | tf_op jit(solution)/shard_map/ppermute | solution.py:27
  28.0 1.8 %collective-permute-start.9 = (bf16[208,1024]{1,0:T(8,128)(2,1)S(1)}, bf16[208,1024]{1,0:T(8,128)(2,1)S(1)}, u32[]{:S(2)}, u32[]{:S(2)}) collective-permute-start(bf16[208,1024]{1,0:T(8,128)(2,1)S(1)} %collective-permute-done.refs_4_), channel_id=1, source_target_pairs={{16,0},{0,16},{17,1},{1,17},{18,2},{2,18},{19,3},{3,19},{20,4},{4,... | collective-permute-start | bytes 1277960 | tf_op jit(solution)/shard_map/ppermute | solution.py:27
  29.8 5.5 %shard_map.46.refs_0_ = bf16[416,640]{1,0:T(8,128)(2,1)S(1)} custom-call(bf16[320,8192]{1,0:T(8,128)(2,1)S(1)} %bitcast.2, bf16[320,8192]{1,0:T(8,128)(2,1)S(1)} %collective-permute-done.1.refs_1_, bf16[208,8192]{1,0:T(8,128)(2,1)S(1)} %copy-done.1, bf16[208,8192]{1,0:T(8,128)(2,1)S(1)} %copy-done.2), custom_call_target="tpu_custom_call" | custom-call | flops 1 | bytes 1 | tf_op jit(solution)/shard_map/pallas_call | solution.py:52
  40.4 5.9 %collective-permute-done.8.refs_8_ = bf16[208,1024]{1,0:T(8,128)(2,1)S(1)} collective-permute-done((bf16[208,1024]{1,0:T(8,128)(2,1)S(1)}, bf16[208,1024]{1,0:T(8,128)(2,1)S(1)}, u32[]{:S(2)}, u32[]{:S(2)}) %collective-permute-start.8) | collective-permute-done | bytes 426016 | tf_op jit(solution)/shard_map/ppermute | solution.py:27
  48.0 7.4 %collective-permute-done.7.refs_2_ = bf16[208,1024]{1,0:T(8,128)(2,1)S(1)} collective-permute-done((bf16[208,1024]{1,0:T(8,128)(2,1)S(1)}, bf16[208,1024]{1,0:T(8,128)(2,1)S(1)}, u32[]{:S(2)}, u32[]{:S(2)}) %collective-permute-start.7) | collective-permute-done | bytes 426016 | tf_op jit(solution)/shard_map/ppermute | solution.py:27
  57.5 6.9 %collective-permute-done.12.refs_4_ = bf16[208,1024]{1,0:T(8,128)(2,1)S(1)} collective-permute-done((bf16[208,1024]{1,0:T(8,128)(2,1)S(1)}, bf16[208,1024]{1,0:T(8,128)(2,1)S(1)}, u32[]{:S(2)}, u32[]{:S(2)}) %collective-permute-start.12) | collective-permute-done | bytes 426016 | tf_op jit(solution)/shard_map/ppermute | solution.py:27
  66.2 2.8 %shard_map.48.refs_8_ = f32[416,640]{1,0:T(8,128)S(1)} custom-call(bf16[320,8192]{1,0:T(8,128)(2,1)S(1)} %bitcast.2, bf16[320,8192]{1,0:T(8,128)(2,1)S(1)} %collective-permute-done.1.refs_1_, bf16[208,1024]{1,0:T(8,128)(2,1)S(1)} %collective-permute-done.3.refs_2_, bf16[208,1024]{1,0:T(8,128)(2,1)S(1)} %collective-permute-done.6.refs_3_, ...), custom_call_target="tpu_custom_call" | custom-call | flops 1 | bytes 1 | tf_op jit(solution)/shard_map/pallas_call | solution.py:52
  69.1 4.5 %collective-permute-done.15.refs_6_ = bf16[208,1024]{1,0:T(8,128)(2,1)S(1)} collective-permute-done((bf16[208,1024]{1,0:T(8,128)(2,1)S(1)}, bf16[208,1024]{1,0:T(8,128)(2,1)S(1)}, u32[]{:S(2)}, u32[]{:S(2)}) %collective-permute-start.15) | collective-permute-done | bytes 426016 | tf_op jit(solution)/shard_map/ppermute | solution.py:27
  75.4 7.4 %collective-permute-done.14.refs_2_ = bf16[208,1024]{1,0:T(8,128)(2,1)S(1)} collective-permute-done((bf16[208,1024]{1,0:T(8,128)(2,1)S(1)}, bf16[208,1024]{1,0:T(8,128)(2,1)S(1)}, u32[]{:S(2)}, u32[]{:S(2)}) %collective-permute-start.14) | collective-permute-done | bytes 426016 | tf_op jit(solution)/shard_map/ppermute | solution.py:27
  84.5 2.2 %shard_map.49.refs_4_ = f32[416,640]{1,0:T(8,128)S(1)} custom-call(bf16[320,8192]{1,0:T(8,128)(2,1)S(1)} %bitcast.2, bf16[320,8192]{1,0:T(8,128)(2,1)S(1)} %collective-permute-done.1.refs_1_, bf16[208,1024]{1,0:T(8,128)(2,1)S(1)} %collective-permute-done.7.refs_2_, bf16[208,1024]{1,0:T(8,128)(2,1)S(1)} %collective-permute-done.16.refs_3_, ...), custom_call_target="tpu_custom_call" | custom-call | flops 1 | bytes 1 | tf_op jit(solution)/shard_map/pallas_call | solution.py:52
  86.7 7.5 %collective-permute-done.19.refs_6_ = bf16[208,1280]{1,0:T(8,128)(2,1)S(1)} collective-permute-done((bf16[208,1280]{1,0:T(8,128)(2,1)S(1)}, bf16[208,1280]{1,0:T(8,128)(2,1)S(1)}, u32[]{:S(2)}, u32[]{:S(2)}) %collective-permute-start.19) | collective-permute-done | bytes 532512 | tf_op jit(solution)/shard_map/ppermute | solution.py:27
  94.1 1.8 %collective-permute-start.25 = (bf16[208,1280]{1,0:T(8,128)(2,1)S(1)}, bf16[208,1280]{1,0:T(8,128)(2,1)S(1)}, u32[]{:S(2)}, u32[]{:S(2)}) collective-permute-start(bf16[208,1280]{1,0:T(8,128)(2,1)S(1)} %collective-permute-done.19.refs_6_), channel_id=1, source_target_pairs={{16,0},{0,16},{17,1},{1,17},{18,2},{2,18},{19,3},{3,19},{20,4},{4,... | collective-permute-start | bytes 1597448 | tf_op jit(solution)/shard_map/ppermute | solution.py:27
  98.4 9.5 %collective-permute-done.22.refs_6_ = bf16[208,1536]{1,0:T(8,128)(2,1)S(1)} collective-permute-done((bf16[208,1536]{1,0:T(8,128)(2,1)S(1)}, bf16[208,1536]{1,0:T(8,128)(2,1)S(1)}, u32[]{:S(2)}, u32[]{:S(2)}) %collective-permute-start.22) | collective-permute-done | bytes 639008 | tf_op jit(solution)/shard_map/ppermute | solution.py:27
  107.8 1.8 %collective-permute-start.24 = (bf16[208,1536]{1,0:T(8,128)(2,1)S(1)}, bf16[208,1536]{1,0:T(8,128)(2,1)S(1)}, u32[]{:S(2)}, u32[]{:S(2)}) collective-permute-start(bf16[208,1536]{1,0:T(8,128)(2,1)S(1)} %collective-permute-done.22.refs_6_), channel_id=1, source_target_pairs={{16,0},{0,16},{17,1},{1,17},{18,2},{2,18},{19,3},{3,19},{20,4},{4,... | collective-permute-start | bytes 1916936 | tf_op jit(solution)/shard_map/ppermute | solution.py:27
  110.6 1.9 %collective-permute-done.23.refs_3_ = bf16[320,208]{1,0:T(8,128)(2,1)S(1)} collective-permute-done((bf16[320,208]{1,0:T(8,128)(2,1)S(1)}, bf16[320,208]{1,0:T(8,128)(2,1)S(1)}, u32[]{:S(2)}, u32[]{:S(2)}) %collective-permute-start.23) | collective-permute-done | bytes 133152 | tf_op jit(solution)/shard_map/ppermute | solution.py:27
  112.5 10.6 %collective-permute-done.24.refs_7_ = bf16[208,1536]{1,0:T(8,128)(2,1)S(1)} collective-permute-done((bf16[208,1536]{1,0:T(8,128)(2,1)S(1)}, bf16[208,1536]{1,0:T(8,128)(2,1)S(1)}, u32[]{:S(2)}, u32[]{:S(2)}) %collective-permute-start.24) | collective-permute-done | bytes 639008 | tf_op jit(solution)/shard_map/ppermute | solution.py:27
  123.1 2.7 %shard_map.52.refs_8_ = bf16[320,8192]{1,0:T(8,128)(2,1)} custom-call(s32[1]{0:T(128)} %bitcast.side_ref, bf16[320,208]{1,0:T(8,128)(2,1)S(1)} %get-tuple-element.76.refs_0_, bf16[320,208]{1,0:T(8,128)(2,1)S(1)} %collective-permute-done.11.refs_1_, bf16[320,208]{1,0:T(8,128)(2,1)S(1)} %get-tuple-element.105.refs_2_, ...), custom_call_target="tpu_custom_call" | custom-call | flops 1 | bytes 1 | tf_op jit(solution)/shard_map/pallas_call | solution.py:52
  125.8 4.3 %collective-permute-done.30.refs_6_ = bf16[208,2560]{1,0:T(8,128)(2,1)S(1)} collective-permute-done((bf16[208,2560]{1,0:T(8,128)(2,1)S(1)}, bf16[208,2560]{1,0:T(8,128)(2,1)S(1)}, u32[]{:S(2)}, u32[]{:S(2)}) %collective-permute-start.30) | collective-permute-done | bytes 1064992 | tf_op jit(solution)/shard_map/ppermute | solution.py:27
  130.6 2.2 %collective-permute-done.31.refs_7_ = bf16[208,2560]{1,0:T(8,128)(2,1)S(1)} collective-permute-done((bf16[208,2560]{1,0:T(8,128)(2,1)S(1)}, bf16[208,2560]{1,0:T(8,128)(2,1)S(1)}, u32[]{:S(2)}, u32[]{:S(2)}) %collective-permute-start.31) | collective-permute-done | bytes 1064992 | tf_op jit(solution)/shard_map/ppermute | solution.py:27
  132.8 2.6 %shard_map.53.refs_10_ = bf16[320,8192]{1,0:T(8,128)(2,1)} custom-call(s32[1]{0:T(128)} %bitcast.side_ref, bf16[320,208]{1,0:T(8,128)(2,1)S(1)} %get-tuple-element.76.refs_0_, bf16[320,208]{1,0:T(8,128)(2,1)S(1)} %collective-permute-done.11.refs_1_, bf16[320,208]{1,0:T(8,128)(2,1)S(1)} %get-tuple-element.105.refs_2_, ...), custom_call_target="tpu_custom_call", output_to_operand_aliasing={{}: (9, {})} | custom-call | flops 1 | bytes 1 | tf_op jit(solution)/shard_map/pallas_call | solution.py:52
  135.4 3.0 %shard_map.54 = bf16[320,8192]{1,0:T(8,128)(2,1)} custom-call(s32[1]{0:T(128)} %bitcast.side_ref, bf16[320,208]{1,0:T(8,128)(2,1)S(1)} %get-tuple-element.76.refs_0_, bf16[320,208]{1,0:T(8,128)(2,1)S(1)} %collective-permute-done.11.refs_1_, bf16[320,208]{1,0:T(8,128)(2,1)S(1)} %get-tuple-element.105.refs_2_, ...), custom_call_target="tpu_custom_call", output_to_operand_aliasing={{}: (11, {})} | custom-call | flops 1 | bytes 1 | tf_op jit(solution)/shard_map/pallas_call | solution.py:52
  (66 shorter events, 26.4 us)
Async XLA Ops:
  1.3 26.6 %collective-permute-start.1 = (bf16[320,8192]{1,0:T(8,128)(2,1)}, bf16[320,8192]{1,0:T(8,128)(2,1)S(1)}, u32[]{:S(2)}, u32[]{:S(2)}) collective-permute-start(bf16[320,8192]{1,0:T(8,128)(2,1)} %refs_0_.6), channel_id=1, source_target_pairs={{1,0},{0,1},{3,2},{2,3},{5,4},{4,5},{7,6},{6,7},{9,8},{8,9},{11,10... | collective-permute-start | bytes 15728648 | tf_op jit(solution)/shard_map/ppermute | solution.py:27
  3.0 24.9 %collective-permute-start.2 = (bf16[208,8192]{1,0:T(8,128)(2,1)}, bf16[208,8192]{1,0:T(8,128)(2,1)S(1)}, u32[]{:S(2)}, u32[]{:S(2)}) collective-permute-start(bf16[208,8192]{1,0:T(8,128)(2,1)} %refs_4_.5), channel_id=1, source_target_pairs={{1,0},{0,1},{3,2},{2,3},{5,4},{4,5},{7,6},{6,7},{9,8},{8,9},{11,10... | collective-permute-start | bytes 10223624 | tf_op jit(solution)/shard_map/ppermute | solution.py:27
  3.2 15.7 %collective-permute-start.3 = (bf16[208,1024]{1,0:T(8,128)(2,1)S(1)}, bf16[208,1024]{1,0:T(8,128)(2,1)S(1)}, u32[]{:S(2)}, u32[]{:S(2)}) collective-permute-start(bf16[208,1024]{1,0:T(8,128)(2,1)S(1)} %slice_select_fusion.9), channel_id=1, source_target_pairs={{12,0},{0,4},{4,8},{8,12},{13,1},{1,5},{5,9},{9,13},{14,2},{2,6},{... | collective-permute-start | bytes 1277960 | tf_op jit(solution)/shard_map/ppermute | solution.py:27
  6.2 21.8 %collective-permute-start = (bf16[208,1024]{1,0:T(8,128)(2,1)S(1)}, bf16[208,1024]{1,0:T(8,128)(2,1)S(1)}, u32[]{:S(2)}, u32[]{:S(2)}) collective-permute-start(bf16[208,1024]{1,0:T(8,128)(2,1)S(1)} %slice_select_fusion.8), channel_id=1, source_target_pairs={{12,0},{0,4},{4,8},{8,12},{13,1},{1,5},{5,9},{9,13},{14,2},{2,6},{... | collective-permute-start | bytes 1277960 | tf_op jit(solution)/shard_map/ppermute | solution.py:27
  18.8 18.3 %collective-permute-start.5 = (bf16[208,1024]{1,0:T(8,128)(2,1)S(1)}, bf16[208,1024]{1,0:T(8,128)(2,1)S(1)}, u32[]{:S(2)}, u32[]{:S(2)}) collective-permute-start(bf16[208,1024]{1,0:T(8,128)(2,1)S(1)} %get-tuple-element.69), channel_id=1, source_target_pairs={{12,0},{0,4},{4,8},{8,12},{13,1},{1,5},{5,9},{9,13},{14,2},{2,6},{... | collective-permute-start | bytes 1277960 | tf_op jit(solution)/shard_map/ppermute | solution.py:27
  18.9 18.2 %collective-permute-start.6 = (bf16[208,1024]{1,0:T(8,128)(2,1)S(1)}, bf16[208,1024]{1,0:T(8,128)(2,1)S(1)}, u32[]{:S(2)}, u32[]{:S(2)}) collective-permute-start(bf16[208,1024]{1,0:T(8,128)(2,1)S(1)} %collective-permute-done.3.refs_2_), channel_id=1, source_target_pairs={{16,0},{0,16},{17,1},{1,17},{18,2},{2,18},{19,3},{3,19},{20,4},{4,... | collective-permute-start | bytes 1277960 | tf_op jit(solution)/shard_map/ppermute | solution.py:27
  28.0 18.3 %collective-permute-start.8 = (bf16[208,1024]{1,0:T(8,128)(2,1)S(1)}, bf16[208,1024]{1,0:T(8,128)(2,1)S(1)}, u32[]{:S(2)}, u32[]{:S(2)}) collective-permute-start(bf16[208,1024]{1,0:T(8,128)(2,1)S(1)} %get-tuple-element.72), channel_id=1, source_target_pairs={{12,0},{0,4},{4,8},{8,12},{13,1},{1,5},{5,9},{9,13},{14,2},{2,6},{... | collective-permute-start | bytes 1277960 | tf_op jit(solution)/shard_map/ppermute | solution.py:27
  28.0 18.2 %collective-permute-start.9 = (bf16[208,1024]{1,0:T(8,128)(2,1)S(1)}, bf16[208,1024]{1,0:T(8,128)(2,1)S(1)}, u32[]{:S(2)}, u32[]{:S(2)}) collective-permute-start(bf16[208,1024]{1,0:T(8,128)(2,1)S(1)} %collective-permute-done.refs_4_), channel_id=1, source_target_pairs={{16,0},{0,16},{17,1},{1,17},{18,2},{2,18},{19,3},{3,19},{20,4},{4,... | collective-permute-start | bytes 1277960 | tf_op jit(solution)/shard_map/ppermute | solution.py:27
  37.1 18.3 %collective-permute-start.7 = (bf16[208,1024]{1,0:T(8,128)(2,1)S(1)}, bf16[208,1024]{1,0:T(8,128)(2,1)S(1)}, u32[]{:S(2)}, u32[]{:S(2)}) collective-permute-start(bf16[208,1024]{1,0:T(8,128)(2,1)S(1)} %get-tuple-element.71), channel_id=1, source_target_pairs={{12,0},{0,4},{4,8},{8,12},{13,1},{1,5},{5,9},{9,13},{14,2},{2,6},{... | collective-permute-start | bytes 1277960 | tf_op jit(solution)/shard_map/ppermute | solution.py:27
  37.1 18.2 %collective-permute-start.10 = (bf16[208,1024]{1,0:T(8,128)(2,1)S(1)}, bf16[208,1024]{1,0:T(8,128)(2,1)S(1)}, u32[]{:S(2)}, u32[]{:S(2)}) collective-permute-start(bf16[208,1024]{1,0:T(8,128)(2,1)S(1)} %collective-permute-done.5.refs_6_), channel_id=1, source_target_pairs={{16,0},{0,16},{17,1},{1,17},{18,2},{2,18},{19,3},{3,19},{20,4},{4,... | collective-permute-start | bytes 1277960 | tf_op jit(solution)/shard_map/ppermute | solution.py:27
  38.9 18.3 %collective-permute-start.4 = (bf16[416,640]{1,0:T(8,128)(2,1)S(1)}, bf16[416,640]{1,0:T(8,128)(2,1)S(1)}, u32[]{:S(2)}, u32[]{:S(2)}) collective-permute-start(bf16[416,640]{1,0:T(8,128)(2,1)S(1)} %shard_map.46.refs_0_), channel_id=1, source_target_pairs={{2,0},{0,2},{3,1},{1,3},{6,4},{4,6},{7,5},{5,7},{10,8},{8,10},{11,... | collective-permute-start | bytes 1597448 | tf_op jit(solution)/shard_map/ppermute | solution.py:27
  46.2 18.3 %collective-permute-start.12 = (bf16[208,1024]{1,0:T(8,128)(2,1)S(1)}, bf16[208,1024]{1,0:T(8,128)(2,1)S(1)}, u32[]{:S(2)}, u32[]{:S(2)}) collective-permute-start(bf16[208,1024]{1,0:T(8,128)(2,1)S(1)} %get-tuple-element.78), channel_id=1, source_target_pairs={{12,0},{0,4},{4,8},{8,12},{13,1},{1,5},{5,9},{9,13},{14,2},{2,6},{... | collective-permute-start | bytes 1277960 | tf_op jit(solution)/shard_map/ppermute | solution.py:27
  46.3 18.2 %collective-permute-start.13 = (bf16[208,1024]{1,0:T(8,128)(2,1)S(1)}, bf16[208,1024]{1,0:T(8,128)(2,1)S(1)}, u32[]{:S(2)}, u32[]{:S(2)}) collective-permute-start(bf16[208,1024]{1,0:T(8,128)(2,1)S(1)} %collective-permute-done.8.refs_8_), channel_id=1, source_target_pairs={{16,0},{0,16},{17,1},{1,17},{18,2},{2,18},{19,3},{3,19},{20,4},{4,... | collective-permute-start | bytes 1277960 | tf_op jit(solution)/shard_map/ppermute | solution.py:27
  55.3 18.3 %collective-permute-start.15 = (bf16[208,1024]{1,0:T(8,128)(2,1)S(1)}, bf16[208,1024]{1,0:T(8,128)(2,1)S(1)}, u32[]{:S(2)}, u32[]{:S(2)}) collective-permute-start(bf16[208,1024]{1,0:T(8,128)(2,1)S(1)} %get-tuple-element.81), channel_id=1, source_target_pairs={{12,0},{0,4},{4,8},{8,12},{13,1},{1,5},{5,9},{9,13},{14,2},{2,6},{... | collective-permute-start | bytes 1277960 | tf_op jit(solution)/shard_map/ppermute | solution.py:27
  55.4 18.2 %collective-permute-start.16 = (bf16[208,1024]{1,0:T(8,128)(2,1)S(1)}, bf16[208,1024]{1,0:T(8,128)(2,1)S(1)}, u32[]{:S(2)}, u32[]{:S(2)}) collective-permute-start(bf16[208,1024]{1,0:T(8,128)(2,1)S(1)} %collective-permute-done.7.refs_2_), channel_id=1, source_target_pairs={{16,0},{0,16},{17,1},{1,17},{18,2},{2,18},{19,3},{3,19},{20,4},{4,... | collective-permute-start | bytes 1277960 | tf_op jit(solution)/shard_map/ppermute | solution.py:27
  64.5 18.3 %collective-permute-start.14 = (bf16[208,1024]{1,0:T(8,128)(2,1)S(1)}, bf16[208,1024]{1,0:T(8,128)(2,1)S(1)}, u32[]{:S(2)}, u32[]{:S(2)}) collective-permute-start(bf16[208,1024]{1,0:T(8,128)(2,1)S(1)} %get-tuple-element.80), channel_id=1, source_target_pairs={{12,0},{0,4},{4,8},{8,12},{13,1},{1,5},{5,9},{9,13},{14,2},{2,6},{... | collective-permute-start | bytes 1277960 | tf_op jit(solution)/shard_map/ppermute | solution.py:27
  64.5 18.2 %collective-permute-start.17 = (bf16[208,1024]{1,0:T(8,128)(2,1)S(1)}, bf16[208,1024]{1,0:T(8,128)(2,1)S(1)}, u32[]{:S(2)}, u32[]{:S(2)}) collective-permute-start(bf16[208,1024]{1,0:T(8,128)(2,1)S(1)} %collective-permute-done.12.refs_4_), channel_id=1, source_target_pairs={{16,0},{0,16},{17,1},{1,17},{18,2},{2,18},{19,3},{3,19},{20,4},{4,... | collective-permute-start | bytes 1277960 | tf_op jit(solution)/shard_map/ppermute | solution.py:27
  73.6 20.5 %collective-permute-start.19 = (bf16[208,1280]{1,0:T(8,128)(2,1)S(1)}, bf16[208,1280]{1,0:T(8,128)(2,1)S(1)}, u32[]{:S(2)}, u32[]{:S(2)}) collective-permute-start(bf16[208,1280]{1,0:T(8,128)(2,1)S(1)} %slice_select_fusion.1), channel_id=1, source_target_pairs={{12,0},{0,4},{4,8},{8,12},{13,1},{1,5},{5,9},{9,13},{14,2},{2,6},{... | collective-permute-start | bytes 1597448 | tf_op jit(solution)/shard_map/ppermute | solution.py:27
  82.7 25.1 %collective-permute-start.22 = (bf16[208,1536]{1,0:T(8,128)(2,1)S(1)}, bf16[208,1536]{1,0:T(8,128)(2,1)S(1)}, u32[]{:S(2)}, u32[]{:S(2)}) collective-permute-start(bf16[208,1536]{1,0:T(8,128)(2,1)S(1)} %slice_select_fusion), channel_id=1, source_target_pairs={{12,0},{0,4},{4,8},{8,12},{13,1},{1,5},{5,9},{9,13},{14,2},{2,6},{... | collective-permute-start | bytes 1916936 | tf_op jit(solution)/shard_map/ppermute | solution.py:27
  94.1 15.5 %collective-permute-start.25 = (bf16[208,1280]{1,0:T(8,128)(2,1)S(1)}, bf16[208,1280]{1,0:T(8,128)(2,1)S(1)}, u32[]{:S(2)}, u32[]{:S(2)}) collective-permute-start(bf16[208,1280]{1,0:T(8,128)(2,1)S(1)} %collective-permute-done.19.refs_6_), channel_id=1, source_target_pairs={{16,0},{0,16},{17,1},{1,17},{18,2},{2,18},{19,3},{3,19},{20,4},{4,... | collective-permute-start | bytes 1597448 | tf_op jit(solution)/shard_map/ppermute | solution.py:27
  95.9 34.2 %collective-permute-start.30 = (bf16[208,2560]{1,0:T(8,128)(2,1)S(1)}, bf16[208,2560]{1,0:T(8,128)(2,1)S(1)}, u32[]{:S(2)}, u32[]{:S(2)}) collective-permute-start(bf16[208,2560]{1,0:T(8,128)(2,1)S(1)} %slice.83), channel_id=1, source_target_pairs={{12,0},{0,4},{4,8},{8,12},{13,1},{1,5},{5,9},{9,13},{14,2},{2,6},{... | collective-permute-start | bytes 3194888 | tf_op jit(solution)/shard_map/ppermute | solution.py:27
  107.8 15.3 %collective-permute-start.24 = (bf16[208,1536]{1,0:T(8,128)(2,1)S(1)}, bf16[208,1536]{1,0:T(8,128)(2,1)S(1)}, u32[]{:S(2)}, u32[]{:S(2)}) collective-permute-start(bf16[208,1536]{1,0:T(8,128)(2,1)S(1)} %collective-permute-done.22.refs_6_), channel_id=1, source_target_pairs={{16,0},{0,16},{17,1},{1,17},{18,2},{2,18},{19,3},{3,19},{20,4},{4,... | collective-permute-start | bytes 1916936 | tf_op jit(solution)/shard_map/ppermute | solution.py:27
  109.6 13.5 %collective-permute-start.27 = (bf16[208,1280]{1,0:T(8,128)(2,1)S(1)}, bf16[208,1280]{1,0:T(8,128)(2,1)S(1)}, u32[]{:S(2)}, u32[]{:S(2)}) collective-permute-start(bf16[208,1280]{1,0:T(8,128)(2,1)S(1)} %collective-permute-done.25.refs_7_), channel_id=1, source_target_pairs={{1,0},{0,1},{3,2},{2,3},{5,4},{4,5},{7,6},{6,7},{9,8},{8,9},{11,10... | collective-permute-start | bytes 1597448 | tf_op jit(solution)/shard_map/ppermute | solution.py:27
  109.6 13.5 %collective-permute-start.26 = (bf16[208,1280]{1,0:T(8,128)(2,1)S(1)}, bf16[208,1280]{1,0:T(8,128)(2,1)S(1)}, u32[]{:S(2)}, u32[]{:S(2)}) collective-permute-start(bf16[208,1280]{1,0:T(8,128)(2,1)S(1)} %collective-permute-done.19.refs_6_), channel_id=1, source_target_pairs={{1,0},{0,1},{3,2},{2,3},{5,4},{4,5},{7,6},{6,7},{9,8},{8,9},{11,10... | collective-permute-start | bytes 1597448 | tf_op jit(solution)/shard_map/ppermute | solution.py:27
  (13 other events, 156.5 us)

commit v13 on v12

--- a/solution.py
+++ b/solution.py
@@ -8,15 +8,15 @@
 from jax.sharding import PartitionSpec as P
 
 FEATURE_SHARES = (1,) * 8
-LANE_SHARES = (10, 12, 10)
+LANE_SHARES = (10, 13, 9)
+WHOLES = 1
 QUEUE = 2
 OWN, OWN_SUM, OWN_MATE = 1, 4, 6
 BATCHES = ((5, 0, 4), (7, 4, 7), (8, 7, 8))
-PASS = (9, 9)
-BEFORE_LAST = (1, 0, 0)
-WHOLE_FIRST = True
+PASS = (8, 9)
+TAIL = (("own", 1), ("write", 0, -1, 1), ("other", 1), ("last", 1), ("write", 2), ("write", -2))
 SWAP_WAIT = 2
-HOLD = 1
+HOLD = 0
 VMEM = 16 * 1024 * 1024
 ANY = pl.BlockSpec(memory_space=pl.ANY)
 
@@ -135,29 +135,20 @@
 
 def blocks_of(parts):
     found = []
-    for i, (a, half, own, other) in enumerate(parts):
-        arrays = [(0, lanes) for lanes in own] + [(1, lanes) for lanes in other]
-        filled = [0, 0]
-        for n, (k, lanes) in enumerate(arrays):
-            for lane in range(0, lanes, 512):
-                size = min(512, lanes - lane)
-                turn = half - 2 * k * half if other else 0
-                found.append((i, n, lane, size, (a + k * half + filled[k] + lane, turn)))
-            filled[k] += lanes
+    for i, (a, lanes, half, others) in enumerate(parts):
+        for lane in range(0, lanes, 512):
+            size = min(512, lanes - lane)
+            fixed = a + lane + (half if others else 0)
+            found.append((i, lane, size, (fixed, -half if others else half)))
     return found
 
 
 def output_kernel(parts, side_ref, *refs):
-    hidden, down = refs[:4], refs[4:6]
-    arrived, at = [], 6
-    for _, _, own, other in parts:
-        count = len(own) + len(other)
-        arrived.append((refs[at : at + count], refs[at + count : at + 2 * count]))
-        at += 2 * count
+    hidden, down, arrived = refs[:4], refs[4:6], refs[6 : 6 + 2 * len(parts)]
     out, result, sems = refs[-3:]
     side = side_ref[0]
     stores, at = [], 0
-    for n, (i, array, lane, size, (fixed, turn)) in enumerate(blocks_of(parts)):
+    for n, (i, lane, size, (fixed, turn)) in enumerate(blocks_of(parts)):
         column = pl.ds(pl.multiple_of(fixed + side * turn, 128), size)
         spot = pl.ds(at, size)
         at += size
@@ -166,7 +157,7 @@
             if m < 2:
                 weight = down[m][:, column]
             else:
-                weight = arrived[i][m - 2][array][:, lane : lane + size]
+                weight = arrived[2 * i + m - 2][:, lane : lane + size]
             term = jnp.dot(hidden[m][...], weight, preferred_element_type=jnp.float32)
             total = term if total is None else total + term
         result[:, spot] = total.astype(result.dtype)
@@ -180,7 +171,7 @@
 
 def output_part(result, parts, side, hidden, down, arrived):
     rows, width = hidden[0].shape[0], down[0].shape[1]
-    lanes = sum(sum(own) + sum(other) for _, _, own, other in parts)
+    lanes = sum(part[1] for part in parts)
     operands = [side, *hidden, *down, *arrived]
     in_specs = (
         [pl.BlockSpec(memory_space=pltpu.SMEM)]
@@ -222,7 +213,7 @@
     lane_cuts = [(2 * a, 2 * b) for a, b in cuts(width // 2, 128, LANE_SHARES)]
     count = len(spans)
     total_count = count + len(lane_cuts)
-    last = total_count - 1
+    relayed = total_count - WHOLES
 
     def piece(i, *after):
         if i < count:
@@ -234,7 +225,7 @@
         a, b = lane_cuts[i - count]
         mid = (a + b) // 2
         down = tied(down_weight, *after)
-        if i == last:
+        if i >= relayed:
             return down[:, a:b]
         return jnp.where(first, down[:, a:mid], down[:, mid:b])
 
@@ -250,7 +241,7 @@
         held += [crossed[j] for j in range(count) if j + SWAP_WAIT == i]
         block = tied(waiting[i], *held)
         landed.append(block)
-        if i < last:
+        if i < relayed:
             crossed[i] = across(block)
         if i + QUEUE < total_count:
             waiting.append(shifted(tied(pieces[i + QUEUE], block), "dp", 1))
@@ -272,7 +263,7 @@
     down_mate = mate(tied(down_weight, pieces[1]))
     due = {0: pieces[2:], OWN: [tokens_mate, down_mate]}
     value = own_value = None
-    for i in range(last):
+    for i in range(relayed):
         now = advance(*due.get(i, []))
         after = due.setdefault(i + 1, [])
         if i == OWN:
@@ -305,16 +296,20 @@
 
     def write(result, *which):
         parts, arrived = [], []
-        for n in which:
+        for mark in which:
+            n = mark if mark >= 0 else -1 - mark
             i = count + n
             a, b = lane_cuts[n]
-            if i == last:
-                parts.append((a, (b - a) // 2, (b - a,), ()))
+            half = (b - a) // 2
+            if i >= relayed:
+                parts.append((a, b - a, 0, False))
                 arrived += [landed[i], mates[i]]
+            elif mark < 0:
+                parts.append((a, half, half, True))
+                arrived += [crossed[i], crossed_mates[i]]
             else:
-                half = (b - a) // 2
-                parts.append((a, half, (half,), (half,)))
-                arrived += [landed[i], crossed[i], mates[i], crossed_mates[i]]
+                parts.append((a, half, half, False))
+                arrived += [landed[i], mates[i]]
         return output_part(
             result,
             tuple(parts),
@@ -324,14 +319,22 @@
             arrived,
         )
 
-    result = write(None, 0)
-    pass_own(1, result)
-    pass_other(1, result)
-    waits = (crossed[count + 1], mates[count + 1], crossed_mates[count + 1])
-    now = advance(result, *(wait for wait, use in zip(waits, BEFORE_LAST) if use))
-    pass_own(2, now)
-    for n in (2, 1) if WHOLE_FIRST else (1, 2):
-        result = write(result, n)
+    result = None
+    for step in TAIL:
+        kind, numbers = step[0], step[1:]
+        if kind == "own":
+            for n in numbers:
+                pass_own(n, now, *([] if result is None else [result]))
+        elif kind == "other":
+            for n in numbers:
+                pass_other(n, now, *([] if result is None else [result]))
+        elif kind == "write":
+            result = write(result, *numbers)
+        elif kind == "last":
+            held = [] if result is None else [result]
+            held += [crossed[count + n] for n in numbers]
+            now = advance(*held)
+            pass_own(len(landed) - 1 - count, now)
     return result
 
 

time: 139 us -> 137 us (0.986)
  waiting for transfers between devices: 83.6 us -> 81.8 us
    ppermute x32, waiting for transfers between devices: 83.6 us -> 81.8 us  [shifted(): return lax.ppermute(block, axis, route)]
  transfers between devices with their start and end apart: 32 -> 32, of which waited for: 14 -> 14; matrix products, arithmetic and copies ran while one was open for 4% -> 4% of each run, Pallas kernels for 13% -> 14%
where the time goes in v13:
time: 137 us
  waiting for transfers between devices  81.8 us (60%)
  starting transfers between devices  27.3 us (20%)
  Pallas kernels  20.8 us (15%)
  other arithmetic  6.33 us (5%)
    ppermute x32, waiting for transfers between devices, shifted(): return lax.ppermute(block, axis, route)  81.8 us
    ppermute x32, starting transfers between devices, shifted(): return lax.ppermute(block, axis, route)  27.3 us
    pallas_call x9, Pallas kernels, call(): pl.pallas_call(kernel, in_specs=in_specs, out_specs=out_spec, out_shape=o...  20.8 us
    select_n x3, other arithmetic, piece(): return jnp.where(first, gate[:, a:b], up[:, a:b])  4.89 us
  transfers between devices with their start and end apart: 32, of which 14 were waited for; matrix products, arithmetic and copies ran while one was open for 4% of the time, Pallas kernels for 14%

profile of v13, /device:TPU:0, one launch (start us, length us, event | category | flops | bytes accessed | tf_op | source)
XLA Modules:
  0.0 136.6 jit_solution(12331769273328488943)
XLA Ops:
  3.4 3.1 %collective-permute-start.3 = (bf16[208,1024]{1,0:T(8,128)(2,1)S(1)}, bf16[208,1024]{1,0:T(8,128)(2,1)S(1)}, u32[]{:S(2)}, u32[]{:S(2)}) collective-permute-start(bf16[208,1024]{1,0:T(8,128)(2,1)S(1)} %slice_select_fusion.9), channel_id=1, source_target_pairs={{12,0},{0,4},{4,8},{8,12},{13,1},{1,5},{5,9},{9,13},{14,2},{2,6},{... | collective-permute-start | bytes 1277960 | tf_op jit(solution)/shard_map/ppermute | solution.py:27
  9.6 2.1 %slice_select_fusion.2 = (bf16[208,1024]{1,0:T(8,128)(2,1)S(1)}, bf16[208,1024]{1,0:T(8,128)(2,1)S(1)}, bf16[208,1024]{1,0:T(8,128)(2,1)S(1)}, bf16[208,1024]{1,...) fusion(bf16[208,8192]{1,0:T(8,128)(2,1)} %refs_3_.1, ...), kind=kLoop, calls=%fused_computation.2 | loop fusion | flops 1277952 | bytes 7667713 | tf_op jit(solution)/shard_map/jit(_where)/select_n | solution.py:224
  11.7 7.3 %collective-permute-done.3.refs_2_ = bf16[208,1024]{1,0:T(8,128)(2,1)S(1)} collective-permute-done((bf16[208,1024]{1,0:T(8,128)(2,1)S(1)}, bf16[208,1024]{1,0:T(8,128)(2,1)S(1)}, u32[]{:S(2)}, u32[]{:S(2)}) %collective-permute-start.3) | collective-permute-done | bytes 426016 | tf_op jit(solution)/shard_map/ppermute | solution.py:27
  20.8 7.4 %collective-permute-done.refs_4_ = bf16[208,1024]{1,0:T(8,128)(2,1)S(1)} collective-permute-done((bf16[208,1024]{1,0:T(8,128)(2,1)S(1)}, bf16[208,1024]{1,0:T(8,128)(2,1)S(1)}, u32[]{:S(2)}, u32[]{:S(2)}) %collective-permute-start) | collective-permute-done | bytes 426016 | tf_op jit(solution)/shard_map/ppermute | solution.py:27
  28.2 1.8 %collective-permute-start.9 = (bf16[208,1024]{1,0:T(8,128)(2,1)S(1)}, bf16[208,1024]{1,0:T(8,128)(2,1)S(1)}, u32[]{:S(2)}, u32[]{:S(2)}) collective-permute-start(bf16[208,1024]{1,0:T(8,128)(2,1)S(1)} %collective-permute-done.refs_4_), channel_id=1, source_target_pairs={{16,0},{0,16},{17,1},{1,17},{18,2},{2,18},{19,3},{3,19},{20,4},{4,... | collective-permute-start | bytes 1277960 | tf_op jit(solution)/shard_map/ppermute | solution.py:27
  30.0 5.5 %shard_map.46.refs_0_ = bf16[416,640]{1,0:T(8,128)(2,1)S(1)} custom-call(bf16[320,8192]{1,0:T(8,128)(2,1)S(1)} %bitcast.2, bf16[320,8192]{1,0:T(8,128)(2,1)S(1)} %collective-permute-done.1.refs_1_, bf16[208,8192]{1,0:T(8,128)(2,1)S(1)} %copy-done.1, bf16[208,8192]{1,0:T(8,128)(2,1)S(1)} %copy-done.2), custom_call_target="tpu_custom_call" | custom-call | flops 1 | bytes 1 | tf_op jit(solution)/shard_map/pallas_call | solution.py:52
  35.5 1.8 %collective-permute-done.5.refs_6_ = bf16[208,1024]{1,0:T(8,128)(2,1)S(1)} collective-permute-done((bf16[208,1024]{1,0:T(8,128)(2,1)S(1)}, bf16[208,1024]{1,0:T(8,128)(2,1)S(1)}, u32[]{:S(2)}, u32[]{:S(2)}) %collective-permute-start.5) | collective-permute-done | bytes 426016 | tf_op jit(solution)/shard_map/ppermute | solution.py:27
  40.6 5.9 %collective-permute-done.8.refs_8_ = bf16[208,1024]{1,0:T(8,128)(2,1)S(1)} collective-permute-done((bf16[208,1024]{1,0:T(8,128)(2,1)S(1)}, bf16[208,1024]{1,0:T(8,128)(2,1)S(1)}, u32[]{:S(2)}, u32[]{:S(2)}) %collective-permute-start.8) | collective-permute-done | bytes 426016 | tf_op jit(solution)/shard_map/ppermute | solution.py:27
  48.2 7.4 %collective-permute-done.7.refs_2_ = bf16[208,1024]{1,0:T(8,128)(2,1)S(1)} collective-permute-done((bf16[208,1024]{1,0:T(8,128)(2,1)S(1)}, bf16[208,1024]{1,0:T(8,128)(2,1)S(1)}, u32[]{:S(2)}, u32[]{:S(2)}) %collective-permute-start.7) | collective-permute-done | bytes 426016 | tf_op jit(solution)/shard_map/ppermute | solution.py:27
  57.7 7.0 %collective-permute-done.12.refs_4_ = bf16[208,1024]{1,0:T(8,128)(2,1)S(1)} collective-permute-done((bf16[208,1024]{1,0:T(8,128)(2,1)S(1)}, bf16[208,1024]{1,0:T(8,128)(2,1)S(1)}, u32[]{:S(2)}, u32[]{:S(2)}) %collective-permute-start.12) | collective-permute-done | bytes 426016 | tf_op jit(solution)/shard_map/ppermute | solution.py:27
  66.5 2.8 %shard_map.48.refs_8_ = f32[416,640]{1,0:T(8,128)S(1)} custom-call(bf16[320,8192]{1,0:T(8,128)(2,1)S(1)} %bitcast.2, bf16[320,8192]{1,0:T(8,128)(2,1)S(1)} %collective-permute-done.1.refs_1_, bf16[208,1024]{1,0:T(8,128)(2,1)S(1)} %collective-permute-done.3.refs_2_, bf16[208,1024]{1,0:T(8,128)(2,1)S(1)} %collective-permute-done.6.refs_3_, ...), custom_call_target="tpu_custom_call" | custom-call | flops 1 | bytes 1 | tf_op jit(solution)/shard_map/pallas_call | solution.py:52
  69.3 4.5 %collective-permute-done.15.refs_6_ = bf16[208,1024]{1,0:T(8,128)(2,1)S(1)} collective-permute-done((bf16[208,1024]{1,0:T(8,128)(2,1)S(1)}, bf16[208,1024]{1,0:T(8,128)(2,1)S(1)}, u32[]{:S(2)}, u32[]{:S(2)}) %collective-permute-start.15) | collective-permute-done | bytes 426016 | tf_op jit(solution)/shard_map/ppermute | solution.py:27
  75.6 7.4 %collective-permute-done.14.refs_2_ = bf16[208,1024]{1,0:T(8,128)(2,1)S(1)} collective-permute-done((bf16[208,1024]{1,0:T(8,128)(2,1)S(1)}, bf16[208,1024]{1,0:T(8,128)(2,1)S(1)}, u32[]{:S(2)}, u32[]{:S(2)}) %collective-permute-start.14) | collective-permute-done | bytes 426016 | tf_op jit(solution)/shard_map/ppermute | solution.py:27
  83.0 1.8 %collective-permute-start.18 = (bf16[208,1024]{1,0:T(8,128)(2,1)S(1)}, bf16[208,1024]{1,0:T(8,128)(2,1)S(1)}, u32[]{:S(2)}, u32[]{:S(2)}) collective-permute-start(bf16[208,1024]{1,0:T(8,128)(2,1)S(1)} %collective-permute-done.14.refs_2_), channel_id=1, source_target_pairs={{16,0},{0,16},{17,1},{1,17},{18,2},{2,18},{19,3},{3,19},{20,4},{4,... | collective-permute-start | bytes 1277960 | tf_op jit(solution)/shard_map/ppermute | solution.py:27
  84.7 2.2 %shard_map.49.refs_4_ = f32[416,640]{1,0:T(8,128)S(1)} custom-call(bf16[320,8192]{1,0:T(8,128)(2,1)S(1)} %bitcast.2, bf16[320,8192]{1,0:T(8,128)(2,1)S(1)} %collective-permute-done.1.refs_1_, bf16[208,1024]{1,0:T(8,128)(2,1)S(1)} %collective-permute-done.7.refs_2_, bf16[208,1024]{1,0:T(8,128)(2,1)S(1)} %collective-permute-done.16.refs_3_, ...), custom_call_target="tpu_custom_call" | custom-call | flops 1 | bytes 1 | tf_op jit(solution)/shard_map/pallas_call | solution.py:52
  86.9 7.4 %collective-permute-done.19.refs_6_ = bf16[208,1280]{1,0:T(8,128)(2,1)S(1)} collective-permute-done((bf16[208,1280]{1,0:T(8,128)(2,1)S(1)}, bf16[208,1280]{1,0:T(8,128)(2,1)S(1)}, u32[]{:S(2)}, u32[]{:S(2)}) %collective-permute-start.19) | collective-permute-done | bytes 532512 | tf_op jit(solution)/shard_map/ppermute | solution.py:27
  94.4 1.8 %collective-permute-start.26 = (bf16[208,1280]{1,0:T(8,128)(2,1)S(1)}, bf16[208,1280]{1,0:T(8,128)(2,1)S(1)}, u32[]{:S(2)}, u32[]{:S(2)}) collective-permute-start(bf16[208,1280]{1,0:T(8,128)(2,1)S(1)} %collective-permute-done.19.refs_6_), channel_id=1, source_target_pairs={{16,0},{0,16},{17,1},{1,17},{18,2},{2,18},{19,3},{3,19},{20,4},{4,... | collective-permute-start | bytes 1597448 | tf_op jit(solution)/shard_map/ppermute | solution.py:27
  98.6 10.6 %collective-permute-done.22.refs_10_ = bf16[208,1664]{1,0:T(8,128)(2,1)S(1)} collective-permute-done((bf16[208,1664]{1,0:T(8,128)(2,1)S(1)}, bf16[208,1664]{1,0:T(8,128)(2,1)S(1)}, u32[]{:S(2)}, u32[]{:S(2)}) %collective-permute-start.22) | collective-permute-done | bytes 692256 | tf_op jit(solution)/shard_map/ppermute | solution.py:27
  109.2 1.8 %collective-permute-start.24 = (bf16[208,1664]{1,0:T(8,128)(2,1)S(1)}, bf16[208,1664]{1,0:T(8,128)(2,1)S(1)}, u32[]{:S(2)}, u32[]{:S(2)}) collective-permute-start(bf16[208,1664]{1,0:T(8,128)(2,1)S(1)} %collective-permute-done.22.refs_10_), channel_id=1, source_target_pairs={{16,0},{0,16},{17,1},{1,17},{18,2},{2,18},{19,3},{3,19},{20,4},{4,... | collective-permute-start | bytes 2076680 | tf_op jit(solution)/shard_map/ppermute | solution.py:27
  114.3 4.0 %shard_map.52.refs_8_ = bf16[320,8192]{1,0:T(8,128)(2,1)} custom-call(s32[1]{0:T(128)} %bitcast.side_ref, bf16[320,208]{1,0:T(8,128)(2,1)S(1)} %get-tuple-element.75.refs_0_, bf16[320,208]{1,0:T(8,128)(2,1)S(1)} %collective-permute-done.11.refs_1_, bf16[320,208]{1,0:T(8,128)(2,1)S(1)} %get-tuple-element.104.refs_2_, ...), custom_call_target="tpu_custom_call" | custom-call | flops 1 | bytes 1 | tf_op jit(solution)/shard_map/pallas_call | solution.py:52
  118.3 10.9 %collective-permute-done.30.refs_6_ = bf16[208,2304]{1,0:T(8,128)(2,1)S(1)} collective-permute-done((bf16[208,2304]{1,0:T(8,128)(2,1)S(1)}, bf16[208,2304]{1,0:T(8,128)(2,1)S(1)}, u32[]{:S(2)}, u32[]{:S(2)}) %collective-permute-start.30) | collective-permute-done | bytes 958496 | tf_op jit(solution)/shard_map/ppermute | solution.py:27
  129.7 2.0 %collective-permute-done.31.refs_7_ = bf16[208,2304]{1,0:T(8,128)(2,1)S(1)} collective-permute-done((bf16[208,2304]{1,0:T(8,128)(2,1)S(1)}, bf16[208,2304]{1,0:T(8,128)(2,1)S(1)}, u32[]{:S(2)}, u32[]{:S(2)}) %collective-permute-start.31) | collective-permute-done | bytes 958496 | tf_op jit(solution)/shard_map/ppermute | solution.py:27
  131.7 2.6 %shard_map.53.refs_8_ = bf16[320,8192]{1,0:T(8,128)(2,1)} custom-call(s32[1]{0:T(128)} %bitcast.side_ref, bf16[320,208]{1,0:T(8,128)(2,1)S(1)} %get-tuple-element.75.refs_0_, bf16[320,208]{1,0:T(8,128)(2,1)S(1)} %collective-permute-done.11.refs_1_, bf16[320,208]{1,0:T(8,128)(2,1)S(1)} %get-tuple-element.104.refs_2_, ...), custom_call_target="tpu_custom_call", output_to_operand_aliasing={{}: (9, {})} | custom-call | flops 1 | bytes 1 | tf_op jit(solution)/shard_map/pallas_call | solution.py:52
  134.3 2.2 %shard_map.54 = bf16[320,8192]{1,0:T(8,128)(2,1)} custom-call(s32[1]{0:T(128)} %bitcast.side_ref, bf16[320,208]{1,0:T(8,128)(2,1)S(1)} %get-tuple-element.75.refs_0_, bf16[320,208]{1,0:T(8,128)(2,1)S(1)} %collective-permute-done.11.refs_1_, bf16[320,208]{1,0:T(8,128)(2,1)S(1)} %get-tuple-element.104.refs_2_, ...), custom_call_target="tpu_custom_call", output_to_operand_aliasing={{}: (9, {})} | custom-call | flops 1 | bytes 1 | tf_op jit(solution)/shard_map/pallas_call | solution.py:52
  (66 shorter events, 25.2 us)
Async XLA Ops:
  1.4 26.8 %collective-permute-start.1 = (bf16[320,8192]{1,0:T(8,128)(2,1)}, bf16[320,8192]{1,0:T(8,128)(2,1)S(1)}, u32[]{:S(2)}, u32[]{:S(2)}) collective-permute-start(bf16[320,8192]{1,0:T(8,128)(2,1)} %refs_0_.6), channel_id=1, source_target_pairs={{1,0},{0,1},{3,2},{2,3},{5,4},{4,5},{7,6},{6,7},{9,8},{8,9},{11,10... | collective-permute-start | bytes 15728648 | tf_op jit(solution)/shard_map/ppermute | solution.py:27
  3.3 24.9 %collective-permute-start.2 = (bf16[208,8192]{1,0:T(8,128)(2,1)}, bf16[208,8192]{1,0:T(8,128)(2,1)S(1)}, u32[]{:S(2)}, u32[]{:S(2)}) collective-permute-start(bf16[208,8192]{1,0:T(8,128)(2,1)} %refs_4_.5), channel_id=1, source_target_pairs={{1,0},{0,1},{3,2},{2,3},{5,4},{4,5},{7,6},{6,7},{9,8},{8,9},{11,10... | collective-permute-start | bytes 10223624 | tf_op jit(solution)/shard_map/ppermute | solution.py:27
  3.4 15.7 %collective-permute-start.3 = (bf16[208,1024]{1,0:T(8,128)(2,1)S(1)}, bf16[208,1024]{1,0:T(8,128)(2,1)S(1)}, u32[]{:S(2)}, u32[]{:S(2)}) collective-permute-start(bf16[208,1024]{1,0:T(8,128)(2,1)S(1)} %slice_select_fusion.9), channel_id=1, source_target_pairs={{12,0},{0,4},{4,8},{8,12},{13,1},{1,5},{5,9},{9,13},{14,2},{2,6},{... | collective-permute-start | bytes 1277960 | tf_op jit(solution)/shard_map/ppermute | solution.py:27
  6.4 21.8 %collective-permute-start = (bf16[208,1024]{1,0:T(8,128)(2,1)S(1)}, bf16[208,1024]{1,0:T(8,128)(2,1)S(1)}, u32[]{:S(2)}, u32[]{:S(2)}) collective-permute-start(bf16[208,1024]{1,0:T(8,128)(2,1)S(1)} %slice_select_fusion.8), channel_id=1, source_target_pairs={{12,0},{0,4},{4,8},{8,12},{13,1},{1,5},{5,9},{9,13},{14,2},{2,6},{... | collective-permute-start | bytes 1277960 | tf_op jit(solution)/shard_map/ppermute | solution.py:27
  19.1 18.3 %collective-permute-start.5 = (bf16[208,1024]{1,0:T(8,128)(2,1)S(1)}, bf16[208,1024]{1,0:T(8,128)(2,1)S(1)}, u32[]{:S(2)}, u32[]{:S(2)}) collective-permute-start(bf16[208,1024]{1,0:T(8,128)(2,1)S(1)} %get-tuple-element.68), channel_id=1, source_target_pairs={{12,0},{0,4},{4,8},{8,12},{13,1},{1,5},{5,9},{9,13},{14,2},{2,6},{... | collective-permute-start | bytes 1277960 | tf_op jit(solution)/shard_map/ppermute | solution.py:27
  19.1 18.2 %collective-permute-start.6 = (bf16[208,1024]{1,0:T(8,128)(2,1)S(1)}, bf16[208,1024]{1,0:T(8,128)(2,1)S(1)}, u32[]{:S(2)}, u32[]{:S(2)}) collective-permute-start(bf16[208,1024]{1,0:T(8,128)(2,1)S(1)} %collective-permute-done.3.refs_2_), channel_id=1, source_target_pairs={{16,0},{0,16},{17,1},{1,17},{18,2},{2,18},{19,3},{3,19},{20,4},{4,... | collective-permute-start | bytes 1277960 | tf_op jit(solution)/shard_map/ppermute | solution.py:27
  28.2 18.3 %collective-permute-start.8 = (bf16[208,1024]{1,0:T(8,128)(2,1)S(1)}, bf16[208,1024]{1,0:T(8,128)(2,1)S(1)}, u32[]{:S(2)}, u32[]{:S(2)}) collective-permute-start(bf16[208,1024]{1,0:T(8,128)(2,1)S(1)} %get-tuple-element.71), channel_id=1, source_target_pairs={{12,0},{0,4},{4,8},{8,12},{13,1},{1,5},{5,9},{9,13},{14,2},{2,6},{... | collective-permute-start | bytes 1277960 | tf_op jit(solution)/shard_map/ppermute | solution.py:27
  28.2 18.2 %collective-permute-start.9 = (bf16[208,1024]{1,0:T(8,128)(2,1)S(1)}, bf16[208,1024]{1,0:T(8,128)(2,1)S(1)}, u32[]{:S(2)}, u32[]{:S(2)}) collective-permute-start(bf16[208,1024]{1,0:T(8,128)(2,1)S(1)} %collective-permute-done.refs_4_), channel_id=1, source_target_pairs={{16,0},{0,16},{17,1},{1,17},{18,2},{2,18},{19,3},{3,19},{20,4},{4,... | collective-permute-start | bytes 1277960 | tf_op jit(solution)/shard_map/ppermute | solution.py:27
  37.3 18.3 %collective-permute-start.7 = (bf16[208,1024]{1,0:T(8,128)(2,1)S(1)}, bf16[208,1024]{1,0:T(8,128)(2,1)S(1)}, u32[]{:S(2)}, u32[]{:S(2)}) collective-permute-start(bf16[208,1024]{1,0:T(8,128)(2,1)S(1)} %get-tuple-element.70), channel_id=1, source_target_pairs={{12,0},{0,4},{4,8},{8,12},{13,1},{1,5},{5,9},{9,13},{14,2},{2,6},{... | collective-permute-start | bytes 1277960 | tf_op jit(solution)/shard_map/ppermute | solution.py:27
  37.4 18.2 %collective-permute-start.10 = (bf16[208,1024]{1,0:T(8,128)(2,1)S(1)}, bf16[208,1024]{1,0:T(8,128)(2,1)S(1)}, u32[]{:S(2)}, u32[]{:S(2)}) collective-permute-start(bf16[208,1024]{1,0:T(8,128)(2,1)S(1)} %collective-permute-done.5.refs_6_), channel_id=1, source_target_pairs={{16,0},{0,16},{17,1},{1,17},{18,2},{2,18},{19,3},{3,19},{20,4},{4,... | collective-permute-start | bytes 1277960 | tf_op jit(solution)/shard_map/ppermute | solution.py:27
  39.1 18.3 %collective-permute-start.4 = (bf16[416,640]{1,0:T(8,128)(2,1)S(1)}, bf16[416,640]{1,0:T(8,128)(2,1)S(1)}, u32[]{:S(2)}, u32[]{:S(2)}) collective-permute-start(bf16[416,640]{1,0:T(8,128)(2,1)S(1)} %shard_map.46.refs_0_), channel_id=1, source_target_pairs={{2,0},{0,2},{3,1},{1,3},{6,4},{4,6},{7,5},{5,7},{10,8},{8,10},{11,... | collective-permute-start | bytes 1597448 | tf_op jit(solution)/shard_map/ppermute | solution.py:27
  46.4 18.3 %collective-permute-start.12 = (bf16[208,1024]{1,0:T(8,128)(2,1)S(1)}, bf16[208,1024]{1,0:T(8,128)(2,1)S(1)}, u32[]{:S(2)}, u32[]{:S(2)}) collective-permute-start(bf16[208,1024]{1,0:T(8,128)(2,1)S(1)} %get-tuple-element.77), channel_id=1, source_target_pairs={{12,0},{0,4},{4,8},{8,12},{13,1},{1,5},{5,9},{9,13},{14,2},{2,6},{... | collective-permute-start | bytes 1277960 | tf_op jit(solution)/shard_map/ppermute | solution.py:27
  46.5 18.2 %collective-permute-start.13 = (bf16[208,1024]{1,0:T(8,128)(2,1)S(1)}, bf16[208,1024]{1,0:T(8,128)(2,1)S(1)}, u32[]{:S(2)}, u32[]{:S(2)}) collective-permute-start(bf16[208,1024]{1,0:T(8,128)(2,1)S(1)} %collective-permute-done.8.refs_8_), channel_id=1, source_target_pairs={{16,0},{0,16},{17,1},{1,17},{18,2},{2,18},{19,3},{3,19},{20,4},{4,... | collective-permute-start | bytes 1277960 | tf_op jit(solution)/shard_map/ppermute | solution.py:27
  55.6 18.3 %collective-permute-start.15 = (bf16[208,1024]{1,0:T(8,128)(2,1)S(1)}, bf16[208,1024]{1,0:T(8,128)(2,1)S(1)}, u32[]{:S(2)}, u32[]{:S(2)}) collective-permute-start(bf16[208,1024]{1,0:T(8,128)(2,1)S(1)} %get-tuple-element.80), channel_id=1, source_target_pairs={{12,0},{0,4},{4,8},{8,12},{13,1},{1,5},{5,9},{9,13},{14,2},{2,6},{... | collective-permute-start | bytes 1277960 | tf_op jit(solution)/shard_map/ppermute | solution.py:27
  55.6 18.2 %collective-permute-start.16 = (bf16[208,1024]{1,0:T(8,128)(2,1)S(1)}, bf16[208,1024]{1,0:T(8,128)(2,1)S(1)}, u32[]{:S(2)}, u32[]{:S(2)}) collective-permute-start(bf16[208,1024]{1,0:T(8,128)(2,1)S(1)} %collective-permute-done.7.refs_2_), channel_id=1, source_target_pairs={{16,0},{0,16},{17,1},{1,17},{18,2},{2,18},{19,3},{3,19},{20,4},{4,... | collective-permute-start | bytes 1277960 | tf_op jit(solution)/shard_map/ppermute | solution.py:27
  64.7 18.3 %collective-permute-start.14 = (bf16[208,1024]{1,0:T(8,128)(2,1)S(1)}, bf16[208,1024]{1,0:T(8,128)(2,1)S(1)}, u32[]{:S(2)}, u32[]{:S(2)}) collective-permute-start(bf16[208,1024]{1,0:T(8,128)(2,1)S(1)} %get-tuple-element.79), channel_id=1, source_target_pairs={{12,0},{0,4},{4,8},{8,12},{13,1},{1,5},{5,9},{9,13},{14,2},{2,6},{... | collective-permute-start | bytes 1277960 | tf_op jit(solution)/shard_map/ppermute | solution.py:27
  64.7 18.2 %collective-permute-start.17 = (bf16[208,1024]{1,0:T(8,128)(2,1)S(1)}, bf16[208,1024]{1,0:T(8,128)(2,1)S(1)}, u32[]{:S(2)}, u32[]{:S(2)}) collective-permute-start(bf16[208,1024]{1,0:T(8,128)(2,1)S(1)} %collective-permute-done.12.refs_4_), channel_id=1, source_target_pairs={{16,0},{0,16},{17,1},{1,17},{18,2},{2,18},{19,3},{3,19},{20,4},{4,... | collective-permute-start | bytes 1277960 | tf_op jit(solution)/shard_map/ppermute | solution.py:27
  73.8 20.5 %collective-permute-start.19 = (bf16[208,1280]{1,0:T(8,128)(2,1)S(1)}, bf16[208,1280]{1,0:T(8,128)(2,1)S(1)}, u32[]{:S(2)}, u32[]{:S(2)}) collective-permute-start(bf16[208,1280]{1,0:T(8,128)(2,1)S(1)} %slice_select_fusion.1), channel_id=1, source_target_pairs={{12,0},{0,4},{4,8},{8,12},{13,1},{1,5},{5,9},{9,13},{14,2},{2,6},{... | collective-permute-start | bytes 1597448 | tf_op jit(solution)/shard_map/ppermute | solution.py:27
  83.0 13.2 %collective-permute-start.18 = (bf16[208,1024]{1,0:T(8,128)(2,1)S(1)}, bf16[208,1024]{1,0:T(8,128)(2,1)S(1)}, u32[]{:S(2)}, u32[]{:S(2)}) collective-permute-start(bf16[208,1024]{1,0:T(8,128)(2,1)S(1)} %collective-permute-done.14.refs_2_), channel_id=1, source_target_pairs={{16,0},{0,16},{17,1},{1,17},{18,2},{2,18},{19,3},{3,19},{20,4},{4,... | collective-permute-start | bytes 1277960 | tf_op jit(solution)/shard_map/ppermute | solution.py:27
  84.7 24.5 %collective-permute-start.22 = (bf16[208,1664]{1,0:T(8,128)(2,1)S(1)}, bf16[208,1664]{1,0:T(8,128)(2,1)S(1)}, u32[]{:S(2)}, u32[]{:S(2)}) collective-permute-start(bf16[208,1664]{1,0:T(8,128)(2,1)S(1)} %slice_select_fusion), channel_id=1, source_target_pairs={{12,0},{0,4},{4,8},{8,12},{13,1},{1,5},{5,9},{9,13},{14,2},{2,6},{... | collective-permute-start | bytes 2076680 | tf_op jit(solution)/shard_map/ppermute | solution.py:27
  94.4 16.6 %collective-permute-start.26 = (bf16[208,1280]{1,0:T(8,128)(2,1)S(1)}, bf16[208,1280]{1,0:T(8,128)(2,1)S(1)}, u32[]{:S(2)}, u32[]{:S(2)}) collective-permute-start(bf16[208,1280]{1,0:T(8,128)(2,1)S(1)} %collective-permute-done.19.refs_6_), channel_id=1, source_target_pairs={{16,0},{0,16},{17,1},{1,17},{18,2},{2,18},{19,3},{3,19},{20,4},{4,... | collective-permute-start | bytes 1597448 | tf_op jit(solution)/shard_map/ppermute | solution.py:27
  97.0 14.2 %collective-permute-start.21 = (bf16[416,640]{1,0:T(8,128)(2,1)S(1)}, bf16[416,640]{1,0:T(8,128)(2,1)S(1)}, u32[]{:S(2)}, u32[]{:S(2)}) collective-permute-start(bf16[416,640]{1,0:T(8,128)(2,1)S(1)} %shard_map.50.refs_0_), channel_id=1, source_target_pairs={{2,0},{0,2},{3,1},{1,3},{6,4},{4,6},{7,5},{5,7},{10,8},{8,10},{11,... | collective-permute-start | bytes 1597448 | tf_op jit(solution)/shard_map/ppermute | solution.py:27
  98.6 30.6 %collective-permute-start.30 = (bf16[208,2304]{1,0:T(8,128)(2,1)S(1)}, bf16[208,2304]{1,0:T(8,128)(2,1)S(1)}, u32[]{:S(2)}, u32[]{:S(2)}) collective-permute-start(bf16[208,2304]{1,0:T(8,128)(2,1)S(1)} %slice.83), channel_id=1, source_target_pairs={{12,0},{0,4},{4,8},{8,12},{13,1},{1,5},{5,9},{9,13},{14,2},{2,6},{... | collective-permute-start | bytes 2875400 | tf_op jit(solution)/shard_map/ppermute | solution.py:27
  109.2 20.0 %collective-permute-start.24 = (bf16[208,1664]{1,0:T(8,128)(2,1)S(1)}, bf16[208,1664]{1,0:T(8,128)(2,1)S(1)}, u32[]{:S(2)}, u32[]{:S(2)}) collective-permute-start(bf16[208,1664]{1,0:T(8,128)(2,1)S(1)} %collective-permute-done.22.refs_10_), channel_id=1, source_target_pairs={{16,0},{0,16},{17,1},{1,17},{18,2},{2,18},{19,3},{3,19},{20,4},{4,... | collective-permute-start | bytes 2076680 | tf_op jit(solution)/shard_map/ppermute | solution.py:27
  (13 other events, 112.0 us)

commit v14 on v13

--- a/solution.py
+++ b/solution.py
@@ -10,11 +10,12 @@
 FEATURE_SHARES = (1,) * 8
 LANE_SHARES = (10, 13, 9)
 WHOLES = 1
+FIRST = 1
 QUEUE = 2
 OWN, OWN_SUM, OWN_MATE = 1, 4, 6
 BATCHES = ((5, 0, 4), (7, 4, 7), (8, 7, 8))
 PASS = (8, 9)
-TAIL = (("own", 1), ("write", 0, -1, 1), ("other", 1), ("last", 1), ("write", 2), ("write", -2))
+TAIL = (("own", 1), ("write", 0, -1, 1), ("ready", 2, -2), ("other", 1), ("last", 1), ("write", 2), ("write", -2))
 SWAP_WAIT = 2
 HOLD = 0
 VMEM = 16 * 1024 * 1024
@@ -143,23 +144,53 @@
     return found
 
 
-def output_kernel(parts, side_ref, *refs):
-    hidden, down, arrived = refs[:4], refs[4:6], refs[6 : 6 + 2 * len(parts)]
+def columns_of(side_ref, parts):
+    side, at = side_ref[0], 0
+    for i, lane, size, (fixed, turn) in blocks_of(parts):
+        column = pl.ds(pl.multiple_of(fixed + side * turn, 128), size)
+        yield pl.ds(at, size), i, slice(lane, lane + size), column
+        at += size
+
+
+def terms_sum(total, terms):
+    for rows, weight in terms:
+        term = jnp.dot(rows[...], weight, preferred_element_type=jnp.float32)
+        total = term if total is None else total + term
+    return total
+
+
+def own_part_kernel(parts, side_ref, *refs):
+    hidden, down, outs = refs[:2], refs[2:4], refs[4:]
+    for _, i, lanes, column in columns_of(side_ref, parts):
+        outs[i][:, lanes] = terms_sum(
+            None, [(rows, ref[:, column]) for rows, ref in zip(hidden, down)]
+        )
+
+
+def own_parts(parts, side, hidden, down):
+    return call(
+        functools.partial(own_part_kernel, parts),
+        [side, *hidden, *down],
+        [pl.BlockSpec(memory_space=pltpu.SMEM)] + [WHOLE] * 4,
+        [jax.ShapeDtypeStruct((hidden[0].shape[0], part[1]), jnp.float32) for part in parts],
+        [WHOLE] * len(parts),
+        [],
+        {},
+    )
+
+
+def output_kernel(parts, known, side_ref, *refs):
+    near = 1 if known else 4
+    arrived = refs[2 : 2 + 2 * len(parts)]
+    given = refs[2 + 2 * len(parts) : 2 + 2 * len(parts) + near]
     out, result, sems = refs[-3:]
-    side = side_ref[0]
-    stores, at = [], 0
-    for n, (i, lane, size, (fixed, turn)) in enumerate(blocks_of(parts)):
-        column = pl.ds(pl.multiple_of(fixed + side * turn, 128), size)
-        spot = pl.ds(at, size)
-        at += size
-        total = None
-        for m in range(4):
-            if m < 2:
-                weight = down[m][:, column]
-            else:
-                weight = arrived[2 * i + m - 2][:, lane : lane + size]
-            term = jnp.dot(hidden[m][...], weight, preferred_element_type=jnp.float32)
-            total = term if total is None else total + term
+    stores = []
+    for n, (spot, i, lanes, column) in enumerate(columns_of(side_ref, parts)):
+        terms = [(refs[m], arrived[2 * i + m][:, lanes]) for m in range(2)]
+        if known:
+            total = terms_sum(given[0][:, lanes], terms)
+        else:
+            total = terms_sum(None, [(given[m], given[2 + m][:, column]) for m in range(2)] + terms)
         result[:, spot] = total.astype(result.dtype)
         stores.append(
             pltpu.make_async_copy(result.at[:, spot], out.at[:, column], sems.at[n])
@@ -169,21 +200,18 @@
         copy.wait()
 
 
-def output_part(result, parts, side, hidden, down, arrived):
-    rows, width = hidden[0].shape[0], down[0].shape[1]
+def output_part(result, parts, side, there, arrived, given, width):
+    rows = there[0].shape[0]
     lanes = sum(part[1] for part in parts)
-    operands = [side, *hidden, *down, *arrived]
-    in_specs = (
-        [pl.BlockSpec(memory_space=pltpu.SMEM)]
-        + [pl.BlockSpec(memory_space=pltpu.VMEM)] * (6 + len(arrived))
-    )
+    operands = [side, *there, *arrived, *given]
+    in_specs = [pl.BlockSpec(memory_space=pltpu.SMEM)] + [WHOLE] * (len(operands) - 1)
     aliases = {}
     if result is not None:
         aliases = {len(operands): 0}
         operands.append(result)
         in_specs.append(ANY)
     return call(
-        functools.partial(output_kernel, parts),
+        functools.partial(output_kernel, parts, len(given) == 1),
         operands,
         in_specs,
         jax.ShapeDtypeStruct((rows, width), jnp.bfloat16),
@@ -231,7 +259,7 @@
 
     pieces = [piece(0)]
     pieces.append(piece(1, pieces[0]))
-    pieces += [piece(i, pieces[1]) for i in range(2, total_count)]
+    pieces += [piece(i, pieces[FIRST]) for i in range(2, total_count)]
     waiting = [shifted(pieces[i], "dp", 1) for i in range(QUEUE)]
     landed, crossed, mates, crossed_mates = [], {}, {}, {}
 
@@ -294,29 +322,34 @@
     if HOLD:
         there_mate = tied(there_mate, crossed[count + 1])
 
+    ready = {}
+
+    def part_of(mark):
+        n = mark if mark >= 0 else -1 - mark
+        a, b = lane_cuts[n]
+        half = (b - a) // 2
+        if count + n >= relayed:
+            return a, b - a, 0, False
+        return a, half, half, mark < 0
+
     def write(result, *which):
-        parts, arrived = [], []
+        arrived = []
         for mark in which:
-            n = mark if mark >= 0 else -1 - mark
-            i = count + n
-            a, b = lane_cuts[n]
-            half = (b - a) // 2
-            if i >= relayed:
-                parts.append((a, b - a, 0, False))
-                arrived += [landed[i], mates[i]]
-            elif mark < 0:
-                parts.append((a, half, half, True))
-                arrived += [crossed[i], crossed_mates[i]]
+            if mark < 0:
+                arrived += [crossed[count - 1 - mark], crossed_mates[count - 1 - mark]]
             else:
-                parts.append((a, half, half, False))
-                arrived += [landed[i], mates[i]]
+                arrived += [landed[count + mark], mates[count + mark]]
+        given = [here, here_mate, down_weight, down_mate]
+        if which[0] in ready:
+            given = [ready[which[0]]]
         return output_part(
             result,
-            tuple(parts),
+            tuple(part_of(mark) for mark in which),
             side,
-            [here, here_mate, there, there_mate],
-            [down_weight, down_mate],
+            [there, there_mate],
             arrived,
+            given,
+            width,
         )
 
     result = None
@@ -330,8 +363,17 @@
                 pass_other(n, now, *([] if result is None else [result]))
         elif kind == "write":
             result = write(result, *numbers)
+        elif kind == "ready":
+            found = own_parts(
+                tuple(part_of(mark) for mark in numbers),
+                side,
+                [here, tied(here_mate, result)],
+                [down_weight, down_mate],
+            )
+            ready.update(zip(numbers, found))
         elif kind == "last":
             held = [] if result is None else [result]
+            held += ready.values()
             held += [crossed[count + n] for n in numbers]
             now = advance(*held)
             pass_own(len(landed) - 1 - count, now)

time: 137 us -> 135 us (0.985)
  waiting for transfers between devices: 81.8 us -> 80.2 us
    ppermute x32, waiting for transfers between devices: 81.8 us -> 80.2 us  [shifted(): return lax.ppermute(block, axis, route)]
    pallas_call x9 -> x10, Pallas kernels: 20.8 us -> 21 us  [call(): pl.pallas_call(kernel, in_specs=in_specs, out_specs=out_spec, out_shape=o...]
where the time goes in v14:
time: 135 us
  waiting for transfers between devices  80.2 us (59%)
  starting transfers between devices  27.3 us (20%)
  Pallas kernels  21 us (16%)
  other arithmetic  6.33 us (5%)
    ppermute x32, waiting for transfers between devices, shifted(): return lax.ppermute(block, axis, route)  80.2 us
    ppermute x32, starting transfers between devices, shifted(): return lax.ppermute(block, axis, route)  27.3 us
    pallas_call x10, Pallas kernels, call(): pl.pallas_call(kernel, in_specs=in_specs, out_specs=out_spec, out_shape=o...  21 us
    select_n x3, other arithmetic, piece(): return jnp.where(first, gate[:, a:b], up[:, a:b])  4.89 us
  transfers between devices with their start and end apart: 32, of which 14 were waited for; matrix products, arithmetic and copies ran while one was open for 4% of the time, Pallas kernels for 14%

profile of v14, /device:TPU:0, one launch (start us, length us, event | category | flops | bytes accessed | tf_op | source)
XLA Modules:
  0.0 135.3 jit_solution(2882931429662310229)
XLA Ops:
  3.4 3.1 %collective-permute-start.3 = (bf16[208,1024]{1,0:T(8,128)(2,1)S(1)}, bf16[208,1024]{1,0:T(8,128)(2,1)S(1)}, u32[]{:S(2)}, u32[]{:S(2)}) collective-permute-start(bf16[208,1024]{1,0:T(8,128)(2,1)S(1)} %slice_select_fusion.9), channel_id=1, source_target_pairs={{12,0},{0,4},{4,8},{8,12},{13,1},{1,5},{5,9},{9,13},{14,2},{2,6},{... | collective-permute-start | bytes 1277960 | tf_op jit(solution)/shard_map/ppermute | solution.py:28
  9.6 2.1 %slice_select_fusion.2 = (bf16[208,1024]{1,0:T(8,128)(2,1)S(1)}, bf16[208,1024]{1,0:T(8,128)(2,1)S(1)}, bf16[208,1024]{1,0:T(8,128)(2,1)S(1)}, bf16[208,1024]{1,...) fusion(bf16[208,8192]{1,0:T(8,128)(2,1)S(1)} %copy-done.1, ...), kind=kLoop, calls=%fused_computation.2 | loop fusion | flops 1277952 | bytes 7667713 | tf_op jit(solution)/shard_map/jit(_where)/select_n | solution.py:252
  11.7 7.3 %collective-permute-done.3.refs_2_ = bf16[208,1024]{1,0:T(8,128)(2,1)S(1)} collective-permute-done((bf16[208,1024]{1,0:T(8,128)(2,1)S(1)}, bf16[208,1024]{1,0:T(8,128)(2,1)S(1)}, u32[]{:S(2)}, u32[]{:S(2)}) %collective-permute-start.3) | collective-permute-done | bytes 426016 | tf_op jit(solution)/shard_map/ppermute | solution.py:28
  20.8 7.4 %collective-permute-done.1.refs_4_ = bf16[208,1024]{1,0:T(8,128)(2,1)S(1)} collective-permute-done((bf16[208,1024]{1,0:T(8,128)(2,1)S(1)}, bf16[208,1024]{1,0:T(8,128)(2,1)S(1)}, u32[]{:S(2)}, u32[]{:S(2)}) %collective-permute-start.1) | collective-permute-done | bytes 426016 | tf_op jit(solution)/shard_map/ppermute | solution.py:28
  28.2 1.8 %collective-permute-start.7 = (bf16[208,1024]{1,0:T(8,128)(2,1)S(1)}, bf16[208,1024]{1,0:T(8,128)(2,1)S(1)}, u32[]{:S(2)}, u32[]{:S(2)}) collective-permute-start(bf16[208,1024]{1,0:T(8,128)(2,1)S(1)} %collective-permute-done.1.refs_4_), channel_id=1, source_target_pairs={{16,0},{0,16},{17,1},{1,17},{18,2},{2,18},{19,3},{3,19},{20,4},{4,... | collective-permute-start | bytes 1277960 | tf_op jit(solution)/shard_map/ppermute | solution.py:28
  30.0 5.5 %shard_map.46.refs_0_ = bf16[416,640]{1,0:T(8,128)(2,1)S(1)} custom-call(bf16[320,8192]{1,0:T(8,128)(2,1)S(1)} %bitcast.2, bf16[320,8192]{1,0:T(8,128)(2,1)S(1)} %collective-permute-done.refs_1_, bf16[208,8192]{1,0:T(8,128)(2,1)S(1)} %copy-done.2, bf16[208,8192]{1,0:T(8,128)(2,1)S(1)} %copy-done.1), custom_call_target="tpu_custom_call" | custom-call | flops 1 | bytes 1 | tf_op jit(solution)/shard_map/pallas_call | solution.py:53
  35.5 1.8 %collective-permute-done.5.refs_6_ = bf16[208,1024]{1,0:T(8,128)(2,1)S(1)} collective-permute-done((bf16[208,1024]{1,0:T(8,128)(2,1)S(1)}, bf16[208,1024]{1,0:T(8,128)(2,1)S(1)}, u32[]{:S(2)}, u32[]{:S(2)}) %collective-permute-start.5) | collective-permute-done | bytes 426016 | tf_op jit(solution)/shard_map/ppermute | solution.py:28
  40.6 5.9 %collective-permute-done.4.refs_8_ = bf16[208,1024]{1,0:T(8,128)(2,1)S(1)} collective-permute-done((bf16[208,1024]{1,0:T(8,128)(2,1)S(1)}, bf16[208,1024]{1,0:T(8,128)(2,1)S(1)}, u32[]{:S(2)}, u32[]{:S(2)}) %collective-permute-start.4) | collective-permute-done | bytes 426016 | tf_op jit(solution)/shard_map/ppermute | solution.py:28
  48.2 7.4 %collective-permute-done.10.refs_2_ = bf16[208,1024]{1,0:T(8,128)(2,1)S(1)} collective-permute-done((bf16[208,1024]{1,0:T(8,128)(2,1)S(1)}, bf16[208,1024]{1,0:T(8,128)(2,1)S(1)}, u32[]{:S(2)}, u32[]{:S(2)}) %collective-permute-start.10) | collective-permute-done | bytes 426016 | tf_op jit(solution)/shard_map/ppermute | solution.py:28
  57.7 7.0 %collective-permute-done.8.refs_4_ = bf16[208,1024]{1,0:T(8,128)(2,1)S(1)} collective-permute-done((bf16[208,1024]{1,0:T(8,128)(2,1)S(1)}, bf16[208,1024]{1,0:T(8,128)(2,1)S(1)}, u32[]{:S(2)}, u32[]{:S(2)}) %collective-permute-start.8) | collective-permute-done | bytes 426016 | tf_op jit(solution)/shard_map/ppermute | solution.py:28
  64.7 1.7 %collective-permute-start.17 = (bf16[208,1024]{1,0:T(8,128)(2,1)S(1)}, bf16[208,1024]{1,0:T(8,128)(2,1)S(1)}, u32[]{:S(2)}, u32[]{:S(2)}) collective-permute-start(bf16[208,1024]{1,0:T(8,128)(2,1)S(1)} %collective-permute-done.8.refs_4_), channel_id=1, source_target_pairs={{16,0},{0,16},{17,1},{1,17},{18,2},{2,18},{19,3},{3,19},{20,4},{4,... | collective-permute-start | bytes 1277960 | tf_op jit(solution)/shard_map/ppermute | solution.py:28
  66.5 2.8 %shard_map.48.refs_8_ = f32[416,640]{1,0:T(8,128)S(1)} custom-call(bf16[320,8192]{1,0:T(8,128)(2,1)S(1)} %bitcast.2, bf16[320,8192]{1,0:T(8,128)(2,1)S(1)} %collective-permute-done.refs_1_, bf16[208,1024]{1,0:T(8,128)(2,1)S(1)} %collective-permute-done.3.refs_2_, bf16[208,1024]{1,0:T(8,128)(2,1)S(1)} %collective-permute-done.6.refs_3_, ...), custom_call_target="tpu_custom_call" | custom-call | flops 1 | bytes 1 | tf_op jit(solution)/shard_map/pallas_call | solution.py:53
  69.3 4.5 %collective-permute-done.14.refs_6_ = bf16[208,1024]{1,0:T(8,128)(2,1)S(1)} collective-permute-done((bf16[208,1024]{1,0:T(8,128)(2,1)S(1)}, bf16[208,1024]{1,0:T(8,128)(2,1)S(1)}, u32[]{:S(2)}, u32[]{:S(2)}) %collective-permute-start.14) | collective-permute-done | bytes 426016 | tf_op jit(solution)/shard_map/ppermute | solution.py:28
  75.6 7.4 %collective-permute-done.13.refs_2_ = bf16[208,1024]{1,0:T(8,128)(2,1)S(1)} collective-permute-done((bf16[208,1024]{1,0:T(8,128)(2,1)S(1)}, bf16[208,1024]{1,0:T(8,128)(2,1)S(1)}, u32[]{:S(2)}, u32[]{:S(2)}) %collective-permute-start.13) | collective-permute-done | bytes 426016 | tf_op jit(solution)/shard_map/ppermute | solution.py:28
  83.0 1.8 %collective-permute-start.18 = (bf16[208,1024]{1,0:T(8,128)(2,1)S(1)}, bf16[208,1024]{1,0:T(8,128)(2,1)S(1)}, u32[]{:S(2)}, u32[]{:S(2)}) collective-permute-start(bf16[208,1024]{1,0:T(8,128)(2,1)S(1)} %collective-permute-done.13.refs_2_), channel_id=1, source_target_pairs={{16,0},{0,16},{17,1},{1,17},{18,2},{2,18},{19,3},{3,19},{20,4},{4,... | collective-permute-start | bytes 1277960 | tf_op jit(solution)/shard_map/ppermute | solution.py:28
  84.7 2.2 %shard_map.49.refs_4_ = f32[416,640]{1,0:T(8,128)S(1)} custom-call(bf16[320,8192]{1,0:T(8,128)(2,1)S(1)} %bitcast.2, bf16[320,8192]{1,0:T(8,128)(2,1)S(1)} %collective-permute-done.refs_1_, bf16[208,1024]{1,0:T(8,128)(2,1)S(1)} %collective-permute-done.10.refs_2_, bf16[208,1024]{1,0:T(8,128)(2,1)S(1)} %collective-permute-done.16.refs_3_, ...), custom_call_target="tpu_custom_call" | custom-call | flops 1 | bytes 1 | tf_op jit(solution)/shard_map/pallas_call | solution.py:53
  86.9 7.5 %collective-permute-done.19.refs_2_ = bf16[208,1280]{1,0:T(8,128)(2,1)S(1)} collective-permute-done((bf16[208,1280]{1,0:T(8,128)(2,1)S(1)}, bf16[208,1280]{1,0:T(8,128)(2,1)S(1)}, u32[]{:S(2)}, u32[]{:S(2)}) %collective-permute-start.19) | collective-permute-done | bytes 532512 | tf_op jit(solution)/shard_map/ppermute | solution.py:28
  94.4 1.8 %collective-permute-start.26 = (bf16[208,1280]{1,0:T(8,128)(2,1)S(1)}, bf16[208,1280]{1,0:T(8,128)(2,1)S(1)}, u32[]{:S(2)}, u32[]{:S(2)}) collective-permute-start(bf16[208,1280]{1,0:T(8,128)(2,1)S(1)} %collective-permute-done.19.refs_2_), channel_id=1, source_target_pairs={{16,0},{0,16},{17,1},{1,17},{18,2},{2,18},{19,3},{3,19},{20,4},{4,... | collective-permute-start | bytes 1597448 | tf_op jit(solution)/shard_map/ppermute | solution.py:28
  98.6 10.6 %collective-permute-done.22.refs_6_ = bf16[208,1664]{1,0:T(8,128)(2,1)S(1)} collective-permute-done((bf16[208,1664]{1,0:T(8,128)(2,1)S(1)}, bf16[208,1664]{1,0:T(8,128)(2,1)S(1)}, u32[]{:S(2)}, u32[]{:S(2)}) %collective-permute-start.22) | collective-permute-done | bytes 692256 | tf_op jit(solution)/shard_map/ppermute | solution.py:28
  109.2 1.8 %collective-permute-start.24 = (bf16[208,1664]{1,0:T(8,128)(2,1)S(1)}, bf16[208,1664]{1,0:T(8,128)(2,1)S(1)}, u32[]{:S(2)}, u32[]{:S(2)}) collective-permute-start(bf16[208,1664]{1,0:T(8,128)(2,1)S(1)} %collective-permute-done.22.refs_6_), channel_id=1, source_target_pairs={{16,0},{0,16},{17,1},{1,17},{18,2},{2,18},{19,3},{3,19},{20,4},{4,... | collective-permute-start | bytes 2076680 | tf_op jit(solution)/shard_map/ppermute | solution.py:28
  114.3 4.0 %shard_map.52.refs_5_ = bf16[320,8192]{1,0:T(8,128)(2,1)} custom-call(s32[1]{0:T(128)} %bitcast.side_ref, bf16[320,208]{1,0:T(8,128)(2,1)S(1)} %get-tuple-element.107.refs_0_, bf16[320,208]{1,0:T(8,128)(2,1)S(1)} %collective-permute-done.23.refs_1_, bf16[208,1280]{1,0:T(8,128)(2,1)S(1)} %collective-permute-done.19.refs_2_, ...), custom_call_target="tpu_custom_call" | custom-call | flops 1 | bytes 1 | tf_op jit(solution)/shard_map/pallas_call | solution.py:53
  119.8 9.3 %collective-permute-done.30.refs_2_ = bf16[208,2304]{1,0:T(8,128)(2,1)S(1)} collective-permute-done((bf16[208,2304]{1,0:T(8,128)(2,1)S(1)}, bf16[208,2304]{1,0:T(8,128)(2,1)S(1)}, u32[]{:S(2)}, u32[]{:S(2)}) %collective-permute-start.30) | collective-permute-done | bytes 958496 | tf_op jit(solution)/shard_map/ppermute | solution.py:28
  129.7 2.0 %collective-permute-done.31.refs_3_ = bf16[208,2304]{1,0:T(8,128)(2,1)S(1)} collective-permute-done((bf16[208,2304]{1,0:T(8,128)(2,1)S(1)}, bf16[208,2304]{1,0:T(8,128)(2,1)S(1)}, u32[]{:S(2)}, u32[]{:S(2)}) %collective-permute-start.31) | collective-permute-done | bytes 958496 | tf_op jit(solution)/shard_map/ppermute | solution.py:28
  131.7 1.8 %shard_map.54.refs_5_ = bf16[320,8192]{1,0:T(8,128)(2,1)} custom-call(s32[1]{0:T(128)} %bitcast.side_ref, bf16[320,208]{1,0:T(8,128)(2,1)S(1)} %get-tuple-element.107.refs_0_, bf16[320,208]{1,0:T(8,128)(2,1)S(1)} %collective-permute-done.23.refs_1_, bf16[208,2304]{1,0:T(8,128)(2,1)S(1)} %collective-permute-done.30.refs_2_, ...), custom_call_target="tpu_custom_call", output_to_operand_aliasing={{}: (6, {})} | custom-call | flops 1 | bytes 1 | tf_op jit(solution)/shard_map/pallas_call | solution.py:53
  (67 shorter events, 26.6 us)
Async XLA Ops:
  1.4 26.8 %collective-permute-start = (bf16[320,8192]{1,0:T(8,128)(2,1)}, bf16[320,8192]{1,0:T(8,128)(2,1)S(1)}, u32[]{:S(2)}, u32[]{:S(2)}) collective-permute-start(bf16[320,8192]{1,0:T(8,128)(2,1)} %refs_0_.6), channel_id=1, source_target_pairs={{1,0},{0,1},{3,2},{2,3},{5,4},{4,5},{7,6},{6,7},{9,8},{8,9},{11,10... | collective-permute-start | bytes 15728648 | tf_op jit(solution)/shard_map/ppermute | solution.py:28
  3.3 24.9 %collective-permute-start.2 = (bf16[208,8192]{1,0:T(8,128)(2,1)}, bf16[208,8192]{1,0:T(8,128)(2,1)S(1)}, u32[]{:S(2)}, u32[]{:S(2)}) collective-permute-start(bf16[208,8192]{1,0:T(8,128)(2,1)} %refs_2_.3), channel_id=1, source_target_pairs={{1,0},{0,1},{3,2},{2,3},{5,4},{4,5},{7,6},{6,7},{9,8},{8,9},{11,10... | collective-permute-start | bytes 10223624 | tf_op jit(solution)/shard_map/ppermute | solution.py:28
  3.4 15.7 %collective-permute-start.3 = (bf16[208,1024]{1,0:T(8,128)(2,1)S(1)}, bf16[208,1024]{1,0:T(8,128)(2,1)S(1)}, u32[]{:S(2)}, u32[]{:S(2)}) collective-permute-start(bf16[208,1024]{1,0:T(8,128)(2,1)S(1)} %slice_select_fusion.9), channel_id=1, source_target_pairs={{12,0},{0,4},{4,8},{8,12},{13,1},{1,5},{5,9},{9,13},{14,2},{2,6},{... | collective-permute-start | bytes 1277960 | tf_op jit(solution)/shard_map/ppermute | solution.py:28
  6.4 21.8 %collective-permute-start.1 = (bf16[208,1024]{1,0:T(8,128)(2,1)S(1)}, bf16[208,1024]{1,0:T(8,128)(2,1)S(1)}, u32[]{:S(2)}, u32[]{:S(2)}) collective-permute-start(bf16[208,1024]{1,0:T(8,128)(2,1)S(1)} %slice_select_fusion.8), channel_id=1, source_target_pairs={{12,0},{0,4},{4,8},{8,12},{13,1},{1,5},{5,9},{9,13},{14,2},{2,6},{... | collective-permute-start | bytes 1277960 | tf_op jit(solution)/shard_map/ppermute | solution.py:28
  19.1 18.3 %collective-permute-start.5 = (bf16[208,1024]{1,0:T(8,128)(2,1)S(1)}, bf16[208,1024]{1,0:T(8,128)(2,1)S(1)}, u32[]{:S(2)}, u32[]{:S(2)}) collective-permute-start(bf16[208,1024]{1,0:T(8,128)(2,1)S(1)} %get-tuple-element.71), channel_id=1, source_target_pairs={{12,0},{0,4},{4,8},{8,12},{13,1},{1,5},{5,9},{9,13},{14,2},{2,6},{... | collective-permute-start | bytes 1277960 | tf_op jit(solution)/shard_map/ppermute | solution.py:28
  19.1 18.2 %collective-permute-start.6 = (bf16[208,1024]{1,0:T(8,128)(2,1)S(1)}, bf16[208,1024]{1,0:T(8,128)(2,1)S(1)}, u32[]{:S(2)}, u32[]{:S(2)}) collective-permute-start(bf16[208,1024]{1,0:T(8,128)(2,1)S(1)} %collective-permute-done.3.refs_2_), channel_id=1, source_target_pairs={{16,0},{0,16},{17,1},{1,17},{18,2},{2,18},{19,3},{3,19},{20,4},{4,... | collective-permute-start | bytes 1277960 | tf_op jit(solution)/shard_map/ppermute | solution.py:28
  28.2 18.3 %collective-permute-start.4 = (bf16[208,1024]{1,0:T(8,128)(2,1)S(1)}, bf16[208,1024]{1,0:T(8,128)(2,1)S(1)}, u32[]{:S(2)}, u32[]{:S(2)}) collective-permute-start(bf16[208,1024]{1,0:T(8,128)(2,1)S(1)} %get-tuple-element.70), channel_id=1, source_target_pairs={{12,0},{0,4},{4,8},{8,12},{13,1},{1,5},{5,9},{9,13},{14,2},{2,6},{... | collective-permute-start | bytes 1277960 | tf_op jit(solution)/shard_map/ppermute | solution.py:28
  28.2 18.2 %collective-permute-start.7 = (bf16[208,1024]{1,0:T(8,128)(2,1)S(1)}, bf16[208,1024]{1,0:T(8,128)(2,1)S(1)}, u32[]{:S(2)}, u32[]{:S(2)}) collective-permute-start(bf16[208,1024]{1,0:T(8,128)(2,1)S(1)} %collective-permute-done.1.refs_4_), channel_id=1, source_target_pairs={{16,0},{0,16},{17,1},{1,17},{18,2},{2,18},{19,3},{3,19},{20,4},{4,... | collective-permute-start | bytes 1277960 | tf_op jit(solution)/shard_map/ppermute | solution.py:28
  37.3 18.3 %collective-permute-start.10 = (bf16[208,1024]{1,0:T(8,128)(2,1)S(1)}, bf16[208,1024]{1,0:T(8,128)(2,1)S(1)}, u32[]{:S(2)}, u32[]{:S(2)}) collective-permute-start(bf16[208,1024]{1,0:T(8,128)(2,1)S(1)} %get-tuple-element.76), channel_id=1, source_target_pairs={{12,0},{0,4},{4,8},{8,12},{13,1},{1,5},{5,9},{9,13},{14,2},{2,6},{... | collective-permute-start | bytes 1277960 | tf_op jit(solution)/shard_map/ppermute | solution.py:28
  37.4 18.2 %collective-permute-start.11 = (bf16[208,1024]{1,0:T(8,128)(2,1)S(1)}, bf16[208,1024]{1,0:T(8,128)(2,1)S(1)}, u32[]{:S(2)}, u32[]{:S(2)}) collective-permute-start(bf16[208,1024]{1,0:T(8,128)(2,1)S(1)} %collective-permute-done.5.refs_6_), channel_id=1, source_target_pairs={{16,0},{0,16},{17,1},{1,17},{18,2},{2,18},{19,3},{3,19},{20,4},{4,... | collective-permute-start | bytes 1277960 | tf_op jit(solution)/shard_map/ppermute | solution.py:28
  39.1 18.3 %collective-permute-start.9 = (bf16[416,640]{1,0:T(8,128)(2,1)S(1)}, bf16[416,640]{1,0:T(8,128)(2,1)S(1)}, u32[]{:S(2)}, u32[]{:S(2)}) collective-permute-start(bf16[416,640]{1,0:T(8,128)(2,1)S(1)} %shard_map.46.refs_0_), channel_id=1, source_target_pairs={{2,0},{0,2},{3,1},{1,3},{6,4},{4,6},{7,5},{5,7},{10,8},{8,10},{11,... | collective-permute-start | bytes 1597448 | tf_op jit(solution)/shard_map/ppermute | solution.py:28
  46.4 18.3 %collective-permute-start.8 = (bf16[208,1024]{1,0:T(8,128)(2,1)S(1)}, bf16[208,1024]{1,0:T(8,128)(2,1)S(1)}, u32[]{:S(2)}, u32[]{:S(2)}) collective-permute-start(bf16[208,1024]{1,0:T(8,128)(2,1)S(1)} %get-tuple-element.75), channel_id=1, source_target_pairs={{12,0},{0,4},{4,8},{8,12},{13,1},{1,5},{5,9},{9,13},{14,2},{2,6},{... | collective-permute-start | bytes 1277960 | tf_op jit(solution)/shard_map/ppermute | solution.py:28
  46.5 18.2 %collective-permute-start.12 = (bf16[208,1024]{1,0:T(8,128)(2,1)S(1)}, bf16[208,1024]{1,0:T(8,128)(2,1)S(1)}, u32[]{:S(2)}, u32[]{:S(2)}) collective-permute-start(bf16[208,1024]{1,0:T(8,128)(2,1)S(1)} %collective-permute-done.4.refs_8_), channel_id=1, source_target_pairs={{16,0},{0,16},{17,1},{1,17},{18,2},{2,18},{19,3},{3,19},{20,4},{4,... | collective-permute-start | bytes 1277960 | tf_op jit(solution)/shard_map/ppermute | solution.py:28
  55.6 18.3 %collective-permute-start.14 = (bf16[208,1024]{1,0:T(8,128)(2,1)S(1)}, bf16[208,1024]{1,0:T(8,128)(2,1)S(1)}, u32[]{:S(2)}, u32[]{:S(2)}) collective-permute-start(bf16[208,1024]{1,0:T(8,128)(2,1)S(1)} %get-tuple-element.82), channel_id=1, source_target_pairs={{12,0},{0,4},{4,8},{8,12},{13,1},{1,5},{5,9},{9,13},{14,2},{2,6},{... | collective-permute-start | bytes 1277960 | tf_op jit(solution)/shard_map/ppermute | solution.py:28
  55.6 18.2 %collective-permute-start.16 = (bf16[208,1024]{1,0:T(8,128)(2,1)S(1)}, bf16[208,1024]{1,0:T(8,128)(2,1)S(1)}, u32[]{:S(2)}, u32[]{:S(2)}) collective-permute-start(bf16[208,1024]{1,0:T(8,128)(2,1)S(1)} %collective-permute-done.10.refs_2_), channel_id=1, source_target_pairs={{16,0},{0,16},{17,1},{1,17},{18,2},{2,18},{19,3},{3,19},{20,4},{4,... | collective-permute-start | bytes 1277960 | tf_op jit(solution)/shard_map/ppermute | solution.py:28
  64.7 18.3 %collective-permute-start.13 = (bf16[208,1024]{1,0:T(8,128)(2,1)S(1)}, bf16[208,1024]{1,0:T(8,128)(2,1)S(1)}, u32[]{:S(2)}, u32[]{:S(2)}) collective-permute-start(bf16[208,1024]{1,0:T(8,128)(2,1)S(1)} %get-tuple-element.81), channel_id=1, source_target_pairs={{12,0},{0,4},{4,8},{8,12},{13,1},{1,5},{5,9},{9,13},{14,2},{2,6},{... | collective-permute-start | bytes 1277960 | tf_op jit(solution)/shard_map/ppermute | solution.py:28
  64.7 18.2 %collective-permute-start.17 = (bf16[208,1024]{1,0:T(8,128)(2,1)S(1)}, bf16[208,1024]{1,0:T(8,128)(2,1)S(1)}, u32[]{:S(2)}, u32[]{:S(2)}) collective-permute-start(bf16[208,1024]{1,0:T(8,128)(2,1)S(1)} %collective-permute-done.8.refs_4_), channel_id=1, source_target_pairs={{16,0},{0,16},{17,1},{1,17},{18,2},{2,18},{19,3},{3,19},{20,4},{4,... | collective-permute-start | bytes 1277960 | tf_op jit(solution)/shard_map/ppermute | solution.py:28
  73.8 20.5 %collective-permute-start.19 = (bf16[208,1280]{1,0:T(8,128)(2,1)S(1)}, bf16[208,1280]{1,0:T(8,128)(2,1)S(1)}, u32[]{:S(2)}, u32[]{:S(2)}) collective-permute-start(bf16[208,1280]{1,0:T(8,128)(2,1)S(1)} %slice_select_fusion.1), channel_id=1, source_target_pairs={{12,0},{0,4},{4,8},{8,12},{13,1},{1,5},{5,9},{9,13},{14,2},{2,6},{... | collective-permute-start | bytes 1597448 | tf_op jit(solution)/shard_map/ppermute | solution.py:28
  83.0 13.2 %collective-permute-start.18 = (bf16[208,1024]{1,0:T(8,128)(2,1)S(1)}, bf16[208,1024]{1,0:T(8,128)(2,1)S(1)}, u32[]{:S(2)}, u32[]{:S(2)}) collective-permute-start(bf16[208,1024]{1,0:T(8,128)(2,1)S(1)} %collective-permute-done.13.refs_2_), channel_id=1, source_target_pairs={{16,0},{0,16},{17,1},{1,17},{18,2},{2,18},{19,3},{3,19},{20,4},{4,... | collective-permute-start | bytes 1277960 | tf_op jit(solution)/shard_map/ppermute | solution.py:28
  84.7 24.5 %collective-permute-start.22 = (bf16[208,1664]{1,0:T(8,128)(2,1)S(1)}, bf16[208,1664]{1,0:T(8,128)(2,1)S(1)}, u32[]{:S(2)}, u32[]{:S(2)}) collective-permute-start(bf16[208,1664]{1,0:T(8,128)(2,1)S(1)} %slice_select_fusion), channel_id=1, source_target_pairs={{12,0},{0,4},{4,8},{8,12},{13,1},{1,5},{5,9},{9,13},{14,2},{2,6},{... | collective-permute-start | bytes 2076680 | tf_op jit(solution)/shard_map/ppermute | solution.py:28
  94.4 16.6 %collective-permute-start.26 = (bf16[208,1280]{1,0:T(8,128)(2,1)S(1)}, bf16[208,1280]{1,0:T(8,128)(2,1)S(1)}, u32[]{:S(2)}, u32[]{:S(2)}) collective-permute-start(bf16[208,1280]{1,0:T(8,128)(2,1)S(1)} %collective-permute-done.19.refs_2_), channel_id=1, source_target_pairs={{16,0},{0,16},{17,1},{1,17},{18,2},{2,18},{19,3},{3,19},{20,4},{4,... | collective-permute-start | bytes 1597448 | tf_op jit(solution)/shard_map/ppermute | solution.py:28
  97.0 14.2 %collective-permute-start.21 = (bf16[416,640]{1,0:T(8,128)(2,1)S(1)}, bf16[416,640]{1,0:T(8,128)(2,1)S(1)}, u32[]{:S(2)}, u32[]{:S(2)}) collective-permute-start(bf16[416,640]{1,0:T(8,128)(2,1)S(1)} %shard_map.50.refs_0_), channel_id=1, source_target_pairs={{2,0},{0,2},{3,1},{1,3},{6,4},{4,6},{7,5},{5,7},{10,8},{8,10},{11,... | collective-permute-start | bytes 1597448 | tf_op jit(solution)/shard_map/ppermute | solution.py:28
  98.6 30.6 %collective-permute-start.30 = (bf16[208,2304]{1,0:T(8,128)(2,1)S(1)}, bf16[208,2304]{1,0:T(8,128)(2,1)S(1)}, u32[]{:S(2)}, u32[]{:S(2)}) collective-permute-start(bf16[208,2304]{1,0:T(8,128)(2,1)S(1)} %slice.83), channel_id=1, source_target_pairs={{12,0},{0,4},{4,8},{8,12},{13,1},{1,5},{5,9},{9,13},{14,2},{2,6},{... | collective-permute-start | bytes 2875400 | tf_op jit(solution)/shard_map/ppermute | solution.py:28
  109.2 20.0 %collective-permute-start.24 = (bf16[208,1664]{1,0:T(8,128)(2,1)S(1)}, bf16[208,1664]{1,0:T(8,128)(2,1)S(1)}, u32[]{:S(2)}, u32[]{:S(2)}) collective-permute-start(bf16[208,1664]{1,0:T(8,128)(2,1)S(1)} %collective-permute-done.22.refs_6_), channel_id=1, source_target_pairs={{16,0},{0,16},{17,1},{1,17},{18,2},{2,18},{19,3},{3,19},{20,4},{4,... | collective-permute-start | bytes 2076680 | tf_op jit(solution)/shard_map/ppermute | solution.py:28
  (13 other events, 111.2 us)

commit v15 on v14

--- a/solution.py
+++ b/solution.py
@@ -10,14 +10,12 @@
 FEATURE_SHARES = (1,) * 8
 LANE_SHARES = (10, 13, 9)
 WHOLES = 1
-FIRST = 1
 QUEUE = 2
 OWN, OWN_SUM, OWN_MATE = 1, 4, 6
 BATCHES = ((5, 0, 4), (7, 4, 7), (8, 7, 8))
 PASS = (8, 9)
 TAIL = (("own", 1), ("write", 0, -1, 1), ("ready", 2, -2), ("other", 1), ("last", 1), ("write", 2), ("write", -2))
 SWAP_WAIT = 2
-HOLD = 0
 VMEM = 16 * 1024 * 1024
 ANY = pl.BlockSpec(memory_space=pl.ANY)
 
@@ -257,9 +255,8 @@
             return down[:, a:b]
         return jnp.where(first, down[:, a:mid], down[:, mid:b])
 
-    pieces = [piece(0)]
-    pieces.append(piece(1, pieces[0]))
-    pieces += [piece(i, pieces[FIRST]) for i in range(2, total_count)]
+    pieces = [piece(0), piece(1)]
+    pieces += [piece(i, pieces[1]) for i in range(2, total_count)]
     waiting = [shifted(pieces[i], "dp", 1) for i in range(QUEUE)]
     landed, crossed, mates, crossed_mates = [], {}, {}, {}
 
@@ -319,8 +316,6 @@
             pass_other(0, now)
     there, given = activated(side, value, [tied(block, now) for block in sent], True)
     there_mate = mate(given)
-    if HOLD:
-        there_mate = tied(there_mate, crossed[count + 1])
 
     ready = {}
 

time: 135 us -> 134 us (level)
    select_n x3 -> x2, other arithmetic: 4.89 us -> 3.78 us  [piece(): return jnp.where(first, gate[:, a:b], up[:, a:b])]
  transfers between devices with their start and end apart: 32 -> 32, of which waited for: 14 -> 14; matrix products, arithmetic and copies ran while one was open for 4% -> 3% of each run, Pallas kernels for 14% -> 14%
where the time goes in v15:
time: 134 us
  waiting for transfers between devices  80.3 us (60%)
  starting transfers between devices  27.2 us (20%)
  Pallas kernels  21 us (16%)
  other arithmetic  5.23 us (4%)
    ppermute x32, waiting for transfers between devices, shifted(): return lax.ppermute(block, axis, route)  80.3 us
    ppermute x32, starting transfers between devices, shifted(): return lax.ppermute(block, axis, route)  27.2 us
    pallas_call x10, Pallas kernels, call(): pl.pallas_call(kernel, in_specs=in_specs, out_specs=out_spec, out_shape=o...  21 us
    select_n x2, other arithmetic, piece(): return jnp.where(first, gate[:, a:b], up[:, a:b])  3.78 us
  transfers between devices with their start and end apart: 32, of which 14 were waited for; matrix products, arithmetic and copies ran while one was open for 3% of the time, Pallas kernels for 14%

profile of v15, /device:TPU:0, one launch (start us, length us, event | category | flops | bytes accessed | tf_op | source)
XLA Modules:
  0.0 134.1 jit_solution(16161642491059495781)
XLA Ops:
  2.3 3.0 %collective-permute-start.3 = (bf16[208,1024]{1,0:T(8,128)(2,1)S(1)}, bf16[208,1024]{1,0:T(8,128)(2,1)S(1)}, u32[]{:S(2)}, u32[]{:S(2)}) collective-permute-start(bf16[208,1024]{1,0:T(8,128)(2,1)S(1)} %get-tuple-element.122), channel_id=1, source_target_pairs={{12,0},{0,4},{4,8},{8,12},{13,1},{1,5},{5,9},{9,13},{14,2},{2,6},{... | collective-permute-start | bytes 1277960 | tf_op jit(solution)/shard_map/ppermute | solution.py:26
  8.4 2.1 %slice_select_fusion.2 = (bf16[208,1024]{1,0:T(8,128)(2,1)S(1)}, bf16[208,1024]{1,0:T(8,128)(2,1)S(1)}, bf16[208,1024]{1,0:T(8,128)(2,1)S(1)}, bf16[208,1024]{1,...) fusion(bf16[208,8192]{1,0:T(8,128)(2,1)S(1)} %copy-done.1, ...), kind=kLoop, calls=%fused_computation.2 | loop fusion | flops 1277952 | bytes 7667713 | tf_op jit(solution)/shard_map/jit(_where)/select_n | solution.py:250
  10.6 7.3 %collective-permute-done.3.refs_2_ = bf16[208,1024]{1,0:T(8,128)(2,1)S(1)} collective-permute-done((bf16[208,1024]{1,0:T(8,128)(2,1)S(1)}, bf16[208,1024]{1,0:T(8,128)(2,1)S(1)}, u32[]{:S(2)}, u32[]{:S(2)}) %collective-permute-start.3) | collective-permute-done | bytes 426016 | tf_op jit(solution)/shard_map/ppermute | solution.py:26
  19.7 7.4 %collective-permute-done.1.refs_4_ = bf16[208,1024]{1,0:T(8,128)(2,1)S(1)} collective-permute-done((bf16[208,1024]{1,0:T(8,128)(2,1)S(1)}, bf16[208,1024]{1,0:T(8,128)(2,1)S(1)}, u32[]{:S(2)}, u32[]{:S(2)}) %collective-permute-start.1) | collective-permute-done | bytes 426016 | tf_op jit(solution)/shard_map/ppermute | solution.py:26
  27.1 1.8 %collective-permute-start.7 = (bf16[208,1024]{1,0:T(8,128)(2,1)S(1)}, bf16[208,1024]{1,0:T(8,128)(2,1)S(1)}, u32[]{:S(2)}, u32[]{:S(2)}) collective-permute-start(bf16[208,1024]{1,0:T(8,128)(2,1)S(1)} %collective-permute-done.1.refs_4_), channel_id=1, source_target_pairs={{16,0},{0,16},{17,1},{1,17},{18,2},{2,18},{19,3},{3,19},{20,4},{4,... | collective-permute-start | bytes 1277960 | tf_op jit(solution)/shard_map/ppermute | solution.py:26
  28.9 5.5 %shard_map.46.refs_0_ = bf16[416,640]{1,0:T(8,128)(2,1)S(1)} custom-call(bf16[320,8192]{1,0:T(8,128)(2,1)S(1)} %bitcast.2, bf16[320,8192]{1,0:T(8,128)(2,1)S(1)} %collective-permute-done.refs_1_, bf16[208,8192]{1,0:T(8,128)(2,1)S(1)} %copy-done.2, bf16[208,8192]{1,0:T(8,128)(2,1)S(1)} %copy-done.1), custom_call_target="tpu_custom_call" | custom-call | flops 1 | bytes 1 | tf_op jit(solution)/shard_map/pallas_call | solution.py:51
  34.4 1.8 %collective-permute-done.5.refs_6_ = bf16[208,1024]{1,0:T(8,128)(2,1)S(1)} collective-permute-done((bf16[208,1024]{1,0:T(8,128)(2,1)S(1)}, bf16[208,1024]{1,0:T(8,128)(2,1)S(1)}, u32[]{:S(2)}, u32[]{:S(2)}) %collective-permute-start.5) | collective-permute-done | bytes 426016 | tf_op jit(solution)/shard_map/ppermute | solution.py:26
  39.4 5.9 %collective-permute-done.4.refs_8_ = bf16[208,1024]{1,0:T(8,128)(2,1)S(1)} collective-permute-done((bf16[208,1024]{1,0:T(8,128)(2,1)S(1)}, bf16[208,1024]{1,0:T(8,128)(2,1)S(1)}, u32[]{:S(2)}, u32[]{:S(2)}) %collective-permute-start.4) | collective-permute-done | bytes 426016 | tf_op jit(solution)/shard_map/ppermute | solution.py:26
  45.3 1.7 %collective-permute-start.12 = (bf16[208,1024]{1,0:T(8,128)(2,1)S(1)}, bf16[208,1024]{1,0:T(8,128)(2,1)S(1)}, u32[]{:S(2)}, u32[]{:S(2)}) collective-permute-start(bf16[208,1024]{1,0:T(8,128)(2,1)S(1)} %collective-permute-done.4.refs_8_), channel_id=1, source_target_pairs={{16,0},{0,16},{17,1},{1,17},{18,2},{2,18},{19,3},{3,19},{20,4},{4,... | collective-permute-start | bytes 1277960 | tf_op jit(solution)/shard_map/ppermute | solution.py:26
  47.1 7.4 %collective-permute-done.10.refs_2_ = bf16[208,1024]{1,0:T(8,128)(2,1)S(1)} collective-permute-done((bf16[208,1024]{1,0:T(8,128)(2,1)S(1)}, bf16[208,1024]{1,0:T(8,128)(2,1)S(1)}, u32[]{:S(2)}, u32[]{:S(2)}) %collective-permute-start.10) | collective-permute-done | bytes 426016 | tf_op jit(solution)/shard_map/ppermute | solution.py:26
  56.5 7.0 %collective-permute-done.8.refs_4_ = bf16[208,1024]{1,0:T(8,128)(2,1)S(1)} collective-permute-done((bf16[208,1024]{1,0:T(8,128)(2,1)S(1)}, bf16[208,1024]{1,0:T(8,128)(2,1)S(1)}, u32[]{:S(2)}, u32[]{:S(2)}) %collective-permute-start.8) | collective-permute-done | bytes 426016 | tf_op jit(solution)/shard_map/ppermute | solution.py:26
  65.3 2.8 %shard_map.48.refs_8_ = f32[416,640]{1,0:T(8,128)S(1)} custom-call(bf16[320,8192]{1,0:T(8,128)(2,1)S(1)} %bitcast.2, bf16[320,8192]{1,0:T(8,128)(2,1)S(1)} %collective-permute-done.refs_1_, bf16[208,1024]{1,0:T(8,128)(2,1)S(1)} %collective-permute-done.3.refs_2_, bf16[208,1024]{1,0:T(8,128)(2,1)S(1)} %collective-permute-done.6.refs_3_, ...), custom_call_target="tpu_custom_call" | custom-call | flops 1 | bytes 1 | tf_op jit(solution)/shard_map/pallas_call | solution.py:51
  68.1 4.5 %collective-permute-done.14.refs_6_ = bf16[208,1024]{1,0:T(8,128)(2,1)S(1)} collective-permute-done((bf16[208,1024]{1,0:T(8,128)(2,1)S(1)}, bf16[208,1024]{1,0:T(8,128)(2,1)S(1)}, u32[]{:S(2)}, u32[]{:S(2)}) %collective-permute-start.14) | collective-permute-done | bytes 426016 | tf_op jit(solution)/shard_map/ppermute | solution.py:26
  74.4 7.4 %collective-permute-done.13.refs_2_ = bf16[208,1024]{1,0:T(8,128)(2,1)S(1)} collective-permute-done((bf16[208,1024]{1,0:T(8,128)(2,1)S(1)}, bf16[208,1024]{1,0:T(8,128)(2,1)S(1)}, u32[]{:S(2)}, u32[]{:S(2)}) %collective-permute-start.13) | collective-permute-done | bytes 426016 | tf_op jit(solution)/shard_map/ppermute | solution.py:26
  81.8 1.8 %collective-permute-start.18 = (bf16[208,1024]{1,0:T(8,128)(2,1)S(1)}, bf16[208,1024]{1,0:T(8,128)(2,1)S(1)}, u32[]{:S(2)}, u32[]{:S(2)}) collective-permute-start(bf16[208,1024]{1,0:T(8,128)(2,1)S(1)} %collective-permute-done.13.refs_2_), channel_id=1, source_target_pairs={{16,0},{0,16},{17,1},{1,17},{18,2},{2,18},{19,3},{3,19},{20,4},{4,... | collective-permute-start | bytes 1277960 | tf_op jit(solution)/shard_map/ppermute | solution.py:26
  83.6 2.2 %shard_map.49.refs_4_ = f32[416,640]{1,0:T(8,128)S(1)} custom-call(bf16[320,8192]{1,0:T(8,128)(2,1)S(1)} %bitcast.2, bf16[320,8192]{1,0:T(8,128)(2,1)S(1)} %collective-permute-done.refs_1_, bf16[208,1024]{1,0:T(8,128)(2,1)S(1)} %collective-permute-done.10.refs_2_, bf16[208,1024]{1,0:T(8,128)(2,1)S(1)} %collective-permute-done.16.refs_3_, ...), custom_call_target="tpu_custom_call" | custom-call | flops 1 | bytes 1 | tf_op jit(solution)/shard_map/pallas_call | solution.py:51
  85.7 7.5 %collective-permute-done.19.refs_2_ = bf16[208,1280]{1,0:T(8,128)(2,1)S(1)} collective-permute-done((bf16[208,1280]{1,0:T(8,128)(2,1)S(1)}, bf16[208,1280]{1,0:T(8,128)(2,1)S(1)}, u32[]{:S(2)}, u32[]{:S(2)}) %collective-permute-start.19) | collective-permute-done | bytes 532512 | tf_op jit(solution)/shard_map/ppermute | solution.py:26
  93.2 1.8 %collective-permute-start.26 = (bf16[208,1280]{1,0:T(8,128)(2,1)S(1)}, bf16[208,1280]{1,0:T(8,128)(2,1)S(1)}, u32[]{:S(2)}, u32[]{:S(2)}) collective-permute-start(bf16[208,1280]{1,0:T(8,128)(2,1)S(1)} %collective-permute-done.19.refs_2_), channel_id=1, source_target_pairs={{16,0},{0,16},{17,1},{1,17},{18,2},{2,18},{19,3},{3,19},{20,4},{4,... | collective-permute-start | bytes 1597448 | tf_op jit(solution)/shard_map/ppermute | solution.py:26
  97.4 10.6 %collective-permute-done.22.refs_6_ = bf16[208,1664]{1,0:T(8,128)(2,1)S(1)} collective-permute-done((bf16[208,1664]{1,0:T(8,128)(2,1)S(1)}, bf16[208,1664]{1,0:T(8,128)(2,1)S(1)}, u32[]{:S(2)}, u32[]{:S(2)}) %collective-permute-start.22) | collective-permute-done | bytes 692256 | tf_op jit(solution)/shard_map/ppermute | solution.py:26
  108.0 1.8 %collective-permute-start.24 = (bf16[208,1664]{1,0:T(8,128)(2,1)S(1)}, bf16[208,1664]{1,0:T(8,128)(2,1)S(1)}, u32[]{:S(2)}, u32[]{:S(2)}) collective-permute-start(bf16[208,1664]{1,0:T(8,128)(2,1)S(1)} %collective-permute-done.22.refs_6_), channel_id=1, source_target_pairs={{16,0},{0,16},{17,1},{1,17},{18,2},{2,18},{19,3},{3,19},{20,4},{4,... | collective-permute-start | bytes 2076680 | tf_op jit(solution)/shard_map/ppermute | solution.py:26
  113.1 4.0 %shard_map.52.refs_5_ = bf16[320,8192]{1,0:T(8,128)(2,1)} custom-call(s32[1]{0:T(128)} %bitcast.side_ref, bf16[320,208]{1,0:T(8,128)(2,1)S(1)} %get-tuple-element.103.refs_0_, bf16[320,208]{1,0:T(8,128)(2,1)S(1)} %collective-permute-done.23.refs_1_, bf16[208,1280]{1,0:T(8,128)(2,1)S(1)} %collective-permute-done.19.refs_2_, ...), custom_call_target="tpu_custom_call" | custom-call | flops 1 | bytes 1 | tf_op jit(solution)/shard_map/pallas_call | solution.py:51
  118.7 9.4 %collective-permute-done.30.refs_2_ = bf16[208,2304]{1,0:T(8,128)(2,1)S(1)} collective-permute-done((bf16[208,2304]{1,0:T(8,128)(2,1)S(1)}, bf16[208,2304]{1,0:T(8,128)(2,1)S(1)}, u32[]{:S(2)}, u32[]{:S(2)}) %collective-permute-start.30) | collective-permute-done | bytes 958496 | tf_op jit(solution)/shard_map/ppermute | solution.py:26
  128.5 2.0 %collective-permute-done.31.refs_3_ = bf16[208,2304]{1,0:T(8,128)(2,1)S(1)} collective-permute-done((bf16[208,2304]{1,0:T(8,128)(2,1)S(1)}, bf16[208,2304]{1,0:T(8,128)(2,1)S(1)}, u32[]{:S(2)}, u32[]{:S(2)}) %collective-permute-start.31) | collective-permute-done | bytes 958496 | tf_op jit(solution)/shard_map/ppermute | solution.py:26
  130.6 1.8 %shard_map.54.refs_5_ = bf16[320,8192]{1,0:T(8,128)(2,1)} custom-call(s32[1]{0:T(128)} %bitcast.side_ref, bf16[320,208]{1,0:T(8,128)(2,1)S(1)} %get-tuple-element.103.refs_0_, bf16[320,208]{1,0:T(8,128)(2,1)S(1)} %collective-permute-done.23.refs_1_, bf16[208,2304]{1,0:T(8,128)(2,1)S(1)} %collective-permute-done.30.refs_2_, ...), custom_call_target="tpu_custom_call", output_to_operand_aliasing={{}: (6, {})} | custom-call | flops 1 | bytes 1 | tf_op jit(solution)/shard_map/pallas_call | solution.py:51
  (66 shorter events, 25.5 us)
Async XLA Ops:
  1.7 25.4 %collective-permute-start = (bf16[320,8192]{1,0:T(8,128)(2,1)}, bf16[320,8192]{1,0:T(8,128)(2,1)S(1)}, u32[]{:S(2)}, u32[]{:S(2)}) collective-permute-start(bf16[320,8192]{1,0:T(8,128)(2,1)} %refs_0_.6), channel_id=1, source_target_pairs={{1,0},{0,1},{3,2},{2,3},{5,4},{4,5},{7,6},{6,7},{9,8},{8,9},{11,10... | collective-permute-start | bytes 15728648 | tf_op jit(solution)/shard_map/ppermute | solution.py:26
  2.2 24.9 %collective-permute-start.2 = (bf16[208,8192]{1,0:T(8,128)(2,1)}, bf16[208,8192]{1,0:T(8,128)(2,1)S(1)}, u32[]{:S(2)}, u32[]{:S(2)}) collective-permute-start(bf16[208,8192]{1,0:T(8,128)(2,1)} %refs_2_.3), channel_id=1, source_target_pairs={{1,0},{0,1},{3,2},{2,3},{5,4},{4,5},{7,6},{6,7},{9,8},{8,9},{11,10... | collective-permute-start | bytes 10223624 | tf_op jit(solution)/shard_map/ppermute | solution.py:26
  2.3 15.6 %collective-permute-start.3 = (bf16[208,1024]{1,0:T(8,128)(2,1)S(1)}, bf16[208,1024]{1,0:T(8,128)(2,1)S(1)}, u32[]{:S(2)}, u32[]{:S(2)}) collective-permute-start(bf16[208,1024]{1,0:T(8,128)(2,1)S(1)} %get-tuple-element.122), channel_id=1, source_target_pairs={{12,0},{0,4},{4,8},{8,12},{13,1},{1,5},{5,9},{9,13},{14,2},{2,6},{... | collective-permute-start | bytes 1277960 | tf_op jit(solution)/shard_map/ppermute | solution.py:26
  5.3 21.8 %collective-permute-start.1 = (bf16[208,1024]{1,0:T(8,128)(2,1)S(1)}, bf16[208,1024]{1,0:T(8,128)(2,1)S(1)}, u32[]{:S(2)}, u32[]{:S(2)}) collective-permute-start(bf16[208,1024]{1,0:T(8,128)(2,1)S(1)} %get-tuple-element.121), channel_id=1, source_target_pairs={{12,0},{0,4},{4,8},{8,12},{13,1},{1,5},{5,9},{9,13},{14,2},{2,6},{... | collective-permute-start | bytes 1277960 | tf_op jit(solution)/shard_map/ppermute | solution.py:26
  17.9 18.3 %collective-permute-start.5 = (bf16[208,1024]{1,0:T(8,128)(2,1)S(1)}, bf16[208,1024]{1,0:T(8,128)(2,1)S(1)}, u32[]{:S(2)}, u32[]{:S(2)}) collective-permute-start(bf16[208,1024]{1,0:T(8,128)(2,1)S(1)} %get-tuple-element.67), channel_id=1, source_target_pairs={{12,0},{0,4},{4,8},{8,12},{13,1},{1,5},{5,9},{9,13},{14,2},{2,6},{... | collective-permute-start | bytes 1277960 | tf_op jit(solution)/shard_map/ppermute | solution.py:26
  17.9 18.2 %collective-permute-start.6 = (bf16[208,1024]{1,0:T(8,128)(2,1)S(1)}, bf16[208,1024]{1,0:T(8,128)(2,1)S(1)}, u32[]{:S(2)}, u32[]{:S(2)}) collective-permute-start(bf16[208,1024]{1,0:T(8,128)(2,1)S(1)} %collective-permute-done.3.refs_2_), channel_id=1, source_target_pairs={{16,0},{0,16},{17,1},{1,17},{18,2},{2,18},{19,3},{3,19},{20,4},{4,... | collective-permute-start | bytes 1277960 | tf_op jit(solution)/shard_map/ppermute | solution.py:26
  27.0 18.3 %collective-permute-start.4 = (bf16[208,1024]{1,0:T(8,128)(2,1)S(1)}, bf16[208,1024]{1,0:T(8,128)(2,1)S(1)}, u32[]{:S(2)}, u32[]{:S(2)}) collective-permute-start(bf16[208,1024]{1,0:T(8,128)(2,1)S(1)} %get-tuple-element.66), channel_id=1, source_target_pairs={{12,0},{0,4},{4,8},{8,12},{13,1},{1,5},{5,9},{9,13},{14,2},{2,6},{... | collective-permute-start | bytes 1277960 | tf_op jit(solution)/shard_map/ppermute | solution.py:26
  27.1 18.2 %collective-permute-start.7 = (bf16[208,1024]{1,0:T(8,128)(2,1)S(1)}, bf16[208,1024]{1,0:T(8,128)(2,1)S(1)}, u32[]{:S(2)}, u32[]{:S(2)}) collective-permute-start(bf16[208,1024]{1,0:T(8,128)(2,1)S(1)} %collective-permute-done.1.refs_4_), channel_id=1, source_target_pairs={{16,0},{0,16},{17,1},{1,17},{18,2},{2,18},{19,3},{3,19},{20,4},{4,... | collective-permute-start | bytes 1277960 | tf_op jit(solution)/shard_map/ppermute | solution.py:26
  36.2 18.3 %collective-permute-start.10 = (bf16[208,1024]{1,0:T(8,128)(2,1)S(1)}, bf16[208,1024]{1,0:T(8,128)(2,1)S(1)}, u32[]{:S(2)}, u32[]{:S(2)}) collective-permute-start(bf16[208,1024]{1,0:T(8,128)(2,1)S(1)} %get-tuple-element.72), channel_id=1, source_target_pairs={{12,0},{0,4},{4,8},{8,12},{13,1},{1,5},{5,9},{9,13},{14,2},{2,6},{... | collective-permute-start | bytes 1277960 | tf_op jit(solution)/shard_map/ppermute | solution.py:26
  36.2 18.2 %collective-permute-start.11 = (bf16[208,1024]{1,0:T(8,128)(2,1)S(1)}, bf16[208,1024]{1,0:T(8,128)(2,1)S(1)}, u32[]{:S(2)}, u32[]{:S(2)}) collective-permute-start(bf16[208,1024]{1,0:T(8,128)(2,1)S(1)} %collective-permute-done.5.refs_6_), channel_id=1, source_target_pairs={{16,0},{0,16},{17,1},{1,17},{18,2},{2,18},{19,3},{3,19},{20,4},{4,... | collective-permute-start | bytes 1277960 | tf_op jit(solution)/shard_map/ppermute | solution.py:26
  37.9 18.3 %collective-permute-start.9 = (bf16[416,640]{1,0:T(8,128)(2,1)S(1)}, bf16[416,640]{1,0:T(8,128)(2,1)S(1)}, u32[]{:S(2)}, u32[]{:S(2)}) collective-permute-start(bf16[416,640]{1,0:T(8,128)(2,1)S(1)} %shard_map.46.refs_0_), channel_id=1, source_target_pairs={{2,0},{0,2},{3,1},{1,3},{6,4},{4,6},{7,5},{5,7},{10,8},{8,10},{11,... | collective-permute-start | bytes 1597448 | tf_op jit(solution)/shard_map/ppermute | solution.py:26
  45.3 18.3 %collective-permute-start.8 = (bf16[208,1024]{1,0:T(8,128)(2,1)S(1)}, bf16[208,1024]{1,0:T(8,128)(2,1)S(1)}, u32[]{:S(2)}, u32[]{:S(2)}) collective-permute-start(bf16[208,1024]{1,0:T(8,128)(2,1)S(1)} %get-tuple-element.71), channel_id=1, source_target_pairs={{12,0},{0,4},{4,8},{8,12},{13,1},{1,5},{5,9},{9,13},{14,2},{2,6},{... | collective-permute-start | bytes 1277960 | tf_op jit(solution)/shard_map/ppermute | solution.py:26
  45.3 18.2 %collective-permute-start.12 = (bf16[208,1024]{1,0:T(8,128)(2,1)S(1)}, bf16[208,1024]{1,0:T(8,128)(2,1)S(1)}, u32[]{:S(2)}, u32[]{:S(2)}) collective-permute-start(bf16[208,1024]{1,0:T(8,128)(2,1)S(1)} %collective-permute-done.4.refs_8_), channel_id=1, source_target_pairs={{16,0},{0,16},{17,1},{1,17},{18,2},{2,18},{19,3},{3,19},{20,4},{4,... | collective-permute-start | bytes 1277960 | tf_op jit(solution)/shard_map/ppermute | solution.py:26
  54.4 18.3 %collective-permute-start.14 = (bf16[208,1024]{1,0:T(8,128)(2,1)S(1)}, bf16[208,1024]{1,0:T(8,128)(2,1)S(1)}, u32[]{:S(2)}, u32[]{:S(2)}) collective-permute-start(bf16[208,1024]{1,0:T(8,128)(2,1)S(1)} %get-tuple-element.78), channel_id=1, source_target_pairs={{12,0},{0,4},{4,8},{8,12},{13,1},{1,5},{5,9},{9,13},{14,2},{2,6},{... | collective-permute-start | bytes 1277960 | tf_op jit(solution)/shard_map/ppermute | solution.py:26
  54.4 18.2 %collective-permute-start.16 = (bf16[208,1024]{1,0:T(8,128)(2,1)S(1)}, bf16[208,1024]{1,0:T(8,128)(2,1)S(1)}, u32[]{:S(2)}, u32[]{:S(2)}) collective-permute-start(bf16[208,1024]{1,0:T(8,128)(2,1)S(1)} %collective-permute-done.10.refs_2_), channel_id=1, source_target_pairs={{16,0},{0,16},{17,1},{1,17},{18,2},{2,18},{19,3},{3,19},{20,4},{4,... | collective-permute-start | bytes 1277960 | tf_op jit(solution)/shard_map/ppermute | solution.py:26
  63.5 18.3 %collective-permute-start.13 = (bf16[208,1024]{1,0:T(8,128)(2,1)S(1)}, bf16[208,1024]{1,0:T(8,128)(2,1)S(1)}, u32[]{:S(2)}, u32[]{:S(2)}) collective-permute-start(bf16[208,1024]{1,0:T(8,128)(2,1)S(1)} %get-tuple-element.77), channel_id=1, source_target_pairs={{12,0},{0,4},{4,8},{8,12},{13,1},{1,5},{5,9},{9,13},{14,2},{2,6},{... | collective-permute-start | bytes 1277960 | tf_op jit(solution)/shard_map/ppermute | solution.py:26
  63.6 18.2 %collective-permute-start.17 = (bf16[208,1024]{1,0:T(8,128)(2,1)S(1)}, bf16[208,1024]{1,0:T(8,128)(2,1)S(1)}, u32[]{:S(2)}, u32[]{:S(2)}) collective-permute-start(bf16[208,1024]{1,0:T(8,128)(2,1)S(1)} %collective-permute-done.8.refs_4_), channel_id=1, source_target_pairs={{16,0},{0,16},{17,1},{1,17},{18,2},{2,18},{19,3},{3,19},{20,4},{4,... | collective-permute-start | bytes 1277960 | tf_op jit(solution)/shard_map/ppermute | solution.py:26
  72.7 20.5 %collective-permute-start.19 = (bf16[208,1280]{1,0:T(8,128)(2,1)S(1)}, bf16[208,1280]{1,0:T(8,128)(2,1)S(1)}, u32[]{:S(2)}, u32[]{:S(2)}) collective-permute-start(bf16[208,1280]{1,0:T(8,128)(2,1)S(1)} %slice_select_fusion.1), channel_id=1, source_target_pairs={{12,0},{0,4},{4,8},{8,12},{13,1},{1,5},{5,9},{9,13},{14,2},{2,6},{... | collective-permute-start | bytes 1597448 | tf_op jit(solution)/shard_map/ppermute | solution.py:26
  81.8 13.2 %collective-permute-start.18 = (bf16[208,1024]{1,0:T(8,128)(2,1)S(1)}, bf16[208,1024]{1,0:T(8,128)(2,1)S(1)}, u32[]{:S(2)}, u32[]{:S(2)}) collective-permute-start(bf16[208,1024]{1,0:T(8,128)(2,1)S(1)} %collective-permute-done.13.refs_2_), channel_id=1, source_target_pairs={{16,0},{0,16},{17,1},{1,17},{18,2},{2,18},{19,3},{3,19},{20,4},{4,... | collective-permute-start | bytes 1277960 | tf_op jit(solution)/shard_map/ppermute | solution.py:26
  83.6 24.5 %collective-permute-start.22 = (bf16[208,1664]{1,0:T(8,128)(2,1)S(1)}, bf16[208,1664]{1,0:T(8,128)(2,1)S(1)}, u32[]{:S(2)}, u32[]{:S(2)}) collective-permute-start(bf16[208,1664]{1,0:T(8,128)(2,1)S(1)} %slice_select_fusion), channel_id=1, source_target_pairs={{12,0},{0,4},{4,8},{8,12},{13,1},{1,5},{5,9},{9,13},{14,2},{2,6},{... | collective-permute-start | bytes 2076680 | tf_op jit(solution)/shard_map/ppermute | solution.py:26
  93.2 16.6 %collective-permute-start.26 = (bf16[208,1280]{1,0:T(8,128)(2,1)S(1)}, bf16[208,1280]{1,0:T(8,128)(2,1)S(1)}, u32[]{:S(2)}, u32[]{:S(2)}) collective-permute-start(bf16[208,1280]{1,0:T(8,128)(2,1)S(1)} %collective-permute-done.19.refs_2_), channel_id=1, source_target_pairs={{16,0},{0,16},{17,1},{1,17},{18,2},{2,18},{19,3},{3,19},{20,4},{4,... | collective-permute-start | bytes 1597448 | tf_op jit(solution)/shard_map/ppermute | solution.py:26
  95.9 14.2 %collective-permute-start.21 = (bf16[416,640]{1,0:T(8,128)(2,1)S(1)}, bf16[416,640]{1,0:T(8,128)(2,1)S(1)}, u32[]{:S(2)}, u32[]{:S(2)}) collective-permute-start(bf16[416,640]{1,0:T(8,128)(2,1)S(1)} %shard_map.50.refs_0_), channel_id=1, source_target_pairs={{2,0},{0,2},{3,1},{1,3},{6,4},{4,6},{7,5},{5,7},{10,8},{8,10},{11,... | collective-permute-start | bytes 1597448 | tf_op jit(solution)/shard_map/ppermute | solution.py:26
  97.4 30.6 %collective-permute-start.30 = (bf16[208,2304]{1,0:T(8,128)(2,1)S(1)}, bf16[208,2304]{1,0:T(8,128)(2,1)S(1)}, u32[]{:S(2)}, u32[]{:S(2)}) collective-permute-start(bf16[208,2304]{1,0:T(8,128)(2,1)S(1)} %slice.83), channel_id=1, source_target_pairs={{12,0},{0,4},{4,8},{8,12},{13,1},{1,5},{5,9},{9,13},{14,2},{2,6},{... | collective-permute-start | bytes 2875400 | tf_op jit(solution)/shard_map/ppermute | solution.py:26
  108.0 20.0 %collective-permute-start.24 = (bf16[208,1664]{1,0:T(8,128)(2,1)S(1)}, bf16[208,1664]{1,0:T(8,128)(2,1)S(1)}, u32[]{:S(2)}, u32[]{:S(2)}) collective-permute-start(bf16[208,1664]{1,0:T(8,128)(2,1)S(1)} %collective-permute-done.22.refs_6_), channel_id=1, source_target_pairs={{16,0},{0,16},{17,1},{1,17},{18,2},{2,18},{19,3},{3,19},{20,4},{4,... | collective-permute-start | bytes 2076680 | tf_op jit(solution)/shard_map/ppermute | solution.py:26
  (13 other events, 108.6 us)

commit v16 on v15

--- a/solution.py
+++ b/solution.py
@@ -8,13 +8,13 @@
 from jax.sharding import PartitionSpec as P
 
 FEATURE_SHARES = (1,) * 8
-LANE_SHARES = (10, 13, 9)
+LANE_SHARES = (10, 14, 8)
 WHOLES = 1
 QUEUE = 2
 OWN, OWN_SUM, OWN_MATE = 1, 4, 6
 BATCHES = ((5, 0, 4), (7, 4, 7), (8, 7, 8))
 PASS = (8, 9)
-TAIL = (("own", 1), ("write", 0, -1, 1), ("ready", 2, -2), ("other", 1), ("last", 1), ("write", 2), ("write", -2))
+TAIL = (("own", 1), ("write", 0, -1, 1), ("ready", 2, -2), ("other", 1), ("last",), ("write", 2), ("write", -2))
 SWAP_WAIT = 2
 VMEM = 16 * 1024 * 1024
 ANY = pl.BlockSpec(memory_space=pl.ANY)

time: 134 us -> 133 us (level)
  transfers between devices with their start and end apart: 32 -> 32, of which waited for: 14 -> 15; matrix products, arithmetic and copies ran while one was open for 3% -> 3% of each run, Pallas kernels for 14% -> 14%
where the time goes in v16:
time: 133 us
  waiting for transfers between devices  79.5 us (60%)
  starting transfers between devices  26.8 us (20%)
  Pallas kernels  20.7 us (16%)
  other arithmetic  5.26 us (4%)
    ppermute x32, waiting for transfers between devices, shifted(): return lax.ppermute(block, axis, route)  79.5 us
    ppermute x32, starting transfers between devices, shifted(): return lax.ppermute(block, axis, route)  26.8 us
    pallas_call x10, Pallas kernels, call(): pl.pallas_call(kernel, in_specs=in_specs, out_specs=out_spec, out_shape=o...  20.7 us
    select_n x2, other arithmetic, piece(): return jnp.where(first, gate[:, a:b], up[:, a:b])  3.78 us
  transfers between devices with their start and end apart: 32, of which 15 were waited for; matrix products, arithmetic and copies ran while one was open for 3% of the time, Pallas kernels for 14%

profile of v16, /device:TPU:0, one launch (start us, length us, event | category | flops | bytes accessed | tf_op | source)
XLA Modules:
  0.0 132.7 jit_solution(13784596554451435892)
XLA Ops:
  2.3 3.0 %collective-permute-start.3 = (bf16[208,1024]{1,0:T(8,128)(2,1)S(1)}, bf16[208,1024]{1,0:T(8,128)(2,1)S(1)}, u32[]{:S(2)}, u32[]{:S(2)}) collective-permute-start(bf16[208,1024]{1,0:T(8,128)(2,1)S(1)} %get-tuple-element.122), channel_id=1, source_target_pairs={{12,0},{0,4},{4,8},{8,12},{13,1},{1,5},{5,9},{9,13},{14,2},{2,6},{... | collective-permute-start | bytes 1277960 | tf_op jit(solution)/shard_map/ppermute | solution.py:26
  8.4 2.1 %slice_select_fusion.2 = (bf16[208,1024]{1,0:T(8,128)(2,1)S(1)}, bf16[208,1024]{1,0:T(8,128)(2,1)S(1)}, bf16[208,1024]{1,0:T(8,128)(2,1)S(1)}, bf16[208,1024]{1,...) fusion(bf16[208,8192]{1,0:T(8,128)(2,1)S(1)} %copy-done.1, ...), kind=kLoop, calls=%fused_computation.2 | loop fusion | flops 1277952 | bytes 7667713 | tf_op jit(solution)/shard_map/jit(_where)/select_n | solution.py:250
  10.6 7.3 %collective-permute-done.3.refs_2_ = bf16[208,1024]{1,0:T(8,128)(2,1)S(1)} collective-permute-done((bf16[208,1024]{1,0:T(8,128)(2,1)S(1)}, bf16[208,1024]{1,0:T(8,128)(2,1)S(1)}, u32[]{:S(2)}, u32[]{:S(2)}) %collective-permute-start.3) | collective-permute-done | bytes 426016 | tf_op jit(solution)/shard_map/ppermute | solution.py:26
  17.9 1.7 %collective-permute-start.6 = (bf16[208,1024]{1,0:T(8,128)(2,1)S(1)}, bf16[208,1024]{1,0:T(8,128)(2,1)S(1)}, u32[]{:S(2)}, u32[]{:S(2)}) collective-permute-start(bf16[208,1024]{1,0:T(8,128)(2,1)S(1)} %collective-permute-done.3.refs_2_), channel_id=1, source_target_pairs={{16,0},{0,16},{17,1},{1,17},{18,2},{2,18},{19,3},{3,19},{20,4},{4,... | collective-permute-start | bytes 1277960 | tf_op jit(solution)/shard_map/ppermute | solution.py:26
  19.7 7.4 %collective-permute-done.1.refs_4_ = bf16[208,1024]{1,0:T(8,128)(2,1)S(1)} collective-permute-done((bf16[208,1024]{1,0:T(8,128)(2,1)S(1)}, bf16[208,1024]{1,0:T(8,128)(2,1)S(1)}, u32[]{:S(2)}, u32[]{:S(2)}) %collective-permute-start.1) | collective-permute-done | bytes 426016 | tf_op jit(solution)/shard_map/ppermute | solution.py:26
  27.1 1.8 %collective-permute-start.7 = (bf16[208,1024]{1,0:T(8,128)(2,1)S(1)}, bf16[208,1024]{1,0:T(8,128)(2,1)S(1)}, u32[]{:S(2)}, u32[]{:S(2)}) collective-permute-start(bf16[208,1024]{1,0:T(8,128)(2,1)S(1)} %collective-permute-done.1.refs_4_), channel_id=1, source_target_pairs={{16,0},{0,16},{17,1},{1,17},{18,2},{2,18},{19,3},{3,19},{20,4},{4,... | collective-permute-start | bytes 1277960 | tf_op jit(solution)/shard_map/ppermute | solution.py:26
  28.9 5.5 %shard_map.46.refs_0_ = bf16[416,640]{1,0:T(8,128)(2,1)S(1)} custom-call(bf16[320,8192]{1,0:T(8,128)(2,1)S(1)} %bitcast.2, bf16[320,8192]{1,0:T(8,128)(2,1)S(1)} %collective-permute-done.refs_1_, bf16[208,8192]{1,0:T(8,128)(2,1)S(1)} %copy-done.2, bf16[208,8192]{1,0:T(8,128)(2,1)S(1)} %copy-done.1), custom_call_target="tpu_custom_call" | custom-call | flops 1 | bytes 1 | tf_op jit(solution)/shard_map/pallas_call | solution.py:51
  34.4 1.8 %collective-permute-done.5.refs_6_ = bf16[208,1024]{1,0:T(8,128)(2,1)S(1)} collective-permute-done((bf16[208,1024]{1,0:T(8,128)(2,1)S(1)}, bf16[208,1024]{1,0:T(8,128)(2,1)S(1)}, u32[]{:S(2)}, u32[]{:S(2)}) %collective-permute-start.5) | collective-permute-done | bytes 426016 | tf_op jit(solution)/shard_map/ppermute | solution.py:26
  39.4 5.9 %collective-permute-done.4.refs_8_ = bf16[208,1024]{1,0:T(8,128)(2,1)S(1)} collective-permute-done((bf16[208,1024]{1,0:T(8,128)(2,1)S(1)}, bf16[208,1024]{1,0:T(8,128)(2,1)S(1)}, u32[]{:S(2)}, u32[]{:S(2)}) %collective-permute-start.4) | collective-permute-done | bytes 426016 | tf_op jit(solution)/shard_map/ppermute | solution.py:26
  45.3 1.7 %collective-permute-start.12 = (bf16[208,1024]{1,0:T(8,128)(2,1)S(1)}, bf16[208,1024]{1,0:T(8,128)(2,1)S(1)}, u32[]{:S(2)}, u32[]{:S(2)}) collective-permute-start(bf16[208,1024]{1,0:T(8,128)(2,1)S(1)} %collective-permute-done.4.refs_8_), channel_id=1, source_target_pairs={{16,0},{0,16},{17,1},{1,17},{18,2},{2,18},{19,3},{3,19},{20,4},{4,... | collective-permute-start | bytes 1277960 | tf_op jit(solution)/shard_map/ppermute | solution.py:26
  47.1 7.4 %collective-permute-done.10.refs_2_ = bf16[208,1024]{1,0:T(8,128)(2,1)S(1)} collective-permute-done((bf16[208,1024]{1,0:T(8,128)(2,1)S(1)}, bf16[208,1024]{1,0:T(8,128)(2,1)S(1)}, u32[]{:S(2)}, u32[]{:S(2)}) %collective-permute-start.10) | collective-permute-done | bytes 426016 | tf_op jit(solution)/shard_map/ppermute | solution.py:26
  56.5 7.0 %collective-permute-done.8.refs_4_ = bf16[208,1024]{1,0:T(8,128)(2,1)S(1)} collective-permute-done((bf16[208,1024]{1,0:T(8,128)(2,1)S(1)}, bf16[208,1024]{1,0:T(8,128)(2,1)S(1)}, u32[]{:S(2)}, u32[]{:S(2)}) %collective-permute-start.8) | collective-permute-done | bytes 426016 | tf_op jit(solution)/shard_map/ppermute | solution.py:26
  65.3 2.8 %shard_map.48.refs_8_ = f32[416,640]{1,0:T(8,128)S(1)} custom-call(bf16[320,8192]{1,0:T(8,128)(2,1)S(1)} %bitcast.2, bf16[320,8192]{1,0:T(8,128)(2,1)S(1)} %collective-permute-done.refs_1_, bf16[208,1024]{1,0:T(8,128)(2,1)S(1)} %collective-permute-done.3.refs_2_, bf16[208,1024]{1,0:T(8,128)(2,1)S(1)} %collective-permute-done.6.refs_3_, ...), custom_call_target="tpu_custom_call" | custom-call | flops 1 | bytes 1 | tf_op jit(solution)/shard_map/pallas_call | solution.py:51
  68.1 4.5 %collective-permute-done.14.refs_6_ = bf16[208,1024]{1,0:T(8,128)(2,1)S(1)} collective-permute-done((bf16[208,1024]{1,0:T(8,128)(2,1)S(1)}, bf16[208,1024]{1,0:T(8,128)(2,1)S(1)}, u32[]{:S(2)}, u32[]{:S(2)}) %collective-permute-start.14) | collective-permute-done | bytes 426016 | tf_op jit(solution)/shard_map/ppermute | solution.py:26
  72.7 1.7 %collective-permute-start.20 = (bf16[208,1024]{1,0:T(8,128)(2,1)S(1)}, bf16[208,1024]{1,0:T(8,128)(2,1)S(1)}, u32[]{:S(2)}, u32[]{:S(2)}) collective-permute-start(bf16[208,1024]{1,0:T(8,128)(2,1)S(1)} %collective-permute-done.14.refs_6_), channel_id=1, source_target_pairs={{16,0},{0,16},{17,1},{1,17},{18,2},{2,18},{19,3},{3,19},{20,4},{4,... | collective-permute-start | bytes 1277960 | tf_op jit(solution)/shard_map/ppermute | solution.py:26
  74.4 7.4 %collective-permute-done.13.refs_2_ = bf16[208,1024]{1,0:T(8,128)(2,1)S(1)} collective-permute-done((bf16[208,1024]{1,0:T(8,128)(2,1)S(1)}, bf16[208,1024]{1,0:T(8,128)(2,1)S(1)}, u32[]{:S(2)}, u32[]{:S(2)}) %collective-permute-start.13) | collective-permute-done | bytes 426016 | tf_op jit(solution)/shard_map/ppermute | solution.py:26
  81.8 1.8 %collective-permute-start.18 = (bf16[208,1024]{1,0:T(8,128)(2,1)S(1)}, bf16[208,1024]{1,0:T(8,128)(2,1)S(1)}, u32[]{:S(2)}, u32[]{:S(2)}) collective-permute-start(bf16[208,1024]{1,0:T(8,128)(2,1)S(1)} %collective-permute-done.13.refs_2_), channel_id=1, source_target_pairs={{16,0},{0,16},{17,1},{1,17},{18,2},{2,18},{19,3},{3,19},{20,4},{4,... | collective-permute-start | bytes 1277960 | tf_op jit(solution)/shard_map/ppermute | solution.py:26
  83.6 2.2 %shard_map.49.refs_4_ = f32[416,640]{1,0:T(8,128)S(1)} custom-call(bf16[320,8192]{1,0:T(8,128)(2,1)S(1)} %bitcast.2, bf16[320,8192]{1,0:T(8,128)(2,1)S(1)} %collective-permute-done.refs_1_, bf16[208,1024]{1,0:T(8,128)(2,1)S(1)} %collective-permute-done.10.refs_2_, bf16[208,1024]{1,0:T(8,128)(2,1)S(1)} %collective-permute-done.16.refs_3_, ...), custom_call_target="tpu_custom_call" | custom-call | flops 1 | bytes 1 | tf_op jit(solution)/shard_map/pallas_call | solution.py:51
  85.7 7.5 %collective-permute-done.19.refs_2_ = bf16[208,1280]{1,0:T(8,128)(2,1)S(1)} collective-permute-done((bf16[208,1280]{1,0:T(8,128)(2,1)S(1)}, bf16[208,1280]{1,0:T(8,128)(2,1)S(1)}, u32[]{:S(2)}, u32[]{:S(2)}) %collective-permute-start.19) | collective-permute-done | bytes 532512 | tf_op jit(solution)/shard_map/ppermute | solution.py:26
  93.2 1.8 %collective-permute-start.26 = (bf16[208,1280]{1,0:T(8,128)(2,1)S(1)}, bf16[208,1280]{1,0:T(8,128)(2,1)S(1)}, u32[]{:S(2)}, u32[]{:S(2)}) collective-permute-start(bf16[208,1280]{1,0:T(8,128)(2,1)S(1)} %collective-permute-done.19.refs_2_), channel_id=1, source_target_pairs={{16,0},{0,16},{17,1},{1,17},{18,2},{2,18},{19,3},{3,19},{20,4},{4,... | collective-permute-start | bytes 1597448 | tf_op jit(solution)/shard_map/ppermute | solution.py:26
  97.4 11.8 %collective-permute-done.22.refs_6_ = bf16[208,1792]{1,0:T(8,128)(2,1)S(1)} collective-permute-done((bf16[208,1792]{1,0:T(8,128)(2,1)S(1)}, bf16[208,1792]{1,0:T(8,128)(2,1)S(1)}, u32[]{:S(2)}, u32[]{:S(2)}) %collective-permute-start.22) | collective-permute-done | bytes 745504 | tf_op jit(solution)/shard_map/ppermute | solution.py:26
  109.7 1.8 %collective-permute-start.24 = (bf16[208,1792]{1,0:T(8,128)(2,1)S(1)}, bf16[208,1792]{1,0:T(8,128)(2,1)S(1)}, u32[]{:S(2)}, u32[]{:S(2)}) collective-permute-start(bf16[208,1792]{1,0:T(8,128)(2,1)S(1)} %collective-permute-done.22.refs_6_), channel_id=1, source_target_pairs={{16,0},{0,16},{17,1},{1,17},{18,2},{2,18},{19,3},{3,19},{20,4},{4,... | collective-permute-start | bytes 2236424 | tf_op jit(solution)/shard_map/ppermute | solution.py:26
  113.6 4.0 %shard_map.52.refs_5_ = bf16[320,8192]{1,0:T(8,128)(2,1)} custom-call(s32[1]{0:T(128)} %bitcast.side_ref, bf16[320,208]{1,0:T(8,128)(2,1)S(1)} %get-tuple-element.103.refs_0_, bf16[320,208]{1,0:T(8,128)(2,1)S(1)} %collective-permute-done.23.refs_1_, bf16[208,1280]{1,0:T(8,128)(2,1)S(1)} %collective-permute-done.19.refs_2_, ...), custom_call_target="tpu_custom_call" | custom-call | flops 1 | bytes 1 | tf_op jit(solution)/shard_map/pallas_call | solution.py:51
  119.1 7.8 %collective-permute-done.30.refs_2_ = bf16[208,2048]{1,0:T(8,128)(2,1)S(1)} collective-permute-done((bf16[208,2048]{1,0:T(8,128)(2,1)S(1)}, bf16[208,2048]{1,0:T(8,128)(2,1)S(1)}, u32[]{:S(2)}, u32[]{:S(2)}) %collective-permute-start.30) | collective-permute-done | bytes 852000 | tf_op jit(solution)/shard_map/ppermute | solution.py:26
  (66 shorter events, 24.9 us)
Async XLA Ops:
  1.7 25.4 %collective-permute-start = (bf16[320,8192]{1,0:T(8,128)(2,1)}, bf16[320,8192]{1,0:T(8,128)(2,1)S(1)}, u32[]{:S(2)}, u32[]{:S(2)}) collective-permute-start(bf16[320,8192]{1,0:T(8,128)(2,1)} %refs_0_.6), channel_id=1, source_target_pairs={{1,0},{0,1},{3,2},{2,3},{5,4},{4,5},{7,6},{6,7},{9,8},{8,9},{11,10... | collective-permute-start | bytes 15728648 | tf_op jit(solution)/shard_map/ppermute | solution.py:26
  2.2 24.9 %collective-permute-start.2 = (bf16[208,8192]{1,0:T(8,128)(2,1)}, bf16[208,8192]{1,0:T(8,128)(2,1)S(1)}, u32[]{:S(2)}, u32[]{:S(2)}) collective-permute-start(bf16[208,8192]{1,0:T(8,128)(2,1)} %refs_2_.3), channel_id=1, source_target_pairs={{1,0},{0,1},{3,2},{2,3},{5,4},{4,5},{7,6},{6,7},{9,8},{8,9},{11,10... | collective-permute-start | bytes 10223624 | tf_op jit(solution)/shard_map/ppermute | solution.py:26
  2.3 15.6 %collective-permute-start.3 = (bf16[208,1024]{1,0:T(8,128)(2,1)S(1)}, bf16[208,1024]{1,0:T(8,128)(2,1)S(1)}, u32[]{:S(2)}, u32[]{:S(2)}) collective-permute-start(bf16[208,1024]{1,0:T(8,128)(2,1)S(1)} %get-tuple-element.122), channel_id=1, source_target_pairs={{12,0},{0,4},{4,8},{8,12},{13,1},{1,5},{5,9},{9,13},{14,2},{2,6},{... | collective-permute-start | bytes 1277960 | tf_op jit(solution)/shard_map/ppermute | solution.py:26
  5.3 21.8 %collective-permute-start.1 = (bf16[208,1024]{1,0:T(8,128)(2,1)S(1)}, bf16[208,1024]{1,0:T(8,128)(2,1)S(1)}, u32[]{:S(2)}, u32[]{:S(2)}) collective-permute-start(bf16[208,1024]{1,0:T(8,128)(2,1)S(1)} %get-tuple-element.121), channel_id=1, source_target_pairs={{12,0},{0,4},{4,8},{8,12},{13,1},{1,5},{5,9},{9,13},{14,2},{2,6},{... | collective-permute-start | bytes 1277960 | tf_op jit(solution)/shard_map/ppermute | solution.py:26
  17.9 18.3 %collective-permute-start.5 = (bf16[208,1024]{1,0:T(8,128)(2,1)S(1)}, bf16[208,1024]{1,0:T(8,128)(2,1)S(1)}, u32[]{:S(2)}, u32[]{:S(2)}) collective-permute-start(bf16[208,1024]{1,0:T(8,128)(2,1)S(1)} %get-tuple-element.67), channel_id=1, source_target_pairs={{12,0},{0,4},{4,8},{8,12},{13,1},{1,5},{5,9},{9,13},{14,2},{2,6},{... | collective-permute-start | bytes 1277960 | tf_op jit(solution)/shard_map/ppermute | solution.py:26
  17.9 18.2 %collective-permute-start.6 = (bf16[208,1024]{1,0:T(8,128)(2,1)S(1)}, bf16[208,1024]{1,0:T(8,128)(2,1)S(1)}, u32[]{:S(2)}, u32[]{:S(2)}) collective-permute-start(bf16[208,1024]{1,0:T(8,128)(2,1)S(1)} %collective-permute-done.3.refs_2_), channel_id=1, source_target_pairs={{16,0},{0,16},{17,1},{1,17},{18,2},{2,18},{19,3},{3,19},{20,4},{4,... | collective-permute-start | bytes 1277960 | tf_op jit(solution)/shard_map/ppermute | solution.py:26
  27.0 18.3 %collective-permute-start.4 = (bf16[208,1024]{1,0:T(8,128)(2,1)S(1)}, bf16[208,1024]{1,0:T(8,128)(2,1)S(1)}, u32[]{:S(2)}, u32[]{:S(2)}) collective-permute-start(bf16[208,1024]{1,0:T(8,128)(2,1)S(1)} %get-tuple-element.66), channel_id=1, source_target_pairs={{12,0},{0,4},{4,8},{8,12},{13,1},{1,5},{5,9},{9,13},{14,2},{2,6},{... | collective-permute-start | bytes 1277960 | tf_op jit(solution)/shard_map/ppermute | solution.py:26
  27.1 18.2 %collective-permute-start.7 = (bf16[208,1024]{1,0:T(8,128)(2,1)S(1)}, bf16[208,1024]{1,0:T(8,128)(2,1)S(1)}, u32[]{:S(2)}, u32[]{:S(2)}) collective-permute-start(bf16[208,1024]{1,0:T(8,128)(2,1)S(1)} %collective-permute-done.1.refs_4_), channel_id=1, source_target_pairs={{16,0},{0,16},{17,1},{1,17},{18,2},{2,18},{19,3},{3,19},{20,4},{4,... | collective-permute-start | bytes 1277960 | tf_op jit(solution)/shard_map/ppermute | solution.py:26
  36.2 18.3 %collective-permute-start.10 = (bf16[208,1024]{1,0:T(8,128)(2,1)S(1)}, bf16[208,1024]{1,0:T(8,128)(2,1)S(1)}, u32[]{:S(2)}, u32[]{:S(2)}) collective-permute-start(bf16[208,1024]{1,0:T(8,128)(2,1)S(1)} %get-tuple-element.72), channel_id=1, source_target_pairs={{12,0},{0,4},{4,8},{8,12},{13,1},{1,5},{5,9},{9,13},{14,2},{2,6},{... | collective-permute-start | bytes 1277960 | tf_op jit(solution)/shard_map/ppermute | solution.py:26
  36.2 18.2 %collective-permute-start.11 = (bf16[208,1024]{1,0:T(8,128)(2,1)S(1)}, bf16[208,1024]{1,0:T(8,128)(2,1)S(1)}, u32[]{:S(2)}, u32[]{:S(2)}) collective-permute-start(bf16[208,1024]{1,0:T(8,128)(2,1)S(1)} %collective-permute-done.5.refs_6_), channel_id=1, source_target_pairs={{16,0},{0,16},{17,1},{1,17},{18,2},{2,18},{19,3},{3,19},{20,4},{4,... | collective-permute-start | bytes 1277960 | tf_op jit(solution)/shard_map/ppermute | solution.py:26
  37.9 18.3 %collective-permute-start.9 = (bf16[416,640]{1,0:T(8,128)(2,1)S(1)}, bf16[416,640]{1,0:T(8,128)(2,1)S(1)}, u32[]{:S(2)}, u32[]{:S(2)}) collective-permute-start(bf16[416,640]{1,0:T(8,128)(2,1)S(1)} %shard_map.46.refs_0_), channel_id=1, source_target_pairs={{2,0},{0,2},{3,1},{1,3},{6,4},{4,6},{7,5},{5,7},{10,8},{8,10},{11,... | collective-permute-start | bytes 1597448 | tf_op jit(solution)/shard_map/ppermute | solution.py:26
  45.3 18.3 %collective-permute-start.8 = (bf16[208,1024]{1,0:T(8,128)(2,1)S(1)}, bf16[208,1024]{1,0:T(8,128)(2,1)S(1)}, u32[]{:S(2)}, u32[]{:S(2)}) collective-permute-start(bf16[208,1024]{1,0:T(8,128)(2,1)S(1)} %get-tuple-element.71), channel_id=1, source_target_pairs={{12,0},{0,4},{4,8},{8,12},{13,1},{1,5},{5,9},{9,13},{14,2},{2,6},{... | collective-permute-start | bytes 1277960 | tf_op jit(solution)/shard_map/ppermute | solution.py:26
  45.3 18.2 %collective-permute-start.12 = (bf16[208,1024]{1,0:T(8,128)(2,1)S(1)}, bf16[208,1024]{1,0:T(8,128)(2,1)S(1)}, u32[]{:S(2)}, u32[]{:S(2)}) collective-permute-start(bf16[208,1024]{1,0:T(8,128)(2,1)S(1)} %collective-permute-done.4.refs_8_), channel_id=1, source_target_pairs={{16,0},{0,16},{17,1},{1,17},{18,2},{2,18},{19,3},{3,19},{20,4},{4,... | collective-permute-start | bytes 1277960 | tf_op jit(solution)/shard_map/ppermute | solution.py:26
  54.4 18.3 %collective-permute-start.14 = (bf16[208,1024]{1,0:T(8,128)(2,1)S(1)}, bf16[208,1024]{1,0:T(8,128)(2,1)S(1)}, u32[]{:S(2)}, u32[]{:S(2)}) collective-permute-start(bf16[208,1024]{1,0:T(8,128)(2,1)S(1)} %get-tuple-element.78), channel_id=1, source_target_pairs={{12,0},{0,4},{4,8},{8,12},{13,1},{1,5},{5,9},{9,13},{14,2},{2,6},{... | collective-permute-start | bytes 1277960 | tf_op jit(solution)/shard_map/ppermute | solution.py:26
  54.4 18.2 %collective-permute-start.16 = (bf16[208,1024]{1,0:T(8,128)(2,1)S(1)}, bf16[208,1024]{1,0:T(8,128)(2,1)S(1)}, u32[]{:S(2)}, u32[]{:S(2)}) collective-permute-start(bf16[208,1024]{1,0:T(8,128)(2,1)S(1)} %collective-permute-done.10.refs_2_), channel_id=1, source_target_pairs={{16,0},{0,16},{17,1},{1,17},{18,2},{2,18},{19,3},{3,19},{20,4},{4,... | collective-permute-start | bytes 1277960 | tf_op jit(solution)/shard_map/ppermute | solution.py:26
  63.5 18.3 %collective-permute-start.13 = (bf16[208,1024]{1,0:T(8,128)(2,1)S(1)}, bf16[208,1024]{1,0:T(8,128)(2,1)S(1)}, u32[]{:S(2)}, u32[]{:S(2)}) collective-permute-start(bf16[208,1024]{1,0:T(8,128)(2,1)S(1)} %get-tuple-element.77), channel_id=1, source_target_pairs={{12,0},{0,4},{4,8},{8,12},{13,1},{1,5},{5,9},{9,13},{14,2},{2,6},{... | collective-permute-start | bytes 1277960 | tf_op jit(solution)/shard_map/ppermute | solution.py:26
  63.6 18.2 %collective-permute-start.17 = (bf16[208,1024]{1,0:T(8,128)(2,1)S(1)}, bf16[208,1024]{1,0:T(8,128)(2,1)S(1)}, u32[]{:S(2)}, u32[]{:S(2)}) collective-permute-start(bf16[208,1024]{1,0:T(8,128)(2,1)S(1)} %collective-permute-done.8.refs_4_), channel_id=1, source_target_pairs={{16,0},{0,16},{17,1},{1,17},{18,2},{2,18},{19,3},{3,19},{20,4},{4,... | collective-permute-start | bytes 1277960 | tf_op jit(solution)/shard_map/ppermute | solution.py:26
  72.7 20.5 %collective-permute-start.19 = (bf16[208,1280]{1,0:T(8,128)(2,1)S(1)}, bf16[208,1280]{1,0:T(8,128)(2,1)S(1)}, u32[]{:S(2)}, u32[]{:S(2)}) collective-permute-start(bf16[208,1280]{1,0:T(8,128)(2,1)S(1)} %slice_select_fusion.1), channel_id=1, source_target_pairs={{12,0},{0,4},{4,8},{8,12},{13,1},{1,5},{5,9},{9,13},{14,2},{2,6},{... | collective-permute-start | bytes 1597448 | tf_op jit(solution)/shard_map/ppermute | solution.py:26
  81.8 13.2 %collective-permute-start.18 = (bf16[208,1024]{1,0:T(8,128)(2,1)S(1)}, bf16[208,1024]{1,0:T(8,128)(2,1)S(1)}, u32[]{:S(2)}, u32[]{:S(2)}) collective-permute-start(bf16[208,1024]{1,0:T(8,128)(2,1)S(1)} %collective-permute-done.13.refs_2_), channel_id=1, source_target_pairs={{16,0},{0,16},{17,1},{1,17},{18,2},{2,18},{19,3},{3,19},{20,4},{4,... | collective-permute-start | bytes 1277960 | tf_op jit(solution)/shard_map/ppermute | solution.py:26
  83.6 25.6 %collective-permute-start.22 = (bf16[208,1792]{1,0:T(8,128)(2,1)S(1)}, bf16[208,1792]{1,0:T(8,128)(2,1)S(1)}, u32[]{:S(2)}, u32[]{:S(2)}) collective-permute-start(bf16[208,1792]{1,0:T(8,128)(2,1)S(1)} %slice_select_fusion), channel_id=1, source_target_pairs={{12,0},{0,4},{4,8},{8,12},{13,1},{1,5},{5,9},{9,13},{14,2},{2,6},{... | collective-permute-start | bytes 2236424 | tf_op jit(solution)/shard_map/ppermute | solution.py:26
  93.2 16.5 %collective-permute-start.26 = (bf16[208,1280]{1,0:T(8,128)(2,1)S(1)}, bf16[208,1280]{1,0:T(8,128)(2,1)S(1)}, u32[]{:S(2)}, u32[]{:S(2)}) collective-permute-start(bf16[208,1280]{1,0:T(8,128)(2,1)S(1)} %collective-permute-done.19.refs_2_), channel_id=1, source_target_pairs={{16,0},{0,16},{17,1},{1,17},{18,2},{2,18},{19,3},{3,19},{20,4},{4,... | collective-permute-start | bytes 1597448 | tf_op jit(solution)/shard_map/ppermute | solution.py:26
  95.9 15.6 %collective-permute-start.21 = (bf16[416,640]{1,0:T(8,128)(2,1)S(1)}, bf16[416,640]{1,0:T(8,128)(2,1)S(1)}, u32[]{:S(2)}, u32[]{:S(2)}) collective-permute-start(bf16[416,640]{1,0:T(8,128)(2,1)S(1)} %shard_map.50.refs_0_), channel_id=1, source_target_pairs={{2,0},{0,2},{3,1},{1,3},{6,4},{4,6},{7,5},{5,7},{10,8},{8,10},{11,... | collective-permute-start | bytes 1597448 | tf_op jit(solution)/shard_map/ppermute | solution.py:26
  97.4 29.5 %collective-permute-start.30 = (bf16[208,2048]{1,0:T(8,128)(2,1)S(1)}, bf16[208,2048]{1,0:T(8,128)(2,1)S(1)}, u32[]{:S(2)}, u32[]{:S(2)}) collective-permute-start(bf16[208,2048]{1,0:T(8,128)(2,1)S(1)} %slice.83), channel_id=1, source_target_pairs={{12,0},{0,4},{4,8},{8,12},{13,1},{1,5},{5,9},{9,13},{14,2},{2,6},{... | collective-permute-start | bytes 2555912 | tf_op jit(solution)/shard_map/ppermute | solution.py:26
  109.7 18.6 %collective-permute-start.24 = (bf16[208,1792]{1,0:T(8,128)(2,1)S(1)}, bf16[208,1792]{1,0:T(8,128)(2,1)S(1)}, u32[]{:S(2)}, u32[]{:S(2)}) collective-permute-start(bf16[208,1792]{1,0:T(8,128)(2,1)S(1)} %collective-permute-done.22.refs_6_), channel_id=1, source_target_pairs={{16,0},{0,16},{17,1},{1,17},{18,2},{2,18},{19,3},{3,19},{20,4},{4,... | collective-permute-start | bytes 2236424 | tf_op jit(solution)/shard_map/ppermute | solution.py:26
  (13 other events, 106.3 us)

commit v17 on v16

--- a/solution.py
+++ b/solution.py
@@ -135,8 +135,8 @@
 def blocks_of(parts):
     found = []
     for i, (a, lanes, half, others) in enumerate(parts):
-        for lane in range(0, lanes, 512):
-            size = min(512, lanes - lane)
+        for lane in range(0, lanes, 256):
+            size = min(256, lanes - lane)
             fixed = a + lane + (half if others else 0)
             found.append((i, lane, size, (fixed, -half if others else half)))
     return found

time: 133 us -> 133 us (level)
  no operation moved by 1% of the time
where the time goes in v17:
time: 133 us
  waiting for transfers between devices  79.5 us (60%)
  starting transfers between devices  26.8 us (20%)
  Pallas kernels  20.8 us (16%)
  other arithmetic  5.26 us (4%)
    ppermute x32, waiting for transfers between devices, shifted(): return lax.ppermute(block, axis, route)  79.5 us
    ppermute x32, starting transfers between devices, shifted(): return lax.ppermute(block, axis, route)  26.8 us
    pallas_call x10, Pallas kernels, call(): pl.pallas_call(kernel, in_specs=in_specs, out_specs=out_spec, out_shape=o...  20.8 us
    select_n x2, other arithmetic, piece(): return jnp.where(first, gate[:, a:b], up[:, a:b])  3.78 us
  transfers between devices with their start and end apart: 32, of which 15 were waited for; matrix products, arithmetic and copies ran while one was open for 3% of the time, Pallas kernels for 14%

profile of v17, /device:TPU:0, one launch (start us, length us, event | category | flops | bytes accessed | tf_op | source)
XLA Modules:
  0.0 132.7 jit_solution(16377088677536995381)
XLA Ops:
  2.3 3.0 %collective-permute-start.3 = (bf16[208,1024]{1,0:T(8,128)(2,1)S(1)}, bf16[208,1024]{1,0:T(8,128)(2,1)S(1)}, u32[]{:S(2)}, u32[]{:S(2)}) collective-permute-start(bf16[208,1024]{1,0:T(8,128)(2,1)S(1)} %get-tuple-element.122), channel_id=1, source_target_pairs={{12,0},{0,4},{4,8},{8,12},{13,1},{1,5},{5,9},{9,13},{14,2},{2,6},{... | collective-permute-start | bytes 1277960 | tf_op jit(solution)/shard_map/ppermute | solution.py:26
  8.4 2.1 %slice_select_fusion.2 = (bf16[208,1024]{1,0:T(8,128)(2,1)S(1)}, bf16[208,1024]{1,0:T(8,128)(2,1)S(1)}, bf16[208,1024]{1,0:T(8,128)(2,1)S(1)}, bf16[208,1024]{1,...) fusion(bf16[208,8192]{1,0:T(8,128)(2,1)S(1)} %copy-done.1, ...), kind=kLoop, calls=%fused_computation.2 | loop fusion | flops 1277952 | bytes 7667713 | tf_op jit(solution)/shard_map/jit(_where)/select_n | solution.py:250
  10.6 7.3 %collective-permute-done.3.refs_2_ = bf16[208,1024]{1,0:T(8,128)(2,1)S(1)} collective-permute-done((bf16[208,1024]{1,0:T(8,128)(2,1)S(1)}, bf16[208,1024]{1,0:T(8,128)(2,1)S(1)}, u32[]{:S(2)}, u32[]{:S(2)}) %collective-permute-start.3) | collective-permute-done | bytes 426016 | tf_op jit(solution)/shard_map/ppermute | solution.py:26
  17.9 1.7 %collective-permute-start.6 = (bf16[208,1024]{1,0:T(8,128)(2,1)S(1)}, bf16[208,1024]{1,0:T(8,128)(2,1)S(1)}, u32[]{:S(2)}, u32[]{:S(2)}) collective-permute-start(bf16[208,1024]{1,0:T(8,128)(2,1)S(1)} %collective-permute-done.3.refs_2_), channel_id=1, source_target_pairs={{16,0},{0,16},{17,1},{1,17},{18,2},{2,18},{19,3},{3,19},{20,4},{4,... | collective-permute-start | bytes 1277960 | tf_op jit(solution)/shard_map/ppermute | solution.py:26
  19.7 7.4 %collective-permute-done.1.refs_4_ = bf16[208,1024]{1,0:T(8,128)(2,1)S(1)} collective-permute-done((bf16[208,1024]{1,0:T(8,128)(2,1)S(1)}, bf16[208,1024]{1,0:T(8,128)(2,1)S(1)}, u32[]{:S(2)}, u32[]{:S(2)}) %collective-permute-start.1) | collective-permute-done | bytes 426016 | tf_op jit(solution)/shard_map/ppermute | solution.py:26
  27.1 1.8 %collective-permute-start.7 = (bf16[208,1024]{1,0:T(8,128)(2,1)S(1)}, bf16[208,1024]{1,0:T(8,128)(2,1)S(1)}, u32[]{:S(2)}, u32[]{:S(2)}) collective-permute-start(bf16[208,1024]{1,0:T(8,128)(2,1)S(1)} %collective-permute-done.1.refs_4_), channel_id=1, source_target_pairs={{16,0},{0,16},{17,1},{1,17},{18,2},{2,18},{19,3},{3,19},{20,4},{4,... | collective-permute-start | bytes 1277960 | tf_op jit(solution)/shard_map/ppermute | solution.py:26
  28.9 5.5 %shard_map.46.refs_0_ = bf16[416,640]{1,0:T(8,128)(2,1)S(1)} custom-call(bf16[320,8192]{1,0:T(8,128)(2,1)S(1)} %bitcast.2, bf16[320,8192]{1,0:T(8,128)(2,1)S(1)} %collective-permute-done.refs_1_, bf16[208,8192]{1,0:T(8,128)(2,1)S(1)} %copy-done.2, bf16[208,8192]{1,0:T(8,128)(2,1)S(1)} %copy-done.1), custom_call_target="tpu_custom_call" | custom-call | flops 1 | bytes 1 | tf_op jit(solution)/shard_map/pallas_call | solution.py:51
  34.4 1.8 %collective-permute-done.5.refs_6_ = bf16[208,1024]{1,0:T(8,128)(2,1)S(1)} collective-permute-done((bf16[208,1024]{1,0:T(8,128)(2,1)S(1)}, bf16[208,1024]{1,0:T(8,128)(2,1)S(1)}, u32[]{:S(2)}, u32[]{:S(2)}) %collective-permute-start.5) | collective-permute-done | bytes 426016 | tf_op jit(solution)/shard_map/ppermute | solution.py:26
  39.4 5.9 %collective-permute-done.4.refs_8_ = bf16[208,1024]{1,0:T(8,128)(2,1)S(1)} collective-permute-done((bf16[208,1024]{1,0:T(8,128)(2,1)S(1)}, bf16[208,1024]{1,0:T(8,128)(2,1)S(1)}, u32[]{:S(2)}, u32[]{:S(2)}) %collective-permute-start.4) | collective-permute-done | bytes 426016 | tf_op jit(solution)/shard_map/ppermute | solution.py:26
  45.3 1.7 %collective-permute-start.12 = (bf16[208,1024]{1,0:T(8,128)(2,1)S(1)}, bf16[208,1024]{1,0:T(8,128)(2,1)S(1)}, u32[]{:S(2)}, u32[]{:S(2)}) collective-permute-start(bf16[208,1024]{1,0:T(8,128)(2,1)S(1)} %collective-permute-done.4.refs_8_), channel_id=1, source_target_pairs={{16,0},{0,16},{17,1},{1,17},{18,2},{2,18},{19,3},{3,19},{20,4},{4,... | collective-permute-start | bytes 1277960 | tf_op jit(solution)/shard_map/ppermute | solution.py:26
  47.1 7.4 %collective-permute-done.10.refs_2_ = bf16[208,1024]{1,0:T(8,128)(2,1)S(1)} collective-permute-done((bf16[208,1024]{1,0:T(8,128)(2,1)S(1)}, bf16[208,1024]{1,0:T(8,128)(2,1)S(1)}, u32[]{:S(2)}, u32[]{:S(2)}) %collective-permute-start.10) | collective-permute-done | bytes 426016 | tf_op jit(solution)/shard_map/ppermute | solution.py:26
  56.5 7.0 %collective-permute-done.8.refs_4_ = bf16[208,1024]{1,0:T(8,128)(2,1)S(1)} collective-permute-done((bf16[208,1024]{1,0:T(8,128)(2,1)S(1)}, bf16[208,1024]{1,0:T(8,128)(2,1)S(1)}, u32[]{:S(2)}, u32[]{:S(2)}) %collective-permute-start.8) | collective-permute-done | bytes 426016 | tf_op jit(solution)/shard_map/ppermute | solution.py:26
  65.3 2.8 %shard_map.48.refs_8_ = f32[416,640]{1,0:T(8,128)S(1)} custom-call(bf16[320,8192]{1,0:T(8,128)(2,1)S(1)} %bitcast.2, bf16[320,8192]{1,0:T(8,128)(2,1)S(1)} %collective-permute-done.refs_1_, bf16[208,1024]{1,0:T(8,128)(2,1)S(1)} %collective-permute-done.3.refs_2_, bf16[208,1024]{1,0:T(8,128)(2,1)S(1)} %collective-permute-done.6.refs_3_, ...), custom_call_target="tpu_custom_call" | custom-call | flops 1 | bytes 1 | tf_op jit(solution)/shard_map/pallas_call | solution.py:51
  68.1 4.5 %collective-permute-done.14.refs_6_ = bf16[208,1024]{1,0:T(8,128)(2,1)S(1)} collective-permute-done((bf16[208,1024]{1,0:T(8,128)(2,1)S(1)}, bf16[208,1024]{1,0:T(8,128)(2,1)S(1)}, u32[]{:S(2)}, u32[]{:S(2)}) %collective-permute-start.14) | collective-permute-done | bytes 426016 | tf_op jit(solution)/shard_map/ppermute | solution.py:26
  72.7 1.7 %collective-permute-start.20 = (bf16[208,1024]{1,0:T(8,128)(2,1)S(1)}, bf16[208,1024]{1,0:T(8,128)(2,1)S(1)}, u32[]{:S(2)}, u32[]{:S(2)}) collective-permute-start(bf16[208,1024]{1,0:T(8,128)(2,1)S(1)} %collective-permute-done.14.refs_6_), channel_id=1, source_target_pairs={{16,0},{0,16},{17,1},{1,17},{18,2},{2,18},{19,3},{3,19},{20,4},{4,... | collective-permute-start | bytes 1277960 | tf_op jit(solution)/shard_map/ppermute | solution.py:26
  74.4 7.4 %collective-permute-done.13.refs_2_ = bf16[208,1024]{1,0:T(8,128)(2,1)S(1)} collective-permute-done((bf16[208,1024]{1,0:T(8,128)(2,1)S(1)}, bf16[208,1024]{1,0:T(8,128)(2,1)S(1)}, u32[]{:S(2)}, u32[]{:S(2)}) %collective-permute-start.13) | collective-permute-done | bytes 426016 | tf_op jit(solution)/shard_map/ppermute | solution.py:26
  81.8 1.8 %collective-permute-start.18 = (bf16[208,1024]{1,0:T(8,128)(2,1)S(1)}, bf16[208,1024]{1,0:T(8,128)(2,1)S(1)}, u32[]{:S(2)}, u32[]{:S(2)}) collective-permute-start(bf16[208,1024]{1,0:T(8,128)(2,1)S(1)} %collective-permute-done.13.refs_2_), channel_id=1, source_target_pairs={{16,0},{0,16},{17,1},{1,17},{18,2},{2,18},{19,3},{3,19},{20,4},{4,... | collective-permute-start | bytes 1277960 | tf_op jit(solution)/shard_map/ppermute | solution.py:26
  83.6 2.2 %shard_map.49.refs_4_ = f32[416,640]{1,0:T(8,128)S(1)} custom-call(bf16[320,8192]{1,0:T(8,128)(2,1)S(1)} %bitcast.2, bf16[320,8192]{1,0:T(8,128)(2,1)S(1)} %collective-permute-done.refs_1_, bf16[208,1024]{1,0:T(8,128)(2,1)S(1)} %collective-permute-done.10.refs_2_, bf16[208,1024]{1,0:T(8,128)(2,1)S(1)} %collective-permute-done.16.refs_3_, ...), custom_call_target="tpu_custom_call" | custom-call | flops 1 | bytes 1 | tf_op jit(solution)/shard_map/pallas_call | solution.py:51
  85.7 7.5 %collective-permute-done.19.refs_2_ = bf16[208,1280]{1,0:T(8,128)(2,1)S(1)} collective-permute-done((bf16[208,1280]{1,0:T(8,128)(2,1)S(1)}, bf16[208,1280]{1,0:T(8,128)(2,1)S(1)}, u32[]{:S(2)}, u32[]{:S(2)}) %collective-permute-start.19) | collective-permute-done | bytes 532512 | tf_op jit(solution)/shard_map/ppermute | solution.py:26
  93.2 1.8 %collective-permute-start.26 = (bf16[208,1280]{1,0:T(8,128)(2,1)S(1)}, bf16[208,1280]{1,0:T(8,128)(2,1)S(1)}, u32[]{:S(2)}, u32[]{:S(2)}) collective-permute-start(bf16[208,1280]{1,0:T(8,128)(2,1)S(1)} %collective-permute-done.19.refs_2_), channel_id=1, source_target_pairs={{16,0},{0,16},{17,1},{1,17},{18,2},{2,18},{19,3},{3,19},{20,4},{4,... | collective-permute-start | bytes 1597448 | tf_op jit(solution)/shard_map/ppermute | solution.py:26
  97.4 11.8 %collective-permute-done.22.refs_6_ = bf16[208,1792]{1,0:T(8,128)(2,1)S(1)} collective-permute-done((bf16[208,1792]{1,0:T(8,128)(2,1)S(1)}, bf16[208,1792]{1,0:T(8,128)(2,1)S(1)}, u32[]{:S(2)}, u32[]{:S(2)}) %collective-permute-start.22) | collective-permute-done | bytes 745504 | tf_op jit(solution)/shard_map/ppermute | solution.py:26
  109.7 1.8 %collective-permute-start.24 = (bf16[208,1792]{1,0:T(8,128)(2,1)S(1)}, bf16[208,1792]{1,0:T(8,128)(2,1)S(1)}, u32[]{:S(2)}, u32[]{:S(2)}) collective-permute-start(bf16[208,1792]{1,0:T(8,128)(2,1)S(1)} %collective-permute-done.22.refs_6_), channel_id=1, source_target_pairs={{16,0},{0,16},{17,1},{1,17},{18,2},{2,18},{19,3},{3,19},{20,4},{4,... | collective-permute-start | bytes 2236424 | tf_op jit(solution)/shard_map/ppermute | solution.py:26
  113.6 4.0 %shard_map.52.refs_5_ = bf16[320,8192]{1,0:T(8,128)(2,1)} custom-call(s32[1]{0:T(128)} %bitcast.side_ref, bf16[320,208]{1,0:T(8,128)(2,1)S(1)} %get-tuple-element.103.refs_0_, bf16[320,208]{1,0:T(8,128)(2,1)S(1)} %collective-permute-done.23.refs_1_, bf16[208,1280]{1,0:T(8,128)(2,1)S(1)} %collective-permute-done.19.refs_2_, ...), custom_call_target="tpu_custom_call" | custom-call | flops 1 | bytes 1 | tf_op jit(solution)/shard_map/pallas_call | solution.py:51
  119.1 7.8 %collective-permute-done.30.refs_2_ = bf16[208,2048]{1,0:T(8,128)(2,1)S(1)} collective-permute-done((bf16[208,2048]{1,0:T(8,128)(2,1)S(1)}, bf16[208,2048]{1,0:T(8,128)(2,1)S(1)}, u32[]{:S(2)}, u32[]{:S(2)}) %collective-permute-start.30) | collective-permute-done | bytes 852000 | tf_op jit(solution)/shard_map/ppermute | solution.py:26
  (66 shorter events, 24.9 us)
Async XLA Ops:
  1.7 25.4 %collective-permute-start = (bf16[320,8192]{1,0:T(8,128)(2,1)}, bf16[320,8192]{1,0:T(8,128)(2,1)S(1)}, u32[]{:S(2)}, u32[]{:S(2)}) collective-permute-start(bf16[320,8192]{1,0:T(8,128)(2,1)} %refs_0_.6), channel_id=1, source_target_pairs={{1,0},{0,1},{3,2},{2,3},{5,4},{4,5},{7,6},{6,7},{9,8},{8,9},{11,10... | collective-permute-start | bytes 15728648 | tf_op jit(solution)/shard_map/ppermute | solution.py:26
  2.2 24.9 %collective-permute-start.2 = (bf16[208,8192]{1,0:T(8,128)(2,1)}, bf16[208,8192]{1,0:T(8,128)(2,1)S(1)}, u32[]{:S(2)}, u32[]{:S(2)}) collective-permute-start(bf16[208,8192]{1,0:T(8,128)(2,1)} %refs_2_.3), channel_id=1, source_target_pairs={{1,0},{0,1},{3,2},{2,3},{5,4},{4,5},{7,6},{6,7},{9,8},{8,9},{11,10... | collective-permute-start | bytes 10223624 | tf_op jit(solution)/shard_map/ppermute | solution.py:26
  2.3 15.6 %collective-permute-start.3 = (bf16[208,1024]{1,0:T(8,128)(2,1)S(1)}, bf16[208,1024]{1,0:T(8,128)(2,1)S(1)}, u32[]{:S(2)}, u32[]{:S(2)}) collective-permute-start(bf16[208,1024]{1,0:T(8,128)(2,1)S(1)} %get-tuple-element.122), channel_id=1, source_target_pairs={{12,0},{0,4},{4,8},{8,12},{13,1},{1,5},{5,9},{9,13},{14,2},{2,6},{... | collective-permute-start | bytes 1277960 | tf_op jit(solution)/shard_map/ppermute | solution.py:26
  5.3 21.8 %collective-permute-start.1 = (bf16[208,1024]{1,0:T(8,128)(2,1)S(1)}, bf16[208,1024]{1,0:T(8,128)(2,1)S(1)}, u32[]{:S(2)}, u32[]{:S(2)}) collective-permute-start(bf16[208,1024]{1,0:T(8,128)(2,1)S(1)} %get-tuple-element.121), channel_id=1, source_target_pairs={{12,0},{0,4},{4,8},{8,12},{13,1},{1,5},{5,9},{9,13},{14,2},{2,6},{... | collective-permute-start | bytes 1277960 | tf_op jit(solution)/shard_map/ppermute | solution.py:26
  17.9 18.3 %collective-permute-start.5 = (bf16[208,1024]{1,0:T(8,128)(2,1)S(1)}, bf16[208,1024]{1,0:T(8,128)(2,1)S(1)}, u32[]{:S(2)}, u32[]{:S(2)}) collective-permute-start(bf16[208,1024]{1,0:T(8,128)(2,1)S(1)} %get-tuple-element.67), channel_id=1, source_target_pairs={{12,0},{0,4},{4,8},{8,12},{13,1},{1,5},{5,9},{9,13},{14,2},{2,6},{... | collective-permute-start | bytes 1277960 | tf_op jit(solution)/shard_map/ppermute | solution.py:26
  17.9 18.2 %collective-permute-start.6 = (bf16[208,1024]{1,0:T(8,128)(2,1)S(1)}, bf16[208,1024]{1,0:T(8,128)(2,1)S(1)}, u32[]{:S(2)}, u32[]{:S(2)}) collective-permute-start(bf16[208,1024]{1,0:T(8,128)(2,1)S(1)} %collective-permute-done.3.refs_2_), channel_id=1, source_target_pairs={{16,0},{0,16},{17,1},{1,17},{18,2},{2,18},{19,3},{3,19},{20,4},{4,... | collective-permute-start | bytes 1277960 | tf_op jit(solution)/shard_map/ppermute | solution.py:26
  27.0 18.3 %collective-permute-start.4 = (bf16[208,1024]{1,0:T(8,128)(2,1)S(1)}, bf16[208,1024]{1,0:T(8,128)(2,1)S(1)}, u32[]{:S(2)}, u32[]{:S(2)}) collective-permute-start(bf16[208,1024]{1,0:T(8,128)(2,1)S(1)} %get-tuple-element.66), channel_id=1, source_target_pairs={{12,0},{0,4},{4,8},{8,12},{13,1},{1,5},{5,9},{9,13},{14,2},{2,6},{... | collective-permute-start | bytes 1277960 | tf_op jit(solution)/shard_map/ppermute | solution.py:26
  27.1 18.2 %collective-permute-start.7 = (bf16[208,1024]{1,0:T(8,128)(2,1)S(1)}, bf16[208,1024]{1,0:T(8,128)(2,1)S(1)}, u32[]{:S(2)}, u32[]{:S(2)}) collective-permute-start(bf16[208,1024]{1,0:T(8,128)(2,1)S(1)} %collective-permute-done.1.refs_4_), channel_id=1, source_target_pairs={{16,0},{0,16},{17,1},{1,17},{18,2},{2,18},{19,3},{3,19},{20,4},{4,... | collective-permute-start | bytes 1277960 | tf_op jit(solution)/shard_map/ppermute | solution.py:26
  36.2 18.3 %collective-permute-start.10 = (bf16[208,1024]{1,0:T(8,128)(2,1)S(1)}, bf16[208,1024]{1,0:T(8,128)(2,1)S(1)}, u32[]{:S(2)}, u32[]{:S(2)}) collective-permute-start(bf16[208,1024]{1,0:T(8,128)(2,1)S(1)} %get-tuple-element.72), channel_id=1, source_target_pairs={{12,0},{0,4},{4,8},{8,12},{13,1},{1,5},{5,9},{9,13},{14,2},{2,6},{... | collective-permute-start | bytes 1277960 | tf_op jit(solution)/shard_map/ppermute | solution.py:26
  36.2 18.2 %collective-permute-start.11 = (bf16[208,1024]{1,0:T(8,128)(2,1)S(1)}, bf16[208,1024]{1,0:T(8,128)(2,1)S(1)}, u32[]{:S(2)}, u32[]{:S(2)}) collective-permute-start(bf16[208,1024]{1,0:T(8,128)(2,1)S(1)} %collective-permute-done.5.refs_6_), channel_id=1, source_target_pairs={{16,0},{0,16},{17,1},{1,17},{18,2},{2,18},{19,3},{3,19},{20,4},{4,... | collective-permute-start | bytes 1277960 | tf_op jit(solution)/shard_map/ppermute | solution.py:26
  37.9 18.3 %collective-permute-start.9 = (bf16[416,640]{1,0:T(8,128)(2,1)S(1)}, bf16[416,640]{1,0:T(8,128)(2,1)S(1)}, u32[]{:S(2)}, u32[]{:S(2)}) collective-permute-start(bf16[416,640]{1,0:T(8,128)(2,1)S(1)} %shard_map.46.refs_0_), channel_id=1, source_target_pairs={{2,0},{0,2},{3,1},{1,3},{6,4},{4,6},{7,5},{5,7},{10,8},{8,10},{11,... | collective-permute-start | bytes 1597448 | tf_op jit(solution)/shard_map/ppermute | solution.py:26
  45.3 18.3 %collective-permute-start.8 = (bf16[208,1024]{1,0:T(8,128)(2,1)S(1)}, bf16[208,1024]{1,0:T(8,128)(2,1)S(1)}, u32[]{:S(2)}, u32[]{:S(2)}) collective-permute-start(bf16[208,1024]{1,0:T(8,128)(2,1)S(1)} %get-tuple-element.71), channel_id=1, source_target_pairs={{12,0},{0,4},{4,8},{8,12},{13,1},{1,5},{5,9},{9,13},{14,2},{2,6},{... | collective-permute-start | bytes 1277960 | tf_op jit(solution)/shard_map/ppermute | solution.py:26
  45.3 18.2 %collective-permute-start.12 = (bf16[208,1024]{1,0:T(8,128)(2,1)S(1)}, bf16[208,1024]{1,0:T(8,128)(2,1)S(1)}, u32[]{:S(2)}, u32[]{:S(2)}) collective-permute-start(bf16[208,1024]{1,0:T(8,128)(2,1)S(1)} %collective-permute-done.4.refs_8_), channel_id=1, source_target_pairs={{16,0},{0,16},{17,1},{1,17},{18,2},{2,18},{19,3},{3,19},{20,4},{4,... | collective-permute-start | bytes 1277960 | tf_op jit(solution)/shard_map/ppermute | solution.py:26
  54.4 18.3 %collective-permute-start.14 = (bf16[208,1024]{1,0:T(8,128)(2,1)S(1)}, bf16[208,1024]{1,0:T(8,128)(2,1)S(1)}, u32[]{:S(2)}, u32[]{:S(2)}) collective-permute-start(bf16[208,1024]{1,0:T(8,128)(2,1)S(1)} %get-tuple-element.78), channel_id=1, source_target_pairs={{12,0},{0,4},{4,8},{8,12},{13,1},{1,5},{5,9},{9,13},{14,2},{2,6},{... | collective-permute-start | bytes 1277960 | tf_op jit(solution)/shard_map/ppermute | solution.py:26
  54.4 18.2 %collective-permute-start.16 = (bf16[208,1024]{1,0:T(8,128)(2,1)S(1)}, bf16[208,1024]{1,0:T(8,128)(2,1)S(1)}, u32[]{:S(2)}, u32[]{:S(2)}) collective-permute-start(bf16[208,1024]{1,0:T(8,128)(2,1)S(1)} %collective-permute-done.10.refs_2_), channel_id=1, source_target_pairs={{16,0},{0,16},{17,1},{1,17},{18,2},{2,18},{19,3},{3,19},{20,4},{4,... | collective-permute-start | bytes 1277960 | tf_op jit(solution)/shard_map/ppermute | solution.py:26
  63.5 18.3 %collective-permute-start.13 = (bf16[208,1024]{1,0:T(8,128)(2,1)S(1)}, bf16[208,1024]{1,0:T(8,128)(2,1)S(1)}, u32[]{:S(2)}, u32[]{:S(2)}) collective-permute-start(bf16[208,1024]{1,0:T(8,128)(2,1)S(1)} %get-tuple-element.77), channel_id=1, source_target_pairs={{12,0},{0,4},{4,8},{8,12},{13,1},{1,5},{5,9},{9,13},{14,2},{2,6},{... | collective-permute-start | bytes 1277960 | tf_op jit(solution)/shard_map/ppermute | solution.py:26
  63.6 18.2 %collective-permute-start.17 = (bf16[208,1024]{1,0:T(8,128)(2,1)S(1)}, bf16[208,1024]{1,0:T(8,128)(2,1)S(1)}, u32[]{:S(2)}, u32[]{:S(2)}) collective-permute-start(bf16[208,1024]{1,0:T(8,128)(2,1)S(1)} %collective-permute-done.8.refs_4_), channel_id=1, source_target_pairs={{16,0},{0,16},{17,1},{1,17},{18,2},{2,18},{19,3},{3,19},{20,4},{4,... | collective-permute-start | bytes 1277960 | tf_op jit(solution)/shard_map/ppermute | solution.py:26
  72.7 20.5 %collective-permute-start.19 = (bf16[208,1280]{1,0:T(8,128)(2,1)S(1)}, bf16[208,1280]{1,0:T(8,128)(2,1)S(1)}, u32[]{:S(2)}, u32[]{:S(2)}) collective-permute-start(bf16[208,1280]{1,0:T(8,128)(2,1)S(1)} %slice_select_fusion.1), channel_id=1, source_target_pairs={{12,0},{0,4},{4,8},{8,12},{13,1},{1,5},{5,9},{9,13},{14,2},{2,6},{... | collective-permute-start | bytes 1597448 | tf_op jit(solution)/shard_map/ppermute | solution.py:26
  81.8 13.2 %collective-permute-start.18 = (bf16[208,1024]{1,0:T(8,128)(2,1)S(1)}, bf16[208,1024]{1,0:T(8,128)(2,1)S(1)}, u32[]{:S(2)}, u32[]{:S(2)}) collective-permute-start(bf16[208,1024]{1,0:T(8,128)(2,1)S(1)} %collective-permute-done.13.refs_2_), channel_id=1, source_target_pairs={{16,0},{0,16},{17,1},{1,17},{18,2},{2,18},{19,3},{3,19},{20,4},{4,... | collective-permute-start | bytes 1277960 | tf_op jit(solution)/shard_map/ppermute | solution.py:26
  83.6 25.6 %collective-permute-start.22 = (bf16[208,1792]{1,0:T(8,128)(2,1)S(1)}, bf16[208,1792]{1,0:T(8,128)(2,1)S(1)}, u32[]{:S(2)}, u32[]{:S(2)}) collective-permute-start(bf16[208,1792]{1,0:T(8,128)(2,1)S(1)} %slice_select_fusion), channel_id=1, source_target_pairs={{12,0},{0,4},{4,8},{8,12},{13,1},{1,5},{5,9},{9,13},{14,2},{2,6},{... | collective-permute-start | bytes 2236424 | tf_op jit(solution)/shard_map/ppermute | solution.py:26
  93.2 16.5 %collective-permute-start.26 = (bf16[208,1280]{1,0:T(8,128)(2,1)S(1)}, bf16[208,1280]{1,0:T(8,128)(2,1)S(1)}, u32[]{:S(2)}, u32[]{:S(2)}) collective-permute-start(bf16[208,1280]{1,0:T(8,128)(2,1)S(1)} %collective-permute-done.19.refs_2_), channel_id=1, source_target_pairs={{16,0},{0,16},{17,1},{1,17},{18,2},{2,18},{19,3},{3,19},{20,4},{4,... | collective-permute-start | bytes 1597448 | tf_op jit(solution)/shard_map/ppermute | solution.py:26
  95.9 15.6 %collective-permute-start.21 = (bf16[416,640]{1,0:T(8,128)(2,1)S(1)}, bf16[416,640]{1,0:T(8,128)(2,1)S(1)}, u32[]{:S(2)}, u32[]{:S(2)}) collective-permute-start(bf16[416,640]{1,0:T(8,128)(2,1)S(1)} %shard_map.50.refs_0_), channel_id=1, source_target_pairs={{2,0},{0,2},{3,1},{1,3},{6,4},{4,6},{7,5},{5,7},{10,8},{8,10},{11,... | collective-permute-start | bytes 1597448 | tf_op jit(solution)/shard_map/ppermute | solution.py:26
  97.4 29.5 %collective-permute-start.30 = (bf16[208,2048]{1,0:T(8,128)(2,1)S(1)}, bf16[208,2048]{1,0:T(8,128)(2,1)S(1)}, u32[]{:S(2)}, u32[]{:S(2)}) collective-permute-start(bf16[208,2048]{1,0:T(8,128)(2,1)S(1)} %slice.83), channel_id=1, source_target_pairs={{12,0},{0,4},{4,8},{8,12},{13,1},{1,5},{5,9},{9,13},{14,2},{2,6},{... | collective-permute-start | bytes 2555912 | tf_op jit(solution)/shard_map/ppermute | solution.py:26
  109.7 18.6 %collective-permute-start.24 = (bf16[208,1792]{1,0:T(8,128)(2,1)S(1)}, bf16[208,1792]{1,0:T(8,128)(2,1)S(1)}, u32[]{:S(2)}, u32[]{:S(2)}) collective-permute-start(bf16[208,1792]{1,0:T(8,128)(2,1)S(1)} %collective-permute-done.22.refs_6_), channel_id=1, source_target_pairs={{16,0},{0,16},{17,1},{1,17},{18,2},{2,18},{19,3},{3,19},{20,4},{4,... | collective-permute-start | bytes 2236424 | tf_op jit(solution)/shard_map/ppermute | solution.py:26
  (13 other events, 106.4 us)
